TPU v7x, 32 devices: a whole 2x2x4 slice. The times are simulated.
32 devices in a mesh: ctx: 8 (over z, y), exp: 4 (over x, core).
Axes of the slice: x: 2, y: 2, z: 4, core: 2. Of those that a mesh axis runs over, the one named last changes fastest.
Arguments:
- inputs: bfloat16 [1024, 4096], P('ctx', 'exp'), may hold values from -6 to 6
- gate_input: bfloat16 [1024, 4096], P('ctx', 'exp')
- b_proj: bfloat16 [1024, 128], P('ctx'), may hold values from -0.5 to 0.5
- c_proj: bfloat16 [1024, 128], P('ctx'), may hold values from -6 to 6
- step_size: float32 [64, 1024], P('exp', 'ctx'), may hold values from 0.03 to 0.3
- decay_rate: float32 [64, 1024], P('exp', 'ctx'), as said below
- skip_gain: float32 [64], P('exp'), may hold values from 0.5 to 2
- start_state: float32 [64, 64, 128], P('exp'), may hold values from -3 to 3
- norm_gain: float32 [4096], P('exp'), may hold values from 0.5 to 1.5
- out_proj: bfloat16 [4096, 4096], P('exp', 'ctx'), may hold values from -0.09375 to 0.09375
- residual: bfloat16 [1024, 4096], P('ctx'), may hold values from -6 to 6
- moe_gain: float32 [4096], replicated, may hold values from 0.5 to 1.5
- w_gate: bfloat16 [8, 4096, 3584], P('ctx', None, 'exp'), may hold values from -0.09375 to 0.09375
- w_up: bfloat16 [8, 4096, 3584], P('ctx', None, 'exp'), may hold values from -0.09375 to 0.09375
- w_down: bfloat16 [8, 3584, 4096], P('ctx', 'exp'), may hold values from -0.0625 to 0.0625
- route_ids: int32 [1024, 2], P('ctx'), may hold values from 0 to 3, all different within a row; in each aligned block of 32 rows (0 to 31, 32 to 63, ...) at most 32 rows name the same one
- route_gates: float32 [1024, 2], P('ctx'), may hold values from 0.3 to 1
Outputs:
- output: bfloat16 [1024, 4096], P(('ctx', 'exp'))
Inputs may be any that keep to these rules, and one draw needn't show every extreme that they name: `route_ids`: each row names two different experts. In each aligned block of 32 rows no expert is named more than 32 times, a bound that some block reaches. `decay_rate`: Non-negative.
All inputs are finite; a program needn't handle non-finite values.
Results may differ from a plain program's by a relative error of at most 0.02.
Values may be sent and summed in bfloat16 or wider, within the bound.
No kernel may reach another device: no remote copies, remote signals or barrier semaphores. Data moves between devices by JAX's collectives and lax.ppermute only.
A program may use at most 128 MiB of HBM per device.

v0:
```python
import jax
import jax.numpy as jnp
from jax import lax
from jax.sharding import PartitionSpec as P

PAIR = 2


eps_norm = 1e-05
top_precision = lax.Precision.HIGHEST


def entering(x, axis, join, neutral):
    place = lax.axis_index(axis)
    gathered = jax.tree.map(
        lambda a, kind: lax.all_gather(a.astype(kind), axis), x, (jnp.bfloat16, jnp.bfloat16)
    )
    state = jax.tree.map(lambda a, e: jnp.zeros_like(a) + jnp.asarray(e, a.dtype), x, neutral)

    def one(hop, state):
        return join(
            state,
            jax.tree.map(
                lambda a, own: lax.dynamic_index_in_dim(a, hop, 0, False).astype(own.dtype),
                gathered,
                x,
            ),
        )

    return lax.fori_loop(0, place, one, state)


def later_state(earlier, later):
    first_decay, first_state = earlier
    second_decay, second_state = later
    return (first_decay * second_decay, second_decay[:, None, None] * first_state + second_state)


def route_ranks(quarter_ids, experts):
    flattened = quarter_ids.reshape(-1)
    onehot = (flattened[:, None] == jnp.arange(experts, dtype=jnp.int32)[None, :]).astype(jnp.int32)
    running = jnp.cumsum(onehot, axis=0)
    rank_ids = jnp.sum(onehot * running, axis=1) - 1
    return (flattened, rank_ids)


def place_rows(normed, quarter_ids, experts, capacity):
    flattened, rank_ids = route_ranks(quarter_ids, experts)
    slot_ids = rank_ids * experts + flattened
    matches = (
        jnp.arange(capacity * experts, dtype=jnp.int32)[:, None] == slot_ids[None, :]
    ).astype(jnp.bfloat16)
    doubled = jnp.repeat(normed, quarter_ids.shape[1], axis=0)
    placed = jnp.dot(matches, doubled, preferred_element_type=jnp.float32).astype(jnp.bfloat16)
    return placed.reshape(capacity, experts, normed.shape[1])


def rms_rows(values, gain_vec):
    scaling = lax.rsqrt(jnp.mean(values * values, axis=1, keepdims=True) + eps_norm)
    return (values * scaling * gain_vec[None, :]).astype(jnp.bfloat16)


def local(
    inputs,
    gate_input,
    b_proj,
    c_proj,
    step_size,
    decay_rate,
    skip_gain,
    start_state,
    norm_gain,
    out_proj,
    residual,
    moe_gain,
    w_gate,
    w_up,
    w_down,
    route_ids,
    route_gates,
):
    tok_ctx = inputs.shape[0]
    head_count = step_size.shape[0]
    head_dim = inputs.shape[1] // head_count
    model_width = residual.shape[1]
    n_ctx = lax.axis_size("ctx")
    n_exp = lax.axis_size("exp")
    experts = n_ctx // PAIR
    tok_quarter = tok_ctx // n_exp
    capacity = 4 * tok_quarter // experts
    x_local = inputs.astype(jnp.float32).reshape(tok_ctx, head_count, head_dim)
    b_local = b_proj.astype(jnp.float32)
    c_local = c_proj.astype(jnp.float32)
    cumulative = jnp.cumsum(decay_rate, axis=1)
    span_total = cumulative[:, -1]
    sequence_indices = jnp.arange(tok_ctx, dtype=jnp.int32)
    causal = sequence_indices[:, None] >= sequence_indices[None, :]
    spread = jnp.where(causal[None], cumulative[:, :, None] - cumulative[:, None, :], 0.0)
    scores = jnp.dot(c_local, b_local.T, precision=top_precision)
    mixing = jnp.where(causal[None], jnp.exp(-spread), 0.0) * scores[None] * step_size[:, None, :]
    inside_part = jnp.einsum("hts,shp->thp", mixing, x_local, precision=top_precision)
    ending = jnp.exp(-(span_total[:, None] - cumulative)) * step_size
    local_state = jnp.einsum("hs,shp,sn->hpn", ending, x_local, b_local, precision=top_precision)
    prior_decay, prior_state = entering(
        (jnp.exp(-span_total), local_state),
        "ctx",
        later_state,
        (jnp.ones_like(span_total), jnp.zeros_like(local_state)),
    )
    incoming = prior_state + prior_decay[:, None, None] * start_state
    carried = (
        jnp.einsum("hpn,tn->thp", incoming, c_local, precision=top_precision)
        * jnp.exp(-cumulative).T[:, :, None]
    )
    ssm_out = inside_part + carried + skip_gain[None, :, None] * x_local
    gated_out = ssm_out.reshape(tok_ctx, head_count * head_dim) * jax.nn.silu(
        gate_input.astype(jnp.float32)
    )
    squares = lax.psum(jnp.sum(gated_out * gated_out, axis=1), "exp")
    scaling = lax.rsqrt(squares / (head_count * head_dim * n_exp) + eps_norm)
    normed_mix = (gated_out * scaling[:, None] * norm_gain[None, :]).astype(jnp.bfloat16)
    partial_value = jnp.dot(
        normed_mix,
        lax.all_gather(out_proj, "ctx", axis=1, tiled=True),
        preferred_element_type=jnp.float32,
    )
    gate_rows = w_gate[0]
    up_rows = w_up[0]
    down_rows = w_down[0]
    piece_width = gate_rows.shape[1]
    first_row = lax.axis_index("exp") * tok_quarter
    own_ids = lax.dynamic_slice_in_dim(route_ids, first_row, tok_quarter, 0)
    own_gates = lax.dynamic_slice_in_dim(route_gates, first_row, tok_quarter, 0)
    mixed_all = lax.psum(partial_value.astype(jnp.bfloat16), "exp").astype(jnp.float32)
    hidden_all = residual.astype(jnp.float32) + mixed_all
    moe_all = rms_rows(hidden_all, moe_gain)

    def place_quarter(quarter_rows, quarter_ids):
        return place_rows(quarter_rows, quarter_ids, experts, capacity)

    placed = jax.vmap(place_quarter)(
        moe_all.reshape(n_exp, tok_quarter, model_width),
        route_ids.reshape(n_exp, tok_quarter, route_ids.shape[1]),
    )
    placed = placed.reshape(n_exp * capacity, experts, model_width)
    outgoing = jnp.repeat(placed, PAIR, axis=1)
    arrived = lax.all_to_all(outgoing, "ctx", split_axis=1, concat_axis=1, tiled=True)
    flattened = arrived.reshape(-1, model_width)
    gate_val = jnp.dot(flattened, gate_rows, preferred_element_type=jnp.float32)
    up_val = jnp.dot(flattened, up_rows, preferred_element_type=jnp.float32)
    activated = (jax.nn.silu(gate_val) * up_val).astype(jnp.bfloat16)
    hidden = activated.reshape(arrived.shape[0], arrived.shape[1], piece_width)
    hidden_own = lax.dynamic_slice_in_dim(hidden_all, first_row, tok_quarter, 0)
    product = jnp.dot(
        hidden.reshape(-1, piece_width), down_rows, preferred_element_type=jnp.float32
    )
    rounded = lax.optimization_barrier(product.astype(jnp.bfloat16)).astype(jnp.float32)
    summed = lax.psum_scatter(
        rounded.reshape(lax.axis_size("exp") * capacity, hidden.shape[1], model_width).astype(
            jnp.bfloat16
        ),
        "exp",
        scatter_dimension=0,
        tiled=True,
    )
    halves = lax.all_to_all(summed, "ctx", split_axis=1, concat_axis=1, tiled=True)
    flattened, rank_ids = route_ranks(own_ids, experts)
    base_rows = rank_ids * n_ctx + flattened * PAIR
    fetch_rows = base_rows[:, None] + jnp.arange(PAIR, dtype=jnp.int32)[None, :]
    fetched = halves.reshape(capacity * n_ctx, model_width)[fetch_rows]
    expert_out = jnp.sum(fetched.astype(jnp.float32), axis=1)
    weighted = expert_out * own_gates.reshape(-1)[:, None]
    moe_out = jnp.sum(weighted.reshape(tok_quarter, -1, model_width), axis=1)
    return (hidden_own + moe_out).astype(jnp.bfloat16)


def solution(mesh):
    in_specs = (
        P("ctx", "exp"),
        P("ctx", "exp"),
        P("ctx", None),
        P("ctx", None),
        P("exp", "ctx"),
        P("exp", "ctx"),
        P("exp"),
        P("exp", None, None),
        P("exp"),
        P("exp", "ctx"),
        P("ctx", None),
        P(),
        P("ctx", None, "exp"),
        P("ctx", None, "exp"),
        P("ctx", "exp", None),
        P("ctx", None),
        P("ctx", None),
    )
    out_specs = P(("ctx", "exp"), None)
    return jax.shard_map(local, mesh=mesh, in_specs=in_specs, out_specs=out_specs, check_vma=False)
```

profile of v0, /device:TPU:0, one launch (start us, length us, event | category | flops | bytes accessed | tf_op | source)
XLA Modules:
  0.0 648.1 jit_solution(447840886182954873)
XLA Ops:
  6.5 1.0 reduce_window_sum.33
  7.5 0.2 slice_reduce_fusion
  7.7 1.1 copy.52
  8.8 0.8 exponential_bitcast_fusion
  9.6 1.1 convolution_convert_fusion.3
  10.8 0.7 all-gather.5.cloned.1.call-update
  11.6 1.3 dynamic-slice
  13.5 0.2 fusion.44
  13.7 0.2 dynamic-update-slice
  14.0 23.2 %all-reduce = bf16[128]{0:T(256)(128)(2,1)S(1)} all-reduce(bf16[128]{0:T(256)(128)(2,1)S(1)} %dynamic-update-slice), channel_id=2, replica_groups=mesh['ctx'=8,'exp'=4] {'ctx'}, use_global_device_ids=true, to_apply=%add | all-reduce | flops 128 | bytes 512
  37.3 0.8 copy.54
  38.2 0.9 fusion.48
  39.1 23.9 %all-gather.7.cloned.1.call-done = bf16[128,64,128]{2,1,0:T(8,128)(2,1)} async-done(((bf16[16,64,128]{2,1,0:T(8,128)(2,1)}), bf16[128,64,128]{2,1,0:T(8,128)(2,1)}) %all-gather.7.cloned.1.call-update) | async-done | bytes 2097168 | tf_op jit(solution)/shard_map/all_gather | solution.py:16
  63.2 0.5 fusion.15
  63.8 1.4 fusion.14
  65.2 0.2 copy.53
  65.4 0.2 multiply_reduce_fusion.2
  65.6 5.7 psum.14
  71.3 117.7 %all-gather.5.cloned.1.call-done = bf16[1024,4096]{1,0:T(8,128)(2,1)} async-done(((bf16[1024,512]{1,0:T(8,128)(2,1)}), bf16[1024,4096]{1,0:T(8,128)(2,1)}) %all-gather.5.cloned.1.call-update) | async-done | bytes 8388624 | tf_op jit(solution)/shard_map/all_gather | solution.py:124
  189.0 5.8 convolution_convert_fusion.2
  194.8 0.6 reduce-scatter.2.cloned.1.call-start
  195.7 0.2 select_reduce_fusion
  195.9 33.4 %all-reduce.3.cloned.1.call-done = bf16[128,4096]{1,0:T(8,128)(2,1)} async-done(((bf16[128,4096]{1,0:T(8,128)(2,1)}), bf16[128,4096]{1,0:T(8,128)(2,1)}) %all-reduce.3.cloned.1.call-update) | async-done | bytes 1048592 | tf_op jit(solution)/shard_map/psum | solution.py:134
  229.3 3.0 convert_add_fusion.1
  232.3 0.4 multiply_convert_fusion.1
  232.7 3.4 broadcast_in_dim.28
  236.2 2.7 reshape.157
  238.9 3.3 convolution_convert_fusion.1
  242.2 7.2 %reshape.158 = bf16[128,4,4096]{2,1,0:T(4,128)(2,1)} reshape(bf16[4,128,4096]{2,1,0:T(8,128)(2,1)} %convolution_convert_fusion.1) | data formatting | bytes 8388608 | tf_op jit(solution)/shard_map/reshape;vmap()/reshape | solution.py:145
  249.4 4.5 copy.55
  253.9 4.3 broadcast_in_dim.29
  258.2 189.0 %all_to_all.10 = bf16[128,8,4096]{2,0,1:T(8,128)(2,1)S(1)} all-to-all(bf16[128,8,4096]{2,0,1:T(8,128)(2,1)} %bitcast.66), channel_id=1, replica_groups=mesh['ctx'=8,'exp'=4] {'ctx'}, dimensions={1} | all-to-all | bytes 16777216 | tf_op jit(solution)/shard_map/all_to_all | solution.py:147
  447.1 17.4 %fusion = f32[1024,896]{1,0:T(8,128)S(1)} fusion(bf16[128,8,4096]{2,0,1:T(8,128)(2,1)S(1)} %all_to_all.10, bf16[1,4096,896]{2,1,0:T(8,128)(2,1)} %param.32), kind=kOutput, calls=%fused_computation.3 | convolution fusion | flops 7516192768 | bytes 19398656 | tf_op jit(solution)/shard_map/dot_general | solution.py:150
  464.6 16.8 %multiply_convert_fusion = bf16[1024,896]{1,0:T(8,128)(2,1)} fusion(f32[1024,896]{1,0:T(8,128)S(1)} %fusion, bf16[1,4096,896]{2,1,0:T(8,128)(2,1)S(1)} %bitcast.74, bf16[128,8,4096]{2,0,1:T(8,128)(2,1)S(1)} %all_to_all.10), kind=kOutput, calls=%fused_computation.15 | convolution fusion | flops 7521697792 | bytes 21233664 | tf_op jit(solution)/shard_map/dot_general | solution.py:149
  481.4 12.7 %convolution_convert_fusion = bf16[1024,4096]{1,0:T(8,128)(2,1)} fusion(bf16[1024,896]{1,0:T(8,128)(2,1)} %multiply_convert_fusion, bf16[1,896,4096]{2,1,0:T(8,128)(2,1)S(1)} %bitcast.76), kind=kOutput, calls=%fused_computation.7 | convolution fusion | flops 7520387072 | bytes 17563648 | tf_op jit(solution)/shard_map/dot_general | solution.py:154
  494.1 11.2 %copy.57 = bf16[128,8,4096]{2,0,1:T(8,128)(2,1)} copy(bf16[128,8,4096]{2,1,0:T(8,128)(2,1)} %bitcast.67) | data formatting | bytes 16777216 | tf_op jit(solution)/shard_map/convert_element_type | solution.py:159
  505.3 70.2 %reduce-scatter.2.cloned.1.call-done = bf16[32,8,4096]{2,0,1:T(8,128)(2,1)} async-done(((bf16[128,8,4096]{2,0,1:T(8,128)(2,1)}), bf16[32,8,4096]{2,0,1:T(8,128)(2,1)}) %reduce-scatter.2.cloned.1.call-update) | async-done | bytes 2097168 | tf_op jit(solution)/shard_map/reduce_scatter | solution.py:158
  575.5 5.5 all-to-all-start.1
  581.5 0.2 select_reduce_fusion.1
  581.8 0.1 reshape.166
  582.1 47.3 %all-to-all-done.1 = bf16[32,8,4096]{2,0,1:T(8,128)(2,1)} async-done(((bf16[32,8,4096]{2,0,1:T(8,128)(2,1)}), bf16[32,8,4096]{2,0,1:T(8,128)(2,1)}, u32[]{:S(2)}, u32[]{:S(2)}) %all-to-all-start.1) | async-done | bytes 2097184 | tf_op jit(solution)/shard_map/all_to_all | solution.py:166
  629.4 2.7 copy.74
  632.1 1.2 gather_fusion
  633.3 1.3 reshape.175
  634.7 2.7 reduce_sum.60
  637.4 0.6 reduce_sum.61
  638.0 1.4 multiply_reduce_fusion.1
  639.5 1.8 add_convert_fusion
  (64 shorter events, 1.6 us)
Async XLA Ops:
  6.5 3.1 copy-start
  6.5 56.5 %all-gather.7.cloned.1.call-start = ((), (), s32[]{:S(2)}) async-start(), calls=%async_computation.6 | async-start | bytes 2359296 | tf_op jit(solution)/shard_map/all_gather | solution.py:16
  10.7 178.2 %all-gather.5.cloned.1.call-start = ((), (), s32[]{:S(2)}) async-start(), calls=%async_computation.3 | async-start | bytes 9437184 | tf_op jit(solution)/shard_map/all_gather | solution.py:124
  11.5 217.8 %all-reduce.3.cloned.1.call-start = ((), (), s32[]{:S(2)}) async-start(), calls=%async_computation.4 | async-start | bytes 2097152 | tf_op jit(solution)/shard_map/psum | solution.py:134
  39.1 24.0 %copy-start.4 = (f32[16,64,128]{2,1,0:T(8,128)S(1)}, f32[16,64,128]{2,1,0:T(8,128)}, u32[]{:S(2)}) copy-start(f32[16,64,128]{2,1,0:T(8,128)} %param.26) | copy-start | bytes 1572868
  39.1 24.1 %copy-start.6 = (bf16[128,128]{1,0:T(8,128)(2,1)S(1)}, bf16[128,128]{1,0:T(8,128)(2,1)}, u32[]{:S(2)}) copy-start(bf16[128,128]{1,0:T(8,128)(2,1)} %param.22) | copy-start | bytes 98308
  63.1 0.7 copy-start.8
  63.1 0.7 copy-start.12
  63.1 2.3 copy-start.5
  63.1 125.8 %copy-start.11 = (f32[1024]{0:T(1024)S(1)}, f32[1024]{0:T(1024)}, u32[]{:S(2)}) copy-start(f32[1024]{0:T(1024)} %param.27) | copy-start | bytes 12292
  71.3 158.0 %copy-start.2 = (bf16[128,4096]{1,0:T(8,128)(2,1)S(1)}, bf16[128,4096]{1,0:T(8,128)(2,1)}, u32[]{:S(2)}) copy-start(bf16[128,4096]{1,0:T(8,128)(2,1)} %param.29) | copy-start | bytes 3145732
  194.8 37.5 %copy-start.7 = (f32[4096]{0:T(1024)S(1)}, f32[4096]{0:T(1024)}, u32[]{:S(2)}) copy-start(f32[4096]{0:T(1024)} %param.30) | copy-start | bytes 49156
  194.8 380.7 %reduce-scatter.2.cloned.1.call-start = ((), (), s32[]{:S(2)}) async-start(), calls=%async_computation.5 | async-start | bytes 10485760 | tf_op jit(solution)/shard_map/reduce_scatter | solution.py:158
  229.3 3.0 copy-start.3
  258.2 206.4 %slice-start = ((s8[7340032]{0:T(1024)(128)(4,1)}), s8[4194304]{0:T(1024)(128)(4,1)S(1)}, s32[]{:S(2)}) async-start(s8[7340032]{0:T(1024)(128)(4,1)} %bitcast.73), calls=%async_computation.7 | async-start | bytes 8388608
  258.2 223.2 %slice-start.2 = ((s8[7340032]{0:T(1024)(128)(4,1)}), s8[4194304]{0:T(1024)(128)(4,1)S(1)}, s32[]{:S(2)}) async-start(s8[7340032]{0:T(1024)(128)(4,1)} %bitcast.75), calls=%async_computation.9 | async-start | bytes 8388608
  447.1 17.5 %slice-start.1 = ((s8[7340032]{0:T(1024)(128)(4,1)}), s8[3145728]{0:T(1024)(128)(4,1)S(1)}, s32[]{:S(2)}) async-start(s8[7340032]{0:T(1024)(128)(4,1)} %bitcast.73), calls=%async_computation.8 | async-start | bytes 6291456
  447.1 34.2 %slice-start.3 = ((s8[7340032]{0:T(1024)(128)(4,1)}), s8[3145728]{0:T(1024)(128)(4,1)S(1)}, s32[]{:S(2)}) async-start(s8[7340032]{0:T(1024)(128)(4,1)} %bitcast.75), calls=%async_computation.10 | async-start | bytes 6291456
  505.3 75.8 %copy-start.9 = (s32[128,2]{0,1:T(2,128)S(1)}, s32[128,2]{0,1:T(2,128)}, u32[]{:S(2)}) copy-start(s32[128,2]{0,1:T(2,128)} %param.34) | copy-start | bytes 3076
  505.3 76.6 %copy-start.10 = (f32[128,2]{0,1:T(2,128)S(1)}, f32[128,2]{0,1:T(2,128)}, u32[]{:S(2)}) copy-start(f32[128,2]{0,1:T(2,128)} %param.35) | copy-start | bytes 3076
  575.5 53.8 %all-to-all-start.1 = ((bf16[32,8,4096]{2,0,1:T(8,128)(2,1)}), bf16[32,8,4096]{2,0,1:T(8,128)(2,1)}, u32[]{:S(2)}, u32[]{:S(2)}) async-start(bf16[32,8,4096]{2,0,1:T(8,128)(2,1)} %reduce-scatter.2.cloned.1.call-done), calls=%async_computation.2 | async-start | bytes 4194304 | tf_op jit(solution)/shard_map/all_to_all | solution.py:166
  633.3 8.0 %copy-start.1 = (bf16[128,128]{1,0:T(8,128)(2,1)S(1)}, bf16[128,128]{1,0:T(8,128)(2,1)}, u32[]{:S(2)}) copy-start(bf16[128,128]{1,0:T(8,128)(2,1)} %param.21) | copy-start | bytes 98308
Sparse Core Ops, SparseCore 0:
  10.9 52.0 all-gather.6
  65.0 123.8 all-gather.4
  195.0 34.2 all-reduce.2
  505.4 70.0 reduce-scatter.1
where the time goes:
time: 653 us; the launch traced here: 648 us
  waiting for transfers between devices  293 us (45%)
  blocking collectives  218 us (33%)
  matrix products  59.9 us (9%)
  local copies, waits for them, and re-layouts  44.1 us (7%)
  between operations  14.4 us (2%)
  other arithmetic  12.5 us (2%)
    all_to_all x1, blocking collectives, local(): lax.all_to_all(outgoing, 'ctx', split_axis=1, concat_axis=1, tiled=True)  189 us
    all_gather x1, waiting for transfers between devices, local(): lax.all_gather(out_proj, 'ctx', axis=1, tiled=True)  118 us
    reduce_scatter x1, waiting for transfers between devices, local(): lax.psum_scatter(rounded.reshape(lax.axis_size('exp') * capacity, hidden....  70.2 us
    all_to_all x1, waiting for transfers between devices, local(): lax.all_to_all(summed, 'ctx', split_axis=1, concat_axis=1, tiled=True)  47.3 us
    psum x1, waiting for transfers between devices, local(): lax.psum(partial_value.astype(jnp.bfloat16), 'exp').astype(jnp.float32)  33.4 us
    all_gather x1, waiting for transfers between devices, entering(): lax.all_gather(a.astype(kind), axis)  23.9 us
    unnamed x1, blocking collectives  23.2 us
    dot_general x1, matrix products, local(): up_val = jnp.dot(flattened, up_rows, preferred_element_type=jnp.float32)  17.4 us
  transfers between devices with their start and end apart: 5, of which 5 were waited for; matrix products, arithmetic and copies ran while one was open for 1% of the time, Pallas kernels for 0%

commit v1 on v0

v1 whole, which is shorter than its diff:
```python
import jax
import jax.numpy as jnp
from jax import lax
from jax.sharding import PartitionSpec as P

PAIR = 2
eps_norm = 1e-05
BF = jnp.bfloat16
F32 = jnp.float32
GROUPS = 4


def swap(x, axis, flip):
    size = lax.axis_size(axis)
    return lax.ppermute(x, axis, [(i, i ^ flip) for i in range(size)])


def mm(a, b):
    return jnp.dot(a, b, preferred_element_type=F32)


def split_total(total):
    high = total.astype(BF)
    low = (total - high.astype(F32)).astype(BF)
    both = jnp.concatenate([high, low])
    return jnp.broadcast_to(both[:, None], (both.shape[0], 128))


def with_total(state, total):
    return jnp.concatenate([state.astype(BF), split_total(total)], axis=0)


def apart(packed, heads):
    rows = packed.shape[0] - 2 * heads
    tail = packed[rows:, 0].astype(F32)
    return packed[:rows].astype(F32), tail[:heads] + tail[heads:]


def incoming_state(state, total, start, head_dim):
    place = lax.axis_index("ctx")
    pairs = lax.axis_size("ctx") // 2
    odd = place % 2 == 1
    z = place // 2
    heads = total.shape[0]
    half = heads // 2
    cut = half * head_dim
    keep = jnp.where(odd, state[cut:], state[:cut])
    keep_total = jnp.where(odd, total[half:], total[:half])
    give = jnp.where(odd, state[:cut], state[cut:])
    give_total = jnp.where(odd, total[:half], total[half:])
    got, got_total = apart(swap(with_total(give, give_total), "ctx", 1), half)

    def spread(v):
        return jnp.repeat(v, head_dim)[:, None]

    first = jnp.where(odd, got, keep)
    first_total = jnp.where(odd, got_total, keep_total)
    second = jnp.where(odd, keep, got)
    second_total = jnp.where(odd, keep_total, got_total)
    pair_state = spread(jnp.exp(-second_total)) * first + second
    pair_total = first_total + second_total
    packed = with_total(pair_state, pair_total)
    others = [apart(swap(packed, "ctx", 2 * d), half) for d in range(1, pairs)]
    states = [o[0] for o in others]
    totals = jnp.stack([o[1] for o in others])
    planes = jnp.stack([z ^ d for d in range(1, pairs)])
    between = (planes[None, :] > planes[:, None]) & (planes[None, :] < z)
    gap = jnp.sum(jnp.where(between[:, :, None], totals[None], 0.0), axis=1)
    weight = jnp.where((planes < z)[:, None], jnp.exp(-gap), 0.0)
    before = jnp.sum(jnp.where((planes < z)[:, None], totals, 0.0), axis=0)
    own_start = jnp.where(odd, start[cut:], start[:cut])
    prefix = spread(jnp.exp(-before)) * own_start
    for i, s in enumerate(states):
        prefix = prefix + spread(weight[i]) * s
    later = spread(jnp.exp(-first_total)) * prefix + first
    mine = jnp.where(odd, later, prefix).astype(BF)
    other = swap(jnp.where(odd, prefix, later).astype(BF), "ctx", 1)
    return jnp.where(odd, other, mine), jnp.where(odd, mine, other)


def mixer_rows(inputs, gate_input, b_proj, c_proj, step_size, decay_rate, skip_gain, start_state):
    tok = inputs.shape[0]
    heads = step_size.shape[0]
    width = inputs.shape[1]
    head_dim = width // heads
    cumulative = jnp.cumsum(decay_rate, axis=1)
    total = cumulative[:, -1]

    def wide(v):
        return jnp.broadcast_to(v.T[:, :, None], (tok, heads, head_dim)).reshape(tok, width)

    x_local = inputs.astype(F32)
    ending = jnp.exp(-(total[:, None] - cumulative)) * step_size
    decayed = (x_local * wide(ending)).astype(BF)
    state = lax.dot_general(decayed, b_proj, (((0,), (0,)), ((), ())), preferred_element_type=F32)
    low, high = incoming_state(state, total, start_state.reshape(width, -1), head_dim)
    order = jnp.arange(tok, dtype=jnp.int32)
    causal = order[:, None] >= order[None, :]
    spread = jnp.where(causal[None], cumulative[:, :, None] - cumulative[:, None, :], 0.0)
    scores = lax.dot_general(c_proj, b_proj, (((1,), (1,)), ((), ())), preferred_element_type=F32)
    mixing = jnp.where(causal[None], jnp.exp(-spread), 0.0) * scores[None] * step_size[:, None, :]
    inside = jnp.einsum(
        "hts,shp->thp",
        mixing.astype(BF),
        inputs.reshape(tok, heads, head_dim),
        preferred_element_type=F32,
    ).reshape(tok, width)
    direct = inside + jnp.repeat(skip_gain, head_dim)[None, :] * x_local
    side = (((1,), (1,)), ((), ()))
    carried = jnp.concatenate(
        [
            lax.dot_general(c_proj, low, side, preferred_element_type=F32),
            lax.dot_general(c_proj, high, side, preferred_element_type=F32),
        ],
        axis=1,
    )
    ssm_out = direct + carried * wide(jnp.exp(-cumulative))
    return ssm_out * jax.nn.silu(gate_input.astype(F32))


def project_rows(gated, norm_gain, out_proj):
    n_exp = lax.axis_size("exp")
    n_ctx = lax.axis_size("ctx")
    me_exp = lax.axis_index("exp")
    me_ctx = lax.axis_index("ctx")
    tok, width = gated.shape
    quarter = tok // n_exp
    both = jnp.concatenate([out_proj, swap(out_proj, "ctx", 2)], axis=1)
    squares = jnp.sum(gated * gated, axis=1)
    for flip in (1, 2):
        squares = squares + swap(squares, "exp", flip)
    own_squares = lax.dynamic_slice_in_dim(squares, me_exp * quarter, quarter, 0)
    scale = lax.rsqrt(own_squares / (width * n_exp) + eps_norm)

    rows = (gated * norm_gain[None, :]).astype(BF)
    rel = [0, 2, 1, 3]
    pieces = [lax.dynamic_slice_in_dim(rows, (me_exp ^ q) * quarter, quarter, 0) for q in rel]
    part_a = jnp.concatenate(pieces[:2])
    part_b = jnp.concatenate(pieces[2:])
    hops = [4 * m for m in range(1, n_ctx // 4)]
    a_z = jnp.stack([part_a] + [swap(part_a, "ctx", h) for h in hops])
    b_y = jnp.stack([part_b, swap(part_b, "ctx", 1)])
    a_all = jnp.stack([a_z, swap(a_z, "ctx", 1)])
    b_all = jnp.stack([b_y] + [swap(b_y, "ctx", h) for h in hops])
    a_all = a_all.swapaxes(0, 1)
    group = [h + y for h in [0] + hops for y in (0, 1)]
    full = jnp.concatenate([a_all, b_all], axis=2).reshape(len(group), n_exp, quarter, width)
    full = full.swapaxes(0, 1).reshape(-1, width)
    partial = mm(full, both).astype(BF)
    for flip in (1, 2):
        cut = partial.shape[0] // 2
        got = swap(partial[cut:], "exp", flip)
        partial = (partial[:cut].astype(F32) + got.astype(F32)).astype(BF)
    partial = partial.reshape(len(group), quarter, -1)
    columns = out_proj.shape[1]
    blocks = [None] * n_ctx
    for i, r in enumerate(group):
        block = partial[i] if r == 0 else swap(partial[i], "ctx", r)
        blocks[r] = block[:, :columns]
        blocks[r ^ 2] = block[:, columns:]
    stacked = jnp.stack(blocks)
    place = me_ctx ^ jnp.arange(n_ctx, dtype=jnp.int32)
    mixed = jnp.concatenate(
        [lax.dynamic_index_in_dim(stacked, place[b], 0, False) for b in range(n_ctx)], axis=1
    )
    return mixed.astype(F32), scale


def gather_plane(pieces):
    half = pieces.shape[1] // 2
    width = pieces.shape[2]
    part_a = pieces[:, :half].reshape(-1, width)
    part_b = pieces[:, half:].reshape(-1, width)
    part_a = jnp.concatenate([part_a, swap(part_a, "ctx", 1)])
    part_b = jnp.concatenate([part_b, swap(part_b, "exp", 2)])
    part_a2 = swap(part_a, "exp", 2)
    part_b2 = swap(part_b, "ctx", 1)
    rows = jnp.concatenate([part_a, part_a2, part_b, part_b2])
    return jnp.concatenate([rows, swap(rows, "exp", 1)])


def scatter_plane(rows, count):
    def fold(values, axis, flip):
        cut = values.shape[0] // 2
        got = swap(values[cut:], axis, flip)
        return (values[:cut].astype(F32) + got.astype(F32)).astype(BF)

    rows = fold(rows, "exp", 1)
    cut = rows.shape[0] // 2
    part_a = fold(fold(rows[:cut], "exp", 2), "ctx", 1)
    part_b = fold(fold(rows[cut:], "ctx", 1), "exp", 2)
    width = rows.shape[1]
    part_a = part_a.reshape(count, -1, width)
    part_b = part_b.reshape(count, -1, width)
    return jnp.concatenate([part_a, part_b], axis=1)


def local(
    inputs,
    gate_input,
    b_proj,
    c_proj,
    step_size,
    decay_rate,
    skip_gain,
    start_state,
    norm_gain,
    out_proj,
    residual,
    moe_gain,
    w_gate,
    w_up,
    w_down,
    route_ids,
    route_gates,
):
    n_ctx = lax.axis_size("ctx")
    n_exp = lax.axis_size("exp")
    me_ctx = lax.axis_index("ctx")
    me_exp = lax.axis_index("exp")
    tok = inputs.shape[0]
    quarter = tok // n_exp
    pairs = n_ctx // 2
    experts = n_ctx // PAIR
    named = route_ids[:, :, None] == jnp.arange(experts, dtype=jnp.int32)[None, None, :]
    weights = jnp.sum(jnp.where(named, route_gates[:, :, None], 0.0), axis=1)
    weights_all = lax.all_gather(weights, "ctx")
    own_weight = lax.dynamic_index_in_dim(weights_all, me_ctx // PAIR, 2, False)
    own_weight = own_weight.reshape(n_ctx, n_exp, quarter)

    gated = mixer_rows(
        inputs, gate_input, b_proj, c_proj, step_size, decay_rate, skip_gain, start_state
    )
    mixed, scale = project_rows(gated, norm_gain, out_proj)
    own_residual = lax.dynamic_slice_in_dim(residual, me_exp * quarter, quarter, 0)
    hidden = own_residual.astype(F32) + mixed * scale[:, None]
    moe_scale = lax.rsqrt(jnp.mean(hidden * hidden, axis=1, keepdims=True) + eps_norm)
    moe_in = (hidden * moe_scale * moe_gain[None, :]).astype(BF)

    planes = [moe_in] + [swap(moe_in, "ctx", 2 * d) for d in range(1, pairs)]
    gate_rows, up_rows, down_rows = w_gate[0], w_up[0], w_down[0]
    half = quarter // 2
    order = [(x, y, "a") for x in (0, 1) for y in (0, 1)]
    order = order + [(x, y, "b") for y in (0, 1) for x in (0, 1)]
    total = hidden
    size = pairs // GROUPS
    for first in range(0, pairs, size):
        offsets = list(range(first, first + size))
        rows = gather_plane(jnp.stack([planes[d] for d in offsets]))
        row_weight = []
        for k in (0, 1):
            for x, y, part in order:
                for d in offsets:
                    whole = own_weight[me_ctx ^ (2 * d + y), me_exp ^ (2 * x + k)]
                    row_weight.append(whole[:half] if part == "a" else whole[half:])
        row_weight = jnp.concatenate(row_weight)
        gate_val = mm(rows, gate_rows)
        up_val = mm(rows, up_rows)
        activated = (jax.nn.silu(gate_val) * up_val).astype(BF)
        result = (mm(activated, down_rows) * row_weight[:, None]).astype(BF)
        summed = scatter_plane(result, size)
        for i, d in enumerate(offsets):
            back = summed[i] if d == 0 else swap(summed[i], "ctx", 2 * d)
            total = total + back.astype(F32)
    return total.astype(BF)


def solution(mesh):
    in_specs = (
        P("ctx", "exp"),
        P("ctx", "exp"),
        P("ctx", None),
        P("ctx", None),
        P("exp", "ctx"),
        P("exp", "ctx"),
        P("exp"),
        P("exp", None, None),
        P("exp"),
        P("exp", "ctx"),
        P("ctx", None),
        P(),
        P("ctx", None, "exp"),
        P("ctx", None, "exp"),
        P("ctx", "exp", None),
        P("ctx", None),
        P("ctx", None),
    )
    out_specs = P(("ctx", "exp"), None)
    return jax.shard_map(local, mesh=mesh, in_specs=in_specs, out_specs=out_specs, check_vma=False)
```

time: 653 us -> 355 us (0.54)
  waiting for transfers between devices: 293 us -> 97.8 us
  blocking collectives: 218 us -> 44.3 us
  starting transfers between devices: 6.16 us -> 69.7 us
  matrix products: 59.9 us -> 69.4 us
    all_to_all x1 -> x0, blocking collectives: 189 us -> none  [local(): lax.all_to_all(outgoing, 'ctx', split_axis=1, concat_axis=1, tiled=True)]
    all_gather x2 -> x0, waiting for transfers between devices: 142 us -> none  [the longest x1 118 us: local(): lax.all_gather(out_proj, 'ctx', axis=1, tiled=True)]
    ppermute x0 -> x63, waiting for transfers between devices: none -> 97.8 us  [swap(): return lax.ppermute(x, axis, [(i, i ^ flip) for i in range(size)])]
    reduce_scatter x1 -> x0, waiting for transfers between devices: 70.2 us -> none  [local(): lax.psum_scatter(rounded.reshape(lax.axis_size('exp') * capacity, hidden....]
    ppermute x0 -> x63, starting transfers between devices: none -> 69.7 us  [swap(): return lax.ppermute(x, axis, [(i, i ^ flip) for i in range(size)])]
    all_to_all x1 -> x0, waiting for transfers between devices: 47.3 us -> none  [local(): lax.all_to_all(summed, 'ctx', split_axis=1, concat_axis=1, tiled=True)]
    all_gather x0 -> x1, blocking collectives: none -> 44.3 us  [local(): weights_all = lax.all_gather(weights, 'ctx')]
    psum x1 -> x0, waiting for transfers between devices: 33.4 us -> none  [local(): lax.psum(partial_value.astype(jnp.bfloat16), 'exp').astype(jnp.float32)]
  transfers between devices with their start and end apart: 5 -> 63, of which waited for: 5 -> 25; matrix products, arithmetic and copies ran while one was open for 1% -> 29% of each run, Pallas kernels for 0% -> 0%
where the time goes in v1:
time: 355 us; the launch traced here: 350 us
  waiting for transfers between devices  97.8 us (28%)
  starting transfers between devices  69.7 us (20%)
  matrix products  69.4 us (20%)
  blocking collectives  44.3 us (12%)
  local copies, waits for them, and re-layouts  38.1 us (11%)
  between operations  16.5 us (5%)
  other arithmetic  13.8 us (4%)
    ppermute x63, waiting for transfers between devices, swap(): return lax.ppermute(x, axis, [(i, i ^ flip) for i in range(size)])  97.8 us
    ppermute x63, starting transfers between devices, swap(): return lax.ppermute(x, axis, [(i, i ^ flip) for i in range(size)])  69.7 us
    dot_general x9, matrix products, mm(): return jnp.dot(a, b, preferred_element_type=F32)  68.2 us
    all_gather x1, blocking collectives, local(): weights_all = lax.all_gather(weights, 'ctx')  44.3 us
    unnamed x95, local copies, waits for them, and re-layouts  23.4 us
  transfers between devices with their start and end apart: 63, of which 25 were waited for; matrix products, arithmetic and copies ran while one was open for 29% of the time, Pallas kernels for 0%

profile of v1, /device:TPU:0, one launch (start us, length us, event | category | flops | bytes accessed | tf_op | source)
XLA Modules:
  0.0 349.6 jit_solution(9718728321013802307)
XLA Ops:
  3.9 3.0 collective-permute-start
  7.0 1.6 collective-permute-start.9
  8.6 44.3 %all-gather = f32[1024,4]{0,1:T(4,128)S(1)} all-gather(f32[128,4]{0,1:T(4,128)S(1)} %select_reduce_fusion.1), channel_id=2, replica_groups=mesh['ctx'=8,'exp'=4] {'ctx'}, dimensions={0}, use_global_device_ids=true | all-gather | bytes 18432 | tf_op jit(solution)/shard_map/all_gather | solution.py:227
  56.0 1.7 collective-permute-start.2
  57.7 2.7 collective-permute-start.1
  60.5 2.4 collective-permute-done.3
  62.9 2.0 collective-permute-done.2
  67.4 5.5 %collective-permute-done.4 = bf16[512,128]{1,0:T(8,128)(2,1)S(1)} collective-permute-done((bf16[512,128]{1,0:T(8,128)(2,1)S(1)}, bf16[512,128]{1,0:T(8,128)(2,1)S(1)}, u32[]{:S(2)}, u32[]{:S(2)}) %collective-permute-start.4) | collective-permute-done | bytes 131104 | tf_op jit(solution)/shard_map/ppermute | solution.py:15
  76.1 7.5 %collective-permute-done.7 = bf16[64,1024]{0,1:T(8,128)(2,1)S(1)} collective-permute-done((bf16[64,1024]{0,1:T(8,128)(2,1)S(1)}, bf16[64,1024]{0,1:T(8,128)(2,1)S(1)}, u32[]{:S(2)}, u32[]{:S(2)}) %collective-permute-start.7) | collective-permute-done | bytes 131104 | tf_op jit(solution)/shard_map/ppermute | solution.py:15
  85.1 12.2 %collective-permute-done.5 = bf16[64,1024]{0,1:T(8,128)(2,1)S(1)} collective-permute-done((bf16[64,1024]{0,1:T(8,128)(2,1)S(1)}, bf16[64,1024]{0,1:T(8,128)(2,1)S(1)}, u32[]{:S(2)}, u32[]{:S(2)}) %collective-permute-start.5) | collective-permute-done | bytes 131104 | tf_op jit(solution)/shard_map/ppermute | solution.py:15
  97.5 1.8 collective-permute-start.6
  99.3 7.4 %collective-permute-done.6 = bf16[2,64,1024]{1,2,0:T(8,128)(2,1)S(1)} collective-permute-done((bf16[2,64,1024]{1,2,0:T(8,128)(2,1)S(1)}, bf16[2,64,1024]{1,2,0:T(8,128)(2,1)S(1)}, u32[]{:S(2)}, u32[]{:S(2)}) %collective-permute-start.6) | collective-permute-done | bytes 262176 | tf_op jit(solution)/shard_map/ppermute | solution.py:15
  108.3 2.8 fusion.52
  127.5 1.6 collective-permute-start.11
  130.8 5.5 %collective-permute-done.16 = f32[128]{0:T(128)S(1)} collective-permute-done((f32[128]{0:T(128)S(1)}, f32[128]{0:T(128)S(1)}, u32[]{:S(2)}, u32[]{:S(2)}) %collective-permute-start.16) | collective-permute-done | bytes 544 | tf_op jit(solution)/shard_map/ppermute | solution.py:15
  136.5 1.8 collective-permute-start.12
  138.3 2.6 collective-permute-start.14
  141.0 3.7 %collective-permute-done.13 = bf16[32,1024]{1,0:T(8,128)(2,1)S(1)} collective-permute-done((bf16[32,1024]{1,0:T(8,128)(2,1)S(1)}, bf16[32,1024]{1,0:T(8,128)(2,1)S(1)}, u32[]{:S(2)}, u32[]{:S(2)}) %collective-permute-start.13) | collective-permute-done | bytes 65568 | tf_op jit(solution)/shard_map/ppermute | solution.py:15
  148.1 2.8 collective-permute-start.27
  153.6 2.3 collective-permute-done.17
  157.5 1.6 collective-permute-start.20
  159.9 9.5 %collective-permute-done.39 = bf16[32,4096]{1,0:T(8,128)(2,1)S(1)} collective-permute-done((bf16[32,4096]{1,0:T(8,128)(2,1)S(1)}, bf16[32,4096]{1,0:T(8,128)(2,1)S(1)}, u32[]{:S(2)}, u32[]{:S(2)}) %collective-permute-start.39) | collective-permute-done | bytes 262176 | tf_op jit(solution)/shard_map/ppermute | solution.py:15
  172.8 1.7 collective-permute-start.40
  175.0 2.0 collective-permute-done.52
  179.2 2.1 collective-permute-start.53
  203.9 3.3 fusion.14
  207.2 10.6 %fusion.45 = bf16[256,4096]{1,0:T(8,128)(2,1)S(1)} fusion(bf16[1,896,4096]{2,1,0:T(8,128)(2,1)} %param.31, f32[256]{0:T(256)S(1)} %concatenate.132, f32[256,896]{1,0:T(8,128)} %fusion.14, bf16[256,4096]{1,0:T(8,128)(2,1)} %copy-done.21, bf16[1,4096,896]{2,1,0:T(8,128)(2,1)} %param.29), kind=kOutput, calls=%fused_computation.31 | convolution fusion | flops 3761569792 | bytes 19792896 | tf_op jit(solution)/shard_map/dot_general | solution.py:19
  218.8 1.7 copy-done.16
  221.9 6.6 %fusion.8 = f32[256,896]{1,0:T(8,128)} fusion(bf16[256,4096]{1,0:T(8,128)(2,1)S(1)} %constant_dynamic-update-slice_fusion.61, bf16[1,4096,896]{2,1,0:T(8,128)(2,1)} %param.30), kind=kOutput, calls=%fused_computation.8 | convolution fusion | flops 1879048192 | bytes 10354688 | tf_op jit(solution)/shard_map/dot_general | solution.py:19
  228.6 10.6 %fusion.36 = bf16[256,4096]{1,0:T(8,128)(2,1)S(1)} fusion(bf16[1,896,4096]{2,1,0:T(8,128)(2,1)} %param.31, f32[256]{0:T(256)S(1)} %concatenate.150, f32[256,896]{1,0:T(8,128)} %fusion.8, bf16[256,4096]{1,0:T(8,128)(2,1)} %copy-done.17, bf16[1,4096,896]{2,1,0:T(8,128)(2,1)} %param.29), kind=kOutput, calls=%fused_computation.28 | convolution fusion | flops 3761569792 | bytes 19792896 | tf_op jit(solution)/shard_map/dot_general | solution.py:19
  240.2 1.6 copy-done.19
  244.5 5.5 %fusion.10 = f32[256,896]{1,0:T(8,128)S(1)} fusion(bf16[256,4096]{1,0:T(8,128)(2,1)S(1)} %constant_dynamic-update-slice_fusion.48, bf16[1,4096,896]{2,1,0:T(8,128)(2,1)} %param.30), kind=kOutput, calls=%fused_computation.10 | convolution fusion | flops 1879048192 | bytes 10354688 | tf_op jit(solution)/shard_map/dot_general | solution.py:19
  250.0 10.3 %fusion.39 = bf16[256,4096]{1,0:T(8,128)(2,1)S(1)} fusion(bf16[1,896,4096]{2,1,0:T(8,128)(2,1)} %param.31, f32[256]{0:T(256)S(1)} %concatenate.144, f32[256,896]{1,0:T(8,128)S(1)} %fusion.10, bf16[256,4096]{1,0:T(8,128)(2,1)} %copy-done.20, bf16[1,4096,896]{2,1,0:T(8,128)(2,1)} %param.29), kind=kOutput, calls=%fused_computation.29 | convolution fusion | flops 3761569792 | bytes 19792896 | tf_op jit(solution)/shard_map/dot_general | solution.py:19
  264.9 6.7 %fusion.12 = f32[256,896]{1,0:T(8,128)} fusion(bf16[256,4096]{1,0:T(8,128)(2,1)S(1)} %constant_dynamic-update-slice_fusion.35, bf16[1,4096,896]{2,1,0:T(8,128)(2,1)} %param.30), kind=kOutput, calls=%fused_computation.12 | convolution fusion | flops 1879048192 | bytes 10354688 | tf_op jit(solution)/shard_map/dot_general | solution.py:19
  271.6 11.9 %fusion.42 = bf16[256,4096]{1,0:T(8,128)(2,1)} fusion(bf16[1,896,4096]{2,1,0:T(8,128)(2,1)} %param.31, f32[256]{0:T(256)S(1)} %concatenate.138, f32[256,896]{1,0:T(8,128)} %fusion.12, bf16[256,4096]{1,0:T(8,128)(2,1)} %copy-done.14, bf16[1,4096,896]{2,1,0:T(8,128)(2,1)} %param.29), kind=kOutput, calls=%fused_computation.30 | convolution fusion | flops 3761569792 | bytes 19792896 | tf_op jit(solution)/shard_map/dot_general | solution.py:19
  285.4 1.6 add_convert_fusion.3
  288.5 1.6 collective-permute-start.25
  294.8 1.6 collective-permute-done.23
  299.6 9.9 %collective-permute-done.26 = bf16[16,4096]{1,0:T(8,128)(2,1)S(1)} collective-permute-done((bf16[16,4096]{1,0:T(8,128)(2,1)S(1)}, bf16[16,4096]{1,0:T(8,128)(2,1)S(1)}, u32[]{:S(2)}, u32[]{:S(2)}) %collective-permute-start.26) | collective-permute-done | bytes 131104 | tf_op jit(solution)/shard_map/ppermute | solution.py:15
  310.8 1.7 collective-permute-start.36
  315.4 3.2 collective-permute-done.34
  320.1 1.6 collective-permute-start.47
  322.8 2.9 collective-permute-done.59
  325.7 1.6 collective-permute-start.35
  327.4 2.7 collective-permute-start.62
  332.3 6.2 %collective-permute-done.62 = bf16[32,4096]{1,0:T(8,128)(2,1)S(1)} collective-permute-done((bf16[32,4096]{1,0:T(8,128)(2,1)S(1)}, bf16[32,4096]{1,0:T(8,128)(2,1)S(1)}, u32[]{:S(2)}, u32[]{:S(2)}) %collective-permute-start.62) | collective-permute-done | bytes 262176 | tf_op jit(solution)/shard_map/ppermute | solution.py:15
  338.5 8.7 %collective-permute-done.50 = bf16[32,4096]{1,0:T(8,128)(2,1)S(1)} collective-permute-done((bf16[32,4096]{1,0:T(8,128)(2,1)S(1)}, bf16[32,4096]{1,0:T(8,128)(2,1)S(1)}, u32[]{:S(2)}, u32[]{:S(2)}) %collective-permute-start.50) | collective-permute-done | bytes 262176 | tf_op jit(solution)/shard_map/ppermute | solution.py:15
  347.2 1.9 fusion.66
  (344 shorter events, 87.1 us)
Async XLA Ops:
  3.9 51.2 %collective-permute-start = (bf16[528,128]{1,0:T(8,128)(2,1)S(1)}, bf16[528,128]{1,0:T(8,128)(2,1)S(1)}, u32[]{:S(2)}, u32[]{:S(2)}) collective-permute-start(bf16[528,128]{1,0:T(8,128)(2,1)S(1)} %pad_maximum_fusion.12), channel_id=1, source_target_pairs={{0,4},{4,0},{8,12},{12,8},{16,20},{20,16},{24,28},{28,24},{1,5},{5... | collective-permute-start | bytes 405512 | tf_op jit(solution)/shard_map/ppermute | solution.py:15
  7.0 101.4 %collective-permute-start.9 = (bf16[1024,512]{1,0:T(8,128)(2,1)}, bf16[1024,512]{1,0:T(8,128)(2,1)}, u32[]{:S(2)}, u32[]{:S(2)}) collective-permute-start(bf16[1024,512]{1,0:T(8,128)(2,1)} %param.26), channel_id=1, source_target_pairs={{0,8},{4,12},{8,0},{12,4},{16,24},{20,28},{24,16},{28,20},{1,9},{5... | collective-permute-start | bytes 3145736 | tf_op jit(solution)/shard_map/ppermute | solution.py:15
  56.0 8.9 %collective-permute-start.2 = (bf16[528,128]{1,0:T(8,128)(2,1)S(1)}, bf16[528,128]{1,0:T(8,128)(2,1)S(1)}, u32[]{:S(2)}, u32[]{:S(2)}) collective-permute-start(bf16[528,128]{1,0:T(8,128)(2,1)S(1)} %pad_maximum_fusion.13), channel_id=1, source_target_pairs={{0,16},{4,20},{8,24},{12,28},{16,0},{20,4},{24,8},{28,12},{1,17},{... | collective-permute-start | bytes 405512 | tf_op jit(solution)/shard_map/ppermute | solution.py:15
  57.7 7.5 %collective-permute-start.1 = (bf16[528,128]{1,0:T(8,128)(2,1)S(1)}, bf16[528,128]{1,0:T(8,128)(2,1)S(1)}, u32[]{:S(2)}, u32[]{:S(2)}) collective-permute-start(bf16[528,128]{1,0:T(8,128)(2,1)S(1)} %pad_maximum_fusion.13), channel_id=1, source_target_pairs={{0,8},{4,12},{8,0},{12,4},{16,24},{20,28},{24,16},{28,20},{1,9},{5... | collective-permute-start | bytes 405512 | tf_op jit(solution)/shard_map/ppermute | solution.py:15
  74.4 9.2 %collective-permute-start.7 = (bf16[64,1024]{0,1:T(8,128)(2,1)S(1)}, bf16[64,1024]{0,1:T(8,128)(2,1)S(1)}, u32[]{:S(2)}, u32[]{:S(2)}) collective-permute-start(bf16[64,1024]{0,1:T(8,128)(2,1)S(1)} %pad_maximum_fusion.3), channel_id=1, source_target_pairs={{0,4},{4,0},{8,12},{12,8},{16,20},{20,16},{24,28},{28,24},{1,5},{5... | collective-permute-start | bytes 393224 | tf_op jit(solution)/shard_map/ppermute | solution.py:15
  75.4 21.9 %collective-permute-start.5 = (bf16[64,1024]{0,1:T(8,128)(2,1)S(1)}, bf16[64,1024]{0,1:T(8,128)(2,1)S(1)}, u32[]{:S(2)}, u32[]{:S(2)}) collective-permute-start(bf16[64,1024]{0,1:T(8,128)(2,1)S(1)} %pad_maximum_fusion.2), channel_id=1, source_target_pairs={{0,16},{4,20},{8,24},{12,28},{16,0},{20,4},{24,8},{28,12},{1,17},{... | collective-permute-start | bytes 393224 | tf_op jit(solution)/shard_map/ppermute | solution.py:15
  83.8 23.1 %collective-permute-start.8 = (bf16[2,64,1024]{1,2,0:T(8,128)(2,1)S(1)}, bf16[2,64,1024]{1,2,0:T(8,128)(2,1)S(1)}, u32[]{:S(2)}, u32[]{:S(2)}) collective-permute-start(bf16[2,64,1024]{1,2,0:T(8,128)(2,1)S(1)} %get-tuple-element.33), channel_id=1, source_target_pairs={{0,16},{4,20},{8,24},{12,28},{16,0},{20,4},{24,8},{28,12},{1,17},{... | collective-permute-start | bytes 786440 | tf_op jit(solution)/shard_map/ppermute | solution.py:15
  97.5 9.2 %collective-permute-start.6 = (bf16[2,64,1024]{1,2,0:T(8,128)(2,1)S(1)}, bf16[2,64,1024]{1,2,0:T(8,128)(2,1)S(1)}, u32[]{:S(2)}, u32[]{:S(2)}) collective-permute-start(bf16[2,64,1024]{1,2,0:T(8,128)(2,1)S(1)} %get-tuple-element.31), channel_id=1, source_target_pairs={{0,4},{4,0},{8,12},{12,8},{16,20},{20,16},{24,28},{28,24},{1,5},{5... | collective-permute-start | bytes 786440 | tf_op jit(solution)/shard_map/ppermute | solution.py:15
  111.2 16.0 %collective-permute-start.10 = (bf16[256,1024]{1,0:T(8,128)(2,1)S(1)}, bf16[256,1024]{1,0:T(8,128)(2,1)S(1)}, u32[]{:S(2)}, u32[]{:S(2)}) collective-permute-start(bf16[256,1024]{1,0:T(8,128)(2,1)S(1)} %slice.971), channel_id=1, source_target_pairs={{0,1},{1,0},{2,3},{3,2},{4,5},{5,4},{6,7},{7,6},{8,9},{9,8},{10,11... | collective-permute-start | bytes 1572872 | tf_op jit(solution)/shard_map/ppermute | solution.py:15
  127.5 8.9 %collective-permute-start.11 = (bf16[128,1024]{1,0:T(8,128)(2,1)S(1)}, bf16[128,1024]{1,0:T(8,128)(2,1)S(1)}, u32[]{:S(2)}, u32[]{:S(2)}) collective-permute-start(bf16[128,1024]{1,0:T(8,128)(2,1)S(1)} %slice.973), channel_id=1, source_target_pairs={{0,2},{1,3},{2,0},{3,1},{4,6},{5,7},{6,4},{7,5},{8,10},{9,11},{10,... | collective-permute-start | bytes 786440 | tf_op jit(solution)/shard_map/ppermute | solution.py:15
  138.3 7.4 %collective-permute-start.14 = (bf16[32,1024]{1,0:T(8,128)(2,1)S(1)}, bf16[32,1024]{1,0:T(8,128)(2,1)S(1)}, u32[]{:S(2)}, u32[]{:S(2)}) collective-permute-start(bf16[32,1024]{1,0:T(8,128)(2,1)S(1)} %get-tuple-element.74), channel_id=1, source_target_pairs={{0,20},{4,16},{8,28},{12,24},{16,4},{20,0},{24,12},{28,8},{1,21},{... | collective-permute-start | bytes 196616 | tf_op jit(solution)/shard_map/ppermute | solution.py:15
  146.4 12.8 %collective-permute-start.51 = (bf16[32,4096]{1,0:T(8,128)(2,1)S(1)}, bf16[32,4096]{1,0:T(8,128)(2,1)S(1)}, u32[]{:S(2)}, u32[]{:S(2)}) collective-permute-start(bf16[32,4096]{1,0:T(8,128)(2,1)S(1)} %multiply_convert_fusion.6), channel_id=1, source_target_pairs={{0,24},{4,28},{8,16},{12,20},{16,8},{20,12},{24,0},{28,4},{1,25},{... | collective-permute-start | bytes 786440 | tf_op jit(solution)/shard_map/ppermute | solution.py:15
  147.8 21.6 %collective-permute-start.39 = (bf16[32,4096]{1,0:T(8,128)(2,1)S(1)}, bf16[32,4096]{1,0:T(8,128)(2,1)S(1)}, u32[]{:S(2)}, u32[]{:S(2)}) collective-permute-start(bf16[32,4096]{1,0:T(8,128)(2,1)S(1)} %multiply_convert_fusion.6), channel_id=1, source_target_pairs={{0,16},{4,20},{8,24},{12,28},{16,0},{20,4},{24,8},{28,12},{1,17},{... | collective-permute-start | bytes 786440 | tf_op jit(solution)/shard_map/ppermute | solution.py:15
  148.1 22.0 %collective-permute-start.27 = (bf16[32,4096]{1,0:T(8,128)(2,1)S(1)}, bf16[32,4096]{1,0:T(8,128)(2,1)S(1)}, u32[]{:S(2)}, u32[]{:S(2)}) collective-permute-start(bf16[32,4096]{1,0:T(8,128)(2,1)S(1)} %multiply_convert_fusion.6), channel_id=1, source_target_pairs={{0,8},{4,12},{8,0},{12,4},{16,24},{20,28},{24,16},{28,20},{1,9},{5... | collective-permute-start | bytes 786440 | tf_op jit(solution)/shard_map/ppermute | solution.py:15
  155.9 18.5 %collective-permute-start.18 = (bf16[32,4096]{1,0:T(8,128)(2,1)S(1)}, bf16[32,4096]{1,0:T(8,128)(2,1)S(1)}, u32[]{:S(2)}, u32[]{:S(2)}) collective-permute-start(bf16[32,4096]{1,0:T(8,128)(2,1)S(1)} %pad_maximum_fusion.4), channel_id=1, source_target_pairs={{0,2},{1,3},{2,0},{3,1},{4,6},{5,7},{6,4},{7,5},{8,10},{9,11},{10,... | collective-permute-start | bytes 786440 | tf_op jit(solution)/shard_map/ppermute | solution.py:15
  157.5 29.4 %collective-permute-start.20 = (bf16[32,4096]{1,0:T(8,128)(2,1)S(1)}, bf16[32,4096]{1,0:T(8,128)(2,1)S(1)}, u32[]{:S(2)}, u32[]{:S(2)}) collective-permute-start(bf16[32,4096]{1,0:T(8,128)(2,1)S(1)} %pad_maximum_fusion.5), channel_id=1, source_target_pairs={{0,4},{4,0},{8,12},{12,8},{16,20},{20,16},{24,28},{28,24},{1,5},{5... | collective-permute-start | bytes 786440 | tf_op jit(solution)/shard_map/ppermute | solution.py:15
  179.2 10.5 %collective-permute-start.53 = (bf16[32,4096]{1,0:T(8,128)(2,1)S(1)}, bf16[32,4096]{1,0:T(8,128)(2,1)S(1)}, u32[]{:S(2)}, u32[]{:S(2)}) collective-permute-start(bf16[32,4096]{1,0:T(8,128)(2,1)S(1)} %pad_maximum_fusion.10), channel_id=1, source_target_pairs={{0,2},{1,3},{2,0},{3,1},{4,6},{5,7},{6,4},{7,5},{8,10},{9,11},{10,... | collective-permute-start | bytes 786440 | tf_op jit(solution)/shard_map/ppermute | solution.py:15
  181.3 11.9 %collective-permute-start.55 = (bf16[32,4096]{1,0:T(8,128)(2,1)S(1)}, bf16[32,4096]{1,0:T(8,128)(2,1)S(1)}, u32[]{:S(2)}, u32[]{:S(2)}) collective-permute-start(bf16[32,4096]{1,0:T(8,128)(2,1)S(1)} %pad_maximum_fusion.11), channel_id=1, source_target_pairs={{0,4},{4,0},{8,12},{12,8},{16,20},{20,16},{24,28},{28,24},{1,5},{5... | collective-permute-start | bytes 786440 | tf_op jit(solution)/shard_map/ppermute | solution.py:15
  183.4 11.3 %collective-permute-start.41 = (bf16[32,4096]{1,0:T(8,128)(2,1)S(1)}, bf16[32,4096]{1,0:T(8,128)(2,1)S(1)}, u32[]{:S(2)}, u32[]{:S(2)}) collective-permute-start(bf16[32,4096]{1,0:T(8,128)(2,1)S(1)} %pad_maximum_fusion.8), channel_id=1, source_target_pairs={{0,2},{1,3},{2,0},{3,1},{4,6},{5,7},{6,4},{7,5},{8,10},{9,11},{10,... | collective-permute-start | bytes 786440 | tf_op jit(solution)/shard_map/ppermute | solution.py:15
  185.0 11.9 %collective-permute-start.43 = (bf16[32,4096]{1,0:T(8,128)(2,1)S(1)}, bf16[32,4096]{1,0:T(8,128)(2,1)S(1)}, u32[]{:S(2)}, u32[]{:S(2)}) collective-permute-start(bf16[32,4096]{1,0:T(8,128)(2,1)S(1)} %pad_maximum_fusion.9), channel_id=1, source_target_pairs={{0,4},{4,0},{8,12},{12,8},{16,20},{20,16},{24,28},{28,24},{1,5},{5... | collective-permute-start | bytes 786440 | tf_op jit(solution)/shard_map/ppermute | solution.py:15
  187.0 11.1 %collective-permute-start.29 = (bf16[32,4096]{1,0:T(8,128)(2,1)S(1)}, bf16[32,4096]{1,0:T(8,128)(2,1)S(1)}, u32[]{:S(2)}, u32[]{:S(2)}) collective-permute-start(bf16[32,4096]{1,0:T(8,128)(2,1)S(1)} %pad_maximum_fusion.6), channel_id=1, source_target_pairs={{0,2},{1,3},{2,0},{3,1},{4,6},{5,7},{6,4},{7,5},{8,10},{9,11},{10,... | collective-permute-start | bytes 786440 | tf_op jit(solution)/shard_map/ppermute | solution.py:15
  189.8 10.6 %collective-permute-start.31 = (bf16[32,4096]{1,0:T(8,128)(2,1)S(1)}, bf16[32,4096]{1,0:T(8,128)(2,1)S(1)}, u32[]{:S(2)}, u32[]{:S(2)}) collective-permute-start(bf16[32,4096]{1,0:T(8,128)(2,1)S(1)} %pad_maximum_fusion.7), channel_id=1, source_target_pairs={{0,4},{4,0},{8,12},{12,8},{16,20},{20,16},{24,28},{28,24},{1,5},{5... | collective-permute-start | bytes 786440 | tf_op jit(solution)/shard_map/ppermute | solution.py:15
  193.3 7.8 %collective-permute-start.21 = (bf16[128,4096]{1,0:T(8,128)(2,1)S(1)}, bf16[128,4096]{1,0:T(8,128)(2,1)S(1)}, u32[]{:S(2)}, u32[]{:S(2)}) collective-permute-start(bf16[128,4096]{1,0:T(8,128)(2,1)S(1)} %get-tuple-element.34), channel_id=1, source_target_pairs={{0,1},{1,0},{2,3},{3,2},{4,5},{5,4},{6,7},{7,6},{8,9},{9,8},{10,11... | collective-permute-start | bytes 3145736 | tf_op jit(solution)/shard_map/ppermute | solution.py:15
  194.7 24.1 %collective-permute-start.56 = (bf16[128,4096]{1,0:T(8,128)(2,1)}, bf16[128,4096]{1,0:T(8,128)(2,1)S(1)}, u32[]{:S(2)}, u32[]{:S(2)}) collective-permute-start(bf16[128,4096]{1,0:T(8,128)(2,1)} %get-tuple-element.64), channel_id=1, source_target_pairs={{0,1},{1,0},{2,3},{3,2},{4,5},{5,4},{6,7},{7,6},{8,9},{9,8},{10,11... | collective-permute-start | bytes 3145736 | tf_op jit(solution)/shard_map/ppermute | solution.py:15
  197.6 42.6 %collective-permute-start.44 = (bf16[128,4096]{1,0:T(8,128)(2,1)}, bf16[128,4096]{1,0:T(8,128)(2,1)}, u32[]{:S(2)}, u32[]{:S(2)}) collective-permute-start(bf16[128,4096]{1,0:T(8,128)(2,1)} %get-tuple-element.54), channel_id=1, source_target_pairs={{0,1},{1,0},{2,3},{3,2},{4,5},{5,4},{6,7},{7,6},{8,9},{9,8},{10,11... | collective-permute-start | bytes 3145736 | tf_op jit(solution)/shard_map/ppermute | solution.py:15
  201.1 60.2 %collective-permute-start.32 = (bf16[128,4096]{1,0:T(8,128)(2,1)}, bf16[128,4096]{1,0:T(8,128)(2,1)}, u32[]{:S(2)}, u32[]{:S(2)}) collective-permute-start(bf16[128,4096]{1,0:T(8,128)(2,1)} %get-tuple-element.44), channel_id=1, source_target_pairs={{0,1},{1,0},{2,3},{3,2},{4,5},{5,4},{6,7},{7,6},{8,9},{9,8},{10,11... | collective-permute-start | bytes 3145736 | tf_op jit(solution)/shard_map/ppermute | solution.py:15
  218.8 66.3 %collective-permute-start.22 = (bf16[128,4096]{1,0:T(8,128)(2,1)}, bf16[128,4096]{1,0:T(8,128)(2,1)}, u32[]{:S(2)}, u32[]{:S(2)}) collective-permute-start(bf16[128,4096]{1,0:T(8,128)(2,1)} %slice.988), channel_id=1, source_target_pairs={{0,1},{1,0},{2,3},{3,2},{4,5},{5,4},{6,7},{7,6},{8,9},{9,8},{10,11... | collective-permute-start | bytes 3145736 | tf_op jit(solution)/shard_map/ppermute | solution.py:15
  240.2 49.9 %collective-permute-start.57 = (bf16[128,4096]{1,0:T(8,128)(2,1)}, bf16[128,4096]{1,0:T(8,128)(2,1)}, u32[]{:S(2)}, u32[]{:S(2)}) collective-permute-start(bf16[128,4096]{1,0:T(8,128)(2,1)} %slice.1024), channel_id=1, source_target_pairs={{0,1},{1,0},{2,3},{3,2},{4,5},{5,4},{6,7},{7,6},{8,9},{9,8},{10,11... | collective-permute-start | bytes 3145736 | tf_op jit(solution)/shard_map/ppermute | solution.py:15
  261.3 30.9 %collective-permute-start.45 = (bf16[128,4096]{1,0:T(8,128)(2,1)}, bf16[128,4096]{1,0:T(8,128)(2,1)S(1)}, u32[]{:S(2)}, u32[]{:S(2)}) collective-permute-start(bf16[128,4096]{1,0:T(8,128)(2,1)} %slice.1012), channel_id=1, source_target_pairs={{0,1},{1,0},{2,3},{3,2},{4,5},{5,4},{6,7},{7,6},{8,9},{9,8},{10,11... | collective-permute-start | bytes 3145736 | tf_op jit(solution)/shard_map/ppermute | solution.py:15
  285.0 8.2 %collective-permute-start.33 = (bf16[128,4096]{1,0:T(8,128)(2,1)S(1)}, bf16[128,4096]{1,0:T(8,128)(2,1)S(1)}, u32[]{:S(2)}, u32[]{:S(2)}) collective-permute-start(bf16[128,4096]{1,0:T(8,128)(2,1)S(1)} %slice.1000), channel_id=1, source_target_pairs={{0,1},{1,0},{2,3},{3,2},{4,5},{5,4},{6,7},{7,6},{8,9},{9,8},{10,11... | collective-permute-start | bytes 3145736 | tf_op jit(solution)/shard_map/ppermute | solution.py:15
  287.1 9.2 %collective-permute-start.23 = (bf16[32,4096]{1,0:T(8,128)(2,1)S(1)}, bf16[32,4096]{1,0:T(8,128)(2,1)S(1)}, u32[]{:S(2)}, u32[]{:S(2)}) collective-permute-start(bf16[32,4096]{1,0:T(8,128)(2,1)S(1)} %get-tuple-element.16), channel_id=1, source_target_pairs={{0,2},{1,3},{2,0},{3,1},{4,6},{5,7},{6,4},{7,5},{8,10},{9,11},{10,... | collective-permute-start | bytes 786440 | tf_op jit(solution)/shard_map/ppermute | solution.py:15
  288.5 9.3 %collective-permute-start.25 = (bf16[32,4096]{1,0:T(8,128)(2,1)S(1)}, bf16[32,4096]{1,0:T(8,128)(2,1)S(1)}, u32[]{:S(2)}, u32[]{:S(2)}) collective-permute-start(bf16[32,4096]{1,0:T(8,128)(2,1)S(1)} %get-tuple-element.17), channel_id=1, source_target_pairs={{0,4},{4,0},{8,12},{12,8},{16,20},{20,16},{24,28},{28,24},{1,5},{5... | collective-permute-start | bytes 786440 | tf_op jit(solution)/shard_map/ppermute | solution.py:15
  291.7 19.1 %collective-permute-start.58 = (bf16[32,4096]{1,0:T(8,128)(2,1)S(1)}, bf16[32,4096]{1,0:T(8,128)(2,1)S(1)}, u32[]{:S(2)}, u32[]{:S(2)}) collective-permute-start(bf16[32,4096]{1,0:T(8,128)(2,1)S(1)} %get-tuple-element.28), channel_id=1, source_target_pairs={{0,2},{1,3},{2,0},{3,1},{4,6},{5,7},{6,4},{7,5},{8,10},{9,11},{10,... | collective-permute-start | bytes 786440 | tf_op jit(solution)/shard_map/ppermute | solution.py:15
  292.2 20.2 %collective-permute-start.60 = (bf16[32,4096]{1,0:T(8,128)(2,1)S(1)}, bf16[32,4096]{1,0:T(8,128)(2,1)S(1)}, u32[]{:S(2)}, u32[]{:S(2)}) collective-permute-start(bf16[32,4096]{1,0:T(8,128)(2,1)S(1)} %get-tuple-element.29), channel_id=1, source_target_pairs={{0,4},{4,0},{8,12},{12,8},{16,20},{20,16},{24,28},{28,24},{1,5},{5... | collective-permute-start | bytes 786440 | tf_op jit(solution)/shard_map/ppermute | solution.py:15
  293.2 19.9 %collective-permute-start.46 = (bf16[32,4096]{1,0:T(8,128)(2,1)S(1)}, bf16[32,4096]{1,0:T(8,128)(2,1)S(1)}, u32[]{:S(2)}, u32[]{:S(2)}) collective-permute-start(bf16[32,4096]{1,0:T(8,128)(2,1)S(1)} %get-tuple-element.24), channel_id=1, source_target_pairs={{0,2},{1,3},{2,0},{3,1},{4,6},{5,7},{6,4},{7,5},{8,10},{9,11},{10,... | collective-permute-start | bytes 786440 | tf_op jit(solution)/shard_map/ppermute | solution.py:15
  296.4 17.5 %collective-permute-start.48 = (bf16[32,4096]{1,0:T(8,128)(2,1)S(1)}, bf16[32,4096]{1,0:T(8,128)(2,1)S(1)}, u32[]{:S(2)}, u32[]{:S(2)}) collective-permute-start(bf16[32,4096]{1,0:T(8,128)(2,1)S(1)} %get-tuple-element.25), channel_id=1, source_target_pairs={{0,4},{4,0},{8,12},{12,8},{16,20},{20,16},{24,28},{28,24},{1,5},{5... | collective-permute-start | bytes 786440 | tf_op jit(solution)/shard_map/ppermute | solution.py:15
  297.9 11.5 %collective-permute-start.26 = (bf16[16,4096]{1,0:T(8,128)(2,1)S(1)}, bf16[16,4096]{1,0:T(8,128)(2,1)S(1)}, u32[]{:S(2)}, u32[]{:S(2)}) collective-permute-start(bf16[16,4096]{1,0:T(8,128)(2,1)S(1)} %slice.996), channel_id=1, source_target_pairs={{0,2},{1,3},{2,0},{3,1},{4,6},{5,7},{6,4},{7,5},{8,10},{9,11},{10,... | collective-permute-start | bytes 393224 | tf_op jit(solution)/shard_map/ppermute | solution.py:15
  309.4 9.2 %collective-permute-start.34 = (bf16[32,4096]{1,0:T(8,128)(2,1)S(1)}, bf16[32,4096]{1,0:T(8,128)(2,1)S(1)}, u32[]{:S(2)}, u32[]{:S(2)}) collective-permute-start(bf16[32,4096]{1,0:T(8,128)(2,1)S(1)} %get-tuple-element.20), channel_id=1, source_target_pairs={{0,2},{1,3},{2,0},{3,1},{4,6},{5,7},{6,4},{7,5},{8,10},{9,11},{10,... | collective-permute-start | bytes 786440 | tf_op jit(solution)/shard_map/ppermute | solution.py:15
  310.8 9.3 %collective-permute-start.36 = (bf16[32,4096]{1,0:T(8,128)(2,1)S(1)}, bf16[32,4096]{1,0:T(8,128)(2,1)S(1)}, u32[]{:S(2)}, u32[]{:S(2)}) collective-permute-start(bf16[32,4096]{1,0:T(8,128)(2,1)S(1)} %get-tuple-element.21), channel_id=1, source_target_pairs={{0,4},{4,0},{8,12},{12,8},{16,20},{20,16},{24,28},{28,24},{1,5},{5... | collective-permute-start | bytes 786440 | tf_op jit(solution)/shard_map/ppermute | solution.py:15
  312.5 19.8 %collective-permute-start.24 = (bf16[16,4096]{1,0:T(8,128)(2,1)S(1)}, bf16[16,4096]{1,0:T(8,128)(2,1)S(1)}, u32[]{:S(2)}, u32[]{:S(2)}) collective-permute-start(bf16[16,4096]{1,0:T(8,128)(2,1)S(1)} %slice.992), channel_id=1, source_target_pairs={{0,4},{4,0},{8,12},{12,8},{16,20},{20,16},{24,28},{28,24},{1,5},{5... | collective-permute-start | bytes 393224 | tf_op jit(solution)/shard_map/ppermute | solution.py:15
  313.1 8.8 %collective-permute-start.61 = (bf16[16,4096]{1,0:T(8,128)(2,1)S(1)}, bf16[16,4096]{1,0:T(8,128)(2,1)S(1)}, u32[]{:S(2)}, u32[]{:S(2)}) collective-permute-start(bf16[16,4096]{1,0:T(8,128)(2,1)S(1)} %slice.1032), channel_id=1, source_target_pairs={{0,2},{1,3},{2,0},{3,1},{4,6},{5,7},{6,4},{7,5},{8,10},{9,11},{10,... | collective-permute-start | bytes 393224 | tf_op jit(solution)/shard_map/ppermute | solution.py:15
  313.8 11.9 %collective-permute-start.59 = (bf16[16,4096]{1,0:T(8,128)(2,1)S(1)}, bf16[16,4096]{1,0:T(8,128)(2,1)S(1)}, u32[]{:S(2)}, u32[]{:S(2)}) collective-permute-start(bf16[16,4096]{1,0:T(8,128)(2,1)S(1)} %slice.1028), channel_id=1, source_target_pairs={{0,4},{4,0},{8,12},{12,8},{16,20},{20,16},{24,28},{28,24},{1,5},{5... | collective-permute-start | bytes 393224 | tf_op jit(solution)/shard_map/ppermute | solution.py:15
  318.7 8.7 %collective-permute-start.49 = (bf16[16,4096]{1,0:T(8,128)(2,1)S(1)}, bf16[16,4096]{1,0:T(8,128)(2,1)S(1)}, u32[]{:S(2)}, u32[]{:S(2)}) collective-permute-start(bf16[16,4096]{1,0:T(8,128)(2,1)S(1)} %slice.1020), channel_id=1, source_target_pairs={{0,2},{1,3},{2,0},{3,1},{4,6},{5,7},{6,4},{7,5},{8,10},{9,11},{10,... | collective-permute-start | bytes 393224 | tf_op jit(solution)/shard_map/ppermute | solution.py:15
  320.1 10.0 %collective-permute-start.47 = (bf16[16,4096]{1,0:T(8,128)(2,1)S(1)}, bf16[16,4096]{1,0:T(8,128)(2,1)S(1)}, u32[]{:S(2)}, u32[]{:S(2)}) collective-permute-start(bf16[16,4096]{1,0:T(8,128)(2,1)S(1)} %slice.1016), channel_id=1, source_target_pairs={{0,4},{4,0},{8,12},{12,8},{16,20},{20,16},{24,28},{28,24},{1,5},{5... | collective-permute-start | bytes 393224 | tf_op jit(solution)/shard_map/ppermute | solution.py:15
  321.9 8.4 %collective-permute-start.37 = (bf16[16,4096]{1,0:T(8,128)(2,1)S(1)}, bf16[16,4096]{1,0:T(8,128)(2,1)S(1)}, u32[]{:S(2)}, u32[]{:S(2)}) collective-permute-start(bf16[16,4096]{1,0:T(8,128)(2,1)S(1)} %slice.1008), channel_id=1, source_target_pairs={{0,2},{1,3},{2,0},{3,1},{4,6},{5,7},{6,4},{7,5},{8,10},{9,11},{10,... | collective-permute-start | bytes 393224 | tf_op jit(solution)/shard_map/ppermute | solution.py:15
  327.4 11.1 %collective-permute-start.62 = (bf16[32,4096]{1,0:T(8,128)(2,1)S(1)}, bf16[32,4096]{1,0:T(8,128)(2,1)S(1)}, u32[]{:S(2)}, u32[]{:S(2)}) collective-permute-start(bf16[32,4096]{1,0:T(8,128)(2,1)S(1)} %maximum_bitcast_fusion.4), channel_id=1, source_target_pairs={{0,24},{4,28},{8,16},{12,20},{16,8},{20,12},{24,0},{28,4},{1,25},{... | collective-permute-start | bytes 786440 | tf_op jit(solution)/shard_map/ppermute | solution.py:15
  330.2 17.0 %collective-permute-start.50 = (bf16[32,4096]{1,0:T(8,128)(2,1)S(1)}, bf16[32,4096]{1,0:T(8,128)(2,1)S(1)}, u32[]{:S(2)}, u32[]{:S(2)}) collective-permute-start(bf16[32,4096]{1,0:T(8,128)(2,1)S(1)} %maximum_bitcast_fusion.3), channel_id=1, source_target_pairs={{0,16},{4,20},{8,24},{12,28},{16,0},{20,4},{24,8},{28,12},{1,17},{... | collective-permute-start | bytes 786440 | tf_op jit(solution)/shard_map/ppermute | solution.py:15
  330.7 16.5 %collective-permute-start.38 = (bf16[32,4096]{1,0:T(8,128)(2,1)S(1)}, bf16[32,4096]{1,0:T(8,128)(2,1)S(1)}, u32[]{:S(2)}, u32[]{:S(2)}) collective-permute-start(bf16[32,4096]{1,0:T(8,128)(2,1)S(1)} %maximum_bitcast_fusion.2), channel_id=1, source_target_pairs={{0,8},{4,12},{8,0},{12,4},{16,24},{20,28},{24,16},{28,20},{1,9},{5... | collective-permute-start | bytes 786440 | tf_op jit(solution)/shard_map/ppermute | solution.py:15
  (44 other events, 462.1 us)

commit v2 on v1

--- a/solution.py
+++ b/solution.py
@@ -1,13 +1,16 @@
 import jax
 import jax.numpy as jnp
 from jax import lax
+from jax.experimental import pallas as pl
+from jax.experimental.pallas import tpu as pltpu
 from jax.sharding import PartitionSpec as P
 
 PAIR = 2
 eps_norm = 1e-05
 BF = jnp.bfloat16
 F32 = jnp.float32
-GROUPS = 4
+LANES = 128
+DOWN_TILE = 512
 
 
 def swap(x, axis, flip):
@@ -166,33 +169,155 @@
     return mixed.astype(F32), scale
 
 
-def gather_plane(pieces):
-    half = pieces.shape[1] // 2
-    width = pieces.shape[2]
-    part_a = pieces[:, :half].reshape(-1, width)
-    part_b = pieces[:, half:].reshape(-1, width)
-    part_a = jnp.concatenate([part_a, swap(part_a, "ctx", 1)])
-    part_b = jnp.concatenate([part_b, swap(part_b, "exp", 2)])
-    part_a2 = swap(part_a, "exp", 2)
-    part_b2 = swap(part_b, "ctx", 1)
-    rows = jnp.concatenate([part_a, part_a2, part_b, part_b2])
-    return jnp.concatenate([rows, swap(rows, "exp", 1)])
-
-
-def scatter_plane(rows, count):
-    def fold(values, axis, flip):
-        cut = values.shape[0] // 2
-        got = swap(values[cut:], axis, flip)
-        return (values[:cut].astype(F32) + got.astype(F32)).astype(BF)
-
-    rows = fold(rows, "exp", 1)
-    cut = rows.shape[0] // 2
-    part_a = fold(fold(rows[:cut], "exp", 2), "ctx", 1)
-    part_b = fold(fold(rows[cut:], "ctx", 1), "exp", 2)
-    width = rows.shape[1]
-    part_a = part_a.reshape(count, -1, width)
-    part_b = part_b.reshape(count, -1, width)
-    return jnp.concatenate([part_a, part_b], axis=1)
+def pack_kernel(*refs):
+    pieces, out, sems = refs[:-2], refs[-2], refs[-1]
+    copies = []
+    row = 0
+    for i, piece in enumerate(pieces):
+        rows = piece.shape[0]
+        copies.append(pltpu.make_async_copy(piece, out.at[pl.ds(row, rows)], sems.at[i]))
+        row += rows
+    for c in copies:
+        c.start()
+    for c in copies:
+        c.wait()
+
+
+def pack(pieces):
+    rows = sum(p.shape[0] for p in pieces)
+    width = pieces[0].shape[1]
+    size = 2 * rows * width
+    return pl.pallas_call(
+        pack_kernel,
+        out_shape=jax.ShapeDtypeStruct((rows, width), pieces[0].dtype),
+        in_specs=[pl.BlockSpec(memory_space=pl.ANY)] * len(pieces),
+        out_specs=pl.BlockSpec(memory_space=pl.ANY),
+        scratch_shapes=[pltpu.SemaphoreType.DMA((len(pieces),))],
+        cost_estimate=pl.CostEstimate(flops=0, bytes_accessed=2 * size, transcendentals=0),
+    )(*pieces)
+
+
+def expert_kernel(
+    own, mate, gate, up, down, pick, out_own, out_mate, rows, hidden, gu, dn, row_sem, gu_sem, dn_sem
+):
+    half = own.shape[0]
+    model = gate.shape[0]
+    tiles = gate.shape[1] // LANES
+    down_tiles = model // DOWN_TILE
+
+    def row_copies():
+        return [
+            pltpu.make_async_copy(own, rows.at[pl.ds(0, half)], row_sem.at[0]),
+            pltpu.make_async_copy(mate, rows.at[pl.ds(half, half)], row_sem.at[1]),
+        ]
+
+    def gu_copies(j, slot):
+        at = pl.ds(pl.multiple_of(j * LANES, LANES), LANES)
+        return [
+            pltpu.make_async_copy(gate.at[:, at], gu.at[slot, :, pl.ds(0, LANES)], gu_sem.at[slot, 0]),
+            pltpu.make_async_copy(up.at[:, at], gu.at[slot, :, pl.ds(LANES, LANES)], gu_sem.at[slot, 1]),
+        ]
+
+    def dn_copy(j, slot):
+        at = pl.ds(pl.multiple_of(j * DOWN_TILE, DOWN_TILE), DOWN_TILE)
+        return pltpu.make_async_copy(down.at[:, at], dn.at[slot], dn_sem.at[slot])
+
+    for c in row_copies() + gu_copies(0, 0):
+        c.start()
+    dn_copy(0, 0).start()
+    for c in row_copies():
+        c.wait()
+
+    def gate_up(j, carry):
+        slot = lax.rem(j, 2)
+
+        @pl.when(j + 1 < tiles)
+        def _():
+            for c in gu_copies(j + 1, lax.rem(j + 1, 2)):
+                c.start()
+
+        for c in gu_copies(j, slot):
+            c.wait()
+        both = jnp.dot(rows[:, :model], gu[slot], preferred_element_type=F32)
+        gate_val = both[:, :LANES]
+        act = gate_val / (1.0 + jnp.exp(-gate_val)) * both[:, LANES:]
+        hidden[:, pl.ds(pl.multiple_of(j * LANES, LANES), LANES)] = act.astype(BF)
+        return carry
+
+    lax.fori_loop(0, tiles, gate_up, 0)
+    weight = jnp.sum(rows[:, model:].astype(F32) * pick[...], axis=1, keepdims=True)
+
+    def down_part(j, carry):
+        slot = lax.rem(j, 2)
+
+        @pl.when(j + 1 < down_tiles)
+        def _():
+            dn_copy(j + 1, lax.rem(j + 1, 2)).start()
+
+        dn_copy(j, slot).wait()
+        part = jnp.dot(hidden[...], dn[slot], preferred_element_type=F32) * weight
+        at = pl.ds(pl.multiple_of(j * DOWN_TILE, DOWN_TILE), DOWN_TILE)
+        out_own[:, at] = part[:half].astype(BF)
+        out_mate[:, at] = part[half:].astype(BF)
+        return carry
+
+    lax.fori_loop(0, down_tiles, down_part, 0)
+
+
+def experts(own, mate, gate, up, down, pick):
+    half, width = own.shape
+    model, units = gate.shape
+    out = jax.ShapeDtypeStruct((half, model), BF)
+    whole = pl.BlockSpec(memory_space=pltpu.VMEM)
+    anywhere = pl.BlockSpec(memory_space=pl.ANY)
+    flops = 2 * 2 * half * model * units * 3
+    moved = 2 * (3 * model * units + 8 * half * model)
+    return pl.pallas_call(
+        expert_kernel,
+        out_shape=(out, out),
+        in_specs=[anywhere] * 5 + [whole],
+        out_specs=(whole, whole),
+        scratch_shapes=[
+            pltpu.VMEM((2 * half, width), BF),
+            pltpu.VMEM((2 * half, units), BF),
+            pltpu.VMEM((2, model, 2 * LANES), BF),
+            pltpu.VMEM((2, units, DOWN_TILE), BF),
+            pltpu.SemaphoreType.DMA((2,)),
+            pltpu.SemaphoreType.DMA((2, 2)),
+            pltpu.SemaphoreType.DMA((2,)),
+        ],
+        compiler_params=pltpu.CompilerParams(vmem_limit_bytes=40 * 1024 * 1024),
+        cost_estimate=pl.CostEstimate(flops=flops, bytes_accessed=moved, transcendentals=2 * half * units),
+    )(own, mate, gate, up, down, pick)
+
+
+def gather_plane(piece):
+    half = piece.shape[0] // 2
+    from_x = swap(piece, "exp", 2)
+    from_y = swap(piece, "ctx", 1)
+    far_a = swap(from_y[:half], "exp", 2)
+    far_b = swap(from_x[half:], "ctx", 1)
+    return pack([piece, from_x, from_y, far_a, far_b])
+
+
+def scatter_plane(own, mate):
+    got = swap(mate, "exp", 1)
+    size = own.shape[0] // 4
+    half = size // 2
+
+    def both(first, rows):
+        last = first + rows
+        return own[first:last].astype(F32) + got[first:last].astype(F32)
+
+    far_a = swap(both(3 * size, half).astype(BF), "exp", 2)
+    far_b = swap(both(3 * size + half, half).astype(BF), "ctx", 1)
+    to_x = both(size, size)
+    to_y = both(2 * size, size)
+    to_y = jnp.concatenate([to_y[:half] + far_a.astype(F32), to_y[half:]])
+    to_x = jnp.concatenate([to_x[:half], to_x[half:] + far_b.astype(F32)])
+    from_x = swap(to_x.astype(BF), "exp", 2)
+    from_y = swap(to_y.astype(BF), "ctx", 1)
+    return both(0, size) + from_x.astype(F32) + from_y.astype(F32)
 
 
 def local(
@@ -221,12 +346,13 @@
     tok = inputs.shape[0]
     quarter = tok // n_exp
     pairs = n_ctx // 2
-    experts = n_ctx // PAIR
-    named = route_ids[:, :, None] == jnp.arange(experts, dtype=jnp.int32)[None, None, :]
+    named = route_ids[:, :, None] == jnp.arange(LANES // 2, dtype=jnp.int32)[None, None, :]
     weights = jnp.sum(jnp.where(named, route_gates[:, :, None], 0.0), axis=1)
-    weights_all = lax.all_gather(weights, "ctx")
-    own_weight = lax.dynamic_index_in_dim(weights_all, me_ctx // PAIR, 2, False)
-    own_weight = own_weight.reshape(n_ctx, n_exp, quarter)
+    weights = lax.dynamic_slice_in_dim(weights, me_exp * quarter, quarter, 0)
+    weights_high = weights.astype(BF)
+    weights_low = (weights - weights_high.astype(F32)).astype(BF)
+    lane = jnp.arange(LANES, dtype=jnp.int32)
+    pick = (lane % (LANES // 2) == me_ctx // PAIR).astype(F32)[None, :]
 
     gated = mixer_rows(
         inputs, gate_input, b_proj, c_proj, step_size, decay_rate, skip_gain, start_state
@@ -237,31 +363,19 @@
     moe_scale = lax.rsqrt(jnp.mean(hidden * hidden, axis=1, keepdims=True) + eps_norm)
     moe_in = (hidden * moe_scale * moe_gain[None, :]).astype(BF)
 
-    planes = [moe_in] + [swap(moe_in, "ctx", 2 * d) for d in range(1, pairs)]
-    gate_rows, up_rows, down_rows = w_gate[0], w_up[0], w_down[0]
-    half = quarter // 2
-    order = [(x, y, "a") for x in (0, 1) for y in (0, 1)]
-    order = order + [(x, y, "b") for y in (0, 1) for x in (0, 1)]
+    payload = jnp.concatenate([moe_in, weights_high, weights_low], axis=1)
+    planes = [payload] + [swap(payload, "ctx", 2 * d) for d in range(1, pairs)]
     total = hidden
-    size = pairs // GROUPS
-    for first in range(0, pairs, size):
-        offsets = list(range(first, first + size))
-        rows = gather_plane(jnp.stack([planes[d] for d in offsets]))
-        row_weight = []
-        for k in (0, 1):
-            for x, y, part in order:
-                for d in offsets:
-                    whole = own_weight[me_ctx ^ (2 * d + y), me_exp ^ (2 * x + k)]
-                    row_weight.append(whole[:half] if part == "a" else whole[half:])
-        row_weight = jnp.concatenate(row_weight)
-        gate_val = mm(rows, gate_rows)
-        up_val = mm(rows, up_rows)
-        activated = (jax.nn.silu(gate_val) * up_val).astype(BF)
-        result = (mm(activated, down_rows) * row_weight[:, None]).astype(BF)
-        summed = scatter_plane(result, size)
+    groups = [[0], [1]] + [[d, d + 1] for d in range(2, pairs, 2)]
+    for offsets in groups:
+        piece = planes[offsets[0]] if len(offsets) == 1 else pack([planes[d] for d in offsets])
+        own = gather_plane(piece)
+        mate = swap(own, "exp", 1)
+        own, mate = experts(own, mate, w_gate[0], w_up[0], w_down[0], pick)
+        summed = scatter_plane(own, mate)
         for i, d in enumerate(offsets):
-            back = summed[i] if d == 0 else swap(summed[i], "ctx", 2 * d)
-            total = total + back.astype(F32)
+            part = summed[i * quarter : (i + 1) * quarter]
+            total = total + (part if d == 0 else swap(part.astype(BF), "ctx", 2 * d).astype(F32))
     return total.astype(BF)
 
 

time: 355 us -> 459 us (1.29)
  Pallas kernels: 0 us -> 204 us
  matrix products: 69.4 us -> 4.06 us
  waiting for transfers between devices: 97.8 us -> 150 us
  blocking collectives: 44.3 us -> 0 us
  local copies, waits for them, and re-layouts: 38.1 us -> 14.3 us
  starting transfers between devices: 69.7 us -> 55.3 us
    pallas_call x0 -> x7, Pallas kernels: none -> 204 us  [the longest x4 152 us: pack(): pl.pallas_call(pack_kernel, out_shape=jax.ShapeDtypeStruct((rows, width),...]
    dot_general x9 -> x1, matrix products: 68.2 us -> 2.79 us  [mm(): return jnp.dot(a, b, preferred_element_type=F32)]
    ppermute x63 -> x53, waiting for transfers between devices: 97.8 us -> 150 us  [swap(): return lax.ppermute(x, axis, [(i, i ^ flip) for i in range(size)])]
    all_gather x1 -> x0, blocking collectives: 44.3 us -> none  [local(): weights_all = lax.all_gather(weights, 'ctx')]
    ppermute x63 -> x53, starting transfers between devices: 69.7 us -> 55.3 us  [swap(): return lax.ppermute(x, axis, [(i, i ^ flip) for i in range(size)])]
    unnamed x95 -> x79, local copies, waits for them, and re-layouts: 23.4 us -> 10.7 us
    slice x32 -> x13, local copies, waits for them, and re-layouts: 5.99 us -> 0.23 us  [the longest x3 0.06 us: scatter_plane(): to_y = jnp.concatenate([to_y[:half] + far_a.astype(F32), to_y[half:]])]
    concatenate x12 -> x1, local copies, waits for them, and re-layouts: 5.36 us -> 0.1 us  [local(): payload = jnp.concatenate([moe_in, weights_high, weights_low], axis=1)]
  transfers between devices with their start and end apart: 63 -> 53, of which waited for: 25 -> 27; matrix products, arithmetic and copies ran while one was open for 29% -> 3% of each run, Pallas kernels for 0% -> 37%
where the time goes in v2:
time: 459 us; the launch traced here: 458 us
  Pallas kernels  204 us (44%)
  waiting for transfers between devices  150 us (33%)
  starting transfers between devices  55.3 us (12%)
  between operations  16.2 us (4%)
  other arithmetic  14.7 us (3%)
  local copies, waits for them, and re-layouts  14.3 us (3%)
    pallas_call x4, Pallas kernels, pack(): pl.pallas_call(pack_kernel, out_shape=jax.ShapeDtypeStruct((rows, width),...  152 us
    ppermute x53, waiting for transfers between devices, swap(): return lax.ppermute(x, axis, [(i, i ^ flip) for i in range(size)])  150 us
    ppermute x53, starting transfers between devices, swap(): return lax.ppermute(x, axis, [(i, i ^ flip) for i in range(size)])  55.3 us
    pallas_call x3, Pallas kernels, experts(): pl.pallas_call(expert_kernel, out_shape=(out, out), in_specs=[anywhere] *...  51.7 us
    unnamed x79, local copies, waits for them, and re-layouts  10.7 us
  transfers between devices with their start and end apart: 53, of which 27 were waited for; matrix products, arithmetic and copies ran while one was open for 3% of the time, Pallas kernels for 37%

profile of v2, /device:TPU:0, one launch (start us, length us, event | category | flops | bytes accessed | tf_op | source)
XLA Modules:
  0.0 457.9 jit_solution(5048110000630711759)
XLA Ops:
  3.9 3.0 collective-permute-start
  6.9 1.6 collective-permute-start.9
  11.2 3.9 collective-permute-start.3
  15.9 22.2 %collective-permute-done.3 = bf16[528,128]{1,0:T(8,128)(2,1)S(1)} collective-permute-done((bf16[528,128]{1,0:T(8,128)(2,1)S(1)}, bf16[528,128]{1,0:T(8,128)(2,1)S(1)}, u32[]{:S(2)}, u32[]{:S(2)}) %collective-permute-start.3) | collective-permute-done | bytes 135200 | tf_op jit(solution)/shard_map/ppermute | solution.py:18
  38.4 2.1 collective-permute-done.1
  42.4 4.5 collective-permute-done.4
  48.3 2.7 collective-permute-start.5
  51.8 8.9 %collective-permute-done.5 = bf16[64,1024]{0,1:T(8,128)(2,1)S(1)} collective-permute-done((bf16[64,1024]{0,1:T(8,128)(2,1)S(1)}, bf16[64,1024]{0,1:T(8,128)(2,1)S(1)}, u32[]{:S(2)}, u32[]{:S(2)}) %collective-permute-start.5) | collective-permute-done | bytes 131104 | tf_op jit(solution)/shard_map/ppermute | solution.py:18
  61.8 11.9 %collective-permute-done.6 = bf16[2,64,1024]{1,2,0:T(8,128)(2,1)S(1)} collective-permute-done((bf16[2,64,1024]{1,2,0:T(8,128)(2,1)S(1)}, bf16[2,64,1024]{1,2,0:T(8,128)(2,1)S(1)}, u32[]{:S(2)}, u32[]{:S(2)}) %collective-permute-start.6) | collective-permute-done | bytes 262176 | tf_op jit(solution)/shard_map/ppermute | solution.py:18
  73.9 12.6 %collective-permute-done.8 = bf16[2,64,1024]{1,2,0:T(8,128)(2,1)S(1)} collective-permute-done((bf16[2,64,1024]{1,2,0:T(8,128)(2,1)S(1)}, bf16[2,64,1024]{1,2,0:T(8,128)(2,1)S(1)}, u32[]{:S(2)}, u32[]{:S(2)}) %collective-permute-start.8) | collective-permute-done | bytes 262176 | tf_op jit(solution)/shard_map/ppermute | solution.py:18
  88.0 2.8 fusion.4
  111.3 3.0 collective-permute-start.14
  114.3 3.9 collective-permute-done.13
  123.1 1.5 collective-permute-start.17
  124.6 4.0 collective-permute-done.18.refs_2_
  128.7 1.7 collective-permute-start.19
  132.2 1.5 collective-permute-done.19.refs_3_
  133.7 2.4 collective-permute-done.20.refs_4_
  136.8 33.9 %shard_map.163.own = bf16[128,4224]{1,0:T(8,128)(2,1)} custom-call(bf16[32,4224]{1,0:T(8,128)(2,1)} %copy-done.11, bf16[32,4224]{1,0:T(8,128)(2,1)} %copy-done.15, bf16[32,4224]{1,0:T(8,128)(2,1)} %copy-done.14, bf16[16,4224]{1,0:T(8,128)(2,1)} %copy-done.22, bf16[16,4224]{1,0:T(8,128)(2,1)} %copy-done.24), custom_call_target="tpu_custom_call" | custom-call | bytes 2162688 | tf_op jit(solution)/shard_map/pallas_call | solution.py:190
  170.9 9.0 %collective-permute-done.27.refs_0_ = bf16[32,4224]{1,0:T(8,128)(2,1)S(1)} collective-permute-done((bf16[32,4224]{1,0:T(8,128)(2,1)}, bf16[32,4224]{1,0:T(8,128)(2,1)S(1)}, u32[]{:S(2)}, u32[]{:S(2)}) %collective-permute-start.27) | collective-permute-done | bytes 270368 | tf_op jit(solution)/shard_map/ppermute | solution.py:18
  181.5 2.0 collective-permute-start.39
  184.8 3.2 collective-permute-done.29.refs_2_
  188.0 1.6 collective-permute-start.30
  190.0 3.1 collective-permute-done.30.refs_3_
  193.1 1.6 collective-permute-done.31.refs_4_
  195.4 33.9 %shard_map.165.own = bf16[128,4224]{1,0:T(8,128)(2,1)} custom-call(bf16[32,4224]{1,0:T(8,128)(2,1)} %copy-done.18, bf16[32,4224]{1,0:T(8,128)(2,1)} %copy-done.13, bf16[32,4224]{1,0:T(8,128)(2,1)} %copy-done.12, bf16[16,4224]{1,0:T(8,128)(2,1)} %copy-done.21, bf16[16,4224]{1,0:T(8,128)(2,1)} %copy-done.23), custom_call_target="tpu_custom_call" | custom-call | bytes 2162688 | tf_op jit(solution)/shard_map/pallas_call | solution.py:190
  229.4 17.5 %shard_map.167.refs_0_ = bf16[64,4224]{1,0:T(8,128)(2,1)} custom-call(bf16[32,4224]{1,0:T(8,128)(2,1)} %collective-permute-done.39.refs_0_, bf16[32,4224]{1,0:T(8,128)(2,1)} %collective-permute-done.40.refs_1_), custom_call_target="tpu_custom_call" | custom-call | bytes 1081344 | tf_op jit(solution)/shard_map/pallas_call | solution.py:190
  248.7 3.1 copy-done.2
  251.8 16.5 %shard_map.164 = (bf16[128,4096]{1,0:T(8,128)(2,1)S(1)}, bf16[128,4096]{1,0:T(8,128)(2,1)}) custom-call(bf16[128,4224]{1,0:T(8,128)(2,1)S(1)} %copy-done.4, bf16[128,4224]{1,0:T(8,128)(2,1)S(1)} %collective-permute-done.21.mate, bf16[4096,896]{1,0:T(8,128)(2,1)S(1)} %bitcast.128, bf16[4096,896]{1,0:T(8,128)(2,1)} %bitcast.130, bf16[896,4096]{1,0:T(8,128)(2,1)} %bitcast.133, ...), custom_call_target="tpu_custom_call" | custom-call | flops 5637144576 | bytes 30408704 | tf_op jit(solution)/shard_map/pallas_call | solution.py:275
  270.1 1.8 collective-permute-start.44
  271.9 6.4 %collective-permute-done.43.refs_3_ = bf16[32,4224]{1,0:T(8,128)(2,1)S(1)} collective-permute-done((bf16[32,4224]{1,0:T(8,128)(2,1)S(1)}, bf16[32,4224]{1,0:T(8,128)(2,1)S(1)}, u32[]{:S(2)}, u32[]{:S(2)}) %collective-permute-start.43) | collective-permute-done | bytes 270368 | tf_op jit(solution)/shard_map/ppermute | solution.py:18
  279.0 66.7 %shard_map.168.own = bf16[256,4224]{1,0:T(8,128)(2,1)} custom-call(bf16[64,4224]{1,0:T(8,128)(2,1)} %shard_map.167.refs_0_, bf16[64,4224]{1,0:T(8,128)(2,1)} %copy-done.9, bf16[64,4224]{1,0:T(8,128)(2,1)} %copy-done.10, bf16[32,4224]{1,0:T(8,128)(2,1)} %copy-done.19, bf16[32,4224]{1,0:T(8,128)(2,1)} %collective-permute-done.44.refs_4_), custom_call_target="tpu_custom_call" | custom-call | bytes 4325376 | tf_op jit(solution)/shard_map/pallas_call | solution.py:190
  345.8 3.1 copy-done.3
  348.9 15.5 %shard_map.166 = (bf16[128,4096]{1,0:T(8,128)(2,1)S(1)}, bf16[128,4096]{1,0:T(8,128)(2,1)S(1)}) custom-call(bf16[128,4224]{1,0:T(8,128)(2,1)S(1)} %copy-done.5, bf16[128,4224]{1,0:T(8,128)(2,1)S(1)} %collective-permute-done.32.mate, bf16[4096,896]{1,0:T(8,128)(2,1)S(1)} %bitcast.129, bf16[4096,896]{1,0:T(8,128)(2,1)} %bitcast.131, ...), custom_call_target="tpu_custom_call" | custom-call | flops 5637144576 | bytes 30408704 | tf_op jit(solution)/shard_map/pallas_call | solution.py:275
  369.7 1.8 collective-permute-done.25
  371.6 1.7 collective-permute-start.26
  374.8 1.5 collective-permute-start.36
  377.3 19.7 %shard_map.169 = (bf16[256,4096]{1,0:T(8,128)(2,1)S(1)}, bf16[256,4096]{1,0:T(8,128)(2,1)S(1)}) custom-call(bf16[256,4224]{1,0:T(8,128)(2,1)S(1)} %copy-done.6, bf16[256,4224]{1,0:T(8,128)(2,1)S(1)} %collective-permute-done.45.mate, bf16[4096,896]{1,0:T(8,128)(2,1)} %bitcast.127, bf16[4096,896]{1,0:T(8,128)(2,1)} %bitcast.132, bf16[896,4096]{1,0:T(8,128)(2,1)} %bitcast.135, ...), custom_call_target="tpu_custom_call" | custom-call | flops 11274289152 | bytes 38797312 | tf_op jit(solution)/shard_map/pallas_call | solution.py:275
  399.0 2.2 collective-permute-done.46
  401.3 1.5 collective-permute-start.49
  403.2 9.3 %collective-permute-done.49 = bf16[32,4096]{1,0:T(8,128)(2,1)S(1)} collective-permute-done((bf16[32,4096]{1,0:T(8,128)(2,1)S(1)}, bf16[32,4096]{1,0:T(8,128)(2,1)S(1)}, u32[]{:S(2)}, u32[]{:S(2)}) %collective-permute-start.49) | collective-permute-done | bytes 262176 | tf_op jit(solution)/shard_map/ppermute | solution.py:18
  413.5 6.6 %collective-permute-done.47 = bf16[32,4096]{1,0:T(8,128)(2,1)S(1)} collective-permute-done((bf16[32,4096]{1,0:T(8,128)(2,1)S(1)}, bf16[32,4096]{1,0:T(8,128)(2,1)S(1)}, u32[]{:S(2)}, u32[]{:S(2)}) %collective-permute-start.47) | collective-permute-done | bytes 262176 | tf_op jit(solution)/shard_map/ppermute | solution.py:18
  421.1 1.5 collective-permute-start.48
  423.2 9.1 %collective-permute-done.50 = bf16[64,4096]{1,0:T(8,128)(2,1)S(1)} collective-permute-done((bf16[64,4096]{1,0:T(8,128)(2,1)S(1)}, bf16[64,4096]{1,0:T(8,128)(2,1)S(1)}, u32[]{:S(2)}, u32[]{:S(2)}) %collective-permute-start.50) | collective-permute-done | bytes 524320 | tf_op jit(solution)/shard_map/ppermute | solution.py:18
  433.5 2.7 collective-permute-start.52
  436.2 7.5 %collective-permute-done.52 = bf16[32,4096]{1,0:T(8,128)(2,1)S(1)} collective-permute-done((bf16[32,4096]{1,0:T(8,128)(2,1)S(1)}, bf16[32,4096]{1,0:T(8,128)(2,1)S(1)}, u32[]{:S(2)}, u32[]{:S(2)}) %collective-permute-start.52) | collective-permute-done | bytes 262176 | tf_op jit(solution)/shard_map/ppermute | solution.py:18
  443.7 12.2 %collective-permute-done.51 = bf16[32,4096]{1,0:T(8,128)(2,1)S(1)} collective-permute-done((bf16[32,4096]{1,0:T(8,128)(2,1)S(1)}, bf16[32,4096]{1,0:T(8,128)(2,1)S(1)}, u32[]{:S(2)}, u32[]{:S(2)}) %collective-permute-start.51) | collective-permute-done | bytes 262176 | tf_op jit(solution)/shard_map/ppermute | solution.py:18
  455.9 2.1 add_convert_fusion.2
  (264 shorter events, 49.3 us)
Async XLA Ops:
  3.9 6.6 %collective-permute-start = (bf16[528,128]{1,0:T(8,128)(2,1)S(1)}, bf16[528,128]{1,0:T(8,128)(2,1)S(1)}, u32[]{:S(2)}, u32[]{:S(2)}) collective-permute-start(bf16[528,128]{1,0:T(8,128)(2,1)S(1)} %pad_maximum_fusion.10), channel_id=1, source_target_pairs={{0,4},{4,0},{8,12},{12,8},{16,20},{20,16},{24,28},{28,24},{1,5},{5... | collective-permute-start | bytes 405512 | tf_op jit(solution)/shard_map/ppermute | solution.py:18
  6.9 81.0 %collective-permute-start.9 = (bf16[1024,512]{1,0:T(8,128)(2,1)}, bf16[1024,512]{1,0:T(8,128)(2,1)}, u32[]{:S(2)}, u32[]{:S(2)}) collective-permute-start(bf16[1024,512]{1,0:T(8,128)(2,1)} %param.26), channel_id=1, source_target_pairs={{0,8},{4,12},{8,0},{12,4},{16,24},{20,28},{24,16},{28,20},{1,9},{5... | collective-permute-start | bytes 3145736 | tf_op jit(solution)/shard_map/ppermute | solution.py:18
  11.2 26.9 %collective-permute-start.3 = (bf16[528,128]{1,0:T(8,128)(2,1)S(1)}, bf16[528,128]{1,0:T(8,128)(2,1)S(1)}, u32[]{:S(2)}, u32[]{:S(2)}) collective-permute-start(bf16[528,128]{1,0:T(8,128)(2,1)S(1)} %pad_maximum_fusion.11), channel_id=1, source_target_pairs={{0,24},{4,28},{8,16},{12,20},{16,8},{20,12},{24,0},{28,4},{1,25},{... | collective-permute-start | bytes 405512 | tf_op jit(solution)/shard_map/ppermute | solution.py:18
  15.2 22.9 %collective-permute-start.2 = (bf16[528,128]{1,0:T(8,128)(2,1)S(1)}, bf16[528,128]{1,0:T(8,128)(2,1)S(1)}, u32[]{:S(2)}, u32[]{:S(2)}) collective-permute-start(bf16[528,128]{1,0:T(8,128)(2,1)S(1)} %pad_maximum_fusion.11), channel_id=1, source_target_pairs={{0,16},{4,20},{8,24},{12,28},{16,0},{20,4},{24,8},{28,12},{1,17},{... | collective-permute-start | bytes 405512 | tf_op jit(solution)/shard_map/ppermute | solution.py:18
  15.2 25.2 %collective-permute-start.1 = (bf16[528,128]{1,0:T(8,128)(2,1)S(1)}, bf16[528,128]{1,0:T(8,128)(2,1)S(1)}, u32[]{:S(2)}, u32[]{:S(2)}) collective-permute-start(bf16[528,128]{1,0:T(8,128)(2,1)S(1)} %pad_maximum_fusion.11), channel_id=1, source_target_pairs={{0,8},{4,12},{8,0},{12,4},{16,24},{20,28},{24,16},{28,20},{1,9},{5... | collective-permute-start | bytes 405512 | tf_op jit(solution)/shard_map/ppermute | solution.py:18
  48.3 12.4 %collective-permute-start.5 = (bf16[64,1024]{0,1:T(8,128)(2,1)S(1)}, bf16[64,1024]{0,1:T(8,128)(2,1)S(1)}, u32[]{:S(2)}, u32[]{:S(2)}) collective-permute-start(bf16[64,1024]{0,1:T(8,128)(2,1)S(1)} %pad_maximum_fusion.4), channel_id=1, source_target_pairs={{0,16},{4,20},{8,24},{12,28},{16,0},{20,4},{24,8},{28,12},{1,17},{... | collective-permute-start | bytes 393224 | tf_op jit(solution)/shard_map/ppermute | solution.py:18
  51.1 10.5 %collective-permute-start.7 = (bf16[64,1024]{0,1:T(8,128)(2,1)S(1)}, bf16[64,1024]{0,1:T(8,128)(2,1)S(1)}, u32[]{:S(2)}, u32[]{:S(2)}) collective-permute-start(bf16[64,1024]{0,1:T(8,128)(2,1)S(1)} %pad_maximum_fusion.5), channel_id=1, source_target_pairs={{0,4},{4,0},{8,12},{12,8},{16,20},{20,16},{24,28},{28,24},{1,5},{5... | collective-permute-start | bytes 393224 | tf_op jit(solution)/shard_map/ppermute | solution.py:18
  60.8 12.9 %collective-permute-start.6 = (bf16[2,64,1024]{1,2,0:T(8,128)(2,1)S(1)}, bf16[2,64,1024]{1,2,0:T(8,128)(2,1)S(1)}, u32[]{:S(2)}, u32[]{:S(2)}) collective-permute-start(bf16[2,64,1024]{1,2,0:T(8,128)(2,1)S(1)} %get-tuple-element.43), channel_id=1, source_target_pairs={{0,4},{4,0},{8,12},{12,8},{16,20},{20,16},{24,28},{28,24},{1,5},{5... | collective-permute-start | bytes 786440 | tf_op jit(solution)/shard_map/ppermute | solution.py:18
  61.7 24.8 %collective-permute-start.8 = (bf16[2,64,1024]{1,2,0:T(8,128)(2,1)S(1)}, bf16[2,64,1024]{1,2,0:T(8,128)(2,1)S(1)}, u32[]{:S(2)}, u32[]{:S(2)}) collective-permute-start(bf16[2,64,1024]{1,2,0:T(8,128)(2,1)S(1)} %get-tuple-element.45), channel_id=1, source_target_pairs={{0,16},{4,20},{8,24},{12,28},{16,0},{20,4},{24,8},{28,12},{1,17},{... | collective-permute-start | bytes 786440 | tf_op jit(solution)/shard_map/ppermute | solution.py:18
  90.8 5.9 %collective-permute-start.10 = (bf16[256,1024]{1,0:T(8,128)(2,1)S(1)}, bf16[256,1024]{1,0:T(8,128)(2,1)S(1)}, u32[]{:S(2)}, u32[]{:S(2)}) collective-permute-start(bf16[256,1024]{1,0:T(8,128)(2,1)S(1)} %slice.451), channel_id=1, source_target_pairs={{0,1},{1,0},{2,3},{3,2},{4,5},{5,4},{6,7},{7,6},{8,9},{9,8},{10,11... | collective-permute-start | bytes 1572872 | tf_op jit(solution)/shard_map/ppermute | solution.py:18
  97.0 12.7 %collective-permute-start.11 = (bf16[128,1024]{1,0:T(8,128)(2,1)S(1)}, bf16[128,1024]{1,0:T(8,128)(2,1)S(1)}, u32[]{:S(2)}, u32[]{:S(2)}) collective-permute-start(bf16[128,1024]{1,0:T(8,128)(2,1)S(1)} %slice.453), channel_id=1, source_target_pairs={{0,2},{1,3},{2,0},{3,1},{4,6},{5,7},{6,4},{7,5},{8,10},{9,11},{10,... | collective-permute-start | bytes 786440 | tf_op jit(solution)/shard_map/ppermute | solution.py:18
  102.5 7.1 %collective-permute-start.16 = (f32[128]{0:T(128)S(1)}, f32[128]{0:T(128)S(1)}, u32[]{:S(2)}, u32[]{:S(2)}) collective-permute-start(f32[128]{0:T(128)S(1)} %add.257), channel_id=1, source_target_pairs={{0,2},{1,3},{2,0},{3,1},{4,6},{5,7},{6,4},{7,5},{8,10},{9,11},{10,... | collective-permute-start | bytes 1544 | tf_op jit(solution)/shard_map/ppermute | solution.py:18
  111.3 6.9 %collective-permute-start.13 = (bf16[32,1024]{1,0:T(8,128)(2,1)S(1)}, bf16[32,1024]{1,0:T(8,128)(2,1)S(1)}, u32[]{:S(2)}, u32[]{:S(2)}) collective-permute-start(bf16[32,1024]{1,0:T(8,128)(2,1)S(1)} %get-tuple-element.47), channel_id=1, source_target_pairs={{0,16},{4,20},{8,24},{12,28},{16,0},{20,4},{24,8},{28,12},{1,17},{... | collective-permute-start | bytes 196616 | tf_op jit(solution)/shard_map/ppermute | solution.py:18
  111.3 7.7 %collective-permute-start.14 = (bf16[32,1024]{1,0:T(8,128)(2,1)S(1)}, bf16[32,1024]{1,0:T(8,128)(2,1)S(1)}, u32[]{:S(2)}, u32[]{:S(2)}) collective-permute-start(bf16[32,1024]{1,0:T(8,128)(2,1)S(1)} %get-tuple-element.46), channel_id=1, source_target_pairs={{0,20},{4,16},{8,28},{12,24},{16,4},{20,0},{24,12},{28,8},{1,21},{... | collective-permute-start | bytes 196616 | tf_op jit(solution)/shard_map/ppermute | solution.py:18
  121.6 7.0 %collective-permute-start.18 = (bf16[32,4224]{1,0:T(8,128)(2,1)S(1)}, bf16[32,4224]{1,0:T(8,128)(2,1)S(1)}, u32[]{:S(2)}, u32[]{:S(2)}) collective-permute-start(bf16[32,4224]{1,0:T(8,128)(2,1)S(1)} %concatenate.75.refs_0_), channel_id=1, source_target_pairs={{0,4},{4,0},{8,12},{12,8},{16,20},{20,16},{24,28},{28,24},{1,5},{5... | collective-permute-start | bytes 811016 | tf_op jit(solution)/shard_map/ppermute | solution.py:18
  123.1 8.0 %collective-permute-start.17 = (bf16[32,4224]{1,0:T(8,128)(2,1)S(1)}, bf16[32,4224]{1,0:T(8,128)(2,1)S(1)}, u32[]{:S(2)}, u32[]{:S(2)}) collective-permute-start(bf16[32,4224]{1,0:T(8,128)(2,1)S(1)} %concatenate.75.refs_0_), channel_id=1, source_target_pairs={{0,2},{1,3},{2,0},{3,1},{4,6},{5,7},{6,4},{7,5},{8,10},{9,11},{10,... | collective-permute-start | bytes 811016 | tf_op jit(solution)/shard_map/ppermute | solution.py:18
  128.7 5.1 %collective-permute-start.19 = (bf16[16,4224]{1,0:T(8,128)(2,1)S(1)}, bf16[16,4224]{1,0:T(8,128)(2,1)S(1)}, u32[]{:S(2)}, u32[]{:S(2)}) collective-permute-start(bf16[16,4224]{1,0:T(8,128)(2,1)S(1)} %slice.465), channel_id=1, source_target_pairs={{0,2},{1,3},{2,0},{3,1},{4,6},{5,7},{6,4},{7,5},{8,10},{9,11},{10,... | collective-permute-start | bytes 405512 | tf_op jit(solution)/shard_map/ppermute | solution.py:18
  131.1 5.1 %collective-permute-start.20 = (bf16[16,4224]{1,0:T(8,128)(2,1)S(1)}, bf16[16,4224]{1,0:T(8,128)(2,1)S(1)}, u32[]{:S(2)}, u32[]{:S(2)}) collective-permute-start(bf16[16,4224]{1,0:T(8,128)(2,1)S(1)} %slice.466), channel_id=1, source_target_pairs={{0,4},{4,0},{8,12},{12,8},{16,20},{20,16},{24,28},{28,24},{1,5},{5... | collective-permute-start | bytes 405512 | tf_op jit(solution)/shard_map/ppermute | solution.py:18
  170.8 77.9 %collective-permute-start.21 = (bf16[128,4224]{1,0:T(8,128)(2,1)}, bf16[128,4224]{1,0:T(8,128)(2,1)S(1)}, u32[]{:S(2)}, u32[]{:S(2)}) collective-permute-start(bf16[128,4224]{1,0:T(8,128)(2,1)} %shard_map.163.own), channel_id=1, source_target_pairs={{0,1},{1,0},{2,3},{3,2},{4,5},{5,4},{6,7},{7,6},{8,9},{9,8},{10,11... | collective-permute-start | bytes 3244040 | tf_op jit(solution)/shard_map/ppermute | solution.py:18
  170.8 9.1 %collective-permute-start.27 = (bf16[32,4224]{1,0:T(8,128)(2,1)}, bf16[32,4224]{1,0:T(8,128)(2,1)S(1)}, u32[]{:S(2)}, u32[]{:S(2)}) collective-permute-start(bf16[32,4224]{1,0:T(8,128)(2,1)} %copy-done.11), channel_id=1, source_target_pairs={{0,8},{4,12},{8,0},{12,4},{16,24},{20,28},{24,16},{28,20},{1,9},{5... | collective-permute-start | bytes 811016 | tf_op jit(solution)/shard_map/ppermute | solution.py:18
  180.0 8.0 %collective-permute-start.29 = (bf16[32,4224]{1,0:T(8,128)(2,1)S(1)}, bf16[32,4224]{1,0:T(8,128)(2,1)S(1)}, u32[]{:S(2)}, u32[]{:S(2)}) collective-permute-start(bf16[32,4224]{1,0:T(8,128)(2,1)S(1)} %collective-permute-done.27.refs_0_), channel_id=1, source_target_pairs={{0,4},{4,0},{8,12},{12,8},{16,20},{20,16},{24,28},{28,24},{1,5},{5... | collective-permute-start | bytes 811016 | tf_op jit(solution)/shard_map/ppermute | solution.py:18
  181.0 8.6 %collective-permute-start.28 = (bf16[32,4224]{1,0:T(8,128)(2,1)S(1)}, bf16[32,4224]{1,0:T(8,128)(2,1)S(1)}, u32[]{:S(2)}, u32[]{:S(2)}) collective-permute-start(bf16[32,4224]{1,0:T(8,128)(2,1)S(1)} %collective-permute-done.27.refs_0_), channel_id=1, source_target_pairs={{0,2},{1,3},{2,0},{3,1},{4,6},{5,7},{6,4},{7,5},{8,10},{9,11},{10,... | collective-permute-start | bytes 811016 | tf_op jit(solution)/shard_map/ppermute | solution.py:18
  181.5 47.9 %collective-permute-start.39 = (bf16[32,4224]{1,0:T(8,128)(2,1)}, bf16[32,4224]{1,0:T(8,128)(2,1)}, u32[]{:S(2)}, u32[]{:S(2)}) collective-permute-start(bf16[32,4224]{1,0:T(8,128)(2,1)} %copy-done.11), channel_id=1, source_target_pairs={{0,16},{4,20},{8,24},{12,28},{16,0},{20,4},{24,8},{28,12},{1,17},{... | collective-permute-start | bytes 811016 | tf_op jit(solution)/shard_map/ppermute | solution.py:18
  183.6 45.9 %collective-permute-start.40 = (bf16[32,4224]{1,0:T(8,128)(2,1)}, bf16[32,4224]{1,0:T(8,128)(2,1)}, u32[]{:S(2)}, u32[]{:S(2)}) collective-permute-start(bf16[32,4224]{1,0:T(8,128)(2,1)} %copy-done.11), channel_id=1, source_target_pairs={{0,24},{4,28},{8,16},{12,20},{16,8},{20,12},{24,0},{28,4},{1,25},{... | collective-permute-start | bytes 811016 | tf_op jit(solution)/shard_map/ppermute | solution.py:18
  188.0 5.1 %collective-permute-start.30 = (bf16[16,4224]{1,0:T(8,128)(2,1)S(1)}, bf16[16,4224]{1,0:T(8,128)(2,1)S(1)}, u32[]{:S(2)}, u32[]{:S(2)}) collective-permute-start(bf16[16,4224]{1,0:T(8,128)(2,1)S(1)} %slice.476), channel_id=1, source_target_pairs={{0,2},{1,3},{2,0},{3,1},{4,6},{5,7},{6,4},{7,5},{8,10},{9,11},{10,... | collective-permute-start | bytes 405512 | tf_op jit(solution)/shard_map/ppermute | solution.py:18
  229.3 116.5 %collective-permute-start.32 = (bf16[128,4224]{1,0:T(8,128)(2,1)}, bf16[128,4224]{1,0:T(8,128)(2,1)S(1)}, u32[]{:S(2)}, u32[]{:S(2)}) collective-permute-start(bf16[128,4224]{1,0:T(8,128)(2,1)} %shard_map.165.own), channel_id=1, source_target_pairs={{0,1},{1,0},{2,3},{3,2},{4,5},{5,4},{6,7},{7,6},{8,9},{9,8},{10,11... | collective-permute-start | bytes 3244040 | tf_op jit(solution)/shard_map/ppermute | solution.py:18
  246.9 23.1 %collective-permute-start.41 = (bf16[64,4224]{1,0:T(8,128)(2,1)}, bf16[64,4224]{1,0:T(8,128)(2,1)S(1)}, u32[]{:S(2)}, u32[]{:S(2)}) collective-permute-start(bf16[64,4224]{1,0:T(8,128)(2,1)} %shard_map.167.refs_0_), channel_id=1, source_target_pairs={{0,2},{1,3},{2,0},{3,1},{4,6},{5,7},{6,4},{7,5},{8,10},{9,11},{10,... | collective-permute-start | bytes 1622024 | tf_op jit(solution)/shard_map/ppermute | solution.py:18
  247.6 21.8 %collective-permute-start.42 = (bf16[64,4224]{1,0:T(8,128)(2,1)}, bf16[64,4224]{1,0:T(8,128)(2,1)S(1)}, u32[]{:S(2)}, u32[]{:S(2)}) collective-permute-start(bf16[64,4224]{1,0:T(8,128)(2,1)} %shard_map.167.refs_0_), channel_id=1, source_target_pairs={{0,4},{4,0},{8,12},{12,8},{16,20},{20,16},{24,28},{28,24},{1,5},{5... | collective-permute-start | bytes 1622024 | tf_op jit(solution)/shard_map/ppermute | solution.py:18
  269.3 95.7 %collective-permute-start.22 = (bf16[128,4096]{1,0:T(8,128)(2,1)}, bf16[128,4096]{1,0:T(8,128)(2,1)}, u32[]{:S(2)}, u32[]{:S(2)}) collective-permute-start(bf16[128,4096]{1,0:T(8,128)(2,1)} %get-tuple-element.12), channel_id=1, source_target_pairs={{0,1},{1,0},{2,3},{3,2},{4,5},{5,4},{6,7},{7,6},{8,9},{9,8},{10,11... | collective-permute-start | bytes 3145736 | tf_op jit(solution)/shard_map/ppermute | solution.py:18
  269.3 9.0 %collective-permute-start.43 = (bf16[32,4224]{1,0:T(8,128)(2,1)S(1)}, bf16[32,4224]{1,0:T(8,128)(2,1)S(1)}, u32[]{:S(2)}, u32[]{:S(2)}) collective-permute-start(bf16[32,4224]{1,0:T(8,128)(2,1)S(1)} %slice.487), channel_id=1, source_target_pairs={{0,2},{1,3},{2,0},{3,1},{4,6},{5,7},{6,4},{7,5},{8,10},{9,11},{10,... | collective-permute-start | bytes 811016 | tf_op jit(solution)/shard_map/ppermute | solution.py:18
  270.1 8.9 %collective-permute-start.44 = (bf16[32,4224]{1,0:T(8,128)(2,1)S(1)}, bf16[32,4224]{1,0:T(8,128)(2,1)}, u32[]{:S(2)}, u32[]{:S(2)}) collective-permute-start(bf16[32,4224]{1,0:T(8,128)(2,1)S(1)} %slice.488), channel_id=1, source_target_pairs={{0,4},{4,0},{8,12},{12,8},{16,20},{20,16},{24,28},{28,24},{1,5},{5... | collective-permute-start | bytes 811016 | tf_op jit(solution)/shard_map/ppermute | solution.py:18
  345.7 31.6 %collective-permute-start.45 = (bf16[256,4224]{1,0:T(8,128)(2,1)}, bf16[256,4224]{1,0:T(8,128)(2,1)S(1)}, u32[]{:S(2)}, u32[]{:S(2)}) collective-permute-start(bf16[256,4224]{1,0:T(8,128)(2,1)} %shard_map.168.own), channel_id=1, source_target_pairs={{0,1},{1,0},{2,3},{3,2},{4,5},{5,4},{6,7},{7,6},{8,9},{9,8},{10,11... | collective-permute-start | bytes 6488072 | tf_op jit(solution)/shard_map/ppermute | solution.py:18
  364.4 10.2 %collective-permute-start.33 = (bf16[128,4096]{1,0:T(8,128)(2,1)S(1)}, bf16[128,4096]{1,0:T(8,128)(2,1)S(1)}, u32[]{:S(2)}, u32[]{:S(2)}) collective-permute-start(bf16[128,4096]{1,0:T(8,128)(2,1)S(1)} %get-tuple-element.14), channel_id=1, source_target_pairs={{0,1},{1,0},{2,3},{3,2},{4,5},{5,4},{6,7},{7,6},{8,9},{9,8},{10,11... | collective-permute-start | bytes 3145736 | tf_op jit(solution)/shard_map/ppermute | solution.py:18
  366.0 5.5 %collective-permute-start.25 = (bf16[16,4096]{1,0:T(8,128)(2,1)S(1)}, bf16[16,4096]{1,0:T(8,128)(2,1)S(1)}, u32[]{:S(2)}, u32[]{:S(2)}) collective-permute-start(bf16[16,4096]{1,0:T(8,128)(2,1)S(1)} %get-tuple-element.33), channel_id=1, source_target_pairs={{0,2},{1,3},{2,0},{3,1},{4,6},{5,7},{6,4},{7,5},{8,10},{9,11},{10,... | collective-permute-start | bytes 393224 | tf_op jit(solution)/shard_map/ppermute | solution.py:18
  368.5 5.4 %collective-permute-start.23 = (bf16[16,4096]{1,0:T(8,128)(2,1)S(1)}, bf16[16,4096]{1,0:T(8,128)(2,1)S(1)}, u32[]{:S(2)}, u32[]{:S(2)}) collective-permute-start(bf16[16,4096]{1,0:T(8,128)(2,1)S(1)} %get-tuple-element.32), channel_id=1, source_target_pairs={{0,4},{4,0},{8,12},{12,8},{16,20},{20,16},{24,28},{28,24},{1,5},{5... | collective-permute-start | bytes 393224 | tf_op jit(solution)/shard_map/ppermute | solution.py:18
  371.6 64.6 %collective-permute-start.26 = (bf16[32,4096]{1,0:T(8,128)(2,1)S(1)}, bf16[32,4096]{1,0:T(8,128)(2,1)S(1)}, u32[]{:S(2)}, u32[]{:S(2)}) collective-permute-start(bf16[32,4096]{1,0:T(8,128)(2,1)S(1)} %pad_maximum_fusion.7), channel_id=1, source_target_pairs={{0,4},{4,0},{8,12},{12,8},{16,20},{20,16},{24,28},{28,24},{1,5},{5... | collective-permute-start | bytes 786440 | tf_op jit(solution)/shard_map/ppermute | solution.py:18
  374.0 62.2 %collective-permute-start.24 = (bf16[32,4096]{1,0:T(8,128)(2,1)S(1)}, bf16[32,4096]{1,0:T(8,128)(2,1)S(1)}, u32[]{:S(2)}, u32[]{:S(2)}) collective-permute-start(bf16[32,4096]{1,0:T(8,128)(2,1)S(1)} %pad_maximum_fusion.6), channel_id=1, source_target_pairs={{0,2},{1,3},{2,0},{3,1},{4,6},{5,7},{6,4},{7,5},{8,10},{9,11},{10,... | collective-permute-start | bytes 786440 | tf_op jit(solution)/shard_map/ppermute | solution.py:18
  374.8 22.2 %collective-permute-start.36 = (bf16[16,4096]{1,0:T(8,128)(2,1)S(1)}, bf16[16,4096]{1,0:T(8,128)(2,1)S(1)}, u32[]{:S(2)}, u32[]{:S(2)}) collective-permute-start(bf16[16,4096]{1,0:T(8,128)(2,1)S(1)} %get-tuple-element.37), channel_id=1, source_target_pairs={{0,2},{1,3},{2,0},{3,1},{4,6},{5,7},{6,4},{7,5},{8,10},{9,11},{10,... | collective-permute-start | bytes 393224 | tf_op jit(solution)/shard_map/ppermute | solution.py:18
  376.3 21.9 %collective-permute-start.34 = (bf16[16,4096]{1,0:T(8,128)(2,1)S(1)}, bf16[16,4096]{1,0:T(8,128)(2,1)S(1)}, u32[]{:S(2)}, u32[]{:S(2)}) collective-permute-start(bf16[16,4096]{1,0:T(8,128)(2,1)S(1)} %get-tuple-element.36), channel_id=1, source_target_pairs={{0,4},{4,0},{8,12},{12,8},{16,20},{20,16},{24,28},{28,24},{1,5},{5... | collective-permute-start | bytes 393224 | tf_op jit(solution)/shard_map/ppermute | solution.py:18
  397.1 23.9 %collective-permute-start.37 = (bf16[32,4096]{1,0:T(8,128)(2,1)S(1)}, bf16[32,4096]{1,0:T(8,128)(2,1)S(1)}, u32[]{:S(2)}, u32[]{:S(2)}) collective-permute-start(bf16[32,4096]{1,0:T(8,128)(2,1)S(1)} %pad_maximum_fusion.9), channel_id=1, source_target_pairs={{0,4},{4,0},{8,12},{12,8},{16,20},{20,16},{24,28},{28,24},{1,5},{5... | collective-permute-start | bytes 786440 | tf_op jit(solution)/shard_map/ppermute | solution.py:18
  398.3 24.3 %collective-permute-start.35 = (bf16[32,4096]{1,0:T(8,128)(2,1)S(1)}, bf16[32,4096]{1,0:T(8,128)(2,1)S(1)}, u32[]{:S(2)}, u32[]{:S(2)}) collective-permute-start(bf16[32,4096]{1,0:T(8,128)(2,1)S(1)} %pad_maximum_fusion.8), channel_id=1, source_target_pairs={{0,2},{1,3},{2,0},{3,1},{4,6},{5,7},{6,4},{7,5},{8,10},{9,11},{10,... | collective-permute-start | bytes 786440 | tf_op jit(solution)/shard_map/ppermute | solution.py:18
  401.3 11.1 %collective-permute-start.49 = (bf16[32,4096]{1,0:T(8,128)(2,1)S(1)}, bf16[32,4096]{1,0:T(8,128)(2,1)S(1)}, u32[]{:S(2)}, u32[]{:S(2)}) collective-permute-start(bf16[32,4096]{1,0:T(8,128)(2,1)S(1)} %get-tuple-element.29), channel_id=1, source_target_pairs={{0,2},{1,3},{2,0},{3,1},{4,6},{5,7},{6,4},{7,5},{8,10},{9,11},{10,... | collective-permute-start | bytes 786440 | tf_op jit(solution)/shard_map/ppermute | solution.py:18
  412.4 7.6 %collective-permute-start.47 = (bf16[32,4096]{1,0:T(8,128)(2,1)S(1)}, bf16[32,4096]{1,0:T(8,128)(2,1)S(1)}, u32[]{:S(2)}, u32[]{:S(2)}) collective-permute-start(bf16[32,4096]{1,0:T(8,128)(2,1)S(1)} %get-tuple-element.28), channel_id=1, source_target_pairs={{0,4},{4,0},{8,12},{12,8},{16,20},{20,16},{24,28},{28,24},{1,5},{5... | collective-permute-start | bytes 786440 | tf_op jit(solution)/shard_map/ppermute | solution.py:18
  420.0 12.3 %collective-permute-start.50 = (bf16[64,4096]{1,0:T(8,128)(2,1)S(1)}, bf16[64,4096]{1,0:T(8,128)(2,1)S(1)}, u32[]{:S(2)}, u32[]{:S(2)}) collective-permute-start(bf16[64,4096]{1,0:T(8,128)(2,1)S(1)} %pad_maximum_fusion.3), channel_id=1, source_target_pairs={{0,4},{4,0},{8,12},{12,8},{16,20},{20,16},{24,28},{28,24},{1,5},{5... | collective-permute-start | bytes 1572872 | tf_op jit(solution)/shard_map/ppermute | solution.py:18
  421.1 12.1 %collective-permute-start.48 = (bf16[64,4096]{1,0:T(8,128)(2,1)S(1)}, bf16[64,4096]{1,0:T(8,128)(2,1)S(1)}, u32[]{:S(2)}, u32[]{:S(2)}) collective-permute-start(bf16[64,4096]{1,0:T(8,128)(2,1)S(1)} %pad_maximum_fusion.2), channel_id=1, source_target_pairs={{0,2},{1,3},{2,0},{3,1},{4,6},{5,7},{6,4},{7,5},{8,10},{9,11},{10,... | collective-permute-start | bytes 1572872 | tf_op jit(solution)/shard_map/ppermute | solution.py:18
  422.7 13.5 %collective-permute-start.38 = (bf16[32,4096]{1,0:T(8,128)(2,1)S(1)}, bf16[32,4096]{1,0:T(8,128)(2,1)S(1)}, u32[]{:S(2)}, u32[]{:S(2)}) collective-permute-start(bf16[32,4096]{1,0:T(8,128)(2,1)S(1)} %add_convert_fusion.5), channel_id=1, source_target_pairs={{0,8},{4,12},{8,0},{12,4},{16,24},{20,28},{24,16},{28,20},{1,9},{5... | collective-permute-start | bytes 786440 | tf_op jit(solution)/shard_map/ppermute | solution.py:18
  433.5 10.2 %collective-permute-start.52 = (bf16[32,4096]{1,0:T(8,128)(2,1)S(1)}, bf16[32,4096]{1,0:T(8,128)(2,1)S(1)}, u32[]{:S(2)}, u32[]{:S(2)}) collective-permute-start(bf16[32,4096]{1,0:T(8,128)(2,1)S(1)} %get-tuple-element.41), channel_id=1, source_target_pairs={{0,24},{4,28},{8,16},{12,20},{16,8},{20,12},{24,0},{28,4},{1,25},{... | collective-permute-start | bytes 786440 | tf_op jit(solution)/shard_map/ppermute | solution.py:18
  436.2 19.7 %collective-permute-start.51 = (bf16[32,4096]{1,0:T(8,128)(2,1)S(1)}, bf16[32,4096]{1,0:T(8,128)(2,1)S(1)}, u32[]{:S(2)}, u32[]{:S(2)}) collective-permute-start(bf16[32,4096]{1,0:T(8,128)(2,1)S(1)} %get-tuple-element.40), channel_id=1, source_target_pairs={{0,16},{4,20},{8,24},{12,28},{16,0},{20,4},{24,8},{28,12},{1,17},{... | collective-permute-start | bytes 786440 | tf_op jit(solution)/shard_map/ppermute | solution.py:18
  (36 other events, 454.2 us)

commit v3 on v2

--- a/solution.py
+++ b/solution.py
@@ -10,7 +10,9 @@
 BF = jnp.bfloat16
 F32 = jnp.float32
 LANES = 128
-DOWN_TILE = 512
+DOWN_TILE = 1024
+GU_SLOTS = 4
+DN_SLOTS = 3
 
 
 def swap(x, axis, flip):
@@ -39,7 +41,7 @@
     return packed[:rows].astype(F32), tail[:heads] + tail[heads:]
 
 
-def incoming_state(state, total, start, head_dim):
+def incoming_state(state, total, start, head_dim, later_use):
     place = lax.axis_index("ctx")
     pairs = lax.axis_size("ctx") // 2
     odd = place % 2 == 1
@@ -71,6 +73,7 @@
     gap = jnp.sum(jnp.where(between[:, :, None], totals[None], 0.0), axis=1)
     weight = jnp.where((planes < z)[:, None], jnp.exp(-gap), 0.0)
     before = jnp.sum(jnp.where((planes < z)[:, None], totals, 0.0), axis=0)
+    states, later_use = lax.optimization_barrier((states, later_use))
     own_start = jnp.where(odd, start[cut:], start[:cut])
     prefix = spread(jnp.exp(-before)) * own_start
     for i, s in enumerate(states):
@@ -78,10 +81,12 @@
     later = spread(jnp.exp(-first_total)) * prefix + first
     mine = jnp.where(odd, later, prefix).astype(BF)
     other = swap(jnp.where(odd, prefix, later).astype(BF), "ctx", 1)
-    return jnp.where(odd, other, mine), jnp.where(odd, mine, other)
-
-
-def mixer_rows(inputs, gate_input, b_proj, c_proj, step_size, decay_rate, skip_gain, start_state):
+    return jnp.where(odd, other, mine), jnp.where(odd, mine, other), later_use
+
+
+def mixer_rows(
+    inputs, gate_input, b_proj, c_proj, step_size, decay_rate, skip_gain, start_state, later_use
+):
     tok = inputs.shape[0]
     heads = step_size.shape[0]
     width = inputs.shape[1]
@@ -96,7 +101,9 @@
     ending = jnp.exp(-(total[:, None] - cumulative)) * step_size
     decayed = (x_local * wide(ending)).astype(BF)
     state = lax.dot_general(decayed, b_proj, (((0,), (0,)), ((), ())), preferred_element_type=F32)
-    low, high = incoming_state(state, total, start_state.reshape(width, -1), head_dim)
+    low, high, later_use = incoming_state(
+        state, total, start_state.reshape(width, -1), head_dim, later_use
+    )
     order = jnp.arange(tok, dtype=jnp.int32)
     causal = order[:, None] >= order[None, :]
     spread = jnp.where(causal[None], cumulative[:, :, None] - cumulative[:, None, :], 0.0)
@@ -118,17 +125,17 @@
         axis=1,
     )
     ssm_out = direct + carried * wide(jnp.exp(-cumulative))
-    return ssm_out * jax.nn.silu(gate_input.astype(F32))
-
-
-def project_rows(gated, norm_gain, out_proj):
+    return ssm_out * jax.nn.silu(gate_input.astype(F32)), later_use
+
+
+def project_rows(gated, norm_gain, out_proj, neighbour_proj):
     n_exp = lax.axis_size("exp")
     n_ctx = lax.axis_size("ctx")
     me_exp = lax.axis_index("exp")
     me_ctx = lax.axis_index("ctx")
     tok, width = gated.shape
     quarter = tok // n_exp
-    both = jnp.concatenate([out_proj, swap(out_proj, "ctx", 2)], axis=1)
+    both = jnp.concatenate([out_proj, neighbour_proj], axis=1)
     squares = jnp.sum(gated * gated, axis=1)
     for flip in (1, 2):
         squares = squares + swap(squares, "exp", flip)
@@ -149,6 +156,7 @@
     group = [h + y for h in [0] + hops for y in (0, 1)]
     full = jnp.concatenate([a_all, b_all], axis=2).reshape(len(group), n_exp, quarter, width)
     full = full.swapaxes(0, 1).reshape(-1, width)
+    full, scale = lax.optimization_barrier((full, scale))
     partial = mm(full, both).astype(BF)
     for flip in (1, 2):
         cut = partial.shape[0] // 2
@@ -162,38 +170,32 @@
         blocks[r] = block[:, :columns]
         blocks[r ^ 2] = block[:, columns:]
     stacked = jnp.stack(blocks)
-    place = me_ctx ^ jnp.arange(n_ctx, dtype=jnp.int32)
     mixed = jnp.concatenate(
-        [lax.dynamic_index_in_dim(stacked, place[b], 0, False) for b in range(n_ctx)], axis=1
+        [lax.dynamic_index_in_dim(stacked, me_ctx ^ b, 0, False) for b in range(n_ctx)], axis=1
     )
     return mixed.astype(F32), scale
 
 
 def pack_kernel(*refs):
-    pieces, out, sems = refs[:-2], refs[-2], refs[-1]
-    copies = []
+    out = refs[-1]
     row = 0
-    for i, piece in enumerate(pieces):
+    for piece in refs[:-1]:
         rows = piece.shape[0]
-        copies.append(pltpu.make_async_copy(piece, out.at[pl.ds(row, rows)], sems.at[i]))
+        out[row : row + rows, :] = piece[...]
         row += rows
-    for c in copies:
-        c.start()
-    for c in copies:
-        c.wait()
 
 
 def pack(pieces):
     rows = sum(p.shape[0] for p in pieces)
     width = pieces[0].shape[1]
-    size = 2 * rows * width
+    whole = pl.BlockSpec(memory_space=pltpu.VMEM)
     return pl.pallas_call(
         pack_kernel,
         out_shape=jax.ShapeDtypeStruct((rows, width), pieces[0].dtype),
-        in_specs=[pl.BlockSpec(memory_space=pl.ANY)] * len(pieces),
-        out_specs=pl.BlockSpec(memory_space=pl.ANY),
-        scratch_shapes=[pltpu.SemaphoreType.DMA((len(pieces),))],
-        cost_estimate=pl.CostEstimate(flops=0, bytes_accessed=2 * size, transcendentals=0),
+        in_specs=[whole] * len(pieces),
+        out_specs=whole,
+        compiler_params=pltpu.CompilerParams(vmem_limit_bytes=32 * 1024 * 1024),
+        cost_estimate=pl.CostEstimate(flops=0, bytes_accessed=4 * rows * width, transcendentals=0),
     )(*pieces)
 
 
@@ -204,41 +206,47 @@
     model = gate.shape[0]
     tiles = gate.shape[1] // LANES
     down_tiles = model // DOWN_TILE
-
-    def row_copies():
+    row_copies = [
+        pltpu.make_async_copy(own, rows.at[pl.ds(0, half)], row_sem.at[0]),
+        pltpu.make_async_copy(mate, rows.at[pl.ds(half, half)], row_sem.at[1]),
+    ]
+
+    def gu_copies(j):
+        at = pl.ds(pl.multiple_of(j * LANES, LANES), LANES)
+        s = lax.rem(j, GU_SLOTS)
         return [
-            pltpu.make_async_copy(own, rows.at[pl.ds(0, half)], row_sem.at[0]),
-            pltpu.make_async_copy(mate, rows.at[pl.ds(half, half)], row_sem.at[1]),
+            pltpu.make_async_copy(gate.at[:, at], gu.at[s, :, pl.ds(0, LANES)], gu_sem.at[s, 0]),
+            pltpu.make_async_copy(up.at[:, at], gu.at[s, :, pl.ds(LANES, LANES)], gu_sem.at[s, 1]),
         ]
 
-    def gu_copies(j, slot):
-        at = pl.ds(pl.multiple_of(j * LANES, LANES), LANES)
-        return [
-            pltpu.make_async_copy(gate.at[:, at], gu.at[slot, :, pl.ds(0, LANES)], gu_sem.at[slot, 0]),
-            pltpu.make_async_copy(up.at[:, at], gu.at[slot, :, pl.ds(LANES, LANES)], gu_sem.at[slot, 1]),
-        ]
-
-    def dn_copy(j, slot):
+    def dn_copy(j):
         at = pl.ds(pl.multiple_of(j * DOWN_TILE, DOWN_TILE), DOWN_TILE)
-        return pltpu.make_async_copy(down.at[:, at], dn.at[slot], dn_sem.at[slot])
-
-    for c in row_copies() + gu_copies(0, 0):
+        s = lax.rem(j, DN_SLOTS)
+        return pltpu.make_async_copy(down.at[:, at], dn.at[s], dn_sem.at[s])
+
+    for c in row_copies:
         c.start()
-    dn_copy(0, 0).start()
-    for c in row_copies():
+    for j in range(GU_SLOTS - 1):
+        for c in gu_copies(j):
+            c.start()
+    for c in row_copies:
         c.wait()
 
     def gate_up(j, carry):
-        slot = lax.rem(j, 2)
-
-        @pl.when(j + 1 < tiles)
+        ahead = j + GU_SLOTS - 1
+        for c in gu_copies(j):
+            c.wait()
+
+        @pl.when(ahead < tiles)
         def _():
-            for c in gu_copies(j + 1, lax.rem(j + 1, 2)):
+            for c in gu_copies(ahead):
                 c.start()
 
-        for c in gu_copies(j, slot):
-            c.wait()
-        both = jnp.dot(rows[:, :model], gu[slot], preferred_element_type=F32)
+        @pl.when((ahead >= tiles) & (ahead - tiles < DN_SLOTS - 1))
+        def _():
+            dn_copy(ahead - tiles).start()
+
+        both = mm(rows[:, :model], gu[lax.rem(j, GU_SLOTS)])
         gate_val = both[:, :LANES]
         act = gate_val / (1.0 + jnp.exp(-gate_val)) * both[:, LANES:]
         hidden[:, pl.ds(pl.multiple_of(j * LANES, LANES), LANES)] = act.astype(BF)
@@ -248,14 +256,13 @@
     weight = jnp.sum(rows[:, model:].astype(F32) * pick[...], axis=1, keepdims=True)
 
     def down_part(j, carry):
-        slot = lax.rem(j, 2)
-
-        @pl.when(j + 1 < down_tiles)
+        dn_copy(j).wait()
+
+        @pl.when(j + DN_SLOTS - 1 < down_tiles)
         def _():
-            dn_copy(j + 1, lax.rem(j + 1, 2)).start()
-
-        dn_copy(j, slot).wait()
-        part = jnp.dot(hidden[...], dn[slot], preferred_element_type=F32) * weight
+            dn_copy(j + DN_SLOTS - 1).start()
+
+        part = mm(hidden[...], dn[lax.rem(j, DN_SLOTS)]) * weight
         at = pl.ds(pl.multiple_of(j * DOWN_TILE, DOWN_TILE), DOWN_TILE)
         out_own[:, at] = part[:half].astype(BF)
         out_mate[:, at] = part[half:].astype(BF)
@@ -270,23 +277,24 @@
     out = jax.ShapeDtypeStruct((half, model), BF)
     whole = pl.BlockSpec(memory_space=pltpu.VMEM)
     anywhere = pl.BlockSpec(memory_space=pl.ANY)
+    hbm = pl.BlockSpec(memory_space=pltpu.HBM)
     flops = 2 * 2 * half * model * units * 3
     moved = 2 * (3 * model * units + 8 * half * model)
     return pl.pallas_call(
         expert_kernel,
         out_shape=(out, out),
-        in_specs=[anywhere] * 5 + [whole],
+        in_specs=[anywhere] * 2 + [hbm] * 3 + [whole],
         out_specs=(whole, whole),
         scratch_shapes=[
             pltpu.VMEM((2 * half, width), BF),
             pltpu.VMEM((2 * half, units), BF),
-            pltpu.VMEM((2, model, 2 * LANES), BF),
-            pltpu.VMEM((2, units, DOWN_TILE), BF),
+            pltpu.VMEM((GU_SLOTS, model, 2 * LANES), BF),
+            pltpu.VMEM((DN_SLOTS, units, DOWN_TILE), BF),
             pltpu.SemaphoreType.DMA((2,)),
-            pltpu.SemaphoreType.DMA((2, 2)),
-            pltpu.SemaphoreType.DMA((2,)),
+            pltpu.SemaphoreType.DMA((GU_SLOTS, 2)),
+            pltpu.SemaphoreType.DMA((DN_SLOTS,)),
         ],
-        compiler_params=pltpu.CompilerParams(vmem_limit_bytes=40 * 1024 * 1024),
+        compiler_params=pltpu.CompilerParams(vmem_limit_bytes=48 * 1024 * 1024),
         cost_estimate=pl.CostEstimate(flops=flops, bytes_accessed=moved, transcendentals=2 * half * units),
     )(own, mate, gate, up, down, pick)
 
@@ -354,10 +362,13 @@
     lane = jnp.arange(LANES, dtype=jnp.int32)
     pick = (lane % (LANES // 2) == me_ctx // PAIR).astype(F32)[None, :]
 
-    gated = mixer_rows(
-        inputs, gate_input, b_proj, c_proj, step_size, decay_rate, skip_gain, start_state
+    cut = out_proj.shape[0] // 2
+    first_part = swap(out_proj[:cut], "ctx", 2)
+    gated, second_part = mixer_rows(
+        inputs, gate_input, b_proj, c_proj, step_size, decay_rate, skip_gain, start_state, out_proj[cut:]
     )
-    mixed, scale = project_rows(gated, norm_gain, out_proj)
+    neighbour_proj = jnp.concatenate([first_part, swap(second_part, "ctx", 2)])
+    mixed, scale = project_rows(gated, norm_gain, out_proj, neighbour_proj)
     own_residual = lax.dynamic_slice_in_dim(residual, me_exp * quarter, quarter, 0)
     hidden = own_residual.astype(F32) + mixed * scale[:, None]
     moe_scale = lax.rsqrt(jnp.mean(hidden * hidden, axis=1, keepdims=True) + eps_norm)

time: 459 us -> 273 us (0.59)
  Pallas kernels: 204 us -> 39.4 us
  between operations: 16.2 us -> 0.92 us
  starting transfers between devices: 55.3 us -> 64.2 us
  local copies, waits for them, and re-layouts: 14.3 us -> 6.08 us
  waiting for transfers between devices: 150 us -> 145 us
    pallas_call x4, Pallas kernels: 152 us -> 0.33 us  [pack(): pl.pallas_call(pack_kernel, out_shape=jax.ShapeDtypeStruct((rows, width),...]
    pallas_call x3, Pallas kernels: 51.7 us -> 39.1 us  [experts(): pl.pallas_call(expert_kernel, out_shape=(out, out), in_specs=[anywhere] *...]
    ppermute x53 -> x54, starting transfers between devices: 55.3 us -> 64.2 us  [swap(): return lax.ppermute(x, axis, [(i, i ^ flip) for i in range(size)])]
    unnamed x79 -> x49, local copies, waits for them, and re-layouts: 10.7 us -> 2.16 us
    ppermute x53 -> x54, waiting for transfers between devices: 150 us -> 145 us  [swap(): return lax.ppermute(x, axis, [(i, i ^ flip) for i in range(size)])]
  transfers between devices with their start and end apart: 53 -> 54, of which waited for: 27 -> 32; matrix products, arithmetic and copies ran while one was open for 3% -> 5% of each run, Pallas kernels for 37% -> 14%
where the time goes in v3:
time: 273 us
  waiting for transfers between devices  145 us (53%)
  starting transfers between devices  64.2 us (24%)
  Pallas kernels  39.4 us (14%)
  other arithmetic  12.7 us (5%)
  local copies, waits for them, and re-layouts  6.08 us (2%)
  matrix products  4.51 us (2%)
    ppermute x54, waiting for transfers between devices, swap(): return lax.ppermute(x, axis, [(i, i ^ flip) for i in range(size)])  145 us
    ppermute x54, starting transfers between devices, swap(): return lax.ppermute(x, axis, [(i, i ^ flip) for i in range(size)])  64.2 us
    pallas_call x3, Pallas kernels, experts(): pl.pallas_call(expert_kernel, out_shape=(out, out), in_specs=[anywhere] *...  39.1 us
  transfers between devices with their start and end apart: 54, of which 32 were waited for; matrix products, arithmetic and copies ran while one was open for 5% of the time, Pallas kernels for 14%

profile of v3, /device:TPU:0, one launch (start us, length us, event | category | flops | bytes accessed | tf_op | source)
XLA Modules:
  0.0 273.0 jit_solution(15450706981575784413)
XLA Ops:
  3.9 3.0 %collective-permute-start = (bf16[528,128]{1,0:T(8,128)(2,1)S(1)}, bf16[528,128]{1,0:T(8,128)(2,1)S(1)}, u32[]{:S(2)}, u32[]{:S(2)}) collective-permute-start(bf16[528,128]{1,0:T(8,128)(2,1)S(1)} %pad_maximum_fusion.10), channel_id=1, source_target_pairs={{0,4},{4,0},{8,12},{12,8},{16,20},{20,16},{24,28},{28,24},{1,5},{5... | collective-permute-start | bytes 405512 | tf_op jit(solution)/shard_map/ppermute | solution.py:20
  8.0 1.6 collective-permute-start.11
  9.8 1.4 fusion.9
  13.8 2.6 collective-permute-start.2
  17.7 9.7 %collective-permute-done.1 = bf16[528,128]{1,0:T(8,128)(2,1)S(1)} collective-permute-done((bf16[528,128]{1,0:T(8,128)(2,1)}, bf16[528,128]{1,0:T(8,128)(2,1)S(1)}, u32[]{:S(2)}, u32[]{:S(2)}) %collective-permute-start.1) | collective-permute-done | bytes 135200 | tf_op jit(solution)/shard_map/ppermute | solution.py:20
  28.7 3.7 %collective-permute-done.3 = bf16[528,128]{1,0:T(8,128)(2,1)} collective-permute-done((bf16[528,128]{1,0:T(8,128)(2,1)}, bf16[528,128]{1,0:T(8,128)(2,1)}, u32[]{:S(2)}, u32[]{:S(2)}) %collective-permute-start.3) | collective-permute-done | bytes 135200 | tf_op jit(solution)/shard_map/ppermute | solution.py:20
  37.1 4.3 %collective-permute-done.4 = bf16[512,128]{1,0:T(8,128)(2,1)S(1)} collective-permute-done((bf16[512,128]{1,0:T(8,128)(2,1)S(1)}, bf16[512,128]{1,0:T(8,128)(2,1)S(1)}, u32[]{:S(2)}, u32[]{:S(2)}) %collective-permute-start.4) | collective-permute-done | bytes 131104 | tf_op jit(solution)/shard_map/ppermute | solution.py:20
  43.8 11.1 %collective-permute-done.5 = bf16[64,1024]{0,1:T(8,128)(2,1)S(1)} collective-permute-done((bf16[64,1024]{0,1:T(8,128)(2,1)S(1)}, bf16[64,1024]{0,1:T(8,128)(2,1)S(1)}, u32[]{:S(2)}, u32[]{:S(2)}) %collective-permute-start.5) | collective-permute-done | bytes 131104 | tf_op jit(solution)/shard_map/ppermute | solution.py:20
  55.4 2.6 collective-permute-start.8
  59.1 1.5 collective-permute-start.10
  60.6 2.0 collective-permute-done.10
  62.8 1.5 collective-permute-done.6
  64.5 13.9 %collective-permute-done.8 = bf16[2,64,1024]{1,2,0:T(8,128)(2,1)S(1)} collective-permute-done((bf16[2,64,1024]{1,2,0:T(8,128)(2,1)S(1)}, bf16[2,64,1024]{1,2,0:T(8,128)(2,1)S(1)}, u32[]{:S(2)}, u32[]{:S(2)}) %collective-permute-start.8) | collective-permute-done | bytes 262176 | tf_op jit(solution)/shard_map/ppermute | solution.py:20
  79.8 2.4 fusion.6
  82.4 1.8 collective-permute-done.13
  84.5 1.6 collective-permute-start.14
  86.2 6.7 %collective-permute-done.14 = bf16[128,1024]{1,0:T(8,128)(2,1)S(1)} collective-permute-done((bf16[128,1024]{1,0:T(8,128)(2,1)S(1)}, bf16[128,1024]{1,0:T(8,128)(2,1)S(1)}, u32[]{:S(2)}, u32[]{:S(2)}) %collective-permute-start.14) | collective-permute-done | bytes 262176 | tf_op jit(solution)/shard_map/ppermute | solution.py:20
  93.6 3.9 %collective-permute-start.17 = (bf16[32,1024]{1,0:T(8,128)(2,1)S(1)}, bf16[32,1024]{1,0:T(8,128)(2,1)S(1)}, u32[]{:S(2)}, u32[]{:S(2)}) collective-permute-start(bf16[32,1024]{1,0:T(8,128)(2,1)S(1)} %get-tuple-element.60), channel_id=1, source_target_pairs={{0,20},{4,16},{8,28},{12,24},{16,4},{20,0},{24,12},{28,8},{1,21},{... | collective-permute-start | bytes 196616 | tf_op jit(solution)/shard_map/ppermute | solution.py:20
  97.5 2.4 collective-permute-done.16
  99.9 2.1 collective-permute-done.17
  102.9 1.5 collective-permute-start.18
  104.4 4.9 %collective-permute-done.19.refs_2_ = bf16[32,4224]{1,0:T(8,128)(2,1)S(1)} collective-permute-done((bf16[32,4224]{1,0:T(8,128)(2,1)S(1)}, bf16[32,4224]{1,0:T(8,128)(2,1)S(1)}, u32[]{:S(2)}, u32[]{:S(2)}) %collective-permute-start.19) | collective-permute-done | bytes 270368 | tf_op jit(solution)/shard_map/ppermute | solution.py:20
  109.3 1.6 collective-permute-start.20
  111.9 2.4 collective-permute-done.20.refs_3_
  114.3 1.6 collective-permute-done.21.refs_4_
  117.3 7.6 %collective-permute-done.28.refs_0_ = bf16[32,4224]{1,0:T(8,128)(2,1)S(1)} collective-permute-done((bf16[32,4224]{1,0:T(8,128)(2,1)S(1)}, bf16[32,4224]{1,0:T(8,128)(2,1)S(1)}, u32[]{:S(2)}, u32[]{:S(2)}) %collective-permute-start.28) | collective-permute-done | bytes 270368 | tf_op jit(solution)/shard_map/ppermute | solution.py:20
  126.0 1.5 collective-permute-start.29
  127.5 1.6 collective-permute-start.40
  129.1 2.0 collective-permute-start.41
  131.1 1.9 collective-permute-done.30.refs_2_
  133.0 1.4 collective-permute-start.31
  135.7 2.4 collective-permute-done.31.refs_3_
  138.1 1.4 collective-permute-done.32.refs_4_
  139.7 8.6 %collective-permute-done.40.refs_0_ = bf16[32,4224]{1,0:T(8,128)(2,1)S(1)} collective-permute-done((bf16[32,4224]{1,0:T(8,128)(2,1)S(1)}, bf16[32,4224]{1,0:T(8,128)(2,1)S(1)}, u32[]{:S(2)}, u32[]{:S(2)}) %collective-permute-start.40) | collective-permute-done | bytes 270368 | tf_op jit(solution)/shard_map/ppermute | solution.py:20
  149.9 10.2 %shard_map.164 = (bf16[128,4096]{1,0:T(8,128)(2,1)S(1)}, bf16[128,4096]{1,0:T(8,128)(2,1)S(1)}) custom-call(bf16[128,4224]{1,0:T(8,128)(2,1)S(1)} %shard_map.163.own, bf16[128,4224]{1,0:T(8,128)(2,1)S(1)} %collective-permute-done.22.mate, bf16[4096,896]{1,0:T(8,128)(2,1)} %bitcast.119, bf16[4096,896]{1,0:T(8,128)(2,1)} %bitcast.122, ...), custom_call_target="tpu_custom_call" | custom-call | flops 5637144576 | bytes 30408704 | tf_op jit(solution)/shard_map/pallas_call | solution.py:283
  161.3 1.6 collective-permute-start.44
  163.7 5.5 %collective-permute-done.44.refs_3_ = bf16[32,4224]{1,0:T(8,128)(2,1)S(1)} collective-permute-done((bf16[32,4224]{1,0:T(8,128)(2,1)S(1)}, bf16[32,4224]{1,0:T(8,128)(2,1)S(1)}, u32[]{:S(2)}, u32[]{:S(2)}) %collective-permute-start.44) | collective-permute-done | bytes 270368 | tf_op jit(solution)/shard_map/ppermute | solution.py:20
  170.8 10.7 %shard_map.166 = (bf16[128,4096]{1,0:T(8,128)(2,1)S(1)}, bf16[128,4096]{1,0:T(8,128)(2,1)S(1)}) custom-call(bf16[128,4224]{1,0:T(8,128)(2,1)S(1)} %shard_map.165.own, bf16[128,4224]{1,0:T(8,128)(2,1)S(1)} %collective-permute-done.33.mate, bf16[4096,896]{1,0:T(8,128)(2,1)} %bitcast.120, bf16[4096,896]{1,0:T(8,128)(2,1)} %bitcast.123, ...), custom_call_target="tpu_custom_call" | custom-call | flops 5637144576 | bytes 30408704 | tf_op jit(solution)/shard_map/pallas_call | solution.py:283
  183.5 4.1 %collective-permute-done.26 = bf16[16,4096]{1,0:T(8,128)(2,1)S(1)} collective-permute-done((bf16[16,4096]{1,0:T(8,128)(2,1)S(1)}, bf16[16,4096]{1,0:T(8,128)(2,1)S(1)}, u32[]{:S(2)}, u32[]{:S(2)}) %collective-permute-start.26) | collective-permute-done | bytes 131104 | tf_op jit(solution)/shard_map/ppermute | solution.py:20
  192.2 18.2 %shard_map.169 = (bf16[256,4096]{1,0:T(8,128)(2,1)S(1)}, bf16[256,4096]{1,0:T(8,128)(2,1)S(1)}) custom-call(bf16[256,4224]{1,0:T(8,128)(2,1)} %copy-done.2, bf16[256,4224]{1,0:T(8,128)(2,1)} %collective-permute-done.46.mate, bf16[4096,896]{1,0:T(8,128)(2,1)} %bitcast.121, bf16[4096,896]{1,0:T(8,128)(2,1)} %bitcast.124, bf16[896,4096]{1,0:T(8,128)(2,1)} %bitcast.127, ...), custom_call_target="tpu_custom_call" | custom-call | flops 11274289152 | bytes 38797312 | tf_op jit(solution)/shard_map/pallas_call | solution.py:283
  212.5 2.1 collective-permute-done.47
  215.9 9.9 %collective-permute-done.50 = bf16[32,4096]{1,0:T(8,128)(2,1)S(1)} collective-permute-done((bf16[32,4096]{1,0:T(8,128)(2,1)S(1)}, bf16[32,4096]{1,0:T(8,128)(2,1)S(1)}, u32[]{:S(2)}, u32[]{:S(2)}) %collective-permute-start.50) | collective-permute-done | bytes 262176 | tf_op jit(solution)/shard_map/ppermute | solution.py:20
  226.8 6.5 %collective-permute-done.48 = bf16[32,4096]{1,0:T(8,128)(2,1)S(1)} collective-permute-done((bf16[32,4096]{1,0:T(8,128)(2,1)S(1)}, bf16[32,4096]{1,0:T(8,128)(2,1)S(1)}, u32[]{:S(2)}, u32[]{:S(2)}) %collective-permute-start.48) | collective-permute-done | bytes 262176 | tf_op jit(solution)/shard_map/ppermute | solution.py:20
  235.5 5.6 %collective-permute-start.39 = (bf16[32,4096]{1,0:T(8,128)(2,1)S(1)}, bf16[32,4096]{1,0:T(8,128)(2,1)S(1)}, u32[]{:S(2)}, u32[]{:S(2)}) collective-permute-start(bf16[32,4096]{1,0:T(8,128)(2,1)S(1)} %add_convert_fusion.5), channel_id=1, source_target_pairs={{0,8},{4,12},{8,0},{12,4},{16,24},{20,28},{24,16},{28,20},{1,9},{5... | collective-permute-start | bytes 786440 | tf_op jit(solution)/shard_map/ppermute | solution.py:20
  241.1 4.6 %collective-permute-done.51 = bf16[64,4096]{1,0:T(8,128)(2,1)S(1)} collective-permute-done((bf16[64,4096]{1,0:T(8,128)(2,1)S(1)}, bf16[64,4096]{1,0:T(8,128)(2,1)S(1)}, u32[]{:S(2)}, u32[]{:S(2)}) %collective-permute-start.51) | collective-permute-done | bytes 524320 | tf_op jit(solution)/shard_map/ppermute | solution.py:20
  246.8 2.7 collective-permute-start.53
  249.5 5.1 %collective-permute-start.52 = (bf16[32,4096]{1,0:T(8,128)(2,1)S(1)}, bf16[32,4096]{1,0:T(8,128)(2,1)S(1)}, u32[]{:S(2)}, u32[]{:S(2)}) collective-permute-start(bf16[32,4096]{1,0:T(8,128)(2,1)S(1)} %get-tuple-element.54), channel_id=1, source_target_pairs={{0,16},{4,20},{8,24},{12,28},{16,0},{20,4},{24,8},{28,12},{1,17},{... | collective-permute-start | bytes 786440 | tf_op jit(solution)/shard_map/ppermute | solution.py:20
  255.2 16.7 %collective-permute-done.52 = bf16[32,4096]{1,0:T(8,128)(2,1)S(1)} collective-permute-done((bf16[32,4096]{1,0:T(8,128)(2,1)S(1)}, bf16[32,4096]{1,0:T(8,128)(2,1)S(1)}, u32[]{:S(2)}, u32[]{:S(2)}) %collective-permute-start.52) | collective-permute-done | bytes 262176 | tf_op jit(solution)/shard_map/ppermute | solution.py:20
  (238 shorter events, 48.4 us)
Async XLA Ops:
  3.9 7.7 %collective-permute-start = (bf16[528,128]{1,0:T(8,128)(2,1)S(1)}, bf16[528,128]{1,0:T(8,128)(2,1)S(1)}, u32[]{:S(2)}, u32[]{:S(2)}) collective-permute-start(bf16[528,128]{1,0:T(8,128)(2,1)S(1)} %pad_maximum_fusion.10), channel_id=1, source_target_pairs={{0,4},{4,0},{8,12},{12,8},{16,20},{20,16},{24,28},{28,24},{1,5},{5... | collective-permute-start | bytes 405512 | tf_op jit(solution)/shard_map/ppermute | solution.py:20
  8.0 71.7 %collective-permute-start.11 = (bf16[512,512]{1,0:T(8,128)(2,1)}, bf16[512,512]{1,0:T(8,128)(2,1)}, u32[]{:S(2)}, u32[]{:S(2)}) collective-permute-start(bf16[512,512]{1,0:T(8,128)(2,1)} %get-tuple-element.52), channel_id=1, source_target_pairs={{0,8},{4,12},{8,0},{12,4},{16,24},{20,28},{24,16},{28,20},{1,9},{5... | collective-permute-start | bytes 1572872 | tf_op jit(solution)/shard_map/ppermute | solution.py:20
  13.1 14.4 %collective-permute-start.1 = (bf16[528,128]{1,0:T(8,128)(2,1)}, bf16[528,128]{1,0:T(8,128)(2,1)S(1)}, u32[]{:S(2)}, u32[]{:S(2)}) collective-permute-start(bf16[528,128]{1,0:T(8,128)(2,1)} %pad_maximum_fusion.11), channel_id=1, source_target_pairs={{0,8},{4,12},{8,0},{12,4},{16,24},{20,28},{24,16},{28,20},{1,9},{5... | collective-permute-start | bytes 405512 | tf_op jit(solution)/shard_map/ppermute | solution.py:20
  13.8 14.2 %collective-permute-start.2 = (bf16[528,128]{1,0:T(8,128)(2,1)}, bf16[528,128]{1,0:T(8,128)(2,1)S(1)}, u32[]{:S(2)}, u32[]{:S(2)}) collective-permute-start(bf16[528,128]{1,0:T(8,128)(2,1)} %pad_maximum_fusion.11), channel_id=1, source_target_pairs={{0,16},{4,20},{8,24},{12,28},{16,0},{20,4},{24,8},{28,12},{1,17},{... | collective-permute-start | bytes 405512 | tf_op jit(solution)/shard_map/ppermute | solution.py:20
  16.4 16.0 %collective-permute-start.3 = (bf16[528,128]{1,0:T(8,128)(2,1)}, bf16[528,128]{1,0:T(8,128)(2,1)}, u32[]{:S(2)}, u32[]{:S(2)}) collective-permute-start(bf16[528,128]{1,0:T(8,128)(2,1)} %pad_maximum_fusion.11), channel_id=1, source_target_pairs={{0,24},{4,28},{8,16},{12,20},{16,8},{20,12},{24,0},{28,4},{1,25},{... | collective-permute-start | bytes 405512 | tf_op jit(solution)/shard_map/ppermute | solution.py:20
  36.9 42.8 %collective-permute-start.12 = (bf16[512,512]{1,0:T(8,128)(2,1)}, bf16[512,512]{1,0:T(8,128)(2,1)}, u32[]{:S(2)}, u32[]{:S(2)}) collective-permute-start(bf16[512,512]{1,0:T(8,128)(2,1)} %get-tuple-element.21), channel_id=1, source_target_pairs={{0,8},{4,12},{8,0},{12,4},{16,24},{20,28},{24,16},{28,20},{1,9},{5... | collective-permute-start | bytes 1572872 | tf_op jit(solution)/shard_map/ppermute | solution.py:20
  42.8 12.0 %collective-permute-start.5 = (bf16[64,1024]{0,1:T(8,128)(2,1)S(1)}, bf16[64,1024]{0,1:T(8,128)(2,1)S(1)}, u32[]{:S(2)}, u32[]{:S(2)}) collective-permute-start(bf16[64,1024]{0,1:T(8,128)(2,1)S(1)} %pad_maximum_fusion.4), channel_id=1, source_target_pairs={{0,16},{4,20},{8,24},{12,28},{16,0},{20,4},{24,8},{28,12},{1,17},{... | collective-permute-start | bytes 393224 | tf_op jit(solution)/shard_map/ppermute | solution.py:20
  43.1 12.2 %collective-permute-start.7 = (bf16[64,1024]{0,1:T(8,128)(2,1)S(1)}, bf16[64,1024]{0,1:T(8,128)(2,1)S(1)}, u32[]{:S(2)}, u32[]{:S(2)}) collective-permute-start(bf16[64,1024]{0,1:T(8,128)(2,1)S(1)} %pad_maximum_fusion.5), channel_id=1, source_target_pairs={{0,4},{4,0},{8,12},{12,8},{16,20},{20,16},{24,28},{28,24},{1,5},{5... | collective-permute-start | bytes 393224 | tf_op jit(solution)/shard_map/ppermute | solution.py:20
  55.0 9.2 %collective-permute-start.6 = (bf16[2,64,1024]{1,2,0:T(8,128)(2,1)S(1)}, bf16[2,64,1024]{1,2,0:T(8,128)(2,1)S(1)}, u32[]{:S(2)}, u32[]{:S(2)}) collective-permute-start(bf16[2,64,1024]{1,2,0:T(8,128)(2,1)S(1)} %get-tuple-element.57), channel_id=1, source_target_pairs={{0,4},{4,0},{8,12},{12,8},{16,20},{20,16},{24,28},{28,24},{1,5},{5... | collective-permute-start | bytes 786440 | tf_op jit(solution)/shard_map/ppermute | solution.py:20
  55.4 23.0 %collective-permute-start.8 = (bf16[2,64,1024]{1,2,0:T(8,128)(2,1)S(1)}, bf16[2,64,1024]{1,2,0:T(8,128)(2,1)S(1)}, u32[]{:S(2)}, u32[]{:S(2)}) collective-permute-start(bf16[2,64,1024]{1,2,0:T(8,128)(2,1)S(1)} %get-tuple-element.59), channel_id=1, source_target_pairs={{0,16},{4,20},{8,24},{12,28},{16,0},{20,4},{24,8},{28,12},{1,17},{... | collective-permute-start | bytes 786440 | tf_op jit(solution)/shard_map/ppermute | solution.py:20
  84.5 8.4 %collective-permute-start.14 = (bf16[128,1024]{1,0:T(8,128)(2,1)S(1)}, bf16[128,1024]{1,0:T(8,128)(2,1)S(1)}, u32[]{:S(2)}, u32[]{:S(2)}) collective-permute-start(bf16[128,1024]{1,0:T(8,128)(2,1)S(1)} %slice.429), channel_id=1, source_target_pairs={{0,2},{1,3},{2,0},{3,1},{4,6},{5,7},{6,4},{7,5},{8,10},{9,11},{10,... | collective-permute-start | bytes 786440 | tf_op jit(solution)/shard_map/ppermute | solution.py:20
  93.6 6.3 %collective-permute-start.16 = (bf16[32,1024]{1,0:T(8,128)(2,1)S(1)}, bf16[32,1024]{1,0:T(8,128)(2,1)S(1)}, u32[]{:S(2)}, u32[]{:S(2)}) collective-permute-start(bf16[32,1024]{1,0:T(8,128)(2,1)S(1)} %get-tuple-element.61), channel_id=1, source_target_pairs={{0,16},{4,20},{8,24},{12,28},{16,0},{20,4},{24,8},{28,12},{1,17},{... | collective-permute-start | bytes 196616 | tf_op jit(solution)/shard_map/ppermute | solution.py:20
  93.6 8.4 %collective-permute-start.17 = (bf16[32,1024]{1,0:T(8,128)(2,1)S(1)}, bf16[32,1024]{1,0:T(8,128)(2,1)S(1)}, u32[]{:S(2)}, u32[]{:S(2)}) collective-permute-start(bf16[32,1024]{1,0:T(8,128)(2,1)S(1)} %get-tuple-element.60), channel_id=1, source_target_pairs={{0,20},{4,16},{8,28},{12,24},{16,4},{20,0},{24,12},{28,8},{1,21},{... | collective-permute-start | bytes 196616 | tf_op jit(solution)/shard_map/ppermute | solution.py:20
  102.7 6.5 %collective-permute-start.19 = (bf16[32,4224]{1,0:T(8,128)(2,1)S(1)}, bf16[32,4224]{1,0:T(8,128)(2,1)S(1)}, u32[]{:S(2)}, u32[]{:S(2)}) collective-permute-start(bf16[32,4224]{1,0:T(8,128)(2,1)S(1)} %concatenate.79.refs_0_), channel_id=1, source_target_pairs={{0,4},{4,0},{8,12},{12,8},{16,20},{20,16},{24,28},{28,24},{1,5},{5... | collective-permute-start | bytes 811016 | tf_op jit(solution)/shard_map/ppermute | solution.py:20
  102.9 8.0 %collective-permute-start.18 = (bf16[32,4224]{1,0:T(8,128)(2,1)S(1)}, bf16[32,4224]{1,0:T(8,128)(2,1)S(1)}, u32[]{:S(2)}, u32[]{:S(2)}) collective-permute-start(bf16[32,4224]{1,0:T(8,128)(2,1)S(1)} %concatenate.79.refs_0_), channel_id=1, source_target_pairs={{0,2},{1,3},{2,0},{3,1},{4,6},{5,7},{6,4},{7,5},{8,10},{9,11},{10,... | collective-permute-start | bytes 811016 | tf_op jit(solution)/shard_map/ppermute | solution.py:20
  109.3 5.1 %collective-permute-start.20 = (bf16[16,4224]{1,0:T(8,128)(2,1)S(1)}, bf16[16,4224]{1,0:T(8,128)(2,1)S(1)}, u32[]{:S(2)}, u32[]{:S(2)}) collective-permute-start(bf16[16,4224]{1,0:T(8,128)(2,1)S(1)} %slice.441), channel_id=1, source_target_pairs={{0,2},{1,3},{2,0},{3,1},{4,6},{5,7},{6,4},{7,5},{8,10},{9,11},{10,... | collective-permute-start | bytes 405512 | tf_op jit(solution)/shard_map/ppermute | solution.py:20
  110.9 5.1 %collective-permute-start.21 = (bf16[16,4224]{1,0:T(8,128)(2,1)S(1)}, bf16[16,4224]{1,0:T(8,128)(2,1)S(1)}, u32[]{:S(2)}, u32[]{:S(2)}) collective-permute-start(bf16[16,4224]{1,0:T(8,128)(2,1)S(1)} %slice.442), channel_id=1, source_target_pairs={{0,4},{4,0},{8,12},{12,8},{16,20},{20,16},{24,28},{28,24},{1,5},{5... | collective-permute-start | bytes 405512 | tf_op jit(solution)/shard_map/ppermute | solution.py:20
  116.0 33.9 %collective-permute-start.22 = (bf16[128,4224]{1,0:T(8,128)(2,1)S(1)}, bf16[128,4224]{1,0:T(8,128)(2,1)S(1)}, u32[]{:S(2)}, u32[]{:S(2)}) collective-permute-start(bf16[128,4224]{1,0:T(8,128)(2,1)S(1)} %shard_map.163.own), channel_id=1, source_target_pairs={{0,1},{1,0},{2,3},{3,2},{4,5},{5,4},{6,7},{7,6},{8,9},{9,8},{10,11... | collective-permute-start | bytes 3244040 | tf_op jit(solution)/shard_map/ppermute | solution.py:20
  116.1 8.9 %collective-permute-start.28 = (bf16[32,4224]{1,0:T(8,128)(2,1)S(1)}, bf16[32,4224]{1,0:T(8,128)(2,1)S(1)}, u32[]{:S(2)}, u32[]{:S(2)}) collective-permute-start(bf16[32,4224]{1,0:T(8,128)(2,1)S(1)} %concatenate.79.refs_0_), channel_id=1, source_target_pairs={{0,8},{4,12},{8,0},{12,4},{16,24},{20,28},{24,16},{28,20},{1,9},{5... | collective-permute-start | bytes 811016 | tf_op jit(solution)/shard_map/ppermute | solution.py:20
  125.0 8.0 %collective-permute-start.30 = (bf16[32,4224]{1,0:T(8,128)(2,1)S(1)}, bf16[32,4224]{1,0:T(8,128)(2,1)S(1)}, u32[]{:S(2)}, u32[]{:S(2)}) collective-permute-start(bf16[32,4224]{1,0:T(8,128)(2,1)S(1)} %collective-permute-done.28.refs_0_), channel_id=1, source_target_pairs={{0,4},{4,0},{8,12},{12,8},{16,20},{20,16},{24,28},{28,24},{1,5},{5... | collective-permute-start | bytes 811016 | tf_op jit(solution)/shard_map/ppermute | solution.py:20
  126.0 8.5 %collective-permute-start.29 = (bf16[32,4224]{1,0:T(8,128)(2,1)S(1)}, bf16[32,4224]{1,0:T(8,128)(2,1)S(1)}, u32[]{:S(2)}, u32[]{:S(2)}) collective-permute-start(bf16[32,4224]{1,0:T(8,128)(2,1)S(1)} %collective-permute-done.28.refs_0_), channel_id=1, source_target_pairs={{0,2},{1,3},{2,0},{3,1},{4,6},{5,7},{6,4},{7,5},{8,10},{9,11},{10,... | collective-permute-start | bytes 811016 | tf_op jit(solution)/shard_map/ppermute | solution.py:20
  127.5 20.8 %collective-permute-start.40 = (bf16[32,4224]{1,0:T(8,128)(2,1)S(1)}, bf16[32,4224]{1,0:T(8,128)(2,1)S(1)}, u32[]{:S(2)}, u32[]{:S(2)}) collective-permute-start(bf16[32,4224]{1,0:T(8,128)(2,1)S(1)} %concatenate.79.refs_0_), channel_id=1, source_target_pairs={{0,16},{4,20},{8,24},{12,28},{16,0},{20,4},{24,8},{28,12},{1,17},{... | collective-permute-start | bytes 811016 | tf_op jit(solution)/shard_map/ppermute | solution.py:20
  129.1 19.2 %collective-permute-start.41 = (bf16[32,4224]{1,0:T(8,128)(2,1)S(1)}, bf16[32,4224]{1,0:T(8,128)(2,1)S(1)}, u32[]{:S(2)}, u32[]{:S(2)}) collective-permute-start(bf16[32,4224]{1,0:T(8,128)(2,1)S(1)} %concatenate.79.refs_0_), channel_id=1, source_target_pairs={{0,24},{4,28},{8,16},{12,20},{16,8},{20,12},{24,0},{28,4},{1,25},{... | collective-permute-start | bytes 811016 | tf_op jit(solution)/shard_map/ppermute | solution.py:20
  133.0 5.1 %collective-permute-start.31 = (bf16[16,4224]{1,0:T(8,128)(2,1)S(1)}, bf16[16,4224]{1,0:T(8,128)(2,1)S(1)}, u32[]{:S(2)}, u32[]{:S(2)}) collective-permute-start(bf16[16,4224]{1,0:T(8,128)(2,1)S(1)} %slice.452), channel_id=1, source_target_pairs={{0,2},{1,3},{2,0},{3,1},{4,6},{5,7},{6,4},{7,5},{8,10},{9,11},{10,... | collective-permute-start | bytes 405512 | tf_op jit(solution)/shard_map/ppermute | solution.py:20
  134.5 5.1 %collective-permute-start.32 = (bf16[16,4224]{1,0:T(8,128)(2,1)S(1)}, bf16[16,4224]{1,0:T(8,128)(2,1)S(1)}, u32[]{:S(2)}, u32[]{:S(2)}) collective-permute-start(bf16[16,4224]{1,0:T(8,128)(2,1)S(1)} %slice.453), channel_id=1, source_target_pairs={{0,4},{4,0},{8,12},{12,8},{16,20},{20,16},{24,28},{28,24},{1,5},{5... | collective-permute-start | bytes 405512 | tf_op jit(solution)/shard_map/ppermute | solution.py:20
  139.6 31.1 %collective-permute-start.33 = (bf16[128,4224]{1,0:T(8,128)(2,1)S(1)}, bf16[128,4224]{1,0:T(8,128)(2,1)S(1)}, u32[]{:S(2)}, u32[]{:S(2)}) collective-permute-start(bf16[128,4224]{1,0:T(8,128)(2,1)S(1)} %shard_map.165.own), channel_id=1, source_target_pairs={{0,1},{1,0},{2,3},{3,2},{4,5},{5,4},{6,7},{7,6},{8,9},{9,8},{10,11... | collective-permute-start | bytes 3244040 | tf_op jit(solution)/shard_map/ppermute | solution.py:20
  148.3 14.5 %collective-permute-start.42 = (bf16[64,4224]{1,0:T(8,128)(2,1)S(1)}, bf16[64,4224]{1,0:T(8,128)(2,1)S(1)}, u32[]{:S(2)}, u32[]{:S(2)}) collective-permute-start(bf16[64,4224]{1,0:T(8,128)(2,1)S(1)} %shard_map.167.refs_0_), channel_id=1, source_target_pairs={{0,2},{1,3},{2,0},{3,1},{4,6},{5,7},{6,4},{7,5},{8,10},{9,11},{10,... | collective-permute-start | bytes 1622024 | tf_op jit(solution)/shard_map/ppermute | solution.py:20
  148.9 12.3 %collective-permute-start.43 = (bf16[64,4224]{1,0:T(8,128)(2,1)S(1)}, bf16[64,4224]{1,0:T(8,128)(2,1)S(1)}, u32[]{:S(2)}, u32[]{:S(2)}) collective-permute-start(bf16[64,4224]{1,0:T(8,128)(2,1)S(1)} %shard_map.167.refs_0_), channel_id=1, source_target_pairs={{0,4},{4,0},{8,12},{12,8},{16,20},{20,16},{24,28},{28,24},{1,5},{5... | collective-permute-start | bytes 1622024 | tf_op jit(solution)/shard_map/ppermute | solution.py:20
  160.2 21.4 %collective-permute-start.23 = (bf16[128,4096]{1,0:T(8,128)(2,1)S(1)}, bf16[128,4096]{1,0:T(8,128)(2,1)S(1)}, u32[]{:S(2)}, u32[]{:S(2)}) collective-permute-start(bf16[128,4096]{1,0:T(8,128)(2,1)S(1)} %get-tuple-element.24), channel_id=1, source_target_pairs={{0,1},{1,0},{2,3},{3,2},{4,5},{5,4},{6,7},{7,6},{8,9},{9,8},{10,11... | collective-permute-start | bytes 3145736 | tf_op jit(solution)/shard_map/ppermute | solution.py:20
  161.3 7.9 %collective-permute-start.44 = (bf16[32,4224]{1,0:T(8,128)(2,1)S(1)}, bf16[32,4224]{1,0:T(8,128)(2,1)S(1)}, u32[]{:S(2)}, u32[]{:S(2)}) collective-permute-start(bf16[32,4224]{1,0:T(8,128)(2,1)S(1)} %slice.463), channel_id=1, source_target_pairs={{0,2},{1,3},{2,0},{3,1},{4,6},{5,7},{6,4},{7,5},{8,10},{9,11},{10,... | collective-permute-start | bytes 811016 | tf_op jit(solution)/shard_map/ppermute | solution.py:20
  162.9 7.6 %collective-permute-start.45 = (bf16[32,4224]{1,0:T(8,128)(2,1)S(1)}, bf16[32,4224]{1,0:T(8,128)(2,1)S(1)}, u32[]{:S(2)}, u32[]{:S(2)}) collective-permute-start(bf16[32,4224]{1,0:T(8,128)(2,1)S(1)} %slice.464), channel_id=1, source_target_pairs={{0,4},{4,0},{8,12},{12,8},{16,20},{20,16},{24,28},{28,24},{1,5},{5... | collective-permute-start | bytes 811016 | tf_op jit(solution)/shard_map/ppermute | solution.py:20
  170.7 21.5 %collective-permute-start.46 = (bf16[256,4224]{1,0:T(8,128)(2,1)S(1)}, bf16[256,4224]{1,0:T(8,128)(2,1)}, u32[]{:S(2)}, u32[]{:S(2)}) collective-permute-start(bf16[256,4224]{1,0:T(8,128)(2,1)S(1)} %shard_map.168.own), channel_id=1, source_target_pairs={{0,1},{1,0},{2,3},{3,2},{4,5},{5,4},{6,7},{7,6},{8,9},{9,8},{10,11... | collective-permute-start | bytes 6488072 | tf_op jit(solution)/shard_map/ppermute | solution.py:20
  181.5 8.2 %collective-permute-start.34 = (bf16[128,4096]{1,0:T(8,128)(2,1)S(1)}, bf16[128,4096]{1,0:T(8,128)(2,1)S(1)}, u32[]{:S(2)}, u32[]{:S(2)}) collective-permute-start(bf16[128,4096]{1,0:T(8,128)(2,1)S(1)} %get-tuple-element.26), channel_id=1, source_target_pairs={{0,1},{1,0},{2,3},{3,2},{4,5},{5,4},{6,7},{7,6},{8,9},{9,8},{10,11... | collective-permute-start | bytes 3145736 | tf_op jit(solution)/shard_map/ppermute | solution.py:20
  181.6 5.9 %collective-permute-start.26 = (bf16[16,4096]{1,0:T(8,128)(2,1)S(1)}, bf16[16,4096]{1,0:T(8,128)(2,1)S(1)}, u32[]{:S(2)}, u32[]{:S(2)}) collective-permute-start(bf16[16,4096]{1,0:T(8,128)(2,1)S(1)} %get-tuple-element.45), channel_id=1, source_target_pairs={{0,2},{1,3},{2,0},{3,1},{4,6},{5,7},{6,4},{7,5},{8,10},{9,11},{10,... | collective-permute-start | bytes 393224 | tf_op jit(solution)/shard_map/ppermute | solution.py:20
  182.4 6.4 %collective-permute-start.24 = (bf16[16,4096]{1,0:T(8,128)(2,1)S(1)}, bf16[16,4096]{1,0:T(8,128)(2,1)S(1)}, u32[]{:S(2)}, u32[]{:S(2)}) collective-permute-start(bf16[16,4096]{1,0:T(8,128)(2,1)S(1)} %get-tuple-element.44), channel_id=1, source_target_pairs={{0,4},{4,0},{8,12},{12,8},{16,20},{20,16},{24,28},{28,24},{1,5},{5... | collective-permute-start | bytes 393224 | tf_op jit(solution)/shard_map/ppermute | solution.py:20
  187.6 67.0 %collective-permute-start.27 = (bf16[32,4096]{1,0:T(8,128)(2,1)S(1)}, bf16[32,4096]{1,0:T(8,128)(2,1)S(1)}, u32[]{:S(2)}, u32[]{:S(2)}) collective-permute-start(bf16[32,4096]{1,0:T(8,128)(2,1)S(1)} %pad_maximum_fusion.7), channel_id=1, source_target_pairs={{0,4},{4,0},{8,12},{12,8},{16,20},{20,16},{24,28},{28,24},{1,5},{5... | collective-permute-start | bytes 786440 | tf_op jit(solution)/shard_map/ppermute | solution.py:20
  188.8 65.8 %collective-permute-start.25 = (bf16[32,4096]{1,0:T(8,128)(2,1)S(1)}, bf16[32,4096]{1,0:T(8,128)(2,1)S(1)}, u32[]{:S(2)}, u32[]{:S(2)}) collective-permute-start(bf16[32,4096]{1,0:T(8,128)(2,1)S(1)} %pad_maximum_fusion.6), channel_id=1, source_target_pairs={{0,2},{1,3},{2,0},{3,1},{4,6},{5,7},{6,4},{7,5},{8,10},{9,11},{10,... | collective-permute-start | bytes 786440 | tf_op jit(solution)/shard_map/ppermute | solution.py:20
  189.8 20.6 %collective-permute-start.37 = (bf16[16,4096]{1,0:T(8,128)(2,1)S(1)}, bf16[16,4096]{1,0:T(8,128)(2,1)S(1)}, u32[]{:S(2)}, u32[]{:S(2)}) collective-permute-start(bf16[16,4096]{1,0:T(8,128)(2,1)S(1)} %get-tuple-element.49), channel_id=1, source_target_pairs={{0,2},{1,3},{2,0},{3,1},{4,6},{5,7},{6,4},{7,5},{8,10},{9,11},{10,... | collective-permute-start | bytes 393224 | tf_op jit(solution)/shard_map/ppermute | solution.py:20
  191.2 20.4 %collective-permute-start.35 = (bf16[16,4096]{1,0:T(8,128)(2,1)S(1)}, bf16[16,4096]{1,0:T(8,128)(2,1)S(1)}, u32[]{:S(2)}, u32[]{:S(2)}) collective-permute-start(bf16[16,4096]{1,0:T(8,128)(2,1)S(1)} %get-tuple-element.48), channel_id=1, source_target_pairs={{0,4},{4,0},{8,12},{12,8},{16,20},{20,16},{24,28},{28,24},{1,5},{5... | collective-permute-start | bytes 393224 | tf_op jit(solution)/shard_map/ppermute | solution.py:20
  210.5 23.9 %collective-permute-start.38 = (bf16[32,4096]{1,0:T(8,128)(2,1)S(1)}, bf16[32,4096]{1,0:T(8,128)(2,1)S(1)}, u32[]{:S(2)}, u32[]{:S(2)}) collective-permute-start(bf16[32,4096]{1,0:T(8,128)(2,1)S(1)} %pad_maximum_fusion.9), channel_id=1, source_target_pairs={{0,4},{4,0},{8,12},{12,8},{16,20},{20,16},{24,28},{28,24},{1,5},{5... | collective-permute-start | bytes 786440 | tf_op jit(solution)/shard_map/ppermute | solution.py:20
  211.7 23.7 %collective-permute-start.36 = (bf16[32,4096]{1,0:T(8,128)(2,1)S(1)}, bf16[32,4096]{1,0:T(8,128)(2,1)S(1)}, u32[]{:S(2)}, u32[]{:S(2)}) collective-permute-start(bf16[32,4096]{1,0:T(8,128)(2,1)S(1)} %pad_maximum_fusion.8), channel_id=1, source_target_pairs={{0,2},{1,3},{2,0},{3,1},{4,6},{5,7},{6,4},{7,5},{8,10},{9,11},{10,... | collective-permute-start | bytes 786440 | tf_op jit(solution)/shard_map/ppermute | solution.py:20
  214.7 11.1 %collective-permute-start.50 = (bf16[32,4096]{1,0:T(8,128)(2,1)S(1)}, bf16[32,4096]{1,0:T(8,128)(2,1)S(1)}, u32[]{:S(2)}, u32[]{:S(2)}) collective-permute-start(bf16[32,4096]{1,0:T(8,128)(2,1)S(1)} %get-tuple-element.41), channel_id=1, source_target_pairs={{0,2},{1,3},{2,0},{3,1},{4,6},{5,7},{6,4},{7,5},{8,10},{9,11},{10,... | collective-permute-start | bytes 786440 | tf_op jit(solution)/shard_map/ppermute | solution.py:20
  225.8 7.6 %collective-permute-start.48 = (bf16[32,4096]{1,0:T(8,128)(2,1)S(1)}, bf16[32,4096]{1,0:T(8,128)(2,1)S(1)}, u32[]{:S(2)}, u32[]{:S(2)}) collective-permute-start(bf16[32,4096]{1,0:T(8,128)(2,1)S(1)} %get-tuple-element.40), channel_id=1, source_target_pairs={{0,4},{4,0},{8,12},{12,8},{16,20},{20,16},{24,28},{28,24},{1,5},{5... | collective-permute-start | bytes 786440 | tf_op jit(solution)/shard_map/ppermute | solution.py:20
  233.4 12.3 %collective-permute-start.51 = (bf16[64,4096]{1,0:T(8,128)(2,1)S(1)}, bf16[64,4096]{1,0:T(8,128)(2,1)S(1)}, u32[]{:S(2)}, u32[]{:S(2)}) collective-permute-start(bf16[64,4096]{1,0:T(8,128)(2,1)S(1)} %pad_maximum_fusion.3), channel_id=1, source_target_pairs={{0,4},{4,0},{8,12},{12,8},{16,20},{20,16},{24,28},{28,24},{1,5},{5... | collective-permute-start | bytes 1572872 | tf_op jit(solution)/shard_map/ppermute | solution.py:20
  234.4 12.1 %collective-permute-start.49 = (bf16[64,4096]{1,0:T(8,128)(2,1)S(1)}, bf16[64,4096]{1,0:T(8,128)(2,1)S(1)}, u32[]{:S(2)}, u32[]{:S(2)}) collective-permute-start(bf16[64,4096]{1,0:T(8,128)(2,1)S(1)} %pad_maximum_fusion.2), channel_id=1, source_target_pairs={{0,2},{1,3},{2,0},{3,1},{4,6},{5,7},{6,4},{7,5},{8,10},{9,11},{10,... | collective-permute-start | bytes 1572872 | tf_op jit(solution)/shard_map/ppermute | solution.py:20
  235.5 19.1 %collective-permute-start.39 = (bf16[32,4096]{1,0:T(8,128)(2,1)S(1)}, bf16[32,4096]{1,0:T(8,128)(2,1)S(1)}, u32[]{:S(2)}, u32[]{:S(2)}) collective-permute-start(bf16[32,4096]{1,0:T(8,128)(2,1)S(1)} %add_convert_fusion.5), channel_id=1, source_target_pairs={{0,8},{4,12},{8,0},{12,4},{16,24},{20,28},{24,16},{28,20},{1,9},{5... | collective-permute-start | bytes 786440 | tf_op jit(solution)/shard_map/ppermute | solution.py:20
  246.8 8.4 %collective-permute-start.53 = (bf16[32,4096]{1,0:T(8,128)(2,1)S(1)}, bf16[32,4096]{1,0:T(8,128)(2,1)S(1)}, u32[]{:S(2)}, u32[]{:S(2)}) collective-permute-start(bf16[32,4096]{1,0:T(8,128)(2,1)S(1)} %get-tuple-element.55), channel_id=1, source_target_pairs={{0,24},{4,28},{8,16},{12,20},{16,8},{20,12},{24,0},{28,4},{1,25},{... | collective-permute-start | bytes 786440 | tf_op jit(solution)/shard_map/ppermute | solution.py:20
  249.5 22.4 %collective-permute-start.52 = (bf16[32,4096]{1,0:T(8,128)(2,1)S(1)}, bf16[32,4096]{1,0:T(8,128)(2,1)S(1)}, u32[]{:S(2)}, u32[]{:S(2)}) collective-permute-start(bf16[32,4096]{1,0:T(8,128)(2,1)S(1)} %get-tuple-element.54), channel_id=1, source_target_pairs={{0,16},{4,20},{8,24},{12,28},{16,0},{20,4},{24,8},{28,12},{1,17},{... | collective-permute-start | bytes 786440 | tf_op jit(solution)/shard_map/ppermute | solution.py:20
  (22 other events, 148.5 us)

commit v4 on v3

--- a/solution.py
+++ b/solution.py
@@ -145,16 +145,10 @@
     rows = (gated * norm_gain[None, :]).astype(BF)
     rel = [0, 2, 1, 3]
     pieces = [lax.dynamic_slice_in_dim(rows, (me_exp ^ q) * quarter, quarter, 0) for q in rel]
-    part_a = jnp.concatenate(pieces[:2])
-    part_b = jnp.concatenate(pieces[2:])
-    hops = [4 * m for m in range(1, n_ctx // 4)]
-    a_z = jnp.stack([part_a] + [swap(part_a, "ctx", h) for h in hops])
-    b_y = jnp.stack([part_b, swap(part_b, "ctx", 1)])
-    a_all = jnp.stack([a_z, swap(a_z, "ctx", 1)])
-    b_all = jnp.stack([b_y] + [swap(b_y, "ctx", h) for h in hops])
-    a_all = a_all.swapaxes(0, 1)
-    group = [h + y for h in [0] + hops for y in (0, 1)]
-    full = jnp.concatenate([a_all, b_all], axis=2).reshape(len(group), n_exp, quarter, width)
+    own_rows = jnp.concatenate(pieces)
+    group = [h + y for h in range(0, n_ctx, 4) for y in (0, 1)]
+    arrived = [own_rows] + [swap(own_rows, "ctx", r) for r in group[1:]]
+    full = jnp.stack(arrived).reshape(len(group), n_exp, quarter, width)
     full = full.swapaxes(0, 1).reshape(-1, width)
     full, scale = lax.optimization_barrier((full, scale))
     partial = mm(full, both).astype(BF)
@@ -299,33 +293,27 @@
     )(own, mate, gate, up, down, pick)
 
 
-def gather_plane(piece):
-    half = piece.shape[0] // 2
-    from_x = swap(piece, "exp", 2)
-    from_y = swap(piece, "ctx", 1)
-    far_a = swap(from_y[:half], "exp", 2)
-    far_b = swap(from_x[half:], "ctx", 1)
-    return pack([piece, from_x, from_y, far_a, far_b])
-
-
-def scatter_plane(own, mate):
-    got = swap(mate, "exp", 1)
+def together(values, others):
+    return lax.optimization_barrier((tuple(values), others))
+
+
+def across(x):
+    n_ctx, n_exp = lax.axis_size("ctx"), lax.axis_size("exp")
+    pairs = [
+        (c * n_exp + e, (c ^ 1) * n_exp + (e ^ 2)) for c in range(n_ctx) for e in range(n_exp)
+    ]
+    return lax.ppermute(x, ("ctx", "exp"), pairs)
+
+
+def summed(own, got, first, rows):
+    last = first + rows
+    return own[first:last].astype(F32) + got[first:last].astype(F32)
+
+
+def plane_sums(own, got):
     size = own.shape[0] // 4
-    half = size // 2
-
-    def both(first, rows):
-        last = first + rows
-        return own[first:last].astype(F32) + got[first:last].astype(F32)
-
-    far_a = swap(both(3 * size, half).astype(BF), "exp", 2)
-    far_b = swap(both(3 * size + half, half).astype(BF), "ctx", 1)
-    to_x = both(size, size)
-    to_y = both(2 * size, size)
-    to_y = jnp.concatenate([to_y[:half] + far_a.astype(F32), to_y[half:]])
-    to_x = jnp.concatenate([to_x[:half], to_x[half:] + far_b.astype(F32)])
-    from_x = swap(to_x.astype(BF), "exp", 2)
-    from_y = swap(to_y.astype(BF), "ctx", 1)
-    return both(0, size) + from_x.astype(F32) + from_y.astype(F32)
+    to_x, to_y, to_xy = [summed(own, got, k * size, size).astype(BF) for k in (1, 2, 3)]
+    return swap(to_x, "exp", 2), swap(to_y, "ctx", 1), across(to_xy)
 
 
 def local(
@@ -375,19 +363,49 @@
     moe_in = (hidden * moe_scale * moe_gain[None, :]).astype(BF)
 
     payload = jnp.concatenate([moe_in, weights_high, weights_low], axis=1)
-    planes = [payload] + [swap(payload, "ctx", 2 * d) for d in range(1, pairs)]
-    total = hidden
-    groups = [[0], [1]] + [[d, d + 1] for d in range(2, pairs, 2)]
-    for offsets in groups:
-        piece = planes[offsets[0]] if len(offsets) == 1 else pack([planes[d] for d in offsets])
-        own = gather_plane(piece)
-        mate = swap(own, "exp", 1)
-        own, mate = experts(own, mate, w_gate[0], w_up[0], w_down[0], pick)
-        summed = scatter_plane(own, mate)
-        for i, d in enumerate(offsets):
-            part = summed[i * quarter : (i + 1) * quarter]
-            total = total + (part if d == 0 else swap(part.astype(BF), "ctx", 2 * d).astype(F32))
-    return total.astype(BF)
+    order = [1] + list(range(pairs - 1, 1, -1)) + [0]
+    count = len(order)
+    by_distance = [payload]
+    for d in range(1, pairs):
+        low = d & -d
+        by_distance.append(swap(by_distance[d - low], "ctx", 2 * low))
+    planes = [by_distance[d] for d in order]
+    near, rows, results, got, far_got = [], [], [], [], []
+
+    def rest(stage):
+        if 0 <= stage - 1 < count:
+            got.append(swap(results[stage - 1][1], "exp", 1))
+        if 0 <= stage - 2 < count:
+            far_got.append(plane_sums(results[stage - 2][0], got[stage - 2]))
+
+    def arrive(stage):
+        if stage + 2 < count:
+            piece = planes[stage + 2]
+            near.append((swap(piece, "exp", 2), swap(piece, "ctx", 1), across(piece)))
+        if 0 <= stage + 1 < count:
+            own = pack((planes[stage + 1], *near[stage + 1]))
+            rows.append((own, swap(own, "exp", 1)))
+
+    for stage in (-2, -1):
+        arrive(stage)
+    for i in range(count):
+        rest(i)
+        arrive(i)
+        beside = (got[-1:], far_got[-1:], rows[i + 1 :], near[i + 2 :])
+        results.append(experts(*rows[i], w_gate[0], w_up[0], w_down[0], pick))
+        results[i], beside = together(results[i], beside)
+        got[-1:], far_got[-1:], rows[i + 1 :], near[i + 2 :] = beside
+    for i in range(count, count + 2):
+        rest(i)
+    parts = [None] * pairs
+    for i, d in enumerate(order):
+        parts[d] = summed(results[i][0], got[i], 0, quarter)
+        for v in far_got[i]:
+            parts[d] = parts[d] + v.astype(F32)
+    for d in sorted(range(1, pairs), key=lambda d: (-bin(d).count("1"), d)):
+        low = d & -d
+        parts[d - low] = parts[d - low] + swap(parts[d].astype(BF), "ctx", 2 * low).astype(F32)
+    return (hidden + parts[0]).astype(BF)
 
 
 def solution(mesh):

time: 273 us -> 229 us (0.84)
  waiting for transfers between devices: 145 us -> 107 us
  other arithmetic: 12.7 us -> 9.21 us
    ppermute x54 -> x47, waiting for transfers between devices: 145 us -> 87.9 us  [swap(): return lax.ppermute(x, axis, [(i, i ^ flip) for i in range(size)])]
    ppermute x0 -> x8, waiting for transfers between devices: none -> 19.2 us  [across(): return lax.ppermute(x, ('ctx', 'exp'), pairs)]
    ppermute x54 -> x47, starting transfers between devices: 64.2 us -> 49.2 us  [swap(): return lax.ppermute(x, axis, [(i, i ^ flip) for i in range(size)])]
    ppermute x0 -> x8, starting transfers between devices: none -> 12.3 us  [across(): return lax.ppermute(x, ('ctx', 'exp'), pairs)]
    pallas_call x3 -> x4, Pallas kernels: 39.1 us -> 40.9 us  [experts(): pl.pallas_call(expert_kernel, out_shape=(out, out), in_specs=[anywhere] *...]
  transfers between devices with their start and end apart: 54 -> 55, of which waited for: 32 -> 28; matrix products, arithmetic and copies ran while one was open for 5% -> 4% of each run, Pallas kernels for 14% -> 18%
where the time goes in v4:
time: 229 us; the launch traced here: 228 us
  waiting for transfers between devices  107 us (47%)
  starting transfers between devices  61.5 us (27%)
  Pallas kernels  41.2 us (18%)
  other arithmetic  9.21 us (4%)
  local copies, waits for them, and re-layouts  5.09 us (2%)
  matrix products  3.7 us (2%)
    ppermute x47, waiting for transfers between devices, swap(): return lax.ppermute(x, axis, [(i, i ^ flip) for i in range(size)])  87.9 us
    ppermute x47, starting transfers between devices, swap(): return lax.ppermute(x, axis, [(i, i ^ flip) for i in range(size)])  49.2 us
    pallas_call x4, Pallas kernels, experts(): pl.pallas_call(expert_kernel, out_shape=(out, out), in_specs=[anywhere] *...  40.9 us
    ppermute x8, waiting for transfers between devices, across(): return lax.ppermute(x, ('ctx', 'exp'), pairs)  19.2 us
    ppermute x8, starting transfers between devices, across(): return lax.ppermute(x, ('ctx', 'exp'), pairs)  12.3 us
  transfers between devices with their start and end apart: 55, of which 28 were waited for; matrix products, arithmetic and copies ran while one was open for 4% of the time, Pallas kernels for 18%

profile of v4, /device:TPU:0, one launch (start us, length us, event | category | flops | bytes accessed | tf_op | source)
XLA Modules:
  0.0 228.5 jit_solution(9771557517413057649)
XLA Ops:
  3.9 3.0 %collective-permute-start = (bf16[528,128]{1,0:T(8,128)(2,1)S(1)}, bf16[528,128]{1,0:T(8,128)(2,1)S(1)}, u32[]{:S(2)}, u32[]{:S(2)}) collective-permute-start(bf16[528,128]{1,0:T(8,128)(2,1)S(1)} %pad_maximum_fusion.1), channel_id=1, source_target_pairs={{0,4},{4,0},{8,12},{12,8},{16,20},{20,16},{24,28},{28,24},{1,5},{5... | collective-permute-start | bytes 405512 | tf_op jit(solution)/shard_map/ppermute | solution.py:20
  8.0 1.6 collective-permute-start.10
  12.3 3.5 %collective-permute-start.3 = (bf16[528,128]{1,0:T(8,128)(2,1)}, bf16[528,128]{1,0:T(8,128)(2,1)S(1)}, u32[]{:S(2)}, u32[]{:S(2)}) collective-permute-start(bf16[528,128]{1,0:T(8,128)(2,1)} %pad_maximum_fusion.2), channel_id=1, source_target_pairs={{0,24},{4,28},{8,16},{12,20},{16,8},{20,12},{24,0},{28,4},{1,25},{... | collective-permute-start | bytes 405512 | tf_op jit(solution)/shard_map/ppermute | solution.py:20
  16.9 11.1 %collective-permute-done.3 = bf16[528,128]{1,0:T(8,128)(2,1)S(1)} collective-permute-done((bf16[528,128]{1,0:T(8,128)(2,1)}, bf16[528,128]{1,0:T(8,128)(2,1)S(1)}, u32[]{:S(2)}, u32[]{:S(2)}) %collective-permute-start.3) | collective-permute-done | bytes 135200 | tf_op jit(solution)/shard_map/ppermute | solution.py:20
  28.3 2.0 collective-permute-done.1
  32.2 1.7 collective-permute-start.11
  34.1 2.7 %collective-permute-done.4 = bf16[512,128]{1,0:T(8,128)(2,1)S(1)} collective-permute-done((bf16[512,128]{1,0:T(8,128)(2,1)S(1)}, bf16[512,128]{1,0:T(8,128)(2,1)S(1)}, u32[]{:S(2)}, u32[]{:S(2)}) %collective-permute-start.4) | collective-permute-done | bytes 131104 | tf_op jit(solution)/shard_map/ppermute | solution.py:20
  38.7 1.5 collective-permute-start.9
  40.6 2.6 %collective-permute-start.7 = (bf16[128,1024]{0,1:T(8,128)(2,1)S(1)}, bf16[128,1024]{0,1:T(8,128)(2,1)S(1)}, u32[]{:S(2)}, u32[]{:S(2)}) collective-permute-start(bf16[128,1024]{0,1:T(8,128)(2,1)S(1)} %pad_maximum_fusion), channel_id=1, source_target_pairs={{0,20},{4,16},{8,28},{12,24},{16,4},{20,0},{24,12},{28,8},{1,21},{... | collective-permute-start | bytes 786440 | tf_op jit(solution)/shard_map/ppermute | solution.py:20
  43.5 1.5 collective-permute-start.5
  45.3 17.6 %collective-permute-done.7 = bf16[128,1024]{0,1:T(8,128)(2,1)S(1)} collective-permute-done((bf16[128,1024]{0,1:T(8,128)(2,1)S(1)}, bf16[128,1024]{0,1:T(8,128)(2,1)S(1)}, u32[]{:S(2)}, u32[]{:S(2)}) %collective-permute-start.7) | collective-permute-done | bytes 262176 | tf_op jit(solution)/shard_map/ppermute | solution.py:20
  63.0 3.5 %collective-permute-done.6 = bf16[128,1024]{0,1:T(8,128)(2,1)S(1)} collective-permute-done((bf16[128,1024]{0,1:T(8,128)(2,1)S(1)}, bf16[128,1024]{0,1:T(8,128)(2,1)S(1)}, u32[]{:S(2)}, u32[]{:S(2)}) %collective-permute-start.6) | collective-permute-done | bytes 262176 | tf_op jit(solution)/shard_map/ppermute | solution.py:20
  67.1 2.4 %fusion.6 = bf16[512,1024]{1,0:T(8,128)(2,1)S(1)} fusion(bf16[512,1024]{1,0:T(8,128)(2,1)S(1)} %bitcast.119, bf16[512,512]{1,0:T(8,128)(2,1)} %collective-permute-done.11, bf16[512,512]{1,0:T(8,128)(2,1)} %collective-permute-done.10, bf16[1024,512]{1,0:T(8,128)(2,1)S(1)} %copy-done.2), kind=kOutput, calls=%fused_computation.6 | convolution fusion | flops 1080557568 | bytes 4194304 | tf_op jit(solution)/shard_map/dot_general | solution.py:24
  69.7 1.8 collective-permute-done.12
  72.6 7.7 %collective-permute-done.13 = bf16[128,1024]{1,0:T(8,128)(2,1)S(1)} collective-permute-done((bf16[128,1024]{1,0:T(8,128)(2,1)S(1)}, bf16[128,1024]{1,0:T(8,128)(2,1)S(1)}, u32[]{:S(2)}, u32[]{:S(2)}) %collective-permute-start.13) | collective-permute-done | bytes 262176 | tf_op jit(solution)/shard_map/ppermute | solution.py:20
  80.3 1.6 collective-permute-start.14
  81.9 2.9 %collective-permute-start.15 = (bf16[32,1024]{1,0:T(8,128)(2,1)S(1)}, bf16[32,1024]{1,0:T(8,128)(2,1)S(1)}, u32[]{:S(2)}, u32[]{:S(2)}) collective-permute-start(bf16[32,1024]{1,0:T(8,128)(2,1)S(1)} %get-tuple-element.117), channel_id=1, source_target_pairs={{0,16},{4,20},{8,24},{12,28},{16,0},{20,4},{24,8},{28,12},{1,17},{... | collective-permute-start | bytes 196616 | tf_op jit(solution)/shard_map/ppermute | solution.py:20
  84.8 4.5 %collective-permute-done.15 = bf16[32,1024]{1,0:T(8,128)(2,1)S(1)} collective-permute-done((bf16[32,1024]{1,0:T(8,128)(2,1)S(1)}, bf16[32,1024]{1,0:T(8,128)(2,1)S(1)}, u32[]{:S(2)}, u32[]{:S(2)}) %collective-permute-start.15) | collective-permute-done | bytes 65568 | tf_op jit(solution)/shard_map/ppermute | solution.py:20
  90.3 1.7 collective-permute-start.17
  92.0 1.8 collective-permute-start.22
  93.8 7.2 %collective-permute-done.17.refs_0_ = bf16[32,4224]{1,0:T(8,128)(2,1)S(1)} collective-permute-done((bf16[32,4224]{1,0:T(8,128)(2,1)S(1)}, bf16[32,4224]{1,0:T(8,128)(2,1)S(1)}, u32[]{:S(2)}, u32[]{:S(2)}) %collective-permute-start.17) | collective-permute-done | bytes 270368 | tf_op jit(solution)/shard_map/ppermute | solution.py:20
  100.9 2.1 collective-permute-start.20
  103.1 1.5 collective-permute-start.18
  104.7 5.0 %collective-permute-done.20.refs_3_ = bf16[32,4224]{1,0:T(8,128)(2,1)S(1)} collective-permute-done((bf16[32,4224]{1,0:T(8,128)(2,1)S(1)}, bf16[32,4224]{1,0:T(8,128)(2,1)S(1)}, u32[]{:S(2)}, u32[]{:S(2)}) %collective-permute-start.20) | collective-permute-done | bytes 270368 | tf_op jit(solution)/shard_map/ppermute | solution.py:305
  109.7 2.8 %collective-permute-done.19.refs_2_ = bf16[32,4224]{1,0:T(8,128)(2,1)S(1)} collective-permute-done((bf16[32,4224]{1,0:T(8,128)(2,1)S(1)}, bf16[32,4224]{1,0:T(8,128)(2,1)S(1)}, u32[]{:S(2)}, u32[]{:S(2)}) %collective-permute-start.19) | collective-permute-done | bytes 270368 | tf_op jit(solution)/shard_map/ppermute | solution.py:20
  113.9 1.4 collective-permute-start.26
  116.0 1.5 collective-permute-start.24
  117.4 6.7 %collective-permute-done.26.refs_3_ = bf16[32,4224]{1,0:T(8,128)(2,1)S(1)} collective-permute-done((bf16[32,4224]{1,0:T(8,128)(2,1)S(1)}, bf16[32,4224]{1,0:T(8,128)(2,1)S(1)}, u32[]{:S(2)}, u32[]{:S(2)}) %collective-permute-start.26) | collective-permute-done | bytes 270368 | tf_op jit(solution)/shard_map/ppermute | solution.py:305
  124.2 5.3 %collective-permute-done.25.refs_2_ = bf16[32,4224]{1,0:T(8,128)(2,1)S(1)} collective-permute-done((bf16[32,4224]{1,0:T(8,128)(2,1)S(1)}, bf16[32,4224]{1,0:T(8,128)(2,1)S(1)}, u32[]{:S(2)}, u32[]{:S(2)}) %collective-permute-start.25) | collective-permute-done | bytes 270368 | tf_op jit(solution)/shard_map/ppermute | solution.py:20
  131.7 1.5 collective-permute-start.28
  133.2 10.2 %shard_map.164 = (bf16[128,4096]{1,0:T(8,128)(2,1)S(1)}, bf16[128,4096]{1,0:T(8,128)(2,1)S(1)}) custom-call(bf16[128,4224]{1,0:T(8,128)(2,1)S(1)} %shard_map.163.own, bf16[128,4224]{1,0:T(8,128)(2,1)S(1)} %collective-permute-done.21.mate, bf16[4096,896]{1,0:T(8,128)(2,1)} %bitcast.106, bf16[4096,896]{1,0:T(8,128)(2,1)} %bitcast.110, ...), custom_call_target="tpu_custom_call" | custom-call | flops 5637144576 | bytes 30408704 | tf_op jit(solution)/shard_map/pallas_call | solution.py:277
  143.4 1.8 collective-permute-done.29.refs_2_
  147.9 1.5 collective-permute-start.33
  149.4 10.2 %shard_map.166 = (bf16[128,4096]{1,0:T(8,128)(2,1)S(1)}, bf16[128,4096]{1,0:T(8,128)(2,1)S(1)}) custom-call(bf16[128,4224]{1,0:T(8,128)(2,1)S(1)} %shard_map.165.own, bf16[128,4224]{1,0:T(8,128)(2,1)S(1)} %collective-permute-done.27.mate, bf16[4096,896]{1,0:T(8,128)(2,1)} %bitcast.107, bf16[4096,896]{1,0:T(8,128)(2,1)} %bitcast.111, ...), custom_call_target="tpu_custom_call" | custom-call | flops 5637144576 | bytes 30408704 | tf_op jit(solution)/shard_map/pallas_call | solution.py:277
  162.0 1.4 collective-permute-start.39
  164.1 1.5 collective-permute-start.37
  165.5 10.2 %shard_map.168 = (bf16[128,4096]{1,0:T(8,128)(2,1)S(1)}, bf16[128,4096]{1,0:T(8,128)(2,1)S(1)}) custom-call(bf16[128,4224]{1,0:T(8,128)(2,1)S(1)} %shard_map.167.own, bf16[128,4224]{1,0:T(8,128)(2,1)S(1)} %collective-permute-done.32.mate, bf16[4096,896]{1,0:T(8,128)(2,1)} %bitcast.108, bf16[4096,896]{1,0:T(8,128)(2,1)} %bitcast.112, ...), custom_call_target="tpu_custom_call" | custom-call | flops 5637144576 | bytes 30408704 | tf_op jit(solution)/shard_map/pallas_call | solution.py:277
  177.1 1.4 collective-permute-start.44
  179.2 1.5 collective-permute-start.42
  180.6 10.2 %shard_map.170 = (bf16[128,4096]{1,0:T(8,128)(2,1)S(1)}, bf16[128,4096]{1,0:T(8,128)(2,1)S(1)}) custom-call(bf16[128,4224]{1,0:T(8,128)(2,1)S(1)} %shard_map.169.own, bf16[128,4224]{1,0:T(8,128)(2,1)S(1)} %collective-permute-done.40.mate, bf16[4096,896]{1,0:T(8,128)(2,1)} %bitcast.109, bf16[4096,896]{1,0:T(8,128)(2,1)} %bitcast.113, ...), custom_call_target="tpu_custom_call" | custom-call | flops 5637144576 | bytes 30408704 | tf_op jit(solution)/shard_map/pallas_call | solution.py:277
  190.9 1.5 collective-permute-done.43
  193.5 1.5 collective-permute-start.52
  196.6 4.3 %collective-permute-done.53 = bf16[32,4096]{1,0:T(8,128)(2,1)S(1)} collective-permute-done((bf16[32,4096]{1,0:T(8,128)(2,1)S(1)}, bf16[32,4096]{1,0:T(8,128)(2,1)S(1)}, u32[]{:S(2)}, u32[]{:S(2)}) %collective-permute-start.53) | collective-permute-done | bytes 262176 | tf_op jit(solution)/shard_map/ppermute | solution.py:20
  202.1 4.9 %collective-permute-done.52 = bf16[32,4096]{1,0:T(8,128)(2,1)S(1)} collective-permute-done((bf16[32,4096]{1,0:T(8,128)(2,1)S(1)}, bf16[32,4096]{1,0:T(8,128)(2,1)S(1)}, u32[]{:S(2)}, u32[]{:S(2)}) %collective-permute-start.52) | collective-permute-done | bytes 262176 | tf_op jit(solution)/shard_map/ppermute | solution.py:305
  208.5 5.5 %collective-permute-start.54 = (bf16[32,4096]{1,0:T(8,128)(2,1)S(1)}, bf16[32,4096]{1,0:T(8,128)(2,1)S(1)}, u32[]{:S(2)}, u32[]{:S(2)}) collective-permute-start(bf16[32,4096]{1,0:T(8,128)(2,1)S(1)} %add_convert_fusion.2), channel_id=1, source_target_pairs={{0,16},{4,20},{8,24},{12,28},{16,0},{20,4},{24,8},{28,12},{1,17},{... | collective-permute-start | bytes 786440 | tf_op jit(solution)/shard_map/ppermute | solution.py:20
  215.5 1.5 collective-permute-start.48
  217.8 5.8 %collective-permute-done.54 = bf16[32,4096]{1,0:T(8,128)(2,1)S(1)} collective-permute-done((bf16[32,4096]{1,0:T(8,128)(2,1)S(1)}, bf16[32,4096]{1,0:T(8,128)(2,1)S(1)}, u32[]{:S(2)}, u32[]{:S(2)}) %collective-permute-start.54) | collective-permute-done | bytes 262176 | tf_op jit(solution)/shard_map/ppermute | solution.py:20
  223.6 2.6 %collective-permute-done.48 = bf16[32,4096]{1,0:T(8,128)(2,1)S(1)} collective-permute-done((bf16[32,4096]{1,0:T(8,128)(2,1)S(1)}, bf16[32,4096]{1,0:T(8,128)(2,1)S(1)}, u32[]{:S(2)}, u32[]{:S(2)}) %collective-permute-start.48) | collective-permute-done | bytes 262176 | tf_op jit(solution)/shard_map/ppermute | solution.py:305
  (206 shorter events, 38.4 us)
Async XLA Ops:
  8.0 59.0 %collective-permute-start.10 = (bf16[512,512]{1,0:T(8,128)(2,1)}, bf16[512,512]{1,0:T(8,128)(2,1)}, u32[]{:S(2)}, u32[]{:S(2)}) collective-permute-start(bf16[512,512]{1,0:T(8,128)(2,1)} %get-tuple-element.114), channel_id=1, source_target_pairs={{0,8},{4,12},{8,0},{12,4},{16,24},{20,28},{24,16},{28,20},{1,9},{5... | collective-permute-start | bytes 1572872 | tf_op jit(solution)/shard_map/ppermute | solution.py:20
  12.3 15.7 %collective-permute-start.3 = (bf16[528,128]{1,0:T(8,128)(2,1)}, bf16[528,128]{1,0:T(8,128)(2,1)S(1)}, u32[]{:S(2)}, u32[]{:S(2)}) collective-permute-start(bf16[528,128]{1,0:T(8,128)(2,1)} %pad_maximum_fusion.2), channel_id=1, source_target_pairs={{0,24},{4,28},{8,16},{12,20},{16,8},{20,12},{24,0},{28,4},{1,25},{... | collective-permute-start | bytes 405512 | tf_op jit(solution)/shard_map/ppermute | solution.py:20
  15.8 12.2 %collective-permute-start.2 = (bf16[528,128]{1,0:T(8,128)(2,1)}, bf16[528,128]{1,0:T(8,128)(2,1)S(1)}, u32[]{:S(2)}, u32[]{:S(2)}) collective-permute-start(bf16[528,128]{1,0:T(8,128)(2,1)} %pad_maximum_fusion.2), channel_id=1, source_target_pairs={{0,16},{4,20},{8,24},{12,28},{16,0},{20,4},{24,8},{28,12},{1,17},{... | collective-permute-start | bytes 405512 | tf_op jit(solution)/shard_map/ppermute | solution.py:20
  15.9 14.5 %collective-permute-start.1 = (bf16[528,128]{1,0:T(8,128)(2,1)}, bf16[528,128]{1,0:T(8,128)(2,1)S(1)}, u32[]{:S(2)}, u32[]{:S(2)}) collective-permute-start(bf16[528,128]{1,0:T(8,128)(2,1)} %pad_maximum_fusion.2), channel_id=1, source_target_pairs={{0,8},{4,12},{8,0},{12,4},{16,24},{20,28},{24,16},{28,20},{1,9},{5... | collective-permute-start | bytes 405512 | tf_op jit(solution)/shard_map/ppermute | solution.py:20
  32.2 34.9 %collective-permute-start.11 = (bf16[512,512]{1,0:T(8,128)(2,1)}, bf16[512,512]{1,0:T(8,128)(2,1)}, u32[]{:S(2)}, u32[]{:S(2)}) collective-permute-start(bf16[512,512]{1,0:T(8,128)(2,1)} %get-tuple-element.52), channel_id=1, source_target_pairs={{0,8},{4,12},{8,0},{12,4},{16,24},{20,28},{24,16},{28,20},{1,9},{5... | collective-permute-start | bytes 1572872 | tf_op jit(solution)/shard_map/ppermute | solution.py:20
  40.6 22.3 %collective-permute-start.7 = (bf16[128,1024]{0,1:T(8,128)(2,1)S(1)}, bf16[128,1024]{0,1:T(8,128)(2,1)S(1)}, u32[]{:S(2)}, u32[]{:S(2)}) collective-permute-start(bf16[128,1024]{0,1:T(8,128)(2,1)S(1)} %pad_maximum_fusion), channel_id=1, source_target_pairs={{0,20},{4,16},{8,28},{12,24},{16,4},{20,0},{24,12},{28,8},{1,21},{... | collective-permute-start | bytes 786440 | tf_op jit(solution)/shard_map/ppermute | solution.py:20
  43.2 23.4 %collective-permute-start.6 = (bf16[128,1024]{0,1:T(8,128)(2,1)S(1)}, bf16[128,1024]{0,1:T(8,128)(2,1)S(1)}, u32[]{:S(2)}, u32[]{:S(2)}) collective-permute-start(bf16[128,1024]{0,1:T(8,128)(2,1)S(1)} %pad_maximum_fusion), channel_id=1, source_target_pairs={{0,16},{4,20},{8,24},{12,28},{16,0},{20,4},{24,8},{28,12},{1,17},{... | collective-permute-start | bytes 786440 | tf_op jit(solution)/shard_map/ppermute | solution.py:20
  43.5 23.2 %collective-permute-start.5 = (bf16[128,1024]{0,1:T(8,128)(2,1)S(1)}, bf16[128,1024]{0,1:T(8,128)(2,1)S(1)}, u32[]{:S(2)}, u32[]{:S(2)}) collective-permute-start(bf16[128,1024]{0,1:T(8,128)(2,1)S(1)} %pad_maximum_fusion), channel_id=1, source_target_pairs={{0,4},{4,0},{8,12},{12,8},{16,20},{20,16},{24,28},{28,24},{1,5},{5... | collective-permute-start | bytes 786440 | tf_op jit(solution)/shard_map/ppermute | solution.py:20
  71.8 8.4 %collective-permute-start.13 = (bf16[128,1024]{1,0:T(8,128)(2,1)S(1)}, bf16[128,1024]{1,0:T(8,128)(2,1)S(1)}, u32[]{:S(2)}, u32[]{:S(2)}) collective-permute-start(bf16[128,1024]{1,0:T(8,128)(2,1)S(1)} %slice.349), channel_id=1, source_target_pairs={{0,2},{1,3},{2,0},{3,1},{4,6},{5,7},{6,4},{7,5},{8,10},{9,11},{10,... | collective-permute-start | bytes 786440 | tf_op jit(solution)/shard_map/ppermute | solution.py:20
  81.9 7.6 %collective-permute-start.16 = (bf16[32,1024]{1,0:T(8,128)(2,1)S(1)}, bf16[32,1024]{1,0:T(8,128)(2,1)S(1)}, u32[]{:S(2)}, u32[]{:S(2)}) collective-permute-start(bf16[32,1024]{1,0:T(8,128)(2,1)S(1)} %get-tuple-element.116), channel_id=1, source_target_pairs={{0,20},{4,16},{8,28},{12,24},{16,4},{20,0},{24,12},{28,8},{1,21},{... | collective-permute-start | bytes 196616 | tf_op jit(solution)/shard_map/ppermute | solution.py:20
  90.3 10.6 %collective-permute-start.17 = (bf16[32,4224]{1,0:T(8,128)(2,1)S(1)}, bf16[32,4224]{1,0:T(8,128)(2,1)S(1)}, u32[]{:S(2)}, u32[]{:S(2)}) collective-permute-start(bf16[32,4224]{1,0:T(8,128)(2,1)S(1)} %concatenate.48.refs_0_), channel_id=1, source_target_pairs={{0,8},{4,12},{8,0},{12,4},{16,24},{20,28},{24,16},{28,20},{1,9},{5... | collective-permute-start | bytes 811016 | tf_op jit(solution)/shard_map/ppermute | solution.py:20
  92.0 12.7 %collective-permute-start.22 = (bf16[32,4224]{1,0:T(8,128)(2,1)S(1)}, bf16[32,4224]{1,0:T(8,128)(2,1)S(1)}, u32[]{:S(2)}, u32[]{:S(2)}) collective-permute-start(bf16[32,4224]{1,0:T(8,128)(2,1)S(1)} %concatenate.48.refs_0_), channel_id=1, source_target_pairs={{0,16},{4,20},{8,24},{12,28},{16,0},{20,4},{24,8},{28,12},{1,17},{... | collective-permute-start | bytes 811016 | tf_op jit(solution)/shard_map/ppermute | solution.py:20
  100.9 8.7 %collective-permute-start.20 = (bf16[32,4224]{1,0:T(8,128)(2,1)S(1)}, bf16[32,4224]{1,0:T(8,128)(2,1)S(1)}, u32[]{:S(2)}, u32[]{:S(2)}) collective-permute-start(bf16[32,4224]{1,0:T(8,128)(2,1)S(1)} %collective-permute-done.17.refs_0_), channel_id=1, source_target_pairs={{0,6},{1,7},{2,4},{3,5},{4,2},{5,3},{6,0},{7,1},{8,14},{9,15},{10,... | collective-permute-start | bytes 811016 | tf_op jit(solution)/shard_map/ppermute | solution.py:305
  103.1 9.4 %collective-permute-start.19 = (bf16[32,4224]{1,0:T(8,128)(2,1)S(1)}, bf16[32,4224]{1,0:T(8,128)(2,1)S(1)}, u32[]{:S(2)}, u32[]{:S(2)}) collective-permute-start(bf16[32,4224]{1,0:T(8,128)(2,1)S(1)} %collective-permute-done.17.refs_0_), channel_id=1, source_target_pairs={{0,4},{4,0},{8,12},{12,8},{16,20},{20,16},{24,28},{28,24},{1,5},{5... | collective-permute-start | bytes 811016 | tf_op jit(solution)/shard_map/ppermute | solution.py:20
  103.1 10.6 %collective-permute-start.18 = (bf16[32,4224]{1,0:T(8,128)(2,1)S(1)}, bf16[32,4224]{1,0:T(8,128)(2,1)S(1)}, u32[]{:S(2)}, u32[]{:S(2)}) collective-permute-start(bf16[32,4224]{1,0:T(8,128)(2,1)S(1)} %collective-permute-done.17.refs_0_), channel_id=1, source_target_pairs={{0,2},{1,3},{2,0},{3,1},{4,6},{5,7},{6,4},{7,5},{8,10},{9,11},{10,... | collective-permute-start | bytes 811016 | tf_op jit(solution)/shard_map/ppermute | solution.py:20
  104.7 9.2 %collective-permute-start.23 = (bf16[32,4224]{1,0:T(8,128)(2,1)S(1)}, bf16[32,4224]{1,0:T(8,128)(2,1)S(1)}, u32[]{:S(2)}, u32[]{:S(2)}) collective-permute-start(bf16[32,4224]{1,0:T(8,128)(2,1)S(1)} %collective-permute-done.22.refs_0_), channel_id=1, source_target_pairs={{0,8},{4,12},{8,0},{12,4},{16,24},{20,28},{24,16},{28,20},{1,9},{5... | collective-permute-start | bytes 811016 | tf_op jit(solution)/shard_map/ppermute | solution.py:20
  113.8 19.4 %collective-permute-start.21 = (bf16[128,4224]{1,0:T(8,128)(2,1)S(1)}, bf16[128,4224]{1,0:T(8,128)(2,1)S(1)}, u32[]{:S(2)}, u32[]{:S(2)}) collective-permute-start(bf16[128,4224]{1,0:T(8,128)(2,1)S(1)} %shard_map.163.own), channel_id=1, source_target_pairs={{0,1},{1,0},{2,3},{3,2},{4,5},{5,4},{6,7},{7,6},{8,9},{9,8},{10,11... | collective-permute-start | bytes 3244040 | tf_op jit(solution)/shard_map/ppermute | solution.py:20
  113.9 10.3 %collective-permute-start.26 = (bf16[32,4224]{1,0:T(8,128)(2,1)S(1)}, bf16[32,4224]{1,0:T(8,128)(2,1)S(1)}, u32[]{:S(2)}, u32[]{:S(2)}) collective-permute-start(bf16[32,4224]{1,0:T(8,128)(2,1)S(1)} %collective-permute-done.23.refs_0_), channel_id=1, source_target_pairs={{0,6},{1,7},{2,4},{3,5},{4,2},{5,3},{6,0},{7,1},{8,14},{9,15},{10,... | collective-permute-start | bytes 811016 | tf_op jit(solution)/shard_map/ppermute | solution.py:305
  115.3 14.1 %collective-permute-start.25 = (bf16[32,4224]{1,0:T(8,128)(2,1)S(1)}, bf16[32,4224]{1,0:T(8,128)(2,1)S(1)}, u32[]{:S(2)}, u32[]{:S(2)}) collective-permute-start(bf16[32,4224]{1,0:T(8,128)(2,1)S(1)} %collective-permute-done.23.refs_0_), channel_id=1, source_target_pairs={{0,4},{4,0},{8,12},{12,8},{16,20},{20,16},{24,28},{28,24},{1,5},{5... | collective-permute-start | bytes 811016 | tf_op jit(solution)/shard_map/ppermute | solution.py:20
  116.0 13.5 %collective-permute-start.24 = (bf16[32,4224]{1,0:T(8,128)(2,1)S(1)}, bf16[32,4224]{1,0:T(8,128)(2,1)S(1)}, u32[]{:S(2)}, u32[]{:S(2)}) collective-permute-start(bf16[32,4224]{1,0:T(8,128)(2,1)S(1)} %collective-permute-done.23.refs_0_), channel_id=1, source_target_pairs={{0,2},{1,3},{2,0},{3,1},{4,6},{5,7},{6,4},{7,5},{8,10},{9,11},{10,... | collective-permute-start | bytes 811016 | tf_op jit(solution)/shard_map/ppermute | solution.py:20
  129.6 15.7 %collective-permute-start.27 = (bf16[128,4224]{1,0:T(8,128)(2,1)S(1)}, bf16[128,4224]{1,0:T(8,128)(2,1)S(1)}, u32[]{:S(2)}, u32[]{:S(2)}) collective-permute-start(bf16[128,4224]{1,0:T(8,128)(2,1)S(1)} %shard_map.165.own), channel_id=1, source_target_pairs={{0,1},{1,0},{2,3},{3,2},{4,5},{5,4},{6,7},{7,6},{8,9},{9,8},{10,11... | collective-permute-start | bytes 3244040 | tf_op jit(solution)/shard_map/ppermute | solution.py:20
  129.7 13.8 %collective-permute-start.30 = (bf16[32,4224]{1,0:T(8,128)(2,1)S(1)}, bf16[32,4224]{1,0:T(8,128)(2,1)S(1)}, u32[]{:S(2)}, u32[]{:S(2)}) collective-permute-start(bf16[32,4224]{1,0:T(8,128)(2,1)S(1)} %collective-permute-done.22.refs_0_), channel_id=1, source_target_pairs={{0,6},{1,7},{2,4},{3,5},{4,2},{5,3},{6,0},{7,1},{8,14},{9,15},{10,... | collective-permute-start | bytes 811016 | tf_op jit(solution)/shard_map/ppermute | solution.py:305
  131.1 14.1 %collective-permute-start.29 = (bf16[32,4224]{1,0:T(8,128)(2,1)S(1)}, bf16[32,4224]{1,0:T(8,128)(2,1)S(1)}, u32[]{:S(2)}, u32[]{:S(2)}) collective-permute-start(bf16[32,4224]{1,0:T(8,128)(2,1)S(1)} %collective-permute-done.22.refs_0_), channel_id=1, source_target_pairs={{0,4},{4,0},{8,12},{12,8},{16,20},{20,16},{24,28},{28,24},{1,5},{5... | collective-permute-start | bytes 811016 | tf_op jit(solution)/shard_map/ppermute | solution.py:20
  131.7 13.5 %collective-permute-start.28 = (bf16[32,4224]{1,0:T(8,128)(2,1)S(1)}, bf16[32,4224]{1,0:T(8,128)(2,1)S(1)}, u32[]{:S(2)}, u32[]{:S(2)}) collective-permute-start(bf16[32,4224]{1,0:T(8,128)(2,1)S(1)} %collective-permute-done.22.refs_0_), channel_id=1, source_target_pairs={{0,2},{1,3},{2,0},{3,1},{4,6},{5,7},{6,4},{7,5},{8,10},{9,11},{10,... | collective-permute-start | bytes 811016 | tf_op jit(solution)/shard_map/ppermute | solution.py:20
  145.3 15.7 %collective-permute-start.32 = (bf16[128,4224]{1,0:T(8,128)(2,1)S(1)}, bf16[128,4224]{1,0:T(8,128)(2,1)S(1)}, u32[]{:S(2)}, u32[]{:S(2)}) collective-permute-start(bf16[128,4224]{1,0:T(8,128)(2,1)S(1)} %shard_map.167.own), channel_id=1, source_target_pairs={{0,1},{1,0},{2,3},{3,2},{4,5},{5,4},{6,7},{7,6},{8,9},{9,8},{10,11... | collective-permute-start | bytes 3244040 | tf_op jit(solution)/shard_map/ppermute | solution.py:20
  145.4 15.6 %collective-permute-start.31 = (bf16[128,4096]{1,0:T(8,128)(2,1)S(1)}, bf16[128,4096]{1,0:T(8,128)(2,1)S(1)}, u32[]{:S(2)}, u32[]{:S(2)}) collective-permute-start(bf16[128,4096]{1,0:T(8,128)(2,1)S(1)} %get-tuple-element.60), channel_id=1, source_target_pairs={{0,1},{1,0},{2,3},{3,2},{4,5},{5,4},{6,7},{7,6},{8,9},{9,8},{10,11... | collective-permute-start | bytes 3145736 | tf_op jit(solution)/shard_map/ppermute | solution.py:20
  145.9 13.7 %collective-permute-start.35 = (bf16[32,4224]{1,0:T(8,128)(2,1)S(1)}, bf16[32,4224]{1,0:T(8,128)(2,1)S(1)}, u32[]{:S(2)}, u32[]{:S(2)}) collective-permute-start(bf16[32,4224]{1,0:T(8,128)(2,1)S(1)} %concatenate.48.refs_0_), channel_id=1, source_target_pairs={{0,6},{1,7},{2,4},{3,5},{4,2},{5,3},{6,0},{7,1},{8,14},{9,15},{10,... | collective-permute-start | bytes 811016 | tf_op jit(solution)/shard_map/ppermute | solution.py:305
  147.3 13.8 %collective-permute-start.34 = (bf16[32,4224]{1,0:T(8,128)(2,1)S(1)}, bf16[32,4224]{1,0:T(8,128)(2,1)S(1)}, u32[]{:S(2)}, u32[]{:S(2)}) collective-permute-start(bf16[32,4224]{1,0:T(8,128)(2,1)S(1)} %concatenate.48.refs_0_), channel_id=1, source_target_pairs={{0,4},{4,0},{8,12},{12,8},{16,20},{20,16},{24,28},{28,24},{1,5},{5... | collective-permute-start | bytes 811016 | tf_op jit(solution)/shard_map/ppermute | solution.py:20
  147.9 13.1 %collective-permute-start.33 = (bf16[32,4224]{1,0:T(8,128)(2,1)S(1)}, bf16[32,4224]{1,0:T(8,128)(2,1)S(1)}, u32[]{:S(2)}, u32[]{:S(2)}) collective-permute-start(bf16[32,4224]{1,0:T(8,128)(2,1)S(1)} %concatenate.48.refs_0_), channel_id=1, source_target_pairs={{0,2},{1,3},{2,0},{3,1},{4,6},{5,7},{6,4},{7,5},{8,10},{9,11},{10,... | collective-permute-start | bytes 811016 | tf_op jit(solution)/shard_map/ppermute | solution.py:20
  161.1 15.7 %collective-permute-start.36 = (bf16[128,4096]{1,0:T(8,128)(2,1)S(1)}, bf16[128,4096]{1,0:T(8,128)(2,1)S(1)}, u32[]{:S(2)}, u32[]{:S(2)}) collective-permute-start(bf16[128,4096]{1,0:T(8,128)(2,1)S(1)} %get-tuple-element.68), channel_id=1, source_target_pairs={{0,1},{1,0},{2,3},{3,2},{4,5},{5,4},{6,7},{7,6},{8,9},{9,8},{10,11... | collective-permute-start | bytes 3145736 | tf_op jit(solution)/shard_map/ppermute | solution.py:20
  161.2 15.6 %collective-permute-start.40 = (bf16[128,4224]{1,0:T(8,128)(2,1)S(1)}, bf16[128,4224]{1,0:T(8,128)(2,1)S(1)}, u32[]{:S(2)}, u32[]{:S(2)}) collective-permute-start(bf16[128,4224]{1,0:T(8,128)(2,1)S(1)} %shard_map.169.own), channel_id=1, source_target_pairs={{0,1},{1,0},{2,3},{3,2},{4,5},{5,4},{6,7},{7,6},{8,9},{9,8},{10,11... | collective-permute-start | bytes 3244040 | tf_op jit(solution)/shard_map/ppermute | solution.py:20
  162.0 13.8 %collective-permute-start.39 = (bf16[32,4096]{1,0:T(8,128)(2,1)S(1)}, bf16[32,4096]{1,0:T(8,128)(2,1)S(1)}, u32[]{:S(2)}, u32[]{:S(2)}) collective-permute-start(bf16[32,4096]{1,0:T(8,128)(2,1)S(1)} %get-tuple-element.111), channel_id=1, source_target_pairs={{0,6},{1,7},{2,4},{3,5},{4,2},{5,3},{6,0},{7,1},{8,14},{9,15},{10,... | collective-permute-start | bytes 786440 | tf_op jit(solution)/shard_map/ppermute | solution.py:305
  163.4 13.4 %collective-permute-start.38 = (bf16[32,4096]{1,0:T(8,128)(2,1)S(1)}, bf16[32,4096]{1,0:T(8,128)(2,1)S(1)}, u32[]{:S(2)}, u32[]{:S(2)}) collective-permute-start(bf16[32,4096]{1,0:T(8,128)(2,1)S(1)} %get-tuple-element.112), channel_id=1, source_target_pairs={{0,4},{4,0},{8,12},{12,8},{16,20},{20,16},{24,28},{28,24},{1,5},{5... | collective-permute-start | bytes 786440 | tf_op jit(solution)/shard_map/ppermute | solution.py:20
  164.1 12.7 %collective-permute-start.37 = (bf16[32,4096]{1,0:T(8,128)(2,1)S(1)}, bf16[32,4096]{1,0:T(8,128)(2,1)S(1)}, u32[]{:S(2)}, u32[]{:S(2)}) collective-permute-start(bf16[32,4096]{1,0:T(8,128)(2,1)S(1)} %get-tuple-element.113), channel_id=1, source_target_pairs={{0,2},{1,3},{2,0},{3,1},{4,6},{5,7},{6,4},{7,5},{8,10},{9,11},{10,... | collective-permute-start | bytes 786440 | tf_op jit(solution)/shard_map/ppermute | solution.py:20
  176.8 15.6 %collective-permute-start.41 = (bf16[128,4096]{1,0:T(8,128)(2,1)S(1)}, bf16[128,4096]{1,0:T(8,128)(2,1)S(1)}, u32[]{:S(2)}, u32[]{:S(2)}) collective-permute-start(bf16[128,4096]{1,0:T(8,128)(2,1)S(1)} %get-tuple-element.78), channel_id=1, source_target_pairs={{0,1},{1,0},{2,3},{3,2},{4,5},{5,4},{6,7},{7,6},{8,9},{9,8},{10,11... | collective-permute-start | bytes 3145736 | tf_op jit(solution)/shard_map/ppermute | solution.py:20
  177.1 13.8 %collective-permute-start.44 = (bf16[32,4096]{1,0:T(8,128)(2,1)S(1)}, bf16[32,4096]{1,0:T(8,128)(2,1)S(1)}, u32[]{:S(2)}, u32[]{:S(2)}) collective-permute-start(bf16[32,4096]{1,0:T(8,128)(2,1)S(1)} %get-tuple-element.108), channel_id=1, source_target_pairs={{0,6},{1,7},{2,4},{3,5},{4,2},{5,3},{6,0},{7,1},{8,14},{9,15},{10,... | collective-permute-start | bytes 786440 | tf_op jit(solution)/shard_map/ppermute | solution.py:305
  178.5 13.8 %collective-permute-start.43 = (bf16[32,4096]{1,0:T(8,128)(2,1)S(1)}, bf16[32,4096]{1,0:T(8,128)(2,1)S(1)}, u32[]{:S(2)}, u32[]{:S(2)}) collective-permute-start(bf16[32,4096]{1,0:T(8,128)(2,1)S(1)} %get-tuple-element.109), channel_id=1, source_target_pairs={{0,4},{4,0},{8,12},{12,8},{16,20},{20,16},{24,28},{28,24},{1,5},{5... | collective-permute-start | bytes 786440 | tf_op jit(solution)/shard_map/ppermute | solution.py:20
  179.2 13.2 %collective-permute-start.42 = (bf16[32,4096]{1,0:T(8,128)(2,1)S(1)}, bf16[32,4096]{1,0:T(8,128)(2,1)S(1)}, u32[]{:S(2)}, u32[]{:S(2)}) collective-permute-start(bf16[32,4096]{1,0:T(8,128)(2,1)S(1)} %get-tuple-element.110), channel_id=1, source_target_pairs={{0,2},{1,3},{2,0},{3,1},{4,6},{5,7},{6,4},{7,5},{8,10},{9,11},{10,... | collective-permute-start | bytes 786440 | tf_op jit(solution)/shard_map/ppermute | solution.py:20
  192.5 8.3 %collective-permute-start.53 = (bf16[32,4096]{1,0:T(8,128)(2,1)S(1)}, bf16[32,4096]{1,0:T(8,128)(2,1)S(1)}, u32[]{:S(2)}, u32[]{:S(2)}) collective-permute-start(bf16[32,4096]{1,0:T(8,128)(2,1)S(1)} %add_convert_fusion.3), channel_id=1, source_target_pairs={{0,8},{4,12},{8,0},{12,4},{16,24},{20,28},{24,16},{28,20},{1,9},{5... | collective-permute-start | bytes 786440 | tf_op jit(solution)/shard_map/ppermute | solution.py:20
  192.8 9.2 %collective-permute-start.50 = (bf16[32,4096]{1,0:T(8,128)(2,1)S(1)}, bf16[32,4096]{1,0:T(8,128)(2,1)S(1)}, u32[]{:S(2)}, u32[]{:S(2)}) collective-permute-start(bf16[32,4096]{1,0:T(8,128)(2,1)S(1)} %get-tuple-element.105), channel_id=1, source_target_pairs={{0,2},{1,3},{2,0},{3,1},{4,6},{5,7},{6,4},{7,5},{8,10},{9,11},{10,... | collective-permute-start | bytes 786440 | tf_op jit(solution)/shard_map/ppermute | solution.py:20
  193.5 13.4 %collective-permute-start.52 = (bf16[32,4096]{1,0:T(8,128)(2,1)S(1)}, bf16[32,4096]{1,0:T(8,128)(2,1)S(1)}, u32[]{:S(2)}, u32[]{:S(2)}) collective-permute-start(bf16[32,4096]{1,0:T(8,128)(2,1)S(1)} %get-tuple-element.106), channel_id=1, source_target_pairs={{0,6},{1,7},{2,4},{3,5},{4,2},{5,3},{6,0},{7,1},{8,14},{9,15},{10,... | collective-permute-start | bytes 786440 | tf_op jit(solution)/shard_map/ppermute | solution.py:305
  195.0 13.3 %collective-permute-start.51 = (bf16[32,4096]{1,0:T(8,128)(2,1)S(1)}, bf16[32,4096]{1,0:T(8,128)(2,1)S(1)}, u32[]{:S(2)}, u32[]{:S(2)}) collective-permute-start(bf16[32,4096]{1,0:T(8,128)(2,1)S(1)} %get-tuple-element.107), channel_id=1, source_target_pairs={{0,4},{4,0},{8,12},{12,8},{16,20},{20,16},{24,28},{28,24},{1,5},{5... | collective-permute-start | bytes 786440 | tf_op jit(solution)/shard_map/ppermute | solution.py:20
  196.4 17.6 %collective-permute-start.45 = (bf16[128,4096]{1,0:T(8,128)(2,1)S(1)}, bf16[128,4096]{1,0:T(8,128)(2,1)S(1)}, u32[]{:S(2)}, u32[]{:S(2)}) collective-permute-start(bf16[128,4096]{1,0:T(8,128)(2,1)S(1)} %get-tuple-element.82), channel_id=1, source_target_pairs={{0,1},{1,0},{2,3},{3,2},{4,5},{5,4},{6,7},{7,6},{8,9},{9,8},{10,11... | collective-permute-start | bytes 3145736 | tf_op jit(solution)/shard_map/ppermute | solution.py:20
  200.9 16.9 %collective-permute-start.49 = (bf16[32,4096]{1,0:T(8,128)(2,1)S(1)}, bf16[32,4096]{1,0:T(8,128)(2,1)S(1)}, u32[]{:S(2)}, u32[]{:S(2)}) collective-permute-start(bf16[32,4096]{1,0:T(8,128)(2,1)S(1)} %add_convert_fusion.7), channel_id=1, source_target_pairs={{0,8},{4,12},{8,0},{12,4},{16,24},{20,28},{24,16},{28,20},{1,9},{5... | collective-permute-start | bytes 786440 | tf_op jit(solution)/shard_map/ppermute | solution.py:20
  208.5 15.1 %collective-permute-start.54 = (bf16[32,4096]{1,0:T(8,128)(2,1)S(1)}, bf16[32,4096]{1,0:T(8,128)(2,1)S(1)}, u32[]{:S(2)}, u32[]{:S(2)}) collective-permute-start(bf16[32,4096]{1,0:T(8,128)(2,1)S(1)} %add_convert_fusion.2), channel_id=1, source_target_pairs={{0,16},{4,20},{8,24},{12,28},{16,0},{20,4},{24,8},{28,12},{1,17},{... | collective-permute-start | bytes 786440 | tf_op jit(solution)/shard_map/ppermute | solution.py:20
  214.2 9.4 %collective-permute-start.46 = (bf16[32,4096]{1,0:T(8,128)(2,1)S(1)}, bf16[32,4096]{1,0:T(8,128)(2,1)S(1)}, u32[]{:S(2)}, u32[]{:S(2)}) collective-permute-start(bf16[32,4096]{1,0:T(8,128)(2,1)S(1)} %get-tuple-element.102), channel_id=1, source_target_pairs={{0,2},{1,3},{2,0},{3,1},{4,6},{5,7},{6,4},{7,5},{8,10},{9,11},{10,... | collective-permute-start | bytes 786440 | tf_op jit(solution)/shard_map/ppermute | solution.py:20
  215.5 10.7 %collective-permute-start.48 = (bf16[32,4096]{1,0:T(8,128)(2,1)S(1)}, bf16[32,4096]{1,0:T(8,128)(2,1)S(1)}, u32[]{:S(2)}, u32[]{:S(2)}) collective-permute-start(bf16[32,4096]{1,0:T(8,128)(2,1)S(1)} %get-tuple-element.103), channel_id=1, source_target_pairs={{0,6},{1,7},{2,4},{3,5},{4,2},{5,3},{6,0},{7,1},{8,14},{9,15},{10,... | collective-permute-start | bytes 786440 | tf_op jit(solution)/shard_map/ppermute | solution.py:305
  217.0 10.5 %collective-permute-start.47 = (bf16[32,4096]{1,0:T(8,128)(2,1)S(1)}, bf16[32,4096]{1,0:T(8,128)(2,1)S(1)}, u32[]{:S(2)}, u32[]{:S(2)}) collective-permute-start(bf16[32,4096]{1,0:T(8,128)(2,1)S(1)} %get-tuple-element.104), channel_id=1, source_target_pairs={{0,4},{4,0},{8,12},{12,8},{16,20},{20,16},{24,28},{28,24},{1,5},{5... | collective-permute-start | bytes 786440 | tf_op jit(solution)/shard_map/ppermute | solution.py:20
  (20 other events, 134.3 us)

commit v5 on v4

--- a/solution.py
+++ b/solution.py
@@ -137,17 +137,17 @@
     quarter = tok // n_exp
     both = jnp.concatenate([out_proj, neighbour_proj], axis=1)
     squares = jnp.sum(gated * gated, axis=1)
-    for flip in (1, 2):
-        squares = squares + swap(squares, "exp", flip)
-    own_squares = lax.dynamic_slice_in_dim(squares, me_exp * quarter, quarter, 0)
-    scale = lax.rsqrt(own_squares / (width * n_exp) + eps_norm)
-
     rows = (gated * norm_gain[None, :]).astype(BF)
     rel = [0, 2, 1, 3]
     pieces = [lax.dynamic_slice_in_dim(rows, (me_exp ^ q) * quarter, quarter, 0) for q in rel]
     own_rows = jnp.concatenate(pieces)
     group = [h + y for h in range(0, n_ctx, 4) for y in (0, 1)]
     arrived = [own_rows] + [swap(own_rows, "ctx", r) for r in group[1:]]
+    squares, arrived[1] = lax.optimization_barrier((squares, arrived[1]))
+    for flip in (1, 2):
+        squares = squares + swap(squares, "exp", flip)
+    own_squares = lax.dynamic_slice_in_dim(squares, me_exp * quarter, quarter, 0)
+    scale = lax.rsqrt(own_squares / (width * n_exp) + eps_norm)
     full = jnp.stack(arrived).reshape(len(group), n_exp, quarter, width)
     full = full.swapaxes(0, 1).reshape(-1, width)
     full, scale = lax.optimization_barrier((full, scale))
@@ -350,10 +350,10 @@
     lane = jnp.arange(LANES, dtype=jnp.int32)
     pick = (lane % (LANES // 2) == me_ctx // PAIR).astype(F32)[None, :]
 
-    cut = out_proj.shape[0] // 2
-    first_part = swap(out_proj[:cut], "ctx", 2)
-    gated, second_part = mixer_rows(
-        inputs, gate_input, b_proj, c_proj, step_size, decay_rate, skip_gain, start_state, out_proj[cut:]
+    cut = out_proj.shape[0] // 4
+    two_parts = (swap(out_proj[:cut], "ctx", 2), out_proj[cut:])
+    gated, (first_part, second_part) = mixer_rows(
+        inputs, gate_input, b_proj, c_proj, step_size, decay_rate, skip_gain, start_state, two_parts
     )
     neighbour_proj = jnp.concatenate([first_part, swap(second_part, "ctx", 2)])
     mixed, scale = project_rows(gated, norm_gain, out_proj, neighbour_proj)
@@ -363,49 +363,64 @@
     moe_in = (hidden * moe_scale * moe_gain[None, :]).astype(BF)
 
     payload = jnp.concatenate([moe_in, weights_high, weights_low], axis=1)
-    order = [1] + list(range(pairs - 1, 1, -1)) + [0]
+    order = [0] + list(range(2, pairs)) + [1]
     count = len(order)
     by_distance = [payload]
     for d in range(1, pairs):
         low = d & -d
         by_distance.append(swap(by_distance[d - low], "ctx", 2 * low))
     planes = [by_distance[d] for d in order]
-    near, rows, results, got, far_got = [], [], [], [], []
-
-    def rest(stage):
-        if 0 <= stage - 1 < count:
-            got.append(swap(results[stage - 1][1], "exp", 1))
-        if 0 <= stage - 2 < count:
-            far_got.append(plane_sums(results[stage - 2][0], got[stage - 2]))
-
-    def arrive(stage):
-        if stage + 2 < count:
-            piece = planes[stage + 2]
-            near.append((swap(piece, "exp", 2), swap(piece, "ctx", 1), across(piece)))
-        if 0 <= stage + 1 < count:
-            own = pack((planes[stage + 1], *near[stage + 1]))
+    near, rows, results, got, far_got, parts = [], [], [], [], [], []
+
+    def neighbours(piece):
+        return swap(piece, "exp", 2), swap(piece, "ctx", 1), across(piece)
+
+    def core(k):
+        if 0 <= k < count:
+            got.append(swap(results[k][1], "exp", 1))
+
+    def spread(k):
+        if 0 <= k < count:
+            far_got.append(plane_sums(results[k][0], got[k]))
+
+    def back(k):
+        if 0 <= k < count:
+            part = summed(results[k][0], got[k], 0, quarter)
+            for v in far_got[k]:
+                part = part + v.astype(F32)
+            d = order[k]
+            parts.append(part if d == 0 else swap(part.astype(BF), "ctx", 2 * d))
+
+    def bring(k):
+        if k < count:
+            near.append(neighbours(planes[k]))
+
+    def ready(k):
+        if k < count:
+            own = pack((planes[k], *near[k]))
             rows.append((own, swap(own, "exp", 1)))
 
-    for stage in (-2, -1):
-        arrive(stage)
+    bring(0)
+    near[0], planes[1] = together(near[0], planes[1])
     for i in range(count):
-        rest(i)
-        arrive(i)
-        beside = (got[-1:], far_got[-1:], rows[i + 1 :], near[i + 2 :])
+        ready(i)
+        core(i - 1)
+        spread(i - 2)
+        back(i - 3)
+        bring(i + 1)
+        beside = (got[-1:], far_got[-1:], parts[-1:], near[i + 1 :], planes[i + 2 :])
         results.append(experts(*rows[i], w_gate[0], w_up[0], w_down[0], pick))
         results[i], beside = together(results[i], beside)
-        got[-1:], far_got[-1:], rows[i + 1 :], near[i + 2 :] = beside
-    for i in range(count, count + 2):
-        rest(i)
-    parts = [None] * pairs
-    for i, d in enumerate(order):
-        parts[d] = summed(results[i][0], got[i], 0, quarter)
-        for v in far_got[i]:
-            parts[d] = parts[d] + v.astype(F32)
-    for d in sorted(range(1, pairs), key=lambda d: (-bin(d).count("1"), d)):
-        low = d & -d
-        parts[d - low] = parts[d - low] + swap(parts[d].astype(BF), "ctx", 2 * low).astype(F32)
-    return (hidden + parts[0]).astype(BF)
+        got[-1:], far_got[-1:], parts[-1:], near[i + 1 :], planes[i + 2 :] = beside
+    core(count - 1)
+    spread(count - 2)
+    back(count - 3)
+    spread(count - 1)
+    back(count - 2)
+    back(count - 1)
+    for part in parts:
+        hidden = hidden + part.astype(F32)
+    return hidden.astype(BF)
 
 
 def solution(mesh):

time: 229 us -> 218 us (0.952)
  waiting for transfers between devices: 107 us -> 91 us
  starting transfers between devices: 61.5 us -> 65.5 us
    ppermute x8, waiting for transfers between devices: 19.2 us -> 7.62 us  [across(): return lax.ppermute(x, ('ctx', 'exp'), pairs)]
    ppermute x8, starting transfers between devices: 12.3 us -> 17.5 us  [across(): return lax.ppermute(x, ('ctx', 'exp'), pairs)]
    ppermute x47, waiting for transfers between devices: 87.9 us -> 83.4 us  [swap(): return lax.ppermute(x, axis, [(i, i ^ flip) for i in range(size)])]
  transfers between devices with their start and end apart: 55 -> 55, of which waited for: 28 -> 26; matrix products, arithmetic and copies ran while one was open for 4% -> 5% of each run, Pallas kernels for 18% -> 19%
where the time goes in v5:
time: 218 us; the launch traced here: 217 us
  waiting for transfers between devices  91 us (42%)
  starting transfers between devices  65.5 us (30%)
  Pallas kernels  41.2 us (19%)
  other arithmetic  8.59 us (4%)
  local copies, waits for them, and re-layouts  5.7 us (3%)
  matrix products  4.54 us (2%)
    ppermute x47, waiting for transfers between devices, swap(): return lax.ppermute(x, axis, [(i, i ^ flip) for i in range(size)])  83.4 us
    ppermute x47, starting transfers between devices, swap(): return lax.ppermute(x, axis, [(i, i ^ flip) for i in range(size)])  47.9 us
    pallas_call x4, Pallas kernels, experts(): pl.pallas_call(expert_kernel, out_shape=(out, out), in_specs=[anywhere] *...  40.9 us
    ppermute x8, starting transfers between devices, across(): return lax.ppermute(x, ('ctx', 'exp'), pairs)  17.5 us
    ppermute x8, waiting for transfers between devices, across(): return lax.ppermute(x, ('ctx', 'exp'), pairs)  7.62 us
  transfers between devices with their start and end apart: 55, of which 26 were waited for; matrix products, arithmetic and copies ran while one was open for 5% of the time, Pallas kernels for 19%

profile of v5, /device:TPU:0, one launch (start us, length us, event | category | flops | bytes accessed | tf_op | source)
XLA Modules:
  0.0 217.2 jit_solution(6034545365133192857)
XLA Ops:
  3.9 3.0 %collective-permute-start = (bf16[528,128]{1,0:T(8,128)(2,1)S(1)}, bf16[528,128]{1,0:T(8,128)(2,1)S(1)}, u32[]{:S(2)}, u32[]{:S(2)}) collective-permute-start(bf16[528,128]{1,0:T(8,128)(2,1)S(1)} %pad_maximum_fusion.1), channel_id=1, source_target_pairs={{0,4},{4,0},{8,12},{12,8},{16,20},{20,16},{24,28},{28,24},{1,5},{5... | collective-permute-start | bytes 405512 | tf_op jit(solution)/shard_map/ppermute | solution.py:20
  7.7 1.6 collective-permute-start.4
  9.5 1.4 fusion.9
  13.6 2.6 %collective-permute-start.2 = (bf16[528,128]{1,0:T(8,128)(2,1)S(1)}, bf16[528,128]{1,0:T(8,128)(2,1)S(1)}, u32[]{:S(2)}, u32[]{:S(2)}) collective-permute-start(bf16[528,128]{1,0:T(8,128)(2,1)S(1)} %pad_maximum_fusion.2), channel_id=1, source_target_pairs={{0,16},{4,20},{8,24},{12,28},{16,0},{20,4},{24,8},{28,12},{1,17},{... | collective-permute-start | bytes 405512 | tf_op jit(solution)/shard_map/ppermute | solution.py:20
  17.7 3.7 %collective-permute-done.1 = bf16[528,128]{1,0:T(8,128)(2,1)S(1)} collective-permute-done((bf16[528,128]{1,0:T(8,128)(2,1)S(1)}, bf16[528,128]{1,0:T(8,128)(2,1)S(1)}, u32[]{:S(2)}, u32[]{:S(2)}) %collective-permute-start.1) | collective-permute-done | bytes 135200 | tf_op jit(solution)/shard_map/ppermute | solution.py:20
  22.3 4.2 %collective-permute-done.3 = bf16[528,128]{1,0:T(8,128)(2,1)S(1)} collective-permute-done((bf16[528,128]{1,0:T(8,128)(2,1)S(1)}, bf16[528,128]{1,0:T(8,128)(2,1)S(1)}, u32[]{:S(2)}, u32[]{:S(2)}) %collective-permute-start.3) | collective-permute-done | bytes 135200 | tf_op jit(solution)/shard_map/ppermute | solution.py:20
  28.0 1.5 collective-permute-start.5
  29.5 1.8 collective-permute-start.11
  31.4 1.6 collective-permute-done.5
  34.7 1.5 collective-permute-start.6
  36.2 2.9 %collective-permute-start.7 = (bf16[128,1024]{0,1:T(8,128)(2,1)S(1)}, bf16[128,1024]{0,1:T(8,128)(2,1)S(1)}, u32[]{:S(2)}, u32[]{:S(2)}) collective-permute-start(bf16[128,1024]{0,1:T(8,128)(2,1)S(1)} %pad_maximum_fusion), channel_id=1, source_target_pairs={{0,16},{4,20},{8,24},{12,28},{16,0},{20,4},{24,8},{28,12},{1,17},{... | collective-permute-start | bytes 786440 | tf_op jit(solution)/shard_map/ppermute | solution.py:20
  41.4 13.6 %collective-permute-done.7 = bf16[128,1024]{0,1:T(8,128)(2,1)S(1)} collective-permute-done((bf16[128,1024]{0,1:T(8,128)(2,1)S(1)}, bf16[128,1024]{0,1:T(8,128)(2,1)S(1)}, u32[]{:S(2)}, u32[]{:S(2)}) %collective-permute-start.7) | collective-permute-done | bytes 262176 | tf_op jit(solution)/shard_map/ppermute | solution.py:20
  55.2 2.7 %collective-permute-done.8 = bf16[128,1024]{0,1:T(8,128)(2,1)S(1)} collective-permute-done((bf16[128,1024]{0,1:T(8,128)(2,1)S(1)}, bf16[128,1024]{0,1:T(8,128)(2,1)S(1)}, u32[]{:S(2)}, u32[]{:S(2)}) %collective-permute-start.8) | collective-permute-done | bytes 262176 | tf_op jit(solution)/shard_map/ppermute | solution.py:20
  58.0 1.5 collective-permute-start.10
  59.8 1.8 collective-permute-done.10
  61.7 2.5 %fusion.6 = bf16[512,1024]{1,0:T(8,128)(2,1)S(1)} fusion(bf16[512,1024]{1,0:T(8,128)(2,1)S(1)} %bitcast.119, bf16[768,512]{1,0:T(8,128)(2,1)} %collective-permute-done.11, bf16[256,512]{1,0:T(8,128)(2,1)} %collective-permute-done.4, bf16[1024,512]{1,0:T(8,128)(2,1)S(1)} %copy-done.2), kind=kOutput, calls=%fused_computation.6 | convolution fusion | flops 1080557568 | bytes 4194304 | tf_op jit(solution)/shard_map/dot_general | solution.py:24
  64.4 1.8 collective-permute-done.12
  66.5 1.5 collective-permute-start.13
  68.2 6.7 %collective-permute-done.13 = bf16[128,1024]{1,0:T(8,128)(2,1)S(1)} collective-permute-done((bf16[128,1024]{1,0:T(8,128)(2,1)S(1)}, bf16[128,1024]{1,0:T(8,128)(2,1)S(1)}, u32[]{:S(2)}, u32[]{:S(2)}) %collective-permute-start.13) | collective-permute-done | bytes 262176 | tf_op jit(solution)/shard_map/ppermute | solution.py:20
  75.0 1.7 collective-permute-start.14
  76.7 3.2 %collective-permute-start.15 = (bf16[32,1024]{1,0:T(8,128)(2,1)S(1)}, bf16[32,1024]{1,0:T(8,128)(2,1)S(1)}, u32[]{:S(2)}, u32[]{:S(2)}) collective-permute-start(bf16[32,1024]{1,0:T(8,128)(2,1)S(1)} %get-tuple-element.131), channel_id=1, source_target_pairs={{0,16},{4,20},{8,24},{12,28},{16,0},{20,4},{24,8},{28,12},{1,17},{... | collective-permute-start | bytes 196616 | tf_op jit(solution)/shard_map/ppermute | solution.py:20
  82.1 5.3 %collective-permute-done.16 = bf16[32,1024]{1,0:T(8,128)(2,1)S(1)} collective-permute-done((bf16[32,1024]{1,0:T(8,128)(2,1)S(1)}, bf16[32,1024]{1,0:T(8,128)(2,1)S(1)}, u32[]{:S(2)}, u32[]{:S(2)}) %collective-permute-start.16) | collective-permute-done | bytes 65568 | tf_op jit(solution)/shard_map/ppermute | solution.py:20
  88.2 1.5 collective-permute-start.17
  91.8 5.9 %collective-permute-done.17.refs_1_ = bf16[32,4224]{1,0:T(8,128)(2,1)S(1)} collective-permute-done((bf16[32,4224]{1,0:T(8,128)(2,1)S(1)}, bf16[32,4224]{1,0:T(8,128)(2,1)S(1)}, u32[]{:S(2)}, u32[]{:S(2)}) %collective-permute-start.17) | collective-permute-done | bytes 270368 | tf_op jit(solution)/shard_map/ppermute | solution.py:20
  97.7 5.4 %collective-permute-done.18.refs_2_ = bf16[32,4224]{1,0:T(8,128)(2,1)S(1)} collective-permute-done((bf16[32,4224]{1,0:T(8,128)(2,1)S(1)}, bf16[32,4224]{1,0:T(8,128)(2,1)S(1)}, u32[]{:S(2)}, u32[]{:S(2)}) %collective-permute-start.18) | collective-permute-done | bytes 270368 | tf_op jit(solution)/shard_map/ppermute | solution.py:20
  103.1 1.6 collective-permute-done.20.refs_0_
  104.9 1.6 collective-permute-start.22
  106.8 1.7 collective-permute-start.24
  108.5 1.9 collective-permute-start.25
  110.5 10.2 %shard_map.164 = (bf16[128,4096]{1,0:T(8,128)(2,1)S(1)}, bf16[128,4096]{1,0:T(8,128)(2,1)S(1)}) custom-call(bf16[128,4224]{1,0:T(8,128)(2,1)S(1)} %shard_map.163.own, bf16[128,4224]{1,0:T(8,128)(2,1)S(1)} %collective-permute-done.21.mate, bf16[4096,896]{1,0:T(8,128)(2,1)} %bitcast.106, bf16[4096,896]{1,0:T(8,128)(2,1)} %bitcast.110, ...), custom_call_target="tpu_custom_call" | custom-call | flops 5637144576 | bytes 30408704 | tf_op jit(solution)/shard_map/pallas_call | solution.py:277
  121.5 1.4 collective-permute-start.29
  123.3 1.8 collective-permute-start.31
  125.0 10.2 %shard_map.166 = (bf16[128,4096]{1,0:T(8,128)(2,1)S(1)}, bf16[128,4096]{1,0:T(8,128)(2,1)S(1)}) custom-call(bf16[128,4224]{1,0:T(8,128)(2,1)S(1)} %shard_map.165.own, bf16[128,4224]{1,0:T(8,128)(2,1)S(1)} %collective-permute-done.27.mate, bf16[4096,896]{1,0:T(8,128)(2,1)} %bitcast.107, bf16[4096,896]{1,0:T(8,128)(2,1)} %bitcast.111, ...), custom_call_target="tpu_custom_call" | custom-call | flops 5637144576 | bytes 30408704 | tf_op jit(solution)/shard_map/pallas_call | solution.py:277
  135.3 1.6 collective-permute-done.30.refs_2_
  140.2 6.8 %collective-permute-done.34 = bf16[32,4096]{1,0:T(8,128)(2,1)S(1)} collective-permute-done((bf16[32,4096]{1,0:T(8,128)(2,1)S(1)}, bf16[32,4096]{1,0:T(8,128)(2,1)S(1)}, u32[]{:S(2)}, u32[]{:S(2)}) %collective-permute-start.34) | collective-permute-done | bytes 262176 | tf_op jit(solution)/shard_map/ppermute | solution.py:20
  147.3 1.8 collective-permute-start.39
  150.3 10.2 %shard_map.168 = (bf16[128,4096]{1,0:T(8,128)(2,1)S(1)}, bf16[128,4096]{1,0:T(8,128)(2,1)S(1)}) custom-call(bf16[128,4224]{1,0:T(8,128)(2,1)S(1)} %shard_map.167.own, bf16[128,4224]{1,0:T(8,128)(2,1)S(1)} %collective-permute-done.32.mate, bf16[4096,896]{1,0:T(8,128)(2,1)} %bitcast.108, bf16[4096,896]{1,0:T(8,128)(2,1)} %bitcast.112, ...), custom_call_target="tpu_custom_call" | custom-call | flops 5637144576 | bytes 30408704 | tf_op jit(solution)/shard_map/pallas_call | solution.py:277
  160.5 2.7 %collective-permute-done.36 = bf16[32,4096]{1,0:T(8,128)(2,1)S(1)} collective-permute-done((bf16[32,4096]{1,0:T(8,128)(2,1)S(1)}, bf16[32,4096]{1,0:T(8,128)(2,1)S(1)}, u32[]{:S(2)}, u32[]{:S(2)}) %collective-permute-start.36) | collective-permute-done | bytes 262176 | tf_op jit(solution)/shard_map/ppermute | solution.py:305
  163.2 1.9 collective-permute-done.38.refs_2_
  167.3 1.8 collective-permute-start.44
  169.3 10.2 %shard_map.170 = (bf16[128,4096]{1,0:T(8,128)(2,1)S(1)}, bf16[128,4096]{1,0:T(8,128)(2,1)S(1)}) custom-call(bf16[128,4224]{1,0:T(8,128)(2,1)S(1)} %shard_map.169.own, bf16[128,4224]{1,0:T(8,128)(2,1)S(1)} %collective-permute-done.40.mate, bf16[4096,896]{1,0:T(8,128)(2,1)} %bitcast.109, bf16[4096,896]{1,0:T(8,128)(2,1)} %bitcast.113, ...), custom_call_target="tpu_custom_call" | custom-call | flops 5637144576 | bytes 30408704 | tf_op jit(solution)/shard_map/pallas_call | solution.py:277
  180.5 2.2 collective-permute-start.45
  184.6 1.8 collective-permute-start.48
  187.2 4.9 %collective-permute-done.46 = bf16[32,4096]{1,0:T(8,128)(2,1)S(1)} collective-permute-done((bf16[32,4096]{1,0:T(8,128)(2,1)S(1)}, bf16[32,4096]{1,0:T(8,128)(2,1)S(1)}, u32[]{:S(2)}, u32[]{:S(2)}) %collective-permute-start.46) | collective-permute-done | bytes 262176 | tf_op jit(solution)/shard_map/ppermute | solution.py:20
  192.8 6.4 %collective-permute-start.53 = (bf16[32,4096]{1,0:T(8,128)(2,1)S(1)}, bf16[32,4096]{1,0:T(8,128)(2,1)S(1)}, u32[]{:S(2)}, u32[]{:S(2)}) collective-permute-start(bf16[32,4096]{1,0:T(8,128)(2,1)S(1)} %get-tuple-element.122), channel_id=1, source_target_pairs={{0,6},{1,7},{2,4},{3,5},{4,2},{5,3},{6,0},{7,1},{8,14},{9,15},{10,... | collective-permute-start | bytes 786440 | tf_op jit(solution)/shard_map/ppermute | solution.py:305
  200.0 3.3 %collective-permute-done.51 = bf16[32,4096]{1,0:T(8,128)(2,1)S(1)} collective-permute-done((bf16[32,4096]{1,0:T(8,128)(2,1)S(1)}, bf16[32,4096]{1,0:T(8,128)(2,1)S(1)}, u32[]{:S(2)}, u32[]{:S(2)}) %collective-permute-start.51) | collective-permute-done | bytes 262176 | tf_op jit(solution)/shard_map/ppermute | solution.py:20
  203.5 4.9 %collective-permute-done.53 = bf16[32,4096]{1,0:T(8,128)(2,1)S(1)} collective-permute-done((bf16[32,4096]{1,0:T(8,128)(2,1)S(1)}, bf16[32,4096]{1,0:T(8,128)(2,1)S(1)}, u32[]{:S(2)}, u32[]{:S(2)}) %collective-permute-start.53) | collective-permute-done | bytes 262176 | tf_op jit(solution)/shard_map/ppermute | solution.py:305
  209.9 6.4 %collective-permute-done.54 = bf16[32,4096]{1,0:T(8,128)(2,1)S(1)} collective-permute-done((bf16[32,4096]{1,0:T(8,128)(2,1)S(1)}, bf16[32,4096]{1,0:T(8,128)(2,1)S(1)}, u32[]{:S(2)}, u32[]{:S(2)}) %collective-permute-start.54) | collective-permute-done | bytes 262176 | tf_op jit(solution)/shard_map/ppermute | solution.py:20
  (210 shorter events, 38.0 us)
Async XLA Ops:
  3.9 8.3 %collective-permute-start = (bf16[528,128]{1,0:T(8,128)(2,1)S(1)}, bf16[528,128]{1,0:T(8,128)(2,1)S(1)}, u32[]{:S(2)}, u32[]{:S(2)}) collective-permute-start(bf16[528,128]{1,0:T(8,128)(2,1)S(1)} %pad_maximum_fusion.1), channel_id=1, source_target_pairs={{0,4},{4,0},{8,12},{12,8},{16,20},{20,16},{24,28},{28,24},{1,5},{5... | collective-permute-start | bytes 405512 | tf_op jit(solution)/shard_map/ppermute | solution.py:20
  7.7 19.9 %collective-permute-start.4 = (bf16[256,512]{1,0:T(8,128)(2,1)}, bf16[256,512]{1,0:T(8,128)(2,1)}, u32[]{:S(2)}, u32[]{:S(2)}) collective-permute-start(bf16[256,512]{1,0:T(8,128)(2,1)} %slice.274), channel_id=1, source_target_pairs={{0,8},{4,12},{8,0},{12,4},{16,24},{20,28},{24,16},{28,20},{1,9},{5... | collective-permute-start | bytes 786440 | tf_op jit(solution)/shard_map/ppermute | solution.py:20
  13.0 8.4 %collective-permute-start.1 = (bf16[528,128]{1,0:T(8,128)(2,1)S(1)}, bf16[528,128]{1,0:T(8,128)(2,1)S(1)}, u32[]{:S(2)}, u32[]{:S(2)}) collective-permute-start(bf16[528,128]{1,0:T(8,128)(2,1)S(1)} %pad_maximum_fusion.2), channel_id=1, source_target_pairs={{0,8},{4,12},{8,0},{12,4},{16,24},{20,28},{24,16},{28,20},{1,9},{5... | collective-permute-start | bytes 405512 | tf_op jit(solution)/shard_map/ppermute | solution.py:20
  13.6 8.5 %collective-permute-start.2 = (bf16[528,128]{1,0:T(8,128)(2,1)S(1)}, bf16[528,128]{1,0:T(8,128)(2,1)S(1)}, u32[]{:S(2)}, u32[]{:S(2)}) collective-permute-start(bf16[528,128]{1,0:T(8,128)(2,1)S(1)} %pad_maximum_fusion.2), channel_id=1, source_target_pairs={{0,16},{4,20},{8,24},{12,28},{16,0},{20,4},{24,8},{28,12},{1,17},{... | collective-permute-start | bytes 405512 | tf_op jit(solution)/shard_map/ppermute | solution.py:20
  16.2 10.3 %collective-permute-start.3 = (bf16[528,128]{1,0:T(8,128)(2,1)S(1)}, bf16[528,128]{1,0:T(8,128)(2,1)S(1)}, u32[]{:S(2)}, u32[]{:S(2)}) collective-permute-start(bf16[528,128]{1,0:T(8,128)(2,1)S(1)} %pad_maximum_fusion.2), channel_id=1, source_target_pairs={{0,24},{4,28},{8,16},{12,20},{16,8},{20,12},{24,0},{28,4},{1,25},{... | collective-permute-start | bytes 405512 | tf_op jit(solution)/shard_map/ppermute | solution.py:20
  29.5 32.2 %collective-permute-start.11 = (bf16[768,512]{1,0:T(8,128)(2,1)}, bf16[768,512]{1,0:T(8,128)(2,1)}, u32[]{:S(2)}, u32[]{:S(2)}) collective-permute-start(bf16[768,512]{1,0:T(8,128)(2,1)} %slice.275), channel_id=1, source_target_pairs={{0,8},{4,12},{8,0},{12,4},{16,24},{20,28},{24,16},{28,20},{1,9},{5... | collective-permute-start | bytes 2359304 | tf_op jit(solution)/shard_map/ppermute | solution.py:20
  34.7 6.4 %collective-permute-start.6 = (bf16[128,1024]{0,1:T(8,128)(2,1)S(1)}, bf16[128,1024]{0,1:T(8,128)(2,1)S(1)}, u32[]{:S(2)}, u32[]{:S(2)}) collective-permute-start(bf16[128,1024]{0,1:T(8,128)(2,1)S(1)} %pad_maximum_fusion), channel_id=1, source_target_pairs={{0,4},{4,0},{8,12},{12,8},{16,20},{20,16},{24,28},{28,24},{1,5},{5... | collective-permute-start | bytes 786440 | tf_op jit(solution)/shard_map/ppermute | solution.py:20
  36.2 18.9 %collective-permute-start.7 = (bf16[128,1024]{0,1:T(8,128)(2,1)S(1)}, bf16[128,1024]{0,1:T(8,128)(2,1)S(1)}, u32[]{:S(2)}, u32[]{:S(2)}) collective-permute-start(bf16[128,1024]{0,1:T(8,128)(2,1)S(1)} %pad_maximum_fusion), channel_id=1, source_target_pairs={{0,16},{4,20},{8,24},{12,28},{16,0},{20,4},{24,8},{28,12},{1,17},{... | collective-permute-start | bytes 786440 | tf_op jit(solution)/shard_map/ppermute | solution.py:20
  39.1 18.7 %collective-permute-start.8 = (bf16[128,1024]{0,1:T(8,128)(2,1)S(1)}, bf16[128,1024]{0,1:T(8,128)(2,1)S(1)}, u32[]{:S(2)}, u32[]{:S(2)}) collective-permute-start(bf16[128,1024]{0,1:T(8,128)(2,1)S(1)} %pad_maximum_fusion), channel_id=1, source_target_pairs={{0,20},{4,16},{8,28},{12,24},{16,4},{20,0},{24,12},{28,8},{1,21},{... | collective-permute-start | bytes 786440 | tf_op jit(solution)/shard_map/ppermute | solution.py:20
  41.1 16.9 %collective-permute-start.9 = (f32[128]{0:T(128)S(1)}, f32[128]{0:T(128)S(1)}, u32[]{:S(2)}, u32[]{:S(2)}) collective-permute-start(f32[128]{0:T(128)S(1)} %get-tuple-element.60), channel_id=1, source_target_pairs={{0,1},{1,0},{2,3},{3,2},{4,5},{5,4},{6,7},{7,6},{8,9},{9,8},{10,11... | collective-permute-start | bytes 1544 | tf_op jit(solution)/shard_map/ppermute | solution.py:20
  66.5 8.4 %collective-permute-start.13 = (bf16[128,1024]{1,0:T(8,128)(2,1)S(1)}, bf16[128,1024]{1,0:T(8,128)(2,1)S(1)}, u32[]{:S(2)}, u32[]{:S(2)}) collective-permute-start(bf16[128,1024]{1,0:T(8,128)(2,1)S(1)} %slice.349), channel_id=1, source_target_pairs={{0,2},{1,3},{2,0},{3,1},{4,6},{5,7},{6,4},{7,5},{8,10},{9,11},{10,... | collective-permute-start | bytes 786440 | tf_op jit(solution)/shard_map/ppermute | solution.py:20
  75.0 6.0 %collective-permute-start.14 = (bf16[32,1024]{1,0:T(8,128)(2,1)S(1)}, bf16[32,1024]{1,0:T(8,128)(2,1)S(1)}, u32[]{:S(2)}, u32[]{:S(2)}) collective-permute-start(bf16[32,1024]{1,0:T(8,128)(2,1)S(1)} %get-tuple-element.132), channel_id=1, source_target_pairs={{0,4},{4,0},{8,12},{12,8},{16,20},{20,16},{24,28},{28,24},{1,5},{5... | collective-permute-start | bytes 196616 | tf_op jit(solution)/shard_map/ppermute | solution.py:20
  79.9 7.6 %collective-permute-start.16 = (bf16[32,1024]{1,0:T(8,128)(2,1)S(1)}, bf16[32,1024]{1,0:T(8,128)(2,1)S(1)}, u32[]{:S(2)}, u32[]{:S(2)}) collective-permute-start(bf16[32,1024]{1,0:T(8,128)(2,1)S(1)} %get-tuple-element.130), channel_id=1, source_target_pairs={{0,20},{4,16},{8,28},{12,24},{16,4},{20,0},{24,12},{28,8},{1,21},{... | collective-permute-start | bytes 196616 | tf_op jit(solution)/shard_map/ppermute | solution.py:20
  88.2 9.5 %collective-permute-start.17 = (bf16[32,4224]{1,0:T(8,128)(2,1)S(1)}, bf16[32,4224]{1,0:T(8,128)(2,1)S(1)}, u32[]{:S(2)}, u32[]{:S(2)}) collective-permute-start(bf16[32,4224]{1,0:T(8,128)(2,1)S(1)} %concatenate.48.refs_0_), channel_id=1, source_target_pairs={{0,2},{1,3},{2,0},{3,1},{4,6},{5,7},{6,4},{7,5},{8,10},{9,11},{10,... | collective-permute-start | bytes 811016 | tf_op jit(solution)/shard_map/ppermute | solution.py:20
  89.8 13.3 %collective-permute-start.18 = (bf16[32,4224]{1,0:T(8,128)(2,1)S(1)}, bf16[32,4224]{1,0:T(8,128)(2,1)S(1)}, u32[]{:S(2)}, u32[]{:S(2)}) collective-permute-start(bf16[32,4224]{1,0:T(8,128)(2,1)S(1)} %concatenate.48.refs_0_), channel_id=1, source_target_pairs={{0,4},{4,0},{8,12},{12,8},{16,20},{20,16},{24,28},{28,24},{1,5},{5... | collective-permute-start | bytes 811016 | tf_op jit(solution)/shard_map/ppermute | solution.py:20
  90.5 12.6 %collective-permute-start.19 = (bf16[32,4224]{1,0:T(8,128)(2,1)S(1)}, bf16[32,4224]{1,0:T(8,128)(2,1)S(1)}, u32[]{:S(2)}, u32[]{:S(2)}) collective-permute-start(bf16[32,4224]{1,0:T(8,128)(2,1)S(1)} %concatenate.48.refs_0_), channel_id=1, source_target_pairs={{0,6},{1,7},{2,4},{3,5},{4,2},{5,3},{6,0},{7,1},{8,14},{9,15},{10,... | collective-permute-start | bytes 811016 | tf_op jit(solution)/shard_map/ppermute | solution.py:305
  91.8 12.9 %collective-permute-start.20 = (bf16[32,4224]{1,0:T(8,128)(2,1)S(1)}, bf16[32,4224]{1,0:T(8,128)(2,1)S(1)}, u32[]{:S(2)}, u32[]{:S(2)}) collective-permute-start(bf16[32,4224]{1,0:T(8,128)(2,1)S(1)} %concatenate.48.refs_0_), channel_id=1, source_target_pairs={{0,16},{4,20},{8,24},{12,28},{16,0},{20,4},{24,8},{28,12},{1,17},{... | collective-permute-start | bytes 811016 | tf_op jit(solution)/shard_map/ppermute | solution.py:20
  104.9 15.8 %collective-permute-start.26 = (bf16[32,4224]{1,0:T(8,128)(2,1)S(1)}, bf16[32,4224]{1,0:T(8,128)(2,1)S(1)}, u32[]{:S(2)}, u32[]{:S(2)}) collective-permute-start(bf16[32,4224]{1,0:T(8,128)(2,1)S(1)} %concatenate.48.refs_0_), channel_id=1, source_target_pairs={{0,8},{4,12},{8,0},{12,4},{16,24},{20,28},{24,16},{28,20},{1,9},{5... | collective-permute-start | bytes 811016 | tf_op jit(solution)/shard_map/ppermute | solution.py:20
  104.9 15.8 %collective-permute-start.22 = (bf16[32,4224]{1,0:T(8,128)(2,1)S(1)}, bf16[32,4224]{1,0:T(8,128)(2,1)S(1)}, u32[]{:S(2)}, u32[]{:S(2)}) collective-permute-start(bf16[32,4224]{1,0:T(8,128)(2,1)S(1)} %collective-permute-done.20.refs_0_), channel_id=1, source_target_pairs={{0,2},{1,3},{2,0},{3,1},{4,6},{5,7},{6,4},{7,5},{8,10},{9,11},{10,... | collective-permute-start | bytes 811016 | tf_op jit(solution)/shard_map/ppermute | solution.py:20
  106.5 14.3 %collective-permute-start.23 = (bf16[32,4224]{1,0:T(8,128)(2,1)S(1)}, bf16[32,4224]{1,0:T(8,128)(2,1)S(1)}, u32[]{:S(2)}, u32[]{:S(2)}) collective-permute-start(bf16[32,4224]{1,0:T(8,128)(2,1)S(1)} %collective-permute-done.20.refs_0_), channel_id=1, source_target_pairs={{0,4},{4,0},{8,12},{12,8},{16,20},{20,16},{24,28},{28,24},{1,5},{5... | collective-permute-start | bytes 811016 | tf_op jit(solution)/shard_map/ppermute | solution.py:20
  106.8 14.0 %collective-permute-start.24 = (bf16[32,4224]{1,0:T(8,128)(2,1)S(1)}, bf16[32,4224]{1,0:T(8,128)(2,1)S(1)}, u32[]{:S(2)}, u32[]{:S(2)}) collective-permute-start(bf16[32,4224]{1,0:T(8,128)(2,1)S(1)} %collective-permute-done.20.refs_0_), channel_id=1, source_target_pairs={{0,6},{1,7},{2,4},{3,5},{4,2},{5,3},{6,0},{7,1},{8,14},{9,15},{10,... | collective-permute-start | bytes 811016 | tf_op jit(solution)/shard_map/ppermute | solution.py:305
  108.5 12.4 %collective-permute-start.25 = (bf16[32,4224]{1,0:T(8,128)(2,1)S(1)}, bf16[32,4224]{1,0:T(8,128)(2,1)S(1)}, u32[]{:S(2)}, u32[]{:S(2)}) collective-permute-start(bf16[32,4224]{1,0:T(8,128)(2,1)S(1)} %collective-permute-done.20.refs_0_), channel_id=1, source_target_pairs={{0,8},{4,12},{8,0},{12,4},{16,24},{20,28},{24,16},{28,20},{1,9},{5... | collective-permute-start | bytes 811016 | tf_op jit(solution)/shard_map/ppermute | solution.py:20
  121.0 15.9 %collective-permute-start.28 = (bf16[128,4096]{1,0:T(8,128)(2,1)S(1)}, bf16[128,4096]{1,0:T(8,128)(2,1)S(1)}, u32[]{:S(2)}, u32[]{:S(2)}) collective-permute-start(bf16[128,4096]{1,0:T(8,128)(2,1)S(1)} %get-tuple-element.76), channel_id=1, source_target_pairs={{0,1},{1,0},{2,3},{3,2},{4,5},{5,4},{6,7},{7,6},{8,9},{9,8},{10,11... | collective-permute-start | bytes 3145736 | tf_op jit(solution)/shard_map/ppermute | solution.py:20
  121.5 13.7 %collective-permute-start.29 = (bf16[32,4224]{1,0:T(8,128)(2,1)S(1)}, bf16[32,4224]{1,0:T(8,128)(2,1)S(1)}, u32[]{:S(2)}, u32[]{:S(2)}) collective-permute-start(bf16[32,4224]{1,0:T(8,128)(2,1)S(1)} %collective-permute-done.25.refs_0_), channel_id=1, source_target_pairs={{0,2},{1,3},{2,0},{3,1},{4,6},{5,7},{6,4},{7,5},{8,10},{9,11},{10,... | collective-permute-start | bytes 811016 | tf_op jit(solution)/shard_map/ppermute | solution.py:20
  122.9 14.0 %collective-permute-start.30 = (bf16[32,4224]{1,0:T(8,128)(2,1)S(1)}, bf16[32,4224]{1,0:T(8,128)(2,1)S(1)}, u32[]{:S(2)}, u32[]{:S(2)}) collective-permute-start(bf16[32,4224]{1,0:T(8,128)(2,1)S(1)} %collective-permute-done.25.refs_0_), channel_id=1, source_target_pairs={{0,4},{4,0},{8,12},{12,8},{16,20},{20,16},{24,28},{28,24},{1,5},{5... | collective-permute-start | bytes 811016 | tf_op jit(solution)/shard_map/ppermute | solution.py:20
  123.3 13.6 %collective-permute-start.31 = (bf16[32,4224]{1,0:T(8,128)(2,1)S(1)}, bf16[32,4224]{1,0:T(8,128)(2,1)S(1)}, u32[]{:S(2)}, u32[]{:S(2)}) collective-permute-start(bf16[32,4224]{1,0:T(8,128)(2,1)S(1)} %collective-permute-done.25.refs_0_), channel_id=1, source_target_pairs={{0,6},{1,7},{2,4},{3,5},{4,2},{5,3},{6,0},{7,1},{8,14},{9,15},{10,... | collective-permute-start | bytes 811016 | tf_op jit(solution)/shard_map/ppermute | solution.py:305
  137.0 12.1 %collective-permute-start.32 = (bf16[128,4224]{1,0:T(8,128)(2,1)S(1)}, bf16[128,4224]{1,0:T(8,128)(2,1)S(1)}, u32[]{:S(2)}, u32[]{:S(2)}) collective-permute-start(bf16[128,4224]{1,0:T(8,128)(2,1)S(1)} %shard_map.167.own), channel_id=1, source_target_pairs={{0,1},{1,0},{2,3},{3,2},{4,5},{5,4},{6,7},{7,6},{8,9},{9,8},{10,11... | collective-permute-start | bytes 3244040 | tf_op jit(solution)/shard_map/ppermute | solution.py:20
  137.1 28.1 %collective-permute-start.33 = (bf16[128,4096]{1,0:T(8,128)(2,1)S(1)}, bf16[128,4096]{1,0:T(8,128)(2,1)S(1)}, u32[]{:S(2)}, u32[]{:S(2)}) collective-permute-start(bf16[128,4096]{1,0:T(8,128)(2,1)S(1)} %get-tuple-element.85), channel_id=1, source_target_pairs={{0,1},{1,0},{2,3},{3,2},{4,5},{5,4},{6,7},{7,6},{8,9},{9,8},{10,11... | collective-permute-start | bytes 3145736 | tf_op jit(solution)/shard_map/ppermute | solution.py:20
  137.8 9.2 %collective-permute-start.34 = (bf16[32,4096]{1,0:T(8,128)(2,1)S(1)}, bf16[32,4096]{1,0:T(8,128)(2,1)S(1)}, u32[]{:S(2)}, u32[]{:S(2)}) collective-permute-start(bf16[32,4096]{1,0:T(8,128)(2,1)S(1)} %get-tuple-element.129), channel_id=1, source_target_pairs={{0,2},{1,3},{2,0},{3,1},{4,6},{5,7},{6,4},{7,5},{8,10},{9,11},{10,... | collective-permute-start | bytes 786440 | tf_op jit(solution)/shard_map/ppermute | solution.py:20
  138.5 8.9 %collective-permute-start.35 = (bf16[32,4096]{1,0:T(8,128)(2,1)S(1)}, bf16[32,4096]{1,0:T(8,128)(2,1)S(1)}, u32[]{:S(2)}, u32[]{:S(2)}) collective-permute-start(bf16[32,4096]{1,0:T(8,128)(2,1)S(1)} %get-tuple-element.128), channel_id=1, source_target_pairs={{0,4},{4,0},{8,12},{12,8},{16,20},{20,16},{24,28},{28,24},{1,5},{5... | collective-permute-start | bytes 786440 | tf_op jit(solution)/shard_map/ppermute | solution.py:20
  139.6 23.6 %collective-permute-start.37 = (bf16[32,4224]{1,0:T(8,128)(2,1)S(1)}, bf16[32,4224]{1,0:T(8,128)(2,1)S(1)}, u32[]{:S(2)}, u32[]{:S(2)}) collective-permute-start(bf16[32,4224]{1,0:T(8,128)(2,1)S(1)} %collective-permute-done.26.refs_0_), channel_id=1, source_target_pairs={{0,2},{1,3},{2,0},{3,1},{4,6},{5,7},{6,4},{7,5},{8,10},{9,11},{10,... | collective-permute-start | bytes 811016 | tf_op jit(solution)/shard_map/ppermute | solution.py:20
  147.0 18.2 %collective-permute-start.38 = (bf16[32,4224]{1,0:T(8,128)(2,1)S(1)}, bf16[32,4224]{1,0:T(8,128)(2,1)S(1)}, u32[]{:S(2)}, u32[]{:S(2)}) collective-permute-start(bf16[32,4224]{1,0:T(8,128)(2,1)S(1)} %collective-permute-done.26.refs_0_), channel_id=1, source_target_pairs={{0,4},{4,0},{8,12},{12,8},{16,20},{20,16},{24,28},{28,24},{1,5},{5... | collective-permute-start | bytes 811016 | tf_op jit(solution)/shard_map/ppermute | solution.py:20
  147.3 17.8 %collective-permute-start.39 = (bf16[32,4224]{1,0:T(8,128)(2,1)S(1)}, bf16[32,4224]{1,0:T(8,128)(2,1)S(1)}, u32[]{:S(2)}, u32[]{:S(2)}) collective-permute-start(bf16[32,4224]{1,0:T(8,128)(2,1)S(1)} %collective-permute-done.26.refs_0_), channel_id=1, source_target_pairs={{0,6},{1,7},{2,4},{3,5},{4,2},{5,3},{6,0},{7,1},{8,14},{9,15},{10,... | collective-permute-start | bytes 811016 | tf_op jit(solution)/shard_map/ppermute | solution.py:305
  149.1 14.1 %collective-permute-start.36 = (bf16[32,4096]{1,0:T(8,128)(2,1)S(1)}, bf16[32,4096]{1,0:T(8,128)(2,1)S(1)}, u32[]{:S(2)}, u32[]{:S(2)}) collective-permute-start(bf16[32,4096]{1,0:T(8,128)(2,1)S(1)} %get-tuple-element.127), channel_id=1, source_target_pairs={{0,6},{1,7},{2,4},{3,5},{4,2},{5,3},{6,0},{7,1},{8,14},{9,15},{10,... | collective-permute-start | bytes 786440 | tf_op jit(solution)/shard_map/ppermute | solution.py:305
  165.5 14.0 %collective-permute-start.42 = (bf16[32,4096]{1,0:T(8,128)(2,1)S(1)}, bf16[32,4096]{1,0:T(8,128)(2,1)S(1)}, u32[]{:S(2)}, u32[]{:S(2)}) collective-permute-start(bf16[32,4096]{1,0:T(8,128)(2,1)S(1)} %get-tuple-element.126), channel_id=1, source_target_pairs={{0,2},{1,3},{2,0},{3,1},{4,6},{5,7},{6,4},{7,5},{8,10},{9,11},{10,... | collective-permute-start | bytes 786440 | tf_op jit(solution)/shard_map/ppermute | solution.py:20
  166.2 14.0 %collective-permute-start.43 = (bf16[32,4096]{1,0:T(8,128)(2,1)S(1)}, bf16[32,4096]{1,0:T(8,128)(2,1)S(1)}, u32[]{:S(2)}, u32[]{:S(2)}) collective-permute-start(bf16[32,4096]{1,0:T(8,128)(2,1)S(1)} %get-tuple-element.125), channel_id=1, source_target_pairs={{0,4},{4,0},{8,12},{12,8},{16,20},{20,16},{24,28},{28,24},{1,5},{5... | collective-permute-start | bytes 786440 | tf_op jit(solution)/shard_map/ppermute | solution.py:20
  167.3 12.9 %collective-permute-start.44 = (bf16[32,4096]{1,0:T(8,128)(2,1)S(1)}, bf16[32,4096]{1,0:T(8,128)(2,1)S(1)}, u32[]{:S(2)}, u32[]{:S(2)}) collective-permute-start(bf16[32,4096]{1,0:T(8,128)(2,1)S(1)} %get-tuple-element.124), channel_id=1, source_target_pairs={{0,6},{1,7},{2,4},{3,5},{4,2},{5,3},{6,0},{7,1},{8,14},{9,15},{10,... | collective-permute-start | bytes 786440 | tf_op jit(solution)/shard_map/ppermute | solution.py:305
  169.1 11.2 %collective-permute-start.41 = (bf16[128,4096]{1,0:T(8,128)(2,1)S(1)}, bf16[128,4096]{1,0:T(8,128)(2,1)S(1)}, u32[]{:S(2)}, u32[]{:S(2)}) collective-permute-start(bf16[128,4096]{1,0:T(8,128)(2,1)S(1)} %get-tuple-element.93), channel_id=1, source_target_pairs={{0,1},{1,0},{2,3},{3,2},{4,5},{5,4},{6,7},{7,6},{8,9},{9,8},{10,11... | collective-permute-start | bytes 3145736 | tf_op jit(solution)/shard_map/ppermute | solution.py:20
  180.3 6.1 %collective-permute-start.50 = (bf16[128,4096]{1,0:T(8,128)(2,1)S(1)}, bf16[128,4096]{1,0:T(8,128)(2,1)S(1)}, u32[]{:S(2)}, u32[]{:S(2)}) collective-permute-start(bf16[128,4096]{1,0:T(8,128)(2,1)S(1)} %get-tuple-element.106), channel_id=1, source_target_pairs={{0,1},{1,0},{2,3},{3,2},{4,5},{5,4},{6,7},{7,6},{8,9},{9,8},{10,11... | collective-permute-start | bytes 3145736 | tf_op jit(solution)/shard_map/ppermute | solution.py:20
  180.5 29.4 %collective-permute-start.45 = (bf16[32,4096]{1,0:T(8,128)(2,1)S(1)}, bf16[32,4096]{1,0:T(8,128)(2,1)S(1)}, u32[]{:S(2)}, u32[]{:S(2)}) collective-permute-start(bf16[32,4096]{1,0:T(8,128)(2,1)S(1)} %add_convert_fusion.10), channel_id=1, source_target_pairs={{0,16},{4,20},{8,24},{12,28},{16,0},{20,4},{24,8},{28,12},{1,17},{... | collective-permute-start | bytes 786440 | tf_op jit(solution)/shard_map/ppermute | solution.py:20
  182.8 9.2 %collective-permute-start.46 = (bf16[32,4096]{1,0:T(8,128)(2,1)S(1)}, bf16[32,4096]{1,0:T(8,128)(2,1)S(1)}, u32[]{:S(2)}, u32[]{:S(2)}) collective-permute-start(bf16[32,4096]{1,0:T(8,128)(2,1)S(1)} %get-tuple-element.118), channel_id=1, source_target_pairs={{0,2},{1,3},{2,0},{3,1},{4,6},{5,7},{6,4},{7,5},{8,10},{9,11},{10,... | collective-permute-start | bytes 786440 | tf_op jit(solution)/shard_map/ppermute | solution.py:20
  183.4 9.4 %collective-permute-start.47 = (bf16[32,4096]{1,0:T(8,128)(2,1)S(1)}, bf16[32,4096]{1,0:T(8,128)(2,1)S(1)}, u32[]{:S(2)}, u32[]{:S(2)}) collective-permute-start(bf16[32,4096]{1,0:T(8,128)(2,1)S(1)} %get-tuple-element.120), channel_id=1, source_target_pairs={{0,4},{4,0},{8,12},{12,8},{16,20},{20,16},{24,28},{28,24},{1,5},{5... | collective-permute-start | bytes 786440 | tf_op jit(solution)/shard_map/ppermute | solution.py:20
  184.6 14.6 %collective-permute-start.48 = (bf16[32,4096]{1,0:T(8,128)(2,1)S(1)}, bf16[32,4096]{1,0:T(8,128)(2,1)S(1)}, u32[]{:S(2)}, u32[]{:S(2)}) collective-permute-start(bf16[32,4096]{1,0:T(8,128)(2,1)S(1)} %get-tuple-element.119), channel_id=1, source_target_pairs={{0,6},{1,7},{2,4},{3,5},{4,2},{5,3},{6,0},{7,1},{8,14},{9,15},{10,... | collective-permute-start | bytes 786440 | tf_op jit(solution)/shard_map/ppermute | solution.py:305
  186.6 16.7 %collective-permute-start.51 = (bf16[32,4096]{1,0:T(8,128)(2,1)S(1)}, bf16[32,4096]{1,0:T(8,128)(2,1)S(1)}, u32[]{:S(2)}, u32[]{:S(2)}) collective-permute-start(bf16[32,4096]{1,0:T(8,128)(2,1)S(1)} %get-tuple-element.121), channel_id=1, source_target_pairs={{0,2},{1,3},{2,0},{3,1},{4,6},{5,7},{6,4},{7,5},{8,10},{9,11},{10,... | collective-permute-start | bytes 786440 | tf_op jit(solution)/shard_map/ppermute | solution.py:20
  192.0 11.5 %collective-permute-start.52 = (bf16[32,4096]{1,0:T(8,128)(2,1)S(1)}, bf16[32,4096]{1,0:T(8,128)(2,1)S(1)}, u32[]{:S(2)}, u32[]{:S(2)}) collective-permute-start(bf16[32,4096]{1,0:T(8,128)(2,1)S(1)} %get-tuple-element.123), channel_id=1, source_target_pairs={{0,4},{4,0},{8,12},{12,8},{16,20},{20,16},{24,28},{28,24},{1,5},{5... | collective-permute-start | bytes 786440 | tf_op jit(solution)/shard_map/ppermute | solution.py:20
  192.8 15.6 %collective-permute-start.53 = (bf16[32,4096]{1,0:T(8,128)(2,1)S(1)}, bf16[32,4096]{1,0:T(8,128)(2,1)S(1)}, u32[]{:S(2)}, u32[]{:S(2)}) collective-permute-start(bf16[32,4096]{1,0:T(8,128)(2,1)S(1)} %get-tuple-element.122), channel_id=1, source_target_pairs={{0,6},{1,7},{2,4},{3,5},{4,2},{5,3},{6,0},{7,1},{8,14},{9,15},{10,... | collective-permute-start | bytes 786440 | tf_op jit(solution)/shard_map/ppermute | solution.py:305
  199.4 10.5 %collective-permute-start.49 = (bf16[32,4096]{1,0:T(8,128)(2,1)S(1)}, bf16[32,4096]{1,0:T(8,128)(2,1)S(1)}, u32[]{:S(2)}, u32[]{:S(2)}) collective-permute-start(bf16[32,4096]{1,0:T(8,128)(2,1)S(1)} %add_convert_fusion.6), channel_id=1, source_target_pairs={{0,24},{4,28},{8,16},{12,20},{16,8},{20,12},{24,0},{28,4},{1,25},{... | collective-permute-start | bytes 786440 | tf_op jit(solution)/shard_map/ppermute | solution.py:20
  208.6 7.7 %collective-permute-start.54 = (bf16[32,4096]{1,0:T(8,128)(2,1)S(1)}, bf16[32,4096]{1,0:T(8,128)(2,1)S(1)}, u32[]{:S(2)}, u32[]{:S(2)}) collective-permute-start(bf16[32,4096]{1,0:T(8,128)(2,1)S(1)} %add_convert_fusion.2), channel_id=1, source_target_pairs={{0,8},{4,12},{8,0},{12,4},{16,24},{20,28},{24,16},{28,20},{1,9},{5... | collective-permute-start | bytes 786440 | tf_op jit(solution)/shard_map/ppermute | solution.py:20
  (21 other events, 144.0 us)

commit v6 on v5

--- a/solution.py
+++ b/solution.py
@@ -310,10 +310,11 @@
     return own[first:last].astype(F32) + got[first:last].astype(F32)
 
 
-def plane_sums(own, got):
+def plane_sums(own, got, others):
     size = own.shape[0] // 4
-    to_x, to_y, to_xy = [summed(own, got, k * size, size).astype(BF) for k in (1, 2, 3)]
-    return swap(to_x, "exp", 2), swap(to_y, "ctx", 1), across(to_xy)
+    sums = [summed(own, got, k * size, size).astype(BF) for k in (1, 2, 3)]
+    (to_x,), others = together(sums[:1], others)
+    return (swap(to_x, "exp", 2), swap(sums[1], "ctx", 1), across(sums[2])), others
 
 
 def local(
@@ -372,8 +373,28 @@
     planes = [by_distance[d] for d in order]
     near, rows, results, got, far_got, parts = [], [], [], [], [], []
 
-    def neighbours(piece):
-        return swap(piece, "exp", 2), swap(piece, "ctx", 1), across(piece)
+    def sides(k):
+        return (("ctx", 1), ("exp", 2)) if k < count - 2 else (("exp", 2), ("ctx", 1))
+
+    def in_steps(k):
+        return k < count - 1
+
+    def bring(k):
+        if k < min(count, 3):
+            one, two = sides(k)
+            near.append((swap(planes[k], *one), swap(planes[k], *two), across(planes[k])))
+
+    def bring_first(k):
+        if 3 <= k < count:
+            near.append((swap(planes[k], *sides(k)[0]),))
+
+    def bring_second(k):
+        if 3 <= k < count:
+            near[k] = (*near[k], swap(pack((planes[k], *near[k])), *sides(k)[1]))
+
+    def ready(k):
+        own = pack((planes[k], *near[k]))
+        rows.append((own, swap(own, "exp", 1)))
 
     def core(k):
         if 0 <= k < count:
@@ -381,43 +402,56 @@
 
     def spread(k):
         if 0 <= k < count:
-            far_got.append(plane_sums(results[k][0], got[k]))
+            own = results[k][0]
+            if in_steps(k):
+                half = own.shape[0] // 2
+                far_got.append((swap(summed(own, got[k], half, half).astype(BF), *sides(k)[1]),))
+            else:
+                last, far_got[1:] = plane_sums(own, got[k], far_got[1:])
+                far_got.append(last)
+
+    def spread_second(k):
+        if 0 <= k < count and len(far_got[k]) == 1:
+            first = far_got[k][0]
+            size = first.shape[0] // 2
+            second = summed(results[k][0], got[k], size, size) + first[size:].astype(F32)
+            far_got[k] = (first, swap(second.astype(BF), *sides(k)[0]))
 
     def back(k):
         if 0 <= k < count:
             part = summed(results[k][0], got[k], 0, quarter)
             for v in far_got[k]:
-                part = part + v.astype(F32)
+                part = part + v[:quarter].astype(F32)
             d = order[k]
             parts.append(part if d == 0 else swap(part.astype(BF), "ctx", 2 * d))
 
-    def bring(k):
-        if k < count:
-            near.append(neighbours(planes[k]))
-
-    def ready(k):
-        if k < count:
-            own = pack((planes[k], *near[k]))
-            rows.append((own, swap(own, "exp", 1)))
+    def sums(stage):
+        core(stage - 1)
+        if stage - 2 < count - 2:
+            spread(stage - 2)
+        spread_second(stage - 3)
+        if stage == count - 1:
+            spread(count - 2)
+        if stage == count:
+            spread_second(count - 2)
+            spread(count - 1)
+        back(stage - 4)
 
     bring(0)
     near[0], planes[1] = together(near[0], planes[1])
     for i in range(count):
         ready(i)
-        core(i - 1)
-        spread(i - 2)
-        back(i - 3)
+        sums(i)
         bring(i + 1)
-        beside = (got[-1:], far_got[-1:], parts[-1:], near[i + 1 :], planes[i + 2 :])
+        bring_second(i + 1)
+        if i > 0:
+            bring_first(i + 2)
+        beside = (got[-1:], far_got[: count - 2], parts[-1:], near[i + 1 :], planes[i + 2 :])
         results.append(experts(*rows[i], w_gate[0], w_up[0], w_down[0], pick))
         results[i], beside = together(results[i], beside)
-        got[-1:], far_got[-1:], parts[-1:], near[i + 1 :], planes[i + 2 :] = beside
-    core(count - 1)
-    spread(count - 2)
-    back(count - 3)
-    spread(count - 1)
-    back(count - 2)
-    back(count - 1)
+        got[-1:], far_got[: count - 2], parts[-1:], near[i + 1 :], planes[i + 2 :] = beside
+    for i in range(count, count + 4):
+        sums(i)
     for part in parts:
         hidden = hidden + part.astype(F32)
     return hidden.astype(BF)

time: 218 us -> 214 us (0.982)
  starting transfers between devices: 65.5 us -> 58.4 us
  other arithmetic: 8.59 us -> 11.4 us
    ppermute x8 -> x4, starting transfers between devices: 17.5 us -> 3.74 us  [across(): return lax.ppermute(x, ('ctx', 'exp'), pairs)]
    ppermute x47, starting transfers between devices: 47.9 us -> 54.6 us  [swap(): return lax.ppermute(x, axis, [(i, i ^ flip) for i in range(size)])]
    ppermute x8 -> x4, waiting for transfers between devices: 7.62 us -> 5.57 us  [across(): return lax.ppermute(x, ('ctx', 'exp'), pairs)]
  transfers between devices with their start and end apart: 55 -> 51, of which waited for: 26 -> 27; matrix products, arithmetic and copies ran while one was open for 5% -> 5% of each run, Pallas kernels for 19% -> 19%
where the time goes in v6:
time: 214 us
  waiting for transfers between devices  91 us (43%)
  starting transfers between devices  58.4 us (27%)
  Pallas kernels  41.2 us (19%)
  other arithmetic  11.4 us (5%)
  local copies, waits for them, and re-layouts  6.34 us (3%)
  matrix products  4.51 us (2%)
    ppermute x47, waiting for transfers between devices, swap(): return lax.ppermute(x, axis, [(i, i ^ flip) for i in range(size)])  85.5 us
    ppermute x47, starting transfers between devices, swap(): return lax.ppermute(x, axis, [(i, i ^ flip) for i in range(size)])  54.6 us
    pallas_call x4, Pallas kernels, experts(): pl.pallas_call(expert_kernel, out_shape=(out, out), in_specs=[anywhere] *...  40.9 us
    ppermute x4, waiting for transfers between devices, across(): return lax.ppermute(x, ('ctx', 'exp'), pairs)  5.57 us
  transfers between devices with their start and end apart: 51, of which 27 were waited for; matrix products, arithmetic and copies ran while one was open for 5% of the time, Pallas kernels for 19%

profile of v6, /device:TPU:0, one launch (start us, length us, event | category | flops | bytes accessed | tf_op | source)
XLA Modules:
  0.0 213.6 jit_solution(7710193185864040560)
XLA Ops:
  3.9 3.0 %collective-permute-start = (bf16[528,128]{1,0:T(8,128)(2,1)S(1)}, bf16[528,128]{1,0:T(8,128)(2,1)S(1)}, u32[]{:S(2)}, u32[]{:S(2)}) collective-permute-start(bf16[528,128]{1,0:T(8,128)(2,1)S(1)} %pad_maximum_fusion.1), channel_id=1, source_target_pairs={{0,4},{4,0},{8,12},{12,8},{16,20},{20,16},{24,28},{28,24},{1,5},{5... | collective-permute-start | bytes 405512 | tf_op jit(solution)/shard_map/ppermute | solution.py:20
  7.7 1.6 collective-permute-start.4
  9.5 1.4 fusion.9
  14.2 2.6 %collective-permute-start.2 = (bf16[528,128]{1,0:T(8,128)(2,1)}, bf16[528,128]{1,0:T(8,128)(2,1)S(1)}, u32[]{:S(2)}, u32[]{:S(2)}) collective-permute-start(bf16[528,128]{1,0:T(8,128)(2,1)} %pad_maximum_fusion.2), channel_id=1, source_target_pairs={{0,16},{4,20},{8,24},{12,28},{16,0},{20,4},{24,8},{28,12},{1,17},{... | collective-permute-start | bytes 405512 | tf_op jit(solution)/shard_map/ppermute | solution.py:20
  18.2 2.5 %collective-permute-done.1 = bf16[528,128]{1,0:T(8,128)(2,1)S(1)} collective-permute-done((bf16[528,128]{1,0:T(8,128)(2,1)}, bf16[528,128]{1,0:T(8,128)(2,1)S(1)}, u32[]{:S(2)}, u32[]{:S(2)}) %collective-permute-start.1) | collective-permute-done | bytes 135200 | tf_op jit(solution)/shard_map/ppermute | solution.py:20
  20.8 6.4 %collective-permute-done.2 = bf16[528,128]{1,0:T(8,128)(2,1)S(1)} collective-permute-done((bf16[528,128]{1,0:T(8,128)(2,1)}, bf16[528,128]{1,0:T(8,128)(2,1)S(1)}, u32[]{:S(2)}, u32[]{:S(2)}) %collective-permute-start.2) | collective-permute-done | bytes 135200 | tf_op jit(solution)/shard_map/ppermute | solution.py:20
  33.1 1.5 collective-permute-start.11
  34.7 2.1 collective-permute-done.5
  39.7 3.7 %collective-permute-start.8 = (bf16[128,1024]{0,1:T(8,128)(2,1)S(1)}, bf16[128,1024]{0,1:T(8,128)(2,1)S(1)}, u32[]{:S(2)}, u32[]{:S(2)}) collective-permute-start(bf16[128,1024]{0,1:T(8,128)(2,1)S(1)} %pad_maximum_fusion), channel_id=1, source_target_pairs={{0,20},{4,16},{8,28},{12,24},{16,4},{20,0},{24,12},{28,8},{1,21},{... | collective-permute-start | bytes 786440 | tf_op jit(solution)/shard_map/ppermute | solution.py:20
  43.4 6.1 %collective-permute-done.6 = bf16[128,1024]{0,1:T(8,128)(2,1)S(1)} collective-permute-done((bf16[128,1024]{0,1:T(8,128)(2,1)S(1)}, bf16[128,1024]{0,1:T(8,128)(2,1)S(1)}, u32[]{:S(2)}, u32[]{:S(2)}) %collective-permute-start.6) | collective-permute-done | bytes 262176 | tf_op jit(solution)/shard_map/ppermute | solution.py:20
  49.8 8.5 %collective-permute-done.8 = bf16[128,1024]{0,1:T(8,128)(2,1)S(1)} collective-permute-done((bf16[128,1024]{0,1:T(8,128)(2,1)S(1)}, bf16[128,1024]{0,1:T(8,128)(2,1)S(1)}, u32[]{:S(2)}, u32[]{:S(2)}) %collective-permute-start.8) | collective-permute-done | bytes 262176 | tf_op jit(solution)/shard_map/ppermute | solution.py:20
  58.5 2.7 %collective-permute-done.7 = bf16[128,1024]{0,1:T(8,128)(2,1)S(1)} collective-permute-done((bf16[128,1024]{0,1:T(8,128)(2,1)S(1)}, bf16[128,1024]{0,1:T(8,128)(2,1)S(1)}, u32[]{:S(2)}, u32[]{:S(2)}) %collective-permute-start.7) | collective-permute-done | bytes 262176 | tf_op jit(solution)/shard_map/ppermute | solution.py:20
  61.3 1.5 collective-permute-start.10
  63.1 1.9 collective-permute-done.10
  65.0 2.5 %fusion.6 = bf16[512,1024]{1,0:T(8,128)(2,1)S(1)} fusion(bf16[512,1024]{1,0:T(8,128)(2,1)S(1)} %bitcast.119, bf16[768,512]{1,0:T(8,128)(2,1)} %collective-permute-done.11, bf16[256,512]{1,0:T(8,128)(2,1)} %collective-permute-done.4, bf16[1024,512]{1,0:T(8,128)(2,1)S(1)} %copy-done.2), kind=kOutput, calls=%fused_computation.6 | convolution fusion | flops 1080557568 | bytes 4194304 | tf_op jit(solution)/shard_map/dot_general | solution.py:24
  67.7 1.8 collective-permute-done.12
  69.8 1.5 collective-permute-start.13
  71.5 6.7 %collective-permute-done.13 = bf16[128,1024]{1,0:T(8,128)(2,1)S(1)} collective-permute-done((bf16[128,1024]{1,0:T(8,128)(2,1)S(1)}, bf16[128,1024]{1,0:T(8,128)(2,1)S(1)}, u32[]{:S(2)}, u32[]{:S(2)}) %collective-permute-start.13) | collective-permute-done | bytes 262176 | tf_op jit(solution)/shard_map/ppermute | solution.py:20
  78.3 1.7 collective-permute-start.14
  80.0 3.4 %collective-permute-start.15 = (bf16[32,1024]{1,0:T(8,128)(2,1)S(1)}, bf16[32,1024]{1,0:T(8,128)(2,1)S(1)}, u32[]{:S(2)}, u32[]{:S(2)}) collective-permute-start(bf16[32,1024]{1,0:T(8,128)(2,1)S(1)} %get-tuple-element.126), channel_id=1, source_target_pairs={{0,16},{4,20},{8,24},{12,28},{16,0},{20,4},{24,8},{28,12},{1,17},{... | collective-permute-start | bytes 196616 | tf_op jit(solution)/shard_map/ppermute | solution.py:20
  83.4 2.5 %collective-permute-done.15 = bf16[32,1024]{1,0:T(8,128)(2,1)S(1)} collective-permute-done((bf16[32,1024]{1,0:T(8,128)(2,1)S(1)}, bf16[32,1024]{1,0:T(8,128)(2,1)S(1)}, u32[]{:S(2)}, u32[]{:S(2)}) %collective-permute-start.15) | collective-permute-done | bytes 65568 | tf_op jit(solution)/shard_map/ppermute | solution.py:20
  85.9 4.2 %collective-permute-done.16 = bf16[32,1024]{1,0:T(8,128)(2,1)S(1)} collective-permute-done((bf16[32,1024]{1,0:T(8,128)(2,1)S(1)}, bf16[32,1024]{1,0:T(8,128)(2,1)S(1)}, u32[]{:S(2)}, u32[]{:S(2)}) %collective-permute-start.16) | collective-permute-done | bytes 65568 | tf_op jit(solution)/shard_map/ppermute | solution.py:20
  92.1 1.5 collective-permute-start.18
  94.5 5.0 %collective-permute-done.17.refs_1_ = bf16[32,4224]{1,0:T(8,128)(2,1)S(1)} collective-permute-done((bf16[32,4224]{1,0:T(8,128)(2,1)S(1)}, bf16[32,4224]{1,0:T(8,128)(2,1)S(1)}, u32[]{:S(2)}, u32[]{:S(2)}) %collective-permute-start.17) | collective-permute-done | bytes 270368 | tf_op jit(solution)/shard_map/ppermute | solution.py:20
  99.5 2.0 collective-permute-done.18.refs_2_
  101.4 4.0 %collective-permute-done.19.refs_3_ = bf16[32,4224]{1,0:T(8,128)(2,1)S(1)} collective-permute-done((bf16[32,4224]{1,0:T(8,128)(2,1)S(1)}, bf16[32,4224]{1,0:T(8,128)(2,1)S(1)}, u32[]{:S(2)}, u32[]{:S(2)}) %collective-permute-start.19) | collective-permute-done | bytes 270368 | tf_op jit(solution)/shard_map/ppermute | solution.py:305
  105.4 1.7 collective-permute-done.20.refs_0_
  108.5 1.5 collective-permute-start.23
  110.9 1.9 collective-permute-start.25
  112.9 10.2 %shard_map.164 = (bf16[128,4096]{1,0:T(8,128)(2,1)S(1)}, bf16[128,4096]{1,0:T(8,128)(2,1)S(1)}) custom-call(bf16[128,4224]{1,0:T(8,128)(2,1)S(1)} %shard_map.163.own, bf16[128,4224]{1,0:T(8,128)(2,1)S(1)} %collective-permute-done.21.mate, bf16[4096,896]{1,0:T(8,128)(2,1)} %bitcast.106, bf16[4096,896]{1,0:T(8,128)(2,1)} %bitcast.110, ...), custom_call_target="tpu_custom_call" | custom-call | flops 5637144576 | bytes 30408704 | tf_op jit(solution)/shard_map/pallas_call | solution.py:277
  123.9 1.5 collective-permute-start.29
  127.4 1.5 collective-permute-start.32
  128.8 10.2 %shard_map.166 = (bf16[128,4096]{1,0:T(8,128)(2,1)S(1)}, bf16[128,4096]{1,0:T(8,128)(2,1)S(1)}) custom-call(bf16[128,4224]{1,0:T(8,128)(2,1)S(1)} %shard_map.165.own, bf16[128,4224]{1,0:T(8,128)(2,1)S(1)} %collective-permute-done.27.mate, bf16[4096,896]{1,0:T(8,128)(2,1)} %bitcast.107, bf16[4096,896]{1,0:T(8,128)(2,1)} %bitcast.111, ...), custom_call_target="tpu_custom_call" | custom-call | flops 5637144576 | bytes 30408704 | tf_op jit(solution)/shard_map/pallas_call | solution.py:277
  139.5 4.4 %collective-permute-done.32.refs_1_ = bf16[32,4224]{1,0:T(8,128)(2,1)S(1)} collective-permute-done((bf16[32,4224]{1,0:T(8,128)(2,1)S(1)}, bf16[32,4224]{1,0:T(8,128)(2,1)S(1)}, u32[]{:S(2)}, u32[]{:S(2)}) %collective-permute-start.32) | collective-permute-done | bytes 270368 | tf_op jit(solution)/shard_map/ppermute | solution.py:20
  145.9 1.5 collective-permute-start.35
  147.4 10.2 %shard_map.168 = (bf16[128,4096]{1,0:T(8,128)(2,1)S(1)}, bf16[128,4096]{1,0:T(8,128)(2,1)S(1)}) custom-call(bf16[128,4224]{1,0:T(8,128)(2,1)S(1)} %shard_map.167.own, bf16[128,4224]{1,0:T(8,128)(2,1)S(1)} %collective-permute-done.33.mate, bf16[4096,896]{1,0:T(8,128)(2,1)} %bitcast.108, bf16[4096,896]{1,0:T(8,128)(2,1)} %bitcast.112, ...), custom_call_target="tpu_custom_call" | custom-call | flops 5637144576 | bytes 30408704 | tf_op jit(solution)/shard_map/pallas_call | solution.py:277
  157.7 1.9 collective-permute-done.35
  161.5 1.5 collective-permute-start.40
  165.1 10.2 %shard_map.171 = (bf16[128,4096]{1,0:T(8,128)(2,1)S(1)}, bf16[128,4096]{1,0:T(8,128)(2,1)S(1)}) custom-call(bf16[128,4224]{1,0:T(8,128)(2,1)S(1)} %shard_map.170.own, bf16[128,4224]{1,0:T(8,128)(2,1)S(1)} %collective-permute-done.37.mate, bf16[4096,896]{1,0:T(8,128)(2,1)} %bitcast.109, bf16[4096,896]{1,0:T(8,128)(2,1)} %bitcast.113, ...), custom_call_target="tpu_custom_call" | custom-call | flops 5637144576 | bytes 30408704 | tf_op jit(solution)/shard_map/pallas_call | solution.py:277
  176.7 4.1 %collective-permute-done.43 = bf16[64,4096]{1,0:T(8,128)(2,1)S(1)} collective-permute-done((bf16[64,4096]{1,0:T(8,128)(2,1)S(1)}, bf16[64,4096]{1,0:T(8,128)(2,1)S(1)}, u32[]{:S(2)}, u32[]{:S(2)}) %collective-permute-start.43) | collective-permute-done | bytes 524320 | tf_op jit(solution)/shard_map/ppermute | solution.py:20
  180.9 1.5 collective-permute-start.44
  184.8 2.8 %collective-permute-done.42 = bf16[32,4096]{1,0:T(8,128)(2,1)S(1)} collective-permute-done((bf16[32,4096]{1,0:T(8,128)(2,1)S(1)}, bf16[32,4096]{1,0:T(8,128)(2,1)S(1)}, u32[]{:S(2)}, u32[]{:S(2)}) %collective-permute-start.42) | collective-permute-done | bytes 262176 | tf_op jit(solution)/shard_map/ppermute | solution.py:20
  187.6 2.7 %collective-permute-done.44 = bf16[32,4096]{1,0:T(8,128)(2,1)S(1)} collective-permute-done((bf16[32,4096]{1,0:T(8,128)(2,1)S(1)}, bf16[32,4096]{1,0:T(8,128)(2,1)S(1)}, u32[]{:S(2)}, u32[]{:S(2)}) %collective-permute-start.44) | collective-permute-done | bytes 262176 | tf_op jit(solution)/shard_map/ppermute | solution.py:20
  190.2 1.4 collective-permute-start.47
  192.9 2.3 %collective-permute-start.45 = (bf16[32,4096]{1,0:T(8,128)(2,1)S(1)}, bf16[32,4096]{1,0:T(8,128)(2,1)S(1)}, u32[]{:S(2)}, u32[]{:S(2)}) collective-permute-start(bf16[32,4096]{1,0:T(8,128)(2,1)S(1)} %add_convert_fusion.9), channel_id=1, source_target_pairs={{0,16},{4,20},{8,24},{12,28},{16,0},{20,4},{24,8},{28,12},{1,17},{... | collective-permute-start | bytes 786440 | tf_op jit(solution)/shard_map/ppermute | solution.py:20
  196.8 2.0 collective-permute-done.47
  199.0 1.7 collective-permute-start.50
  200.7 11.8 %collective-permute-done.45 = bf16[32,4096]{1,0:T(8,128)(2,1)S(1)} collective-permute-done((bf16[32,4096]{1,0:T(8,128)(2,1)S(1)}, bf16[32,4096]{1,0:T(8,128)(2,1)S(1)}, u32[]{:S(2)}, u32[]{:S(2)}) %collective-permute-start.45) | collective-permute-done | bytes 262176 | tf_op jit(solution)/shard_map/ppermute | solution.py:20
  (207 shorter events, 41.9 us)
Async XLA Ops:
  3.9 8.3 %collective-permute-start = (bf16[528,128]{1,0:T(8,128)(2,1)S(1)}, bf16[528,128]{1,0:T(8,128)(2,1)S(1)}, u32[]{:S(2)}, u32[]{:S(2)}) collective-permute-start(bf16[528,128]{1,0:T(8,128)(2,1)S(1)} %pad_maximum_fusion.1), channel_id=1, source_target_pairs={{0,4},{4,0},{8,12},{12,8},{16,20},{20,16},{24,28},{28,24},{1,5},{5... | collective-permute-start | bytes 405512 | tf_op jit(solution)/shard_map/ppermute | solution.py:20
  7.7 21.0 %collective-permute-start.4 = (bf16[256,512]{1,0:T(8,128)(2,1)}, bf16[256,512]{1,0:T(8,128)(2,1)}, u32[]{:S(2)}, u32[]{:S(2)}) collective-permute-start(bf16[256,512]{1,0:T(8,128)(2,1)} %slice.274), channel_id=1, source_target_pairs={{0,8},{4,12},{8,0},{12,4},{16,24},{20,28},{24,16},{28,20},{1,9},{5... | collective-permute-start | bytes 786440 | tf_op jit(solution)/shard_map/ppermute | solution.py:20
  13.6 7.1 %collective-permute-start.1 = (bf16[528,128]{1,0:T(8,128)(2,1)}, bf16[528,128]{1,0:T(8,128)(2,1)S(1)}, u32[]{:S(2)}, u32[]{:S(2)}) collective-permute-start(bf16[528,128]{1,0:T(8,128)(2,1)} %pad_maximum_fusion.2), channel_id=1, source_target_pairs={{0,8},{4,12},{8,0},{12,4},{16,24},{20,28},{24,16},{28,20},{1,9},{5... | collective-permute-start | bytes 405512 | tf_op jit(solution)/shard_map/ppermute | solution.py:20
  14.2 13.0 %collective-permute-start.2 = (bf16[528,128]{1,0:T(8,128)(2,1)}, bf16[528,128]{1,0:T(8,128)(2,1)S(1)}, u32[]{:S(2)}, u32[]{:S(2)}) collective-permute-start(bf16[528,128]{1,0:T(8,128)(2,1)} %pad_maximum_fusion.2), channel_id=1, source_target_pairs={{0,16},{4,20},{8,24},{12,28},{16,0},{20,4},{24,8},{28,12},{1,17},{... | collective-permute-start | bytes 405512 | tf_op jit(solution)/shard_map/ppermute | solution.py:20
  16.7 11.1 %collective-permute-start.3 = (bf16[528,128]{1,0:T(8,128)(2,1)}, bf16[528,128]{1,0:T(8,128)(2,1)}, u32[]{:S(2)}, u32[]{:S(2)}) collective-permute-start(bf16[528,128]{1,0:T(8,128)(2,1)} %pad_maximum_fusion.2), channel_id=1, source_target_pairs={{0,24},{4,28},{8,16},{12,20},{16,8},{20,12},{24,0},{28,4},{1,25},{... | collective-permute-start | bytes 405512 | tf_op jit(solution)/shard_map/ppermute | solution.py:20
  31.7 5.0 %collective-permute-start.5 = (bf16[512,128]{1,0:T(8,128)(2,1)S(1)}, bf16[512,128]{1,0:T(8,128)(2,1)S(1)}, u32[]{:S(2)}, u32[]{:S(2)}) collective-permute-start(bf16[512,128]{1,0:T(8,128)(2,1)S(1)} %get-tuple-element.118), channel_id=1, source_target_pairs={{0,4},{4,0},{8,12},{12,8},{16,20},{20,16},{24,28},{28,24},{1,5},{5... | collective-permute-start | bytes 393224 | tf_op jit(solution)/shard_map/ppermute | solution.py:20
  33.1 32.0 %collective-permute-start.11 = (bf16[768,512]{1,0:T(8,128)(2,1)}, bf16[768,512]{1,0:T(8,128)(2,1)}, u32[]{:S(2)}, u32[]{:S(2)}) collective-permute-start(bf16[768,512]{1,0:T(8,128)(2,1)} %slice.275), channel_id=1, source_target_pairs={{0,8},{4,12},{8,0},{12,4},{16,24},{20,28},{24,16},{28,20},{1,9},{5... | collective-permute-start | bytes 2359304 | tf_op jit(solution)/shard_map/ppermute | solution.py:20
  38.4 11.1 %collective-permute-start.6 = (bf16[128,1024]{0,1:T(8,128)(2,1)S(1)}, bf16[128,1024]{0,1:T(8,128)(2,1)S(1)}, u32[]{:S(2)}, u32[]{:S(2)}) collective-permute-start(bf16[128,1024]{0,1:T(8,128)(2,1)S(1)} %pad_maximum_fusion), channel_id=1, source_target_pairs={{0,4},{4,0},{8,12},{12,8},{16,20},{20,16},{24,28},{28,24},{1,5},{5... | collective-permute-start | bytes 786440 | tf_op jit(solution)/shard_map/ppermute | solution.py:20
  39.7 18.6 %collective-permute-start.8 = (bf16[128,1024]{0,1:T(8,128)(2,1)S(1)}, bf16[128,1024]{0,1:T(8,128)(2,1)S(1)}, u32[]{:S(2)}, u32[]{:S(2)}) collective-permute-start(bf16[128,1024]{0,1:T(8,128)(2,1)S(1)} %pad_maximum_fusion), channel_id=1, source_target_pairs={{0,20},{4,16},{8,28},{12,24},{16,4},{20,0},{24,12},{28,8},{1,21},{... | collective-permute-start | bytes 786440 | tf_op jit(solution)/shard_map/ppermute | solution.py:20
  43.4 17.8 %collective-permute-start.7 = (bf16[128,1024]{0,1:T(8,128)(2,1)S(1)}, bf16[128,1024]{0,1:T(8,128)(2,1)S(1)}, u32[]{:S(2)}, u32[]{:S(2)}) collective-permute-start(bf16[128,1024]{0,1:T(8,128)(2,1)S(1)} %pad_maximum_fusion), channel_id=1, source_target_pairs={{0,16},{4,20},{8,24},{12,28},{16,0},{20,4},{24,8},{28,12},{1,17},{... | collective-permute-start | bytes 786440 | tf_op jit(solution)/shard_map/ppermute | solution.py:20
  49.5 11.8 %collective-permute-start.9 = (f32[128]{0:T(128)S(1)}, f32[128]{0:T(128)S(1)}, u32[]{:S(2)}, u32[]{:S(2)}) collective-permute-start(f32[128]{0:T(128)S(1)} %get-tuple-element.62), channel_id=1, source_target_pairs={{0,1},{1,0},{2,3},{3,2},{4,5},{5,4},{6,7},{7,6},{8,9},{9,8},{10,11... | collective-permute-start | bytes 1544 | tf_op jit(solution)/shard_map/ppermute | solution.py:20
  69.8 8.4 %collective-permute-start.13 = (bf16[128,1024]{1,0:T(8,128)(2,1)S(1)}, bf16[128,1024]{1,0:T(8,128)(2,1)S(1)}, u32[]{:S(2)}, u32[]{:S(2)}) collective-permute-start(bf16[128,1024]{1,0:T(8,128)(2,1)S(1)} %slice.349), channel_id=1, source_target_pairs={{0,2},{1,3},{2,0},{3,1},{4,6},{5,7},{6,4},{7,5},{8,10},{9,11},{10,... | collective-permute-start | bytes 786440 | tf_op jit(solution)/shard_map/ppermute | solution.py:20
  78.3 5.1 %collective-permute-start.14 = (bf16[32,1024]{1,0:T(8,128)(2,1)S(1)}, bf16[32,1024]{1,0:T(8,128)(2,1)S(1)}, u32[]{:S(2)}, u32[]{:S(2)}) collective-permute-start(bf16[32,1024]{1,0:T(8,128)(2,1)S(1)} %get-tuple-element.127), channel_id=1, source_target_pairs={{0,4},{4,0},{8,12},{12,8},{16,20},{20,16},{24,28},{28,24},{1,5},{5... | collective-permute-start | bytes 196616 | tf_op jit(solution)/shard_map/ppermute | solution.py:20
  80.0 5.9 %collective-permute-start.15 = (bf16[32,1024]{1,0:T(8,128)(2,1)S(1)}, bf16[32,1024]{1,0:T(8,128)(2,1)S(1)}, u32[]{:S(2)}, u32[]{:S(2)}) collective-permute-start(bf16[32,1024]{1,0:T(8,128)(2,1)S(1)} %get-tuple-element.126), channel_id=1, source_target_pairs={{0,16},{4,20},{8,24},{12,28},{16,0},{20,4},{24,8},{28,12},{1,17},{... | collective-permute-start | bytes 196616 | tf_op jit(solution)/shard_map/ppermute | solution.py:20
  83.4 6.7 %collective-permute-start.16 = (bf16[32,1024]{1,0:T(8,128)(2,1)S(1)}, bf16[32,1024]{1,0:T(8,128)(2,1)S(1)}, u32[]{:S(2)}, u32[]{:S(2)}) collective-permute-start(bf16[32,1024]{1,0:T(8,128)(2,1)S(1)} %get-tuple-element.125), channel_id=1, source_target_pairs={{0,20},{4,16},{8,28},{12,24},{16,4},{20,0},{24,12},{28,8},{1,21},{... | collective-permute-start | bytes 196616 | tf_op jit(solution)/shard_map/ppermute | solution.py:20
  90.9 8.6 %collective-permute-start.17 = (bf16[32,4224]{1,0:T(8,128)(2,1)S(1)}, bf16[32,4224]{1,0:T(8,128)(2,1)S(1)}, u32[]{:S(2)}, u32[]{:S(2)}) collective-permute-start(bf16[32,4224]{1,0:T(8,128)(2,1)S(1)} %concatenate.48.refs_0_), channel_id=1, source_target_pairs={{0,4},{4,0},{8,12},{12,8},{16,20},{20,16},{24,28},{28,24},{1,5},{5... | collective-permute-start | bytes 811016 | tf_op jit(solution)/shard_map/ppermute | solution.py:20
  92.1 9.3 %collective-permute-start.18 = (bf16[32,4224]{1,0:T(8,128)(2,1)S(1)}, bf16[32,4224]{1,0:T(8,128)(2,1)S(1)}, u32[]{:S(2)}, u32[]{:S(2)}) collective-permute-start(bf16[32,4224]{1,0:T(8,128)(2,1)S(1)} %concatenate.48.refs_0_), channel_id=1, source_target_pairs={{0,2},{1,3},{2,0},{3,1},{4,6},{5,7},{6,4},{7,5},{8,10},{9,11},{10,... | collective-permute-start | bytes 811016 | tf_op jit(solution)/shard_map/ppermute | solution.py:20
  93.6 11.8 %collective-permute-start.19 = (bf16[32,4224]{1,0:T(8,128)(2,1)S(1)}, bf16[32,4224]{1,0:T(8,128)(2,1)S(1)}, u32[]{:S(2)}, u32[]{:S(2)}) collective-permute-start(bf16[32,4224]{1,0:T(8,128)(2,1)S(1)} %concatenate.48.refs_0_), channel_id=1, source_target_pairs={{0,6},{1,7},{2,4},{3,5},{4,2},{5,3},{6,0},{7,1},{8,14},{9,15},{10,... | collective-permute-start | bytes 811016 | tf_op jit(solution)/shard_map/ppermute | solution.py:305
  94.4 12.7 %collective-permute-start.20 = (bf16[32,4224]{1,0:T(8,128)(2,1)S(1)}, bf16[32,4224]{1,0:T(8,128)(2,1)S(1)}, u32[]{:S(2)}, u32[]{:S(2)}) collective-permute-start(bf16[32,4224]{1,0:T(8,128)(2,1)S(1)} %concatenate.48.refs_0_), channel_id=1, source_target_pairs={{0,16},{4,20},{8,24},{12,28},{16,0},{20,4},{24,8},{28,12},{1,17},{... | collective-permute-start | bytes 811016 | tf_op jit(solution)/shard_map/ppermute | solution.py:20
  107.2 3.7 %collective-permute-start.21 = (bf16[128,4224]{1,0:T(8,128)(2,1)S(1)}, bf16[128,4224]{1,0:T(8,128)(2,1)S(1)}, u32[]{:S(2)}, u32[]{:S(2)}) collective-permute-start(bf16[128,4224]{1,0:T(8,128)(2,1)S(1)} %shard_map.163.own), channel_id=1, source_target_pairs={{0,1},{1,0},{2,3},{3,2},{4,5},{5,4},{6,7},{7,6},{8,9},{9,8},{10,11... | collective-permute-start | bytes 3244040 | tf_op jit(solution)/shard_map/ppermute | solution.py:20
  107.3 15.8 %collective-permute-start.26 = (bf16[32,4224]{1,0:T(8,128)(2,1)S(1)}, bf16[32,4224]{1,0:T(8,128)(2,1)S(1)}, u32[]{:S(2)}, u32[]{:S(2)}) collective-permute-start(bf16[32,4224]{1,0:T(8,128)(2,1)S(1)} %concatenate.48.refs_0_), channel_id=1, source_target_pairs={{0,8},{4,12},{8,0},{12,4},{16,24},{20,28},{24,16},{28,20},{1,9},{5... | collective-permute-start | bytes 811016 | tf_op jit(solution)/shard_map/ppermute | solution.py:20
  107.4 15.8 %collective-permute-start.22 = (bf16[32,4224]{1,0:T(8,128)(2,1)S(1)}, bf16[32,4224]{1,0:T(8,128)(2,1)S(1)}, u32[]{:S(2)}, u32[]{:S(2)}) collective-permute-start(bf16[32,4224]{1,0:T(8,128)(2,1)S(1)} %collective-permute-done.20.refs_0_), channel_id=1, source_target_pairs={{0,4},{4,0},{8,12},{12,8},{16,20},{20,16},{24,28},{28,24},{1,5},{5... | collective-permute-start | bytes 811016 | tf_op jit(solution)/shard_map/ppermute | solution.py:20
  108.5 14.6 %collective-permute-start.23 = (bf16[32,4224]{1,0:T(8,128)(2,1)S(1)}, bf16[32,4224]{1,0:T(8,128)(2,1)S(1)}, u32[]{:S(2)}, u32[]{:S(2)}) collective-permute-start(bf16[32,4224]{1,0:T(8,128)(2,1)S(1)} %collective-permute-done.20.refs_0_), channel_id=1, source_target_pairs={{0,2},{1,3},{2,0},{3,1},{4,6},{5,7},{6,4},{7,5},{8,10},{9,11},{10,... | collective-permute-start | bytes 811016 | tf_op jit(solution)/shard_map/ppermute | solution.py:20
  110.0 13.2 %collective-permute-start.24 = (bf16[32,4224]{1,0:T(8,128)(2,1)S(1)}, bf16[32,4224]{1,0:T(8,128)(2,1)S(1)}, u32[]{:S(2)}, u32[]{:S(2)}) collective-permute-start(bf16[32,4224]{1,0:T(8,128)(2,1)S(1)} %collective-permute-done.20.refs_0_), channel_id=1, source_target_pairs={{0,6},{1,7},{2,4},{3,5},{4,2},{5,3},{6,0},{7,1},{8,14},{9,15},{10,... | collective-permute-start | bytes 811016 | tf_op jit(solution)/shard_map/ppermute | solution.py:305
  110.9 12.3 %collective-permute-start.25 = (bf16[32,4224]{1,0:T(8,128)(2,1)S(1)}, bf16[32,4224]{1,0:T(8,128)(2,1)S(1)}, u32[]{:S(2)}, u32[]{:S(2)}) collective-permute-start(bf16[32,4224]{1,0:T(8,128)(2,1)S(1)} %collective-permute-done.20.refs_0_), channel_id=1, source_target_pairs={{0,8},{4,12},{8,0},{12,4},{16,24},{20,28},{24,16},{28,20},{1,9},{5... | collective-permute-start | bytes 811016 | tf_op jit(solution)/shard_map/ppermute | solution.py:20
  123.3 4.1 %collective-permute-start.27 = (bf16[128,4224]{1,0:T(8,128)(2,1)S(1)}, bf16[128,4224]{1,0:T(8,128)(2,1)S(1)}, u32[]{:S(2)}, u32[]{:S(2)}) collective-permute-start(bf16[128,4224]{1,0:T(8,128)(2,1)S(1)} %shard_map.165.own), channel_id=1, source_target_pairs={{0,1},{1,0},{2,3},{3,2},{4,5},{5,4},{6,7},{7,6},{8,9},{9,8},{10,11... | collective-permute-start | bytes 3244040 | tf_op jit(solution)/shard_map/ppermute | solution.py:20
  123.4 20.6 %collective-permute-start.28 = (bf16[128,4096]{1,0:T(8,128)(2,1)S(1)}, bf16[128,4096]{1,0:T(8,128)(2,1)S(1)}, u32[]{:S(2)}, u32[]{:S(2)}) collective-permute-start(bf16[128,4096]{1,0:T(8,128)(2,1)S(1)} %get-tuple-element.79), channel_id=1, source_target_pairs={{0,1},{1,0},{2,3},{3,2},{4,5},{5,4},{6,7},{7,6},{8,9},{9,8},{10,11... | collective-permute-start | bytes 3145736 | tf_op jit(solution)/shard_map/ppermute | solution.py:20
  123.9 15.2 %collective-permute-start.29 = (bf16[32,4224]{1,0:T(8,128)(2,1)S(1)}, bf16[32,4224]{1,0:T(8,128)(2,1)S(1)}, u32[]{:S(2)}, u32[]{:S(2)}) collective-permute-start(bf16[32,4224]{1,0:T(8,128)(2,1)S(1)} %collective-permute-done.25.refs_0_), channel_id=1, source_target_pairs={{0,2},{1,3},{2,0},{3,1},{4,6},{5,7},{6,4},{7,5},{8,10},{9,11},{10,... | collective-permute-start | bytes 811016 | tf_op jit(solution)/shard_map/ppermute | solution.py:20
  125.3 13.7 %collective-permute-start.30 = (bf16[32,4224]{1,0:T(8,128)(2,1)S(1)}, bf16[32,4224]{1,0:T(8,128)(2,1)S(1)}, u32[]{:S(2)}, u32[]{:S(2)}) collective-permute-start(bf16[32,4224]{1,0:T(8,128)(2,1)S(1)} %collective-permute-done.25.refs_0_), channel_id=1, source_target_pairs={{0,4},{4,0},{8,12},{12,8},{16,20},{20,16},{24,28},{28,24},{1,5},{5... | collective-permute-start | bytes 811016 | tf_op jit(solution)/shard_map/ppermute | solution.py:20
  126.4 13.1 %collective-permute-start.31 = (bf16[32,4224]{1,0:T(8,128)(2,1)S(1)}, bf16[32,4224]{1,0:T(8,128)(2,1)S(1)}, u32[]{:S(2)}, u32[]{:S(2)}) collective-permute-start(bf16[32,4224]{1,0:T(8,128)(2,1)S(1)} %collective-permute-done.25.refs_0_), channel_id=1, source_target_pairs={{0,6},{1,7},{2,4},{3,5},{4,2},{5,3},{6,0},{7,1},{8,14},{9,15},{10,... | collective-permute-start | bytes 811016 | tf_op jit(solution)/shard_map/ppermute | solution.py:305
  127.4 16.6 %collective-permute-start.32 = (bf16[32,4224]{1,0:T(8,128)(2,1)S(1)}, bf16[32,4224]{1,0:T(8,128)(2,1)S(1)}, u32[]{:S(2)}, u32[]{:S(2)}) collective-permute-start(bf16[32,4224]{1,0:T(8,128)(2,1)S(1)} %collective-permute-done.26.refs_0_), channel_id=1, source_target_pairs={{0,2},{1,3},{2,0},{3,1},{4,6},{5,7},{6,4},{7,5},{8,10},{9,11},{10,... | collective-permute-start | bytes 811016 | tf_op jit(solution)/shard_map/ppermute | solution.py:20
  144.1 15.5 %collective-permute-start.34 = (bf16[128,4096]{1,0:T(8,128)(2,1)S(1)}, bf16[128,4096]{1,0:T(8,128)(2,1)S(1)}, u32[]{:S(2)}, u32[]{:S(2)}) collective-permute-start(bf16[128,4096]{1,0:T(8,128)(2,1)S(1)} %get-tuple-element.89), channel_id=1, source_target_pairs={{0,1},{1,0},{2,3},{3,2},{4,5},{5,4},{6,7},{7,6},{8,9},{9,8},{10,11... | collective-permute-start | bytes 3145736 | tf_op jit(solution)/shard_map/ppermute | solution.py:20
  144.7 15.0 %collective-permute-start.36 = (bf16[64,4224]{1,0:T(8,128)(2,1)S(1)}, bf16[64,4224]{1,0:T(8,128)(2,1)S(1)}, u32[]{:S(2)}, u32[]{:S(2)}) collective-permute-start(bf16[64,4224]{1,0:T(8,128)(2,1)S(1)} %shard_map.169), channel_id=1, source_target_pairs={{0,4},{4,0},{8,12},{12,8},{16,20},{20,16},{24,28},{28,24},{1,5},{5... | collective-permute-start | bytes 1622024 | tf_op jit(solution)/shard_map/ppermute | solution.py:20
  145.9 13.7 %collective-permute-start.35 = (bf16[64,4096]{1,0:T(8,128)(2,1)S(1)}, bf16[64,4096]{1,0:T(8,128)(2,1)S(1)}, u32[]{:S(2)}, u32[]{:S(2)}) collective-permute-start(bf16[64,4096]{1,0:T(8,128)(2,1)S(1)} %add_convert_fusion.2), channel_id=1, source_target_pairs={{0,2},{1,3},{2,0},{3,1},{4,6},{5,7},{6,4},{7,5},{8,10},{9,11},{10,... | collective-permute-start | bytes 1572872 | tf_op jit(solution)/shard_map/ppermute | solution.py:20
  159.7 5.4 %collective-permute-start.37 = (bf16[128,4224]{1,0:T(8,128)(2,1)S(1)}, bf16[128,4224]{1,0:T(8,128)(2,1)S(1)}, u32[]{:S(2)}, u32[]{:S(2)}) collective-permute-start(bf16[128,4224]{1,0:T(8,128)(2,1)S(1)} %shard_map.170.own), channel_id=1, source_target_pairs={{0,1},{1,0},{2,3},{3,2},{4,5},{5,4},{6,7},{7,6},{8,9},{9,8},{10,11... | collective-permute-start | bytes 3244040 | tf_op jit(solution)/shard_map/ppermute | solution.py:20
  159.8 4.2 %collective-permute-start.38 = (bf16[128,4096]{1,0:T(8,128)(2,1)S(1)}, bf16[128,4096]{1,0:T(8,128)(2,1)S(1)}, u32[]{:S(2)}, u32[]{:S(2)}) collective-permute-start(bf16[128,4096]{1,0:T(8,128)(2,1)S(1)} %get-tuple-element.95), channel_id=1, source_target_pairs={{0,1},{1,0},{2,3},{3,2},{4,5},{5,4},{6,7},{7,6},{8,9},{9,8},{10,11... | collective-permute-start | bytes 3145736 | tf_op jit(solution)/shard_map/ppermute | solution.py:20
  160.4 15.0 %collective-permute-start.39 = (bf16[32,4096]{1,0:T(8,128)(2,1)S(1)}, bf16[32,4096]{1,0:T(8,128)(2,1)S(1)}, u32[]{:S(2)}, u32[]{:S(2)}) collective-permute-start(bf16[32,4096]{1,0:T(8,128)(2,1)S(1)} %add_convert_fusion.13), channel_id=1, source_target_pairs={{0,4},{4,0},{8,12},{12,8},{16,20},{20,16},{24,28},{28,24},{1,5},{5... | collective-permute-start | bytes 786440 | tf_op jit(solution)/shard_map/ppermute | solution.py:20
  161.5 13.8 %collective-permute-start.40 = (bf16[64,4096]{1,0:T(8,128)(2,1)S(1)}, bf16[64,4096]{1,0:T(8,128)(2,1)S(1)}, u32[]{:S(2)}, u32[]{:S(2)}) collective-permute-start(bf16[64,4096]{1,0:T(8,128)(2,1)S(1)} %add_convert_fusion.1), channel_id=1, source_target_pairs={{0,2},{1,3},{2,0},{3,1},{4,6},{5,7},{6,4},{7,5},{8,10},{9,11},{10,... | collective-permute-start | bytes 1572872 | tf_op jit(solution)/shard_map/ppermute | solution.py:20
  164.1 16.7 %collective-permute-start.43 = (bf16[64,4096]{1,0:T(8,128)(2,1)S(1)}, bf16[64,4096]{1,0:T(8,128)(2,1)S(1)}, u32[]{:S(2)}, u32[]{:S(2)}) collective-permute-start(bf16[64,4096]{1,0:T(8,128)(2,1)S(1)} %add_convert_fusion), channel_id=1, source_target_pairs={{0,4},{4,0},{8,12},{12,8},{16,20},{20,16},{24,28},{28,24},{1,5},{5... | collective-permute-start | bytes 1572872 | tf_op jit(solution)/shard_map/ppermute | solution.py:20
  175.4 7.1 %collective-permute-start.41 = (bf16[128,4096]{1,0:T(8,128)(2,1)S(1)}, bf16[128,4096]{1,0:T(8,128)(2,1)S(1)}, u32[]{:S(2)}, u32[]{:S(2)}) collective-permute-start(bf16[128,4096]{1,0:T(8,128)(2,1)S(1)} %get-tuple-element.102), channel_id=1, source_target_pairs={{0,1},{1,0},{2,3},{3,2},{4,5},{5,4},{6,7},{7,6},{8,9},{9,8},{10,11... | collective-permute-start | bytes 3145736 | tf_op jit(solution)/shard_map/ppermute | solution.py:20
  175.6 12.0 %collective-permute-start.42 = (bf16[32,4096]{1,0:T(8,128)(2,1)S(1)}, bf16[32,4096]{1,0:T(8,128)(2,1)S(1)}, u32[]{:S(2)}, u32[]{:S(2)}) collective-permute-start(bf16[32,4096]{1,0:T(8,128)(2,1)S(1)} %add_convert_fusion.11), channel_id=1, source_target_pairs={{0,4},{4,0},{8,12},{12,8},{16,20},{20,16},{24,28},{28,24},{1,5},{5... | collective-permute-start | bytes 786440 | tf_op jit(solution)/shard_map/ppermute | solution.py:20
  180.9 9.3 %collective-permute-start.44 = (bf16[32,4096]{1,0:T(8,128)(2,1)S(1)}, bf16[32,4096]{1,0:T(8,128)(2,1)S(1)}, u32[]{:S(2)}, u32[]{:S(2)}) collective-permute-start(bf16[32,4096]{1,0:T(8,128)(2,1)S(1)} %add_convert_fusion.10), channel_id=1, source_target_pairs={{0,2},{1,3},{2,0},{3,1},{4,6},{5,7},{6,4},{7,5},{8,10},{9,11},{10,... | collective-permute-start | bytes 786440 | tf_op jit(solution)/shard_map/ppermute | solution.py:20
  182.7 13.6 %collective-permute-start.49 = (bf16[32,4096]{1,0:T(8,128)(2,1)S(1)}, bf16[32,4096]{1,0:T(8,128)(2,1)S(1)}, u32[]{:S(2)}, u32[]{:S(2)}) collective-permute-start(bf16[32,4096]{1,0:T(8,128)(2,1)S(1)} %get-tuple-element.123), channel_id=1, source_target_pairs={{0,6},{1,7},{2,4},{3,5},{4,2},{5,3},{6,0},{7,1},{8,14},{9,15},{10,... | collective-permute-start | bytes 786440 | tf_op jit(solution)/shard_map/ppermute | solution.py:305
  183.7 13.1 %collective-permute-start.48 = (bf16[32,4096]{1,0:T(8,128)(2,1)S(1)}, bf16[32,4096]{1,0:T(8,128)(2,1)S(1)}, u32[]{:S(2)}, u32[]{:S(2)}) collective-permute-start(bf16[32,4096]{1,0:T(8,128)(2,1)S(1)} %get-tuple-element.124), channel_id=1, source_target_pairs={{0,4},{4,0},{8,12},{12,8},{16,20},{20,16},{24,28},{28,24},{1,5},{5... | collective-permute-start | bytes 786440 | tf_op jit(solution)/shard_map/ppermute | solution.py:20
  190.2 8.6 %collective-permute-start.47 = (bf16[32,4096]{1,0:T(8,128)(2,1)S(1)}, bf16[32,4096]{1,0:T(8,128)(2,1)S(1)}, u32[]{:S(2)}, u32[]{:S(2)}) collective-permute-start(bf16[32,4096]{1,0:T(8,128)(2,1)S(1)} %get-tuple-element.110), channel_id=1, source_target_pairs={{0,2},{1,3},{2,0},{3,1},{4,6},{5,7},{6,4},{7,5},{8,10},{9,11},{10,... | collective-permute-start | bytes 786440 | tf_op jit(solution)/shard_map/ppermute | solution.py:20
  191.8 8.9 %collective-permute-start.46 = (bf16[32,4096]{1,0:T(8,128)(2,1)S(1)}, bf16[32,4096]{1,0:T(8,128)(2,1)S(1)}, u32[]{:S(2)}, u32[]{:S(2)}) collective-permute-start(bf16[32,4096]{1,0:T(8,128)(2,1)S(1)} %add_convert_fusion.8), channel_id=1, source_target_pairs={{0,24},{4,28},{8,16},{12,20},{16,8},{20,12},{24,0},{28,4},{1,25},{... | collective-permute-start | bytes 786440 | tf_op jit(solution)/shard_map/ppermute | solution.py:20
  192.9 19.6 %collective-permute-start.45 = (bf16[32,4096]{1,0:T(8,128)(2,1)S(1)}, bf16[32,4096]{1,0:T(8,128)(2,1)S(1)}, u32[]{:S(2)}, u32[]{:S(2)}) collective-permute-start(bf16[32,4096]{1,0:T(8,128)(2,1)S(1)} %add_convert_fusion.9), channel_id=1, source_target_pairs={{0,16},{4,20},{8,24},{12,28},{16,0},{20,4},{24,8},{28,12},{1,17},{... | collective-permute-start | bytes 786440 | tf_op jit(solution)/shard_map/ppermute | solution.py:20
  199.0 13.6 %collective-permute-start.50 = (bf16[32,4096]{1,0:T(8,128)(2,1)S(1)}, bf16[32,4096]{1,0:T(8,128)(2,1)S(1)}, u32[]{:S(2)}, u32[]{:S(2)}) collective-permute-start(bf16[32,4096]{1,0:T(8,128)(2,1)S(1)} %add_convert_fusion.5), channel_id=1, source_target_pairs={{0,8},{4,12},{8,0},{12,4},{16,24},{20,28},{24,16},{28,20},{1,9},{5... | collective-permute-start | bytes 786440 | tf_op jit(solution)/shard_map/ppermute | solution.py:20
  (18 other events, 127.8 us)

commit v7 on v6

--- a/solution.py
+++ b/solution.py
@@ -150,12 +150,12 @@
     scale = lax.rsqrt(own_squares / (width * n_exp) + eps_norm)
     full = jnp.stack(arrived).reshape(len(group), n_exp, quarter, width)
     full = full.swapaxes(0, 1).reshape(-1, width)
-    full, scale = lax.optimization_barrier((full, scale))
     partial = mm(full, both).astype(BF)
     for flip in (1, 2):
         cut = partial.shape[0] // 2
         got = swap(partial[cut:], "exp", flip)
         partial = (partial[:cut].astype(F32) + got.astype(F32)).astype(BF)
+    partial, scale = lax.optimization_barrier((partial, scale))
     partial = partial.reshape(len(group), quarter, -1)
     columns = out_proj.shape[1]
     blocks = [None] * n_ctx
@@ -446,10 +446,10 @@
         bring_second(i + 1)
         if i > 0:
             bring_first(i + 2)
-        beside = (got[-1:], far_got[: count - 2], parts[-1:], near[i + 1 :], planes[i + 2 :])
+        beside = (got[-1:], far_got[: count - 2], parts[-1:], near[i + 1 : i + 2], planes[i + 2 :])
         results.append(experts(*rows[i], w_gate[0], w_up[0], w_down[0], pick))
         results[i], beside = together(results[i], beside)
-        got[-1:], far_got[: count - 2], parts[-1:], near[i + 1 :], planes[i + 2 :] = beside
+        got[-1:], far_got[: count - 2], parts[-1:], near[i + 1 : i + 2], planes[i + 2 :] = beside
     for i in range(count, count + 4):
         sums(i)
     for part in parts:

time: 214 us -> 209 us (0.977)
  waiting for transfers between devices: 91 us -> 87.3 us
    ppermute x47, waiting for transfers between devices: 85.5 us -> 83.2 us  [swap(): return lax.ppermute(x, axis, [(i, i ^ flip) for i in range(size)])]
  transfers between devices with their start and end apart: 51 -> 51, of which waited for: 27 -> 28; matrix products, arithmetic and copies ran while one was open for 5% -> 5% of each run, Pallas kernels for 19% -> 20%
where the time goes in v7:
time: 209 us
  waiting for transfers between devices  87.3 us (42%)
  starting transfers between devices  57 us (27%)
  Pallas kernels  41.2 us (20%)
  other arithmetic  11.4 us (5%)
  local copies, waits for them, and re-layouts  6.33 us (3%)
  matrix products  4.51 us (2%)
    ppermute x47, waiting for transfers between devices, swap(): return lax.ppermute(x, axis, [(i, i ^ flip) for i in range(size)])  83.2 us
    ppermute x47, starting transfers between devices, swap(): return lax.ppermute(x, axis, [(i, i ^ flip) for i in range(size)])  55 us
    pallas_call x4, Pallas kernels, experts(): pl.pallas_call(expert_kernel, out_shape=(out, out), in_specs=[anywhere] *...  40.9 us
  transfers between devices with their start and end apart: 51, of which 28 were waited for; matrix products, arithmetic and copies ran while one was open for 5% of the time, Pallas kernels for 20%

profile of v7, /device:TPU:0, one launch (start us, length us, event | category | flops | bytes accessed | tf_op | source)
XLA Modules:
  0.0 208.5 jit_solution(7520448064652821833)
XLA Ops:
  3.9 3.0 %collective-permute-start = (bf16[528,128]{1,0:T(8,128)(2,1)S(1)}, bf16[528,128]{1,0:T(8,128)(2,1)S(1)}, u32[]{:S(2)}, u32[]{:S(2)}) collective-permute-start(bf16[528,128]{1,0:T(8,128)(2,1)S(1)} %pad_maximum_fusion.1), channel_id=1, source_target_pairs={{0,4},{4,0},{8,12},{12,8},{16,20},{20,16},{24,28},{28,24},{1,5},{5... | collective-permute-start | bytes 405512 | tf_op jit(solution)/shard_map/ppermute | solution.py:20
  7.7 1.6 collective-permute-start.4
  14.2 2.6 %collective-permute-start.2 = (bf16[528,128]{1,0:T(8,128)(2,1)}, bf16[528,128]{1,0:T(8,128)(2,1)S(1)}, u32[]{:S(2)}, u32[]{:S(2)}) collective-permute-start(bf16[528,128]{1,0:T(8,128)(2,1)} %pad_maximum_fusion.2), channel_id=1, source_target_pairs={{0,16},{4,20},{8,24},{12,28},{16,0},{20,4},{24,8},{28,12},{1,17},{... | collective-permute-start | bytes 405512 | tf_op jit(solution)/shard_map/ppermute | solution.py:20
  18.2 2.5 %collective-permute-done.1 = bf16[528,128]{1,0:T(8,128)(2,1)S(1)} collective-permute-done((bf16[528,128]{1,0:T(8,128)(2,1)}, bf16[528,128]{1,0:T(8,128)(2,1)S(1)}, u32[]{:S(2)}, u32[]{:S(2)}) %collective-permute-start.1) | collective-permute-done | bytes 135200 | tf_op jit(solution)/shard_map/ppermute | solution.py:20
  20.8 6.4 %collective-permute-done.2 = bf16[528,128]{1,0:T(8,128)(2,1)S(1)} collective-permute-done((bf16[528,128]{1,0:T(8,128)(2,1)}, bf16[528,128]{1,0:T(8,128)(2,1)S(1)}, u32[]{:S(2)}, u32[]{:S(2)}) %collective-permute-start.2) | collective-permute-done | bytes 135200 | tf_op jit(solution)/shard_map/ppermute | solution.py:20
  33.1 1.5 collective-permute-start.9
  34.7 2.1 %collective-permute-done.5 = bf16[512,128]{1,0:T(8,128)(2,1)S(1)} collective-permute-done((bf16[512,128]{1,0:T(8,128)(2,1)S(1)}, bf16[512,128]{1,0:T(8,128)(2,1)S(1)}, u32[]{:S(2)}, u32[]{:S(2)}) %collective-permute-start.5) | collective-permute-done | bytes 131104 | tf_op jit(solution)/shard_map/ppermute | solution.py:20
  39.7 3.7 %collective-permute-start.8 = (bf16[128,1024]{0,1:T(8,128)(2,1)S(1)}, bf16[128,1024]{0,1:T(8,128)(2,1)S(1)}, u32[]{:S(2)}, u32[]{:S(2)}) collective-permute-start(bf16[128,1024]{0,1:T(8,128)(2,1)S(1)} %pad_maximum_fusion), channel_id=1, source_target_pairs={{0,20},{4,16},{8,28},{12,24},{16,4},{20,0},{24,12},{28,8},{1,21},{... | collective-permute-start | bytes 786440 | tf_op jit(solution)/shard_map/ppermute | solution.py:20
  43.6 6.0 %collective-permute-done.6 = bf16[128,1024]{0,1:T(8,128)(2,1)S(1)} collective-permute-done((bf16[128,1024]{0,1:T(8,128)(2,1)S(1)}, bf16[128,1024]{0,1:T(8,128)(2,1)S(1)}, u32[]{:S(2)}, u32[]{:S(2)}) %collective-permute-start.6) | collective-permute-done | bytes 262176 | tf_op jit(solution)/shard_map/ppermute | solution.py:20
  49.7 8.7 %collective-permute-done.8 = bf16[128,1024]{0,1:T(8,128)(2,1)S(1)} collective-permute-done((bf16[128,1024]{0,1:T(8,128)(2,1)S(1)}, bf16[128,1024]{0,1:T(8,128)(2,1)S(1)}, u32[]{:S(2)}, u32[]{:S(2)}) %collective-permute-start.8) | collective-permute-done | bytes 262176 | tf_op jit(solution)/shard_map/ppermute | solution.py:20
  58.5 2.7 %collective-permute-done.7 = bf16[128,1024]{0,1:T(8,128)(2,1)S(1)} collective-permute-done((bf16[128,1024]{0,1:T(8,128)(2,1)S(1)}, bf16[128,1024]{0,1:T(8,128)(2,1)S(1)}, u32[]{:S(2)}, u32[]{:S(2)}) %collective-permute-start.7) | collective-permute-done | bytes 262176 | tf_op jit(solution)/shard_map/ppermute | solution.py:20
  62.0 2.5 %fusion.6 = bf16[512,1024]{1,0:T(8,128)(2,1)S(1)} fusion(bf16[512,1024]{1,0:T(8,128)(2,1)S(1)} %bitcast.115, bf16[768,512]{1,0:T(8,128)(2,1)} %collective-permute-done.9, bf16[256,512]{1,0:T(8,128)(2,1)} %collective-permute-done.4, bf16[1024,512]{1,0:T(8,128)(2,1)S(1)} %copy-done.2), kind=kOutput, calls=%fused_computation.6 | convolution fusion | flops 1080557568 | bytes 4194304 | tf_op jit(solution)/shard_map/dot_general | solution.py:24
  64.8 1.7 collective-permute-done.10
  66.7 1.5 collective-permute-start.11
  70.0 5.3 %collective-permute-done.13 = f32[128]{0:T(128)S(1)} collective-permute-done((f32[128]{0:T(128)S(1)}, f32[128]{0:T(128)S(1)}, u32[]{:S(2)}, u32[]{:S(2)}) %collective-permute-start.13) | collective-permute-done | bytes 544 | tf_op jit(solution)/shard_map/ppermute | solution.py:20
  75.4 1.7 collective-permute-start.14
  77.1 2.9 %collective-permute-start.15 = (bf16[32,1024]{1,0:T(8,128)(2,1)S(1)}, bf16[32,1024]{1,0:T(8,128)(2,1)S(1)}, u32[]{:S(2)}, u32[]{:S(2)}) collective-permute-start(bf16[32,1024]{1,0:T(8,128)(2,1)S(1)} %get-tuple-element.124), channel_id=1, source_target_pairs={{0,16},{4,20},{8,24},{12,28},{16,0},{20,4},{24,8},{28,12},{1,17},{... | collective-permute-start | bytes 196616 | tf_op jit(solution)/shard_map/ppermute | solution.py:20
  80.1 4.0 %collective-permute-done.15 = bf16[32,1024]{1,0:T(8,128)(2,1)S(1)} collective-permute-done((bf16[32,1024]{1,0:T(8,128)(2,1)S(1)}, bf16[32,1024]{1,0:T(8,128)(2,1)S(1)}, u32[]{:S(2)}, u32[]{:S(2)}) %collective-permute-start.15) | collective-permute-done | bytes 65568 | tf_op jit(solution)/shard_map/ppermute | solution.py:20
  84.1 2.7 %collective-permute-done.16 = bf16[32,1024]{1,0:T(8,128)(2,1)S(1)} collective-permute-done((bf16[32,1024]{1,0:T(8,128)(2,1)S(1)}, bf16[32,1024]{1,0:T(8,128)(2,1)S(1)}, u32[]{:S(2)}, u32[]{:S(2)}) %collective-permute-start.16) | collective-permute-done | bytes 65568 | tf_op jit(solution)/shard_map/ppermute | solution.py:20
  88.8 1.5 collective-permute-start.18
  91.1 5.8 %collective-permute-done.17.refs_1_ = bf16[32,4224]{1,0:T(8,128)(2,1)S(1)} collective-permute-done((bf16[32,4224]{1,0:T(8,128)(2,1)S(1)}, bf16[32,4224]{1,0:T(8,128)(2,1)S(1)}, u32[]{:S(2)}, u32[]{:S(2)}) %collective-permute-start.17) | collective-permute-done | bytes 270368 | tf_op jit(solution)/shard_map/ppermute | solution.py:20
  97.8 2.8 %collective-permute-done.19.refs_3_ = bf16[32,4224]{1,0:T(8,128)(2,1)S(1)} collective-permute-done((bf16[32,4224]{1,0:T(8,128)(2,1)S(1)}, bf16[32,4224]{1,0:T(8,128)(2,1)S(1)}, u32[]{:S(2)}, u32[]{:S(2)}) %collective-permute-start.19) | collective-permute-done | bytes 270368 | tf_op jit(solution)/shard_map/ppermute | solution.py:305
  100.6 2.4 %collective-permute-done.20.refs_0_ = bf16[32,4224]{1,0:T(8,128)(2,1)S(1)} collective-permute-done((bf16[32,4224]{1,0:T(8,128)(2,1)S(1)}, bf16[32,4224]{1,0:T(8,128)(2,1)S(1)}, u32[]{:S(2)}, u32[]{:S(2)}) %collective-permute-start.20) | collective-permute-done | bytes 270368 | tf_op jit(solution)/shard_map/ppermute | solution.py:20
  103.3 1.6 collective-permute-start.22
  104.9 1.5 collective-permute-start.23
  106.8 1.9 collective-permute-start.25
  108.8 10.2 %shard_map.164 = (bf16[128,4096]{1,0:T(8,128)(2,1)S(1)}, bf16[128,4096]{1,0:T(8,128)(2,1)S(1)}) custom-call(bf16[128,4224]{1,0:T(8,128)(2,1)S(1)} %shard_map.163.own, bf16[128,4224]{1,0:T(8,128)(2,1)S(1)} %collective-permute-done.21.mate, bf16[4096,896]{1,0:T(8,128)(2,1)} %bitcast.102, bf16[4096,896]{1,0:T(8,128)(2,1)} %bitcast.106, ...), custom_call_target="tpu_custom_call" | custom-call | flops 5637144576 | bytes 30408704 | tf_op jit(solution)/shard_map/pallas_call | solution.py:277
  119.8 1.5 collective-permute-start.29
  121.3 1.5 collective-permute-start.30
  123.3 1.5 collective-permute-start.35
  124.8 10.2 %shard_map.166 = (bf16[128,4096]{1,0:T(8,128)(2,1)S(1)}, bf16[128,4096]{1,0:T(8,128)(2,1)S(1)}) custom-call(bf16[128,4224]{1,0:T(8,128)(2,1)S(1)} %shard_map.165.own, bf16[128,4224]{1,0:T(8,128)(2,1)S(1)} %collective-permute-done.27.mate, bf16[4096,896]{1,0:T(8,128)(2,1)} %bitcast.103, bf16[4096,896]{1,0:T(8,128)(2,1)} %bitcast.107, ...), custom_call_target="tpu_custom_call" | custom-call | flops 5637144576 | bytes 30408704 | tf_op jit(solution)/shard_map/pallas_call | solution.py:277
  136.6 3.3 %collective-permute-done.35.refs_1_ = bf16[32,4224]{1,0:T(8,128)(2,1)S(1)} collective-permute-done((bf16[32,4224]{1,0:T(8,128)(2,1)S(1)}, bf16[32,4224]{1,0:T(8,128)(2,1)S(1)}, u32[]{:S(2)}, u32[]{:S(2)}) %collective-permute-start.35) | collective-permute-done | bytes 270368 | tf_op jit(solution)/shard_map/ppermute | solution.py:20
  139.9 1.6 collective-permute-start.36
  141.7 1.5 collective-permute-start.34
  143.2 10.2 %shard_map.168 = (bf16[128,4096]{1,0:T(8,128)(2,1)S(1)}, bf16[128,4096]{1,0:T(8,128)(2,1)S(1)}) custom-call(bf16[128,4224]{1,0:T(8,128)(2,1)S(1)} %shard_map.167.own, bf16[128,4224]{1,0:T(8,128)(2,1)S(1)} %collective-permute-done.32.mate, bf16[4096,896]{1,0:T(8,128)(2,1)} %bitcast.104, bf16[4096,896]{1,0:T(8,128)(2,1)} %bitcast.108, ...), custom_call_target="tpu_custom_call" | custom-call | flops 5637144576 | bytes 30408704 | tf_op jit(solution)/shard_map/pallas_call | solution.py:277
  155.9 1.6 collective-permute-start.40
  159.5 10.2 %shard_map.171 = (bf16[128,4096]{1,0:T(8,128)(2,1)S(1)}, bf16[128,4096]{1,0:T(8,128)(2,1)S(1)}) custom-call(bf16[128,4224]{1,0:T(8,128)(2,1)S(1)} %shard_map.170.own, bf16[128,4224]{1,0:T(8,128)(2,1)S(1)} %collective-permute-done.37.mate, bf16[4096,896]{1,0:T(8,128)(2,1)} %bitcast.105, bf16[4096,896]{1,0:T(8,128)(2,1)} %bitcast.109, ...), custom_call_target="tpu_custom_call" | custom-call | flops 5637144576 | bytes 30408704 | tf_op jit(solution)/shard_map/pallas_call | solution.py:277
  170.0 1.6 collective-permute-start.42
  171.6 4.1 %collective-permute-done.43 = bf16[64,4096]{1,0:T(8,128)(2,1)S(1)} collective-permute-done((bf16[64,4096]{1,0:T(8,128)(2,1)S(1)}, bf16[64,4096]{1,0:T(8,128)(2,1)S(1)}, u32[]{:S(2)}, u32[]{:S(2)}) %collective-permute-start.43) | collective-permute-done | bytes 524320 | tf_op jit(solution)/shard_map/ppermute | solution.py:20
  175.8 1.5 collective-permute-start.44
  177.8 1.9 collective-permute-start.48
  179.7 3.0 %collective-permute-done.42 = bf16[32,4096]{1,0:T(8,128)(2,1)S(1)} collective-permute-done((bf16[32,4096]{1,0:T(8,128)(2,1)S(1)}, bf16[32,4096]{1,0:T(8,128)(2,1)S(1)}, u32[]{:S(2)}, u32[]{:S(2)}) %collective-permute-start.42) | collective-permute-done | bytes 262176 | tf_op jit(solution)/shard_map/ppermute | solution.py:20
  182.7 2.4 %collective-permute-done.44 = bf16[32,4096]{1,0:T(8,128)(2,1)S(1)} collective-permute-done((bf16[32,4096]{1,0:T(8,128)(2,1)S(1)}, bf16[32,4096]{1,0:T(8,128)(2,1)S(1)}, u32[]{:S(2)}, u32[]{:S(2)}) %collective-permute-start.44) | collective-permute-done | bytes 262176 | tf_op jit(solution)/shard_map/ppermute | solution.py:20
  185.2 1.4 collective-permute-start.47
  188.1 2.0 collective-permute-start.45
  191.7 2.0 collective-permute-done.47
  193.9 1.7 collective-permute-start.50
  195.6 11.8 %collective-permute-done.45 = bf16[32,4096]{1,0:T(8,128)(2,1)S(1)} collective-permute-done((bf16[32,4096]{1,0:T(8,128)(2,1)S(1)}, bf16[32,4096]{1,0:T(8,128)(2,1)S(1)}, u32[]{:S(2)}, u32[]{:S(2)}) %collective-permute-start.45) | collective-permute-done | bytes 262176 | tf_op jit(solution)/shard_map/ppermute | solution.py:20
  (207 shorter events, 40.3 us)
Async XLA Ops:
  3.9 8.3 %collective-permute-start = (bf16[528,128]{1,0:T(8,128)(2,1)S(1)}, bf16[528,128]{1,0:T(8,128)(2,1)S(1)}, u32[]{:S(2)}, u32[]{:S(2)}) collective-permute-start(bf16[528,128]{1,0:T(8,128)(2,1)S(1)} %pad_maximum_fusion.1), channel_id=1, source_target_pairs={{0,4},{4,0},{8,12},{12,8},{16,20},{20,16},{24,28},{28,24},{1,5},{5... | collective-permute-start | bytes 405512 | tf_op jit(solution)/shard_map/ppermute | solution.py:20
  7.7 21.0 %collective-permute-start.4 = (bf16[256,512]{1,0:T(8,128)(2,1)}, bf16[256,512]{1,0:T(8,128)(2,1)}, u32[]{:S(2)}, u32[]{:S(2)}) collective-permute-start(bf16[256,512]{1,0:T(8,128)(2,1)} %slice.274), channel_id=1, source_target_pairs={{0,8},{4,12},{8,0},{12,4},{16,24},{20,28},{24,16},{28,20},{1,9},{5... | collective-permute-start | bytes 786440 | tf_op jit(solution)/shard_map/ppermute | solution.py:20
  13.6 7.1 %collective-permute-start.1 = (bf16[528,128]{1,0:T(8,128)(2,1)}, bf16[528,128]{1,0:T(8,128)(2,1)S(1)}, u32[]{:S(2)}, u32[]{:S(2)}) collective-permute-start(bf16[528,128]{1,0:T(8,128)(2,1)} %pad_maximum_fusion.2), channel_id=1, source_target_pairs={{0,8},{4,12},{8,0},{12,4},{16,24},{20,28},{24,16},{28,20},{1,9},{5... | collective-permute-start | bytes 405512 | tf_op jit(solution)/shard_map/ppermute | solution.py:20
  14.2 13.0 %collective-permute-start.2 = (bf16[528,128]{1,0:T(8,128)(2,1)}, bf16[528,128]{1,0:T(8,128)(2,1)S(1)}, u32[]{:S(2)}, u32[]{:S(2)}) collective-permute-start(bf16[528,128]{1,0:T(8,128)(2,1)} %pad_maximum_fusion.2), channel_id=1, source_target_pairs={{0,16},{4,20},{8,24},{12,28},{16,0},{20,4},{24,8},{28,12},{1,17},{... | collective-permute-start | bytes 405512 | tf_op jit(solution)/shard_map/ppermute | solution.py:20
  16.7 11.1 %collective-permute-start.3 = (bf16[528,128]{1,0:T(8,128)(2,1)}, bf16[528,128]{1,0:T(8,128)(2,1)}, u32[]{:S(2)}, u32[]{:S(2)}) collective-permute-start(bf16[528,128]{1,0:T(8,128)(2,1)} %pad_maximum_fusion.2), channel_id=1, source_target_pairs={{0,24},{4,28},{8,16},{12,20},{16,8},{20,12},{24,0},{28,4},{1,25},{... | collective-permute-start | bytes 405512 | tf_op jit(solution)/shard_map/ppermute | solution.py:20
  31.7 5.0 %collective-permute-start.5 = (bf16[512,128]{1,0:T(8,128)(2,1)S(1)}, bf16[512,128]{1,0:T(8,128)(2,1)S(1)}, u32[]{:S(2)}, u32[]{:S(2)}) collective-permute-start(bf16[512,128]{1,0:T(8,128)(2,1)S(1)} %get-tuple-element.116), channel_id=1, source_target_pairs={{0,4},{4,0},{8,12},{12,8},{16,20},{20,16},{24,28},{28,24},{1,5},{5... | collective-permute-start | bytes 393224 | tf_op jit(solution)/shard_map/ppermute | solution.py:20
  33.1 29.0 %collective-permute-start.9 = (bf16[768,512]{1,0:T(8,128)(2,1)}, bf16[768,512]{1,0:T(8,128)(2,1)}, u32[]{:S(2)}, u32[]{:S(2)}) collective-permute-start(bf16[768,512]{1,0:T(8,128)(2,1)} %slice.275), channel_id=1, source_target_pairs={{0,8},{4,12},{8,0},{12,4},{16,24},{20,28},{24,16},{28,20},{1,9},{5... | collective-permute-start | bytes 2359304 | tf_op jit(solution)/shard_map/ppermute | solution.py:20
  38.4 11.1 %collective-permute-start.6 = (bf16[128,1024]{0,1:T(8,128)(2,1)S(1)}, bf16[128,1024]{0,1:T(8,128)(2,1)S(1)}, u32[]{:S(2)}, u32[]{:S(2)}) collective-permute-start(bf16[128,1024]{0,1:T(8,128)(2,1)S(1)} %pad_maximum_fusion), channel_id=1, source_target_pairs={{0,4},{4,0},{8,12},{12,8},{16,20},{20,16},{24,28},{28,24},{1,5},{5... | collective-permute-start | bytes 786440 | tf_op jit(solution)/shard_map/ppermute | solution.py:20
  39.7 18.6 %collective-permute-start.8 = (bf16[128,1024]{0,1:T(8,128)(2,1)S(1)}, bf16[128,1024]{0,1:T(8,128)(2,1)S(1)}, u32[]{:S(2)}, u32[]{:S(2)}) collective-permute-start(bf16[128,1024]{0,1:T(8,128)(2,1)S(1)} %pad_maximum_fusion), channel_id=1, source_target_pairs={{0,20},{4,16},{8,28},{12,24},{16,4},{20,0},{24,12},{28,8},{1,21},{... | collective-permute-start | bytes 786440 | tf_op jit(solution)/shard_map/ppermute | solution.py:20
  43.4 17.8 %collective-permute-start.7 = (bf16[128,1024]{0,1:T(8,128)(2,1)S(1)}, bf16[128,1024]{0,1:T(8,128)(2,1)S(1)}, u32[]{:S(2)}, u32[]{:S(2)}) collective-permute-start(bf16[128,1024]{0,1:T(8,128)(2,1)S(1)} %pad_maximum_fusion), channel_id=1, source_target_pairs={{0,16},{4,20},{8,24},{12,28},{16,0},{20,4},{24,8},{28,12},{1,17},{... | collective-permute-start | bytes 786440 | tf_op jit(solution)/shard_map/ppermute | solution.py:20
  66.7 8.6 %collective-permute-start.11 = (bf16[128,1024]{1,0:T(8,128)(2,1)S(1)}, bf16[128,1024]{1,0:T(8,128)(2,1)S(1)}, u32[]{:S(2)}, u32[]{:S(2)}) collective-permute-start(bf16[128,1024]{1,0:T(8,128)(2,1)S(1)} %slice.349), channel_id=1, source_target_pairs={{0,2},{1,3},{2,0},{3,1},{4,6},{5,7},{6,4},{7,5},{8,10},{9,11},{10,... | collective-permute-start | bytes 786440 | tf_op jit(solution)/shard_map/ppermute | solution.py:20
  69.4 5.8 %collective-permute-start.13 = (f32[128]{0:T(128)S(1)}, f32[128]{0:T(128)S(1)}, u32[]{:S(2)}, u32[]{:S(2)}) collective-permute-start(f32[128]{0:T(128)S(1)} %add.243), channel_id=1, source_target_pairs={{0,2},{1,3},{2,0},{3,1},{4,6},{5,7},{6,4},{7,5},{8,10},{9,11},{10,... | collective-permute-start | bytes 1544 | tf_op jit(solution)/shard_map/ppermute | solution.py:20
  75.4 4.7 %collective-permute-start.14 = (bf16[32,1024]{1,0:T(8,128)(2,1)S(1)}, bf16[32,1024]{1,0:T(8,128)(2,1)S(1)}, u32[]{:S(2)}, u32[]{:S(2)}) collective-permute-start(bf16[32,1024]{1,0:T(8,128)(2,1)S(1)} %get-tuple-element.125), channel_id=1, source_target_pairs={{0,4},{4,0},{8,12},{12,8},{16,20},{20,16},{24,28},{28,24},{1,5},{5... | collective-permute-start | bytes 196616 | tf_op jit(solution)/shard_map/ppermute | solution.py:20
  77.1 6.9 %collective-permute-start.15 = (bf16[32,1024]{1,0:T(8,128)(2,1)S(1)}, bf16[32,1024]{1,0:T(8,128)(2,1)S(1)}, u32[]{:S(2)}, u32[]{:S(2)}) collective-permute-start(bf16[32,1024]{1,0:T(8,128)(2,1)S(1)} %get-tuple-element.124), channel_id=1, source_target_pairs={{0,16},{4,20},{8,24},{12,28},{16,0},{20,4},{24,8},{28,12},{1,17},{... | collective-permute-start | bytes 196616 | tf_op jit(solution)/shard_map/ppermute | solution.py:20
  80.1 6.7 %collective-permute-start.16 = (bf16[32,1024]{1,0:T(8,128)(2,1)S(1)}, bf16[32,1024]{1,0:T(8,128)(2,1)S(1)}, u32[]{:S(2)}, u32[]{:S(2)}) collective-permute-start(bf16[32,1024]{1,0:T(8,128)(2,1)S(1)} %get-tuple-element.123), channel_id=1, source_target_pairs={{0,20},{4,16},{8,28},{12,24},{16,4},{20,0},{24,12},{28,8},{1,21},{... | collective-permute-start | bytes 196616 | tf_op jit(solution)/shard_map/ppermute | solution.py:20
  87.6 9.4 %collective-permute-start.17 = (bf16[32,4224]{1,0:T(8,128)(2,1)S(1)}, bf16[32,4224]{1,0:T(8,128)(2,1)S(1)}, u32[]{:S(2)}, u32[]{:S(2)}) collective-permute-start(bf16[32,4224]{1,0:T(8,128)(2,1)S(1)} %concatenate.48.refs_0_), channel_id=1, source_target_pairs={{0,4},{4,0},{8,12},{12,8},{16,20},{20,16},{24,28},{28,24},{1,5},{5... | collective-permute-start | bytes 811016 | tf_op jit(solution)/shard_map/ppermute | solution.py:20
  88.8 9.0 %collective-permute-start.18 = (bf16[32,4224]{1,0:T(8,128)(2,1)S(1)}, bf16[32,4224]{1,0:T(8,128)(2,1)S(1)}, u32[]{:S(2)}, u32[]{:S(2)}) collective-permute-start(bf16[32,4224]{1,0:T(8,128)(2,1)S(1)} %concatenate.48.refs_0_), channel_id=1, source_target_pairs={{0,2},{1,3},{2,0},{3,1},{4,6},{5,7},{6,4},{7,5},{8,10},{9,11},{10,... | collective-permute-start | bytes 811016 | tf_op jit(solution)/shard_map/ppermute | solution.py:20
  90.3 10.4 %collective-permute-start.19 = (bf16[32,4224]{1,0:T(8,128)(2,1)S(1)}, bf16[32,4224]{1,0:T(8,128)(2,1)S(1)}, u32[]{:S(2)}, u32[]{:S(2)}) collective-permute-start(bf16[32,4224]{1,0:T(8,128)(2,1)S(1)} %concatenate.48.refs_0_), channel_id=1, source_target_pairs={{0,6},{1,7},{2,4},{3,5},{4,2},{5,3},{6,0},{7,1},{8,14},{9,15},{10,... | collective-permute-start | bytes 811016 | tf_op jit(solution)/shard_map/ppermute | solution.py:305
  91.1 11.9 %collective-permute-start.20 = (bf16[32,4224]{1,0:T(8,128)(2,1)S(1)}, bf16[32,4224]{1,0:T(8,128)(2,1)S(1)}, u32[]{:S(2)}, u32[]{:S(2)}) collective-permute-start(bf16[32,4224]{1,0:T(8,128)(2,1)S(1)} %concatenate.48.refs_0_), channel_id=1, source_target_pairs={{0,16},{4,20},{8,24},{12,28},{16,0},{20,4},{24,8},{28,12},{1,17},{... | collective-permute-start | bytes 811016 | tf_op jit(solution)/shard_map/ppermute | solution.py:20
  103.2 15.8 %collective-permute-start.26 = (bf16[32,4224]{1,0:T(8,128)(2,1)S(1)}, bf16[32,4224]{1,0:T(8,128)(2,1)S(1)}, u32[]{:S(2)}, u32[]{:S(2)}) collective-permute-start(bf16[32,4224]{1,0:T(8,128)(2,1)S(1)} %concatenate.48.refs_0_), channel_id=1, source_target_pairs={{0,8},{4,12},{8,0},{12,4},{16,24},{20,28},{24,16},{28,20},{1,9},{5... | collective-permute-start | bytes 811016 | tf_op jit(solution)/shard_map/ppermute | solution.py:20
  103.3 15.8 %collective-permute-start.22 = (bf16[32,4224]{1,0:T(8,128)(2,1)S(1)}, bf16[32,4224]{1,0:T(8,128)(2,1)S(1)}, u32[]{:S(2)}, u32[]{:S(2)}) collective-permute-start(bf16[32,4224]{1,0:T(8,128)(2,1)S(1)} %collective-permute-done.20.refs_0_), channel_id=1, source_target_pairs={{0,4},{4,0},{8,12},{12,8},{16,20},{20,16},{24,28},{28,24},{1,5},{5... | collective-permute-start | bytes 811016 | tf_op jit(solution)/shard_map/ppermute | solution.py:20
  104.9 14.1 %collective-permute-start.23 = (bf16[32,4224]{1,0:T(8,128)(2,1)S(1)}, bf16[32,4224]{1,0:T(8,128)(2,1)S(1)}, u32[]{:S(2)}, u32[]{:S(2)}) collective-permute-start(bf16[32,4224]{1,0:T(8,128)(2,1)S(1)} %collective-permute-done.20.refs_0_), channel_id=1, source_target_pairs={{0,2},{1,3},{2,0},{3,1},{4,6},{5,7},{6,4},{7,5},{8,10},{9,11},{10,... | collective-permute-start | bytes 811016 | tf_op jit(solution)/shard_map/ppermute | solution.py:20
  106.4 12.8 %collective-permute-start.24 = (bf16[32,4224]{1,0:T(8,128)(2,1)S(1)}, bf16[32,4224]{1,0:T(8,128)(2,1)S(1)}, u32[]{:S(2)}, u32[]{:S(2)}) collective-permute-start(bf16[32,4224]{1,0:T(8,128)(2,1)S(1)} %collective-permute-done.20.refs_0_), channel_id=1, source_target_pairs={{0,6},{1,7},{2,4},{3,5},{4,2},{5,3},{6,0},{7,1},{8,14},{9,15},{10,... | collective-permute-start | bytes 811016 | tf_op jit(solution)/shard_map/ppermute | solution.py:305
  106.8 12.3 %collective-permute-start.25 = (bf16[32,4224]{1,0:T(8,128)(2,1)S(1)}, bf16[32,4224]{1,0:T(8,128)(2,1)S(1)}, u32[]{:S(2)}, u32[]{:S(2)}) collective-permute-start(bf16[32,4224]{1,0:T(8,128)(2,1)S(1)} %collective-permute-done.20.refs_0_), channel_id=1, source_target_pairs={{0,8},{4,12},{8,0},{12,4},{16,24},{20,28},{24,16},{28,20},{1,9},{5... | collective-permute-start | bytes 811016 | tf_op jit(solution)/shard_map/ppermute | solution.py:20
  119.2 4.1 %collective-permute-start.27 = (bf16[128,4224]{1,0:T(8,128)(2,1)S(1)}, bf16[128,4224]{1,0:T(8,128)(2,1)S(1)}, u32[]{:S(2)}, u32[]{:S(2)}) collective-permute-start(bf16[128,4224]{1,0:T(8,128)(2,1)S(1)} %shard_map.165.own), channel_id=1, source_target_pairs={{0,1},{1,0},{2,3},{3,2},{4,5},{5,4},{6,7},{7,6},{8,9},{9,8},{10,11... | collective-permute-start | bytes 3244040 | tf_op jit(solution)/shard_map/ppermute | solution.py:20
  119.3 16.7 %collective-permute-start.28 = (bf16[128,4096]{1,0:T(8,128)(2,1)S(1)}, bf16[128,4096]{1,0:T(8,128)(2,1)S(1)}, u32[]{:S(2)}, u32[]{:S(2)}) collective-permute-start(bf16[128,4096]{1,0:T(8,128)(2,1)S(1)} %get-tuple-element.78), channel_id=1, source_target_pairs={{0,1},{1,0},{2,3},{3,2},{4,5},{5,4},{6,7},{7,6},{8,9},{9,8},{10,11... | collective-permute-start | bytes 3145736 | tf_op jit(solution)/shard_map/ppermute | solution.py:20
  119.8 15.2 %collective-permute-start.29 = (bf16[32,4224]{1,0:T(8,128)(2,1)S(1)}, bf16[32,4224]{1,0:T(8,128)(2,1)S(1)}, u32[]{:S(2)}, u32[]{:S(2)}) collective-permute-start(bf16[32,4224]{1,0:T(8,128)(2,1)S(1)} %collective-permute-done.25.refs_0_), channel_id=1, source_target_pairs={{0,2},{1,3},{2,0},{3,1},{4,6},{5,7},{6,4},{7,5},{8,10},{9,11},{10,... | collective-permute-start | bytes 811016 | tf_op jit(solution)/shard_map/ppermute | solution.py:20
  121.3 13.7 %collective-permute-start.30 = (bf16[32,4224]{1,0:T(8,128)(2,1)S(1)}, bf16[32,4224]{1,0:T(8,128)(2,1)S(1)}, u32[]{:S(2)}, u32[]{:S(2)}) collective-permute-start(bf16[32,4224]{1,0:T(8,128)(2,1)S(1)} %collective-permute-done.25.refs_0_), channel_id=1, source_target_pairs={{0,4},{4,0},{8,12},{12,8},{16,20},{20,16},{24,28},{28,24},{1,5},{5... | collective-permute-start | bytes 811016 | tf_op jit(solution)/shard_map/ppermute | solution.py:20
  122.8 13.1 %collective-permute-start.31 = (bf16[32,4224]{1,0:T(8,128)(2,1)S(1)}, bf16[32,4224]{1,0:T(8,128)(2,1)S(1)}, u32[]{:S(2)}, u32[]{:S(2)}) collective-permute-start(bf16[32,4224]{1,0:T(8,128)(2,1)S(1)} %collective-permute-done.25.refs_0_), channel_id=1, source_target_pairs={{0,6},{1,7},{2,4},{3,5},{4,2},{5,3},{6,0},{7,1},{8,14},{9,15},{10,... | collective-permute-start | bytes 811016 | tf_op jit(solution)/shard_map/ppermute | solution.py:305
  123.3 16.6 %collective-permute-start.35 = (bf16[32,4224]{1,0:T(8,128)(2,1)S(1)}, bf16[32,4224]{1,0:T(8,128)(2,1)S(1)}, u32[]{:S(2)}, u32[]{:S(2)}) collective-permute-start(bf16[32,4224]{1,0:T(8,128)(2,1)S(1)} %collective-permute-done.26.refs_0_), channel_id=1, source_target_pairs={{0,2},{1,3},{2,0},{3,1},{4,6},{5,7},{6,4},{7,5},{8,10},{9,11},{10,... | collective-permute-start | bytes 811016 | tf_op jit(solution)/shard_map/ppermute | solution.py:20
  136.0 7.1 %collective-permute-start.32 = (bf16[128,4224]{1,0:T(8,128)(2,1)S(1)}, bf16[128,4224]{1,0:T(8,128)(2,1)S(1)}, u32[]{:S(2)}, u32[]{:S(2)}) collective-permute-start(bf16[128,4224]{1,0:T(8,128)(2,1)S(1)} %shard_map.167.own), channel_id=1, source_target_pairs={{0,1},{1,0},{2,3},{3,2},{4,5},{5,4},{6,7},{7,6},{8,9},{9,8},{10,11... | collective-permute-start | bytes 3244040 | tf_op jit(solution)/shard_map/ppermute | solution.py:20
  136.1 18.4 %collective-permute-start.33 = (bf16[128,4096]{1,0:T(8,128)(2,1)S(1)}, bf16[128,4096]{1,0:T(8,128)(2,1)S(1)}, u32[]{:S(2)}, u32[]{:S(2)}) collective-permute-start(bf16[128,4096]{1,0:T(8,128)(2,1)S(1)} %get-tuple-element.88), channel_id=1, source_target_pairs={{0,1},{1,0},{2,3},{3,2},{4,5},{5,4},{6,7},{7,6},{8,9},{9,8},{10,11... | collective-permute-start | bytes 3145736 | tf_op jit(solution)/shard_map/ppermute | solution.py:20
  139.9 14.6 %collective-permute-start.36 = (bf16[64,4224]{1,0:T(8,128)(2,1)S(1)}, bf16[64,4224]{1,0:T(8,128)(2,1)S(1)}, u32[]{:S(2)}, u32[]{:S(2)}) collective-permute-start(bf16[64,4224]{1,0:T(8,128)(2,1)S(1)} %shard_map.169), channel_id=1, source_target_pairs={{0,4},{4,0},{8,12},{12,8},{16,20},{20,16},{24,28},{28,24},{1,5},{5... | collective-permute-start | bytes 1622024 | tf_op jit(solution)/shard_map/ppermute | solution.py:20
  141.7 12.9 %collective-permute-start.34 = (bf16[64,4096]{1,0:T(8,128)(2,1)S(1)}, bf16[64,4096]{1,0:T(8,128)(2,1)S(1)}, u32[]{:S(2)}, u32[]{:S(2)}) collective-permute-start(bf16[64,4096]{1,0:T(8,128)(2,1)S(1)} %add_convert_fusion.2), channel_id=1, source_target_pairs={{0,2},{1,3},{2,0},{3,1},{4,6},{5,7},{6,4},{7,5},{8,10},{9,11},{10,... | collective-permute-start | bytes 1572872 | tf_op jit(solution)/shard_map/ppermute | solution.py:20
  154.6 4.9 %collective-permute-start.37 = (bf16[128,4224]{1,0:T(8,128)(2,1)S(1)}, bf16[128,4224]{1,0:T(8,128)(2,1)S(1)}, u32[]{:S(2)}, u32[]{:S(2)}) collective-permute-start(bf16[128,4224]{1,0:T(8,128)(2,1)S(1)} %shard_map.170.own), channel_id=1, source_target_pairs={{0,1},{1,0},{2,3},{3,2},{4,5},{5,4},{6,7},{7,6},{8,9},{9,8},{10,11... | collective-permute-start | bytes 3244040 | tf_op jit(solution)/shard_map/ppermute | solution.py:20
  154.7 4.2 %collective-permute-start.38 = (bf16[128,4096]{1,0:T(8,128)(2,1)S(1)}, bf16[128,4096]{1,0:T(8,128)(2,1)S(1)}, u32[]{:S(2)}, u32[]{:S(2)}) collective-permute-start(bf16[128,4096]{1,0:T(8,128)(2,1)S(1)} %get-tuple-element.93), channel_id=1, source_target_pairs={{0,1},{1,0},{2,3},{3,2},{4,5},{5,4},{6,7},{7,6},{8,9},{9,8},{10,11... | collective-permute-start | bytes 3145736 | tf_op jit(solution)/shard_map/ppermute | solution.py:20
  155.3 14.5 %collective-permute-start.39 = (bf16[32,4096]{1,0:T(8,128)(2,1)S(1)}, bf16[32,4096]{1,0:T(8,128)(2,1)S(1)}, u32[]{:S(2)}, u32[]{:S(2)}) collective-permute-start(bf16[32,4096]{1,0:T(8,128)(2,1)S(1)} %add_convert_fusion.13), channel_id=1, source_target_pairs={{0,4},{4,0},{8,12},{12,8},{16,20},{20,16},{24,28},{28,24},{1,5},{5... | collective-permute-start | bytes 786440 | tf_op jit(solution)/shard_map/ppermute | solution.py:20
  155.9 13.8 %collective-permute-start.40 = (bf16[64,4096]{1,0:T(8,128)(2,1)S(1)}, bf16[64,4096]{1,0:T(8,128)(2,1)S(1)}, u32[]{:S(2)}, u32[]{:S(2)}) collective-permute-start(bf16[64,4096]{1,0:T(8,128)(2,1)S(1)} %add_convert_fusion.1), channel_id=1, source_target_pairs={{0,2},{1,3},{2,0},{3,1},{4,6},{5,7},{6,4},{7,5},{8,10},{9,11},{10,... | collective-permute-start | bytes 1572872 | tf_op jit(solution)/shard_map/ppermute | solution.py:20
  159.0 16.7 %collective-permute-start.43 = (bf16[64,4096]{1,0:T(8,128)(2,1)S(1)}, bf16[64,4096]{1,0:T(8,128)(2,1)S(1)}, u32[]{:S(2)}, u32[]{:S(2)}) collective-permute-start(bf16[64,4096]{1,0:T(8,128)(2,1)S(1)} %add_convert_fusion), channel_id=1, source_target_pairs={{0,4},{4,0},{8,12},{12,8},{16,20},{20,16},{24,28},{28,24},{1,5},{5... | collective-permute-start | bytes 1572872 | tf_op jit(solution)/shard_map/ppermute | solution.py:20
  169.8 7.5 %collective-permute-start.41 = (bf16[128,4096]{1,0:T(8,128)(2,1)S(1)}, bf16[128,4096]{1,0:T(8,128)(2,1)S(1)}, u32[]{:S(2)}, u32[]{:S(2)}) collective-permute-start(bf16[128,4096]{1,0:T(8,128)(2,1)S(1)} %get-tuple-element.100), channel_id=1, source_target_pairs={{0,1},{1,0},{2,3},{3,2},{4,5},{5,4},{6,7},{7,6},{8,9},{9,8},{10,11... | collective-permute-start | bytes 3145736 | tf_op jit(solution)/shard_map/ppermute | solution.py:20
  170.0 12.7 %collective-permute-start.42 = (bf16[32,4096]{1,0:T(8,128)(2,1)S(1)}, bf16[32,4096]{1,0:T(8,128)(2,1)S(1)}, u32[]{:S(2)}, u32[]{:S(2)}) collective-permute-start(bf16[32,4096]{1,0:T(8,128)(2,1)S(1)} %add_convert_fusion.11), channel_id=1, source_target_pairs={{0,4},{4,0},{8,12},{12,8},{16,20},{20,16},{24,28},{28,24},{1,5},{5... | collective-permute-start | bytes 786440 | tf_op jit(solution)/shard_map/ppermute | solution.py:20
  175.8 9.3 %collective-permute-start.44 = (bf16[32,4096]{1,0:T(8,128)(2,1)S(1)}, bf16[32,4096]{1,0:T(8,128)(2,1)S(1)}, u32[]{:S(2)}, u32[]{:S(2)}) collective-permute-start(bf16[32,4096]{1,0:T(8,128)(2,1)S(1)} %add_convert_fusion.10), channel_id=1, source_target_pairs={{0,2},{1,3},{2,0},{3,1},{4,6},{5,7},{6,4},{7,5},{8,10},{9,11},{10,... | collective-permute-start | bytes 786440 | tf_op jit(solution)/shard_map/ppermute | solution.py:20
  177.5 12.8 %collective-permute-start.49 = (bf16[32,4096]{1,0:T(8,128)(2,1)S(1)}, bf16[32,4096]{1,0:T(8,128)(2,1)S(1)}, u32[]{:S(2)}, u32[]{:S(2)}) collective-permute-start(bf16[32,4096]{1,0:T(8,128)(2,1)S(1)} %get-tuple-element.121), channel_id=1, source_target_pairs={{0,6},{1,7},{2,4},{3,5},{4,2},{5,3},{6,0},{7,1},{8,14},{9,15},{10,... | collective-permute-start | bytes 786440 | tf_op jit(solution)/shard_map/ppermute | solution.py:305
  177.8 13.9 %collective-permute-start.48 = (bf16[32,4096]{1,0:T(8,128)(2,1)S(1)}, bf16[32,4096]{1,0:T(8,128)(2,1)S(1)}, u32[]{:S(2)}, u32[]{:S(2)}) collective-permute-start(bf16[32,4096]{1,0:T(8,128)(2,1)S(1)} %get-tuple-element.122), channel_id=1, source_target_pairs={{0,4},{4,0},{8,12},{12,8},{16,20},{20,16},{24,28},{28,24},{1,5},{5... | collective-permute-start | bytes 786440 | tf_op jit(solution)/shard_map/ppermute | solution.py:20
  185.2 8.6 %collective-permute-start.47 = (bf16[32,4096]{1,0:T(8,128)(2,1)S(1)}, bf16[32,4096]{1,0:T(8,128)(2,1)S(1)}, u32[]{:S(2)}, u32[]{:S(2)}) collective-permute-start(bf16[32,4096]{1,0:T(8,128)(2,1)S(1)} %get-tuple-element.108), channel_id=1, source_target_pairs={{0,2},{1,3},{2,0},{3,1},{4,6},{5,7},{6,4},{7,5},{8,10},{9,11},{10,... | collective-permute-start | bytes 786440 | tf_op jit(solution)/shard_map/ppermute | solution.py:20
  186.7 8.9 %collective-permute-start.46 = (bf16[32,4096]{1,0:T(8,128)(2,1)S(1)}, bf16[32,4096]{1,0:T(8,128)(2,1)S(1)}, u32[]{:S(2)}, u32[]{:S(2)}) collective-permute-start(bf16[32,4096]{1,0:T(8,128)(2,1)S(1)} %add_convert_fusion.8), channel_id=1, source_target_pairs={{0,24},{4,28},{8,16},{12,20},{16,8},{20,12},{24,0},{28,4},{1,25},{... | collective-permute-start | bytes 786440 | tf_op jit(solution)/shard_map/ppermute | solution.py:20
  188.1 19.4 %collective-permute-start.45 = (bf16[32,4096]{1,0:T(8,128)(2,1)S(1)}, bf16[32,4096]{1,0:T(8,128)(2,1)S(1)}, u32[]{:S(2)}, u32[]{:S(2)}) collective-permute-start(bf16[32,4096]{1,0:T(8,128)(2,1)S(1)} %add_convert_fusion.9), channel_id=1, source_target_pairs={{0,16},{4,20},{8,24},{12,28},{16,0},{20,4},{24,8},{28,12},{1,17},{... | collective-permute-start | bytes 786440 | tf_op jit(solution)/shard_map/ppermute | solution.py:20
  193.9 13.6 %collective-permute-start.50 = (bf16[32,4096]{1,0:T(8,128)(2,1)S(1)}, bf16[32,4096]{1,0:T(8,128)(2,1)S(1)}, u32[]{:S(2)}, u32[]{:S(2)}) collective-permute-start(bf16[32,4096]{1,0:T(8,128)(2,1)S(1)} %add_convert_fusion.5), channel_id=1, source_target_pairs={{0,8},{4,12},{8,0},{12,4},{16,24},{20,28},{24,16},{28,20},{1,9},{5... | collective-permute-start | bytes 786440 | tf_op jit(solution)/shard_map/ppermute | solution.py:20
  (18 other events, 126.5 us)

commit v8 on v7

--- a/solution.py
+++ b/solution.py
@@ -39,6 +39,51 @@
     rows = packed.shape[0] - 2 * heads
     tail = packed[rows:, 0].astype(F32)
     return packed[:rows].astype(F32), tail[:heads] + tail[heads:]
+
+
+def prefix_kernel(where, start, first, first_total, *refs):
+    arrived, (mine, other) = refs[:-2], refs[-2:]
+    z, odd = where[0], where[1] == 1
+    rows, lanes = first.shape
+    heads = first_total.shape[0]
+
+    def by_head(values):
+        return values.reshape(heads, rows // heads, lanes)
+
+    totals = [
+        a[rows : rows + heads, :].astype(F32) + a[rows + heads : rows + 2 * heads, :].astype(F32)
+        for a in arrived
+    ]
+    planes = [z ^ d for d in range(1, len(arrived) + 1)]
+    before = jnp.zeros_like(totals[0])
+    weights = []
+    for i in range(len(arrived)):
+        gap = jnp.zeros_like(before)
+        for j in range(len(arrived)):
+            if j != i:
+                between = (planes[j] > planes[i]) & (planes[j] < z)
+                gap = gap + jnp.where(between, totals[j], 0.0)
+        weights.append(jnp.where(planes[i] < z, jnp.exp(-gap), 0.0))
+        before = before + jnp.where(planes[i] < z, totals[i], 0.0)
+    own_start = jnp.where(odd, start[rows:, :], start[:rows, :])
+    prefix = jnp.exp(-before)[:, None, :] * by_head(own_start)
+    for weight, a in zip(weights, arrived):
+        prefix = prefix + weight[:, None, :] * by_head(a[:rows, :].astype(F32))
+    later = jnp.exp(-first_total[...])[:, None, :] * prefix + by_head(first[...])
+    mine[...] = jnp.where(odd, later, prefix).reshape(rows, lanes).astype(BF)
+    other[...] = jnp.where(odd, prefix, later).reshape(rows, lanes).astype(BF)
+
+
+def prefix_states(where, start, first, first_total, arrived):
+    out = jax.ShapeDtypeStruct(first.shape, BF)
+    whole = pl.BlockSpec(memory_space=pltpu.VMEM)
+    return pl.pallas_call(
+        prefix_kernel,
+        out_shape=(out, out),
+        in_specs=[pl.BlockSpec(memory_space=pltpu.SMEM)] + [whole] * (3 + len(arrived)),
+        out_specs=(whole, whole),
+        compiler_params=pltpu.CompilerParams(vmem_limit_bytes=16 * 1024 * 1024),
+    )(where, start, first, first_total, *arrived)
 
 
 def incoming_state(state, total, start, head_dim, later_use):
@@ -65,22 +110,13 @@
     pair_state = spread(jnp.exp(-second_total)) * first + second
     pair_total = first_total + second_total
     packed = with_total(pair_state, pair_total)
-    others = [apart(swap(packed, "ctx", 2 * d), half) for d in range(1, pairs)]
-    states = [o[0] for o in others]
-    totals = jnp.stack([o[1] for o in others])
-    planes = jnp.stack([z ^ d for d in range(1, pairs)])
-    between = (planes[None, :] > planes[:, None]) & (planes[None, :] < z)
-    gap = jnp.sum(jnp.where(between[:, :, None], totals[None], 0.0), axis=1)
-    weight = jnp.where((planes < z)[:, None], jnp.exp(-gap), 0.0)
-    before = jnp.sum(jnp.where((planes < z)[:, None], totals, 0.0), axis=0)
-    states, later_use = lax.optimization_barrier((states, later_use))
-    own_start = jnp.where(odd, start[cut:], start[:cut])
-    prefix = spread(jnp.exp(-before)) * own_start
-    for i, s in enumerate(states):
-        prefix = prefix + spread(weight[i]) * s
-    later = spread(jnp.exp(-first_total)) * prefix + first
-    mine = jnp.where(odd, later, prefix).astype(BF)
-    other = swap(jnp.where(odd, prefix, later).astype(BF), "ctx", 1)
+    arrived = [swap(packed, "ctx", 2 * d) for d in range(1, pairs)]
+    arrived, later_use = lax.optimization_barrier((arrived, later_use))
+    where = jnp.stack([z, place % 2]).astype(jnp.int32)
+    lanes = state.shape[1]
+    first_wide = jnp.broadcast_to(first_total[:, None], (half, lanes))
+    mine, sent = prefix_states(where, start, first, first_wide, arrived)
+    other = swap(sent, "ctx", 1)
     return jnp.where(odd, other, mine), jnp.where(odd, mine, other), later_use
 
 

time: 209 us -> 205 us (0.981)
  other arithmetic: 11.4 us -> 7.2 us
    ppermute x4, starting transfers between devices: 2 us -> 6.22 us  [across(): return lax.ppermute(x, ('ctx', 'exp'), pairs)]
    ppermute x47, starting transfers between devices: 55 us -> 50.9 us  [swap(): return lax.ppermute(x, axis, [(i, i ^ flip) for i in range(size)])]
  transfers between devices with their start and end apart: 51 -> 51, of which waited for: 28 -> 31; matrix products, arithmetic and copies ran while one was open for 5% -> 4% of each run, Pallas kernels for 20% -> 20%
where the time goes in v8:
time: 205 us; the launch traced here: 204 us
  waiting for transfers between devices  87.9 us (43%)
  starting transfers between devices  57.2 us (28%)
  Pallas kernels  42 us (20%)
  other arithmetic  7.2 us (4%)
  matrix products  5.19 us (3%)
  local copies, waits for them, and re-layouts  4.28 us (2%)
    ppermute x47, waiting for transfers between devices, swap(): return lax.ppermute(x, axis, [(i, i ^ flip) for i in range(size)])  82 us
    ppermute x47, starting transfers between devices, swap(): return lax.ppermute(x, axis, [(i, i ^ flip) for i in range(size)])  50.9 us
    pallas_call x4, Pallas kernels, experts(): pl.pallas_call(expert_kernel, out_shape=(out, out), in_specs=[anywhere] *...  40.9 us
    ppermute x4, starting transfers between devices, across(): return lax.ppermute(x, ('ctx', 'exp'), pairs)  6.22 us
    ppermute x4, waiting for transfers between devices, across(): return lax.ppermute(x, ('ctx', 'exp'), pairs)  5.86 us
  transfers between devices with their start and end apart: 51, of which 31 were waited for; matrix products, arithmetic and copies ran while one was open for 4% of the time, Pallas kernels for 20%

profile of v8, /device:TPU:0, one launch (start us, length us, event | category | flops | bytes accessed | tf_op | source)
XLA Modules:
  0.0 204.3 jit_solution(13009488506348335557)
XLA Ops:
  3.9 3.1 %collective-permute-start = (bf16[528,128]{1,0:T(8,128)(2,1)S(1)}, bf16[528,128]{1,0:T(8,128)(2,1)S(1)}, u32[]{:S(2)}, u32[]{:S(2)}) collective-permute-start(bf16[528,128]{1,0:T(8,128)(2,1)S(1)} %pad_maximum_fusion.1), channel_id=1, source_target_pairs={{0,4},{4,0},{8,12},{12,8},{16,20},{20,16},{24,28},{28,24},{1,5},{5... | collective-permute-start | bytes 405512 | tf_op jit(solution)/shard_map/ppermute | solution.py:20
  7.0 1.6 collective-permute-start.4
  11.3 1.9 collective-permute-start.1
  13.2 2.6 %collective-permute-start.2 = (bf16[528,128]{1,0:T(8,128)(2,1)S(1)}, bf16[528,128]{1,0:T(8,128)(2,1)S(1)}, u32[]{:S(2)}, u32[]{:S(2)}) collective-permute-start(bf16[528,128]{1,0:T(8,128)(2,1)S(1)} %pad_maximum_fusion.2), channel_id=1, source_target_pairs={{0,16},{4,20},{8,24},{12,28},{16,0},{20,4},{24,8},{28,12},{1,17},{... | collective-permute-start | bytes 405512 | tf_op jit(solution)/shard_map/ppermute | solution.py:20
  17.9 2.2 %collective-permute-done.1.refs_0_ = bf16[528,128]{1,0:T(8,128)(2,1)S(1)} collective-permute-done((bf16[528,128]{1,0:T(8,128)(2,1)S(1)}, bf16[528,128]{1,0:T(8,128)(2,1)S(1)}, u32[]{:S(2)}, u32[]{:S(2)}) %collective-permute-start.1) | collective-permute-done | bytes 135200 | tf_op jit(solution)/shard_map/ppermute | solution.py:20
  21.3 4.4 %collective-permute-done.3.refs_2_ = bf16[528,128]{1,0:T(8,128)(2,1)S(1)} collective-permute-done((bf16[528,128]{1,0:T(8,128)(2,1)S(1)}, bf16[528,128]{1,0:T(8,128)(2,1)S(1)}, u32[]{:S(2)}, u32[]{:S(2)}) %collective-permute-start.3) | collective-permute-done | bytes 135200 | tf_op jit(solution)/shard_map/ppermute | solution.py:20
  29.3 2.1 %collective-permute-start.9 = (bf16[768,512]{1,0:T(8,128)(2,1)}, bf16[768,512]{1,0:T(8,128)(2,1)}, u32[]{:S(2)}, u32[]{:S(2)}) collective-permute-start(bf16[768,512]{1,0:T(8,128)(2,1)} %slice.201), channel_id=1, source_target_pairs={{0,8},{4,12},{8,0},{12,4},{16,24},{20,28},{24,16},{28,20},{1,9},{5... | collective-permute-start | bytes 2359304 | tf_op jit(solution)/shard_map/ppermute | solution.py:20
  34.6 3.0 %collective-permute-start.8 = (bf16[128,1024]{0,1:T(8,128)(2,1)S(1)}, bf16[128,1024]{0,1:T(8,128)(2,1)S(1)}, u32[]{:S(2)}, u32[]{:S(2)}) collective-permute-start(bf16[128,1024]{0,1:T(8,128)(2,1)S(1)} %pad_maximum_fusion), channel_id=1, source_target_pairs={{0,20},{4,16},{8,28},{12,24},{16,4},{20,0},{24,12},{28,8},{1,21},{... | collective-permute-start | bytes 786440 | tf_op jit(solution)/shard_map/ppermute | solution.py:20
  37.8 4.9 %collective-permute-done.6 = bf16[128,1024]{0,1:T(8,128)(2,1)S(1)} collective-permute-done((bf16[128,1024]{0,1:T(8,128)(2,1)S(1)}, bf16[128,1024]{0,1:T(8,128)(2,1)S(1)}, u32[]{:S(2)}, u32[]{:S(2)}) %collective-permute-start.6) | collective-permute-done | bytes 262176 | tf_op jit(solution)/shard_map/ppermute | solution.py:20
  42.8 11.6 %collective-permute-done.8 = bf16[128,1024]{0,1:T(8,128)(2,1)S(1)} collective-permute-done((bf16[128,1024]{0,1:T(8,128)(2,1)S(1)}, bf16[128,1024]{0,1:T(8,128)(2,1)S(1)}, u32[]{:S(2)}, u32[]{:S(2)}) %collective-permute-start.8) | collective-permute-done | bytes 262176 | tf_op jit(solution)/shard_map/ppermute | solution.py:20
  54.5 2.7 %collective-permute-done.7 = bf16[128,1024]{0,1:T(8,128)(2,1)S(1)} collective-permute-done((bf16[128,1024]{0,1:T(8,128)(2,1)S(1)}, bf16[128,1024]{0,1:T(8,128)(2,1)S(1)}, u32[]{:S(2)}, u32[]{:S(2)}) %collective-permute-start.7) | collective-permute-done | bytes 262176 | tf_op jit(solution)/shard_map/ppermute | solution.py:20
  58.0 2.5 %fusion.6 = bf16[512,1024]{1,0:T(8,128)(2,1)S(1)} fusion(bf16[512,1024]{1,0:T(8,128)(2,1)S(1)} %bitcast.98, bf16[768,512]{1,0:T(8,128)(2,1)} %collective-permute-done.9, bf16[256,512]{1,0:T(8,128)(2,1)} %collective-permute-done.4, bf16[1024,512]{1,0:T(8,128)(2,1)S(1)} %copy-done.3), kind=kOutput, calls=%fused_computation.6 | convolution fusion | flops 1080557568 | bytes 4194304 | tf_op jit(solution)/shard_map/dot_general | solution.py:24
  60.8 1.7 collective-permute-done.10
  62.7 1.6 collective-permute-start.11
  66.0 5.3 %collective-permute-done.13 = f32[128]{0:T(128)S(1)} collective-permute-done((f32[128]{0:T(128)S(1)}, f32[128]{0:T(128)S(1)}, u32[]{:S(2)}, u32[]{:S(2)}) %collective-permute-start.13) | collective-permute-done | bytes 544 | tf_op jit(solution)/shard_map/ppermute | solution.py:20
  72.5 2.2 %collective-permute-start.15 = (bf16[32,1024]{1,0:T(8,128)(2,1)S(1)}, bf16[32,1024]{1,0:T(8,128)(2,1)S(1)}, u32[]{:S(2)}, u32[]{:S(2)}) collective-permute-start(bf16[32,1024]{1,0:T(8,128)(2,1)S(1)} %get-tuple-element.125), channel_id=1, source_target_pairs={{0,16},{4,20},{8,24},{12,28},{16,0},{20,4},{24,8},{28,12},{1,17},{... | collective-permute-start | bytes 196616 | tf_op jit(solution)/shard_map/ppermute | solution.py:20
  75.9 4.2 %collective-permute-done.15 = bf16[32,1024]{1,0:T(8,128)(2,1)S(1)} collective-permute-done((bf16[32,1024]{1,0:T(8,128)(2,1)S(1)}, bf16[32,1024]{1,0:T(8,128)(2,1)S(1)}, u32[]{:S(2)}, u32[]{:S(2)}) %collective-permute-start.15) | collective-permute-done | bytes 65568 | tf_op jit(solution)/shard_map/ppermute | solution.py:20
  80.1 2.2 %collective-permute-done.16 = bf16[32,1024]{1,0:T(8,128)(2,1)S(1)} collective-permute-done((bf16[32,1024]{1,0:T(8,128)(2,1)S(1)}, bf16[32,1024]{1,0:T(8,128)(2,1)S(1)}, u32[]{:S(2)}, u32[]{:S(2)}) %collective-permute-start.16) | collective-permute-done | bytes 65568 | tf_op jit(solution)/shard_map/ppermute | solution.py:20
  84.2 1.5 collective-permute-start.18
  86.6 4.9 %collective-permute-done.17.refs_1_ = bf16[32,4224]{1,0:T(8,128)(2,1)S(1)} collective-permute-done((bf16[32,4224]{1,0:T(8,128)(2,1)S(1)}, bf16[32,4224]{1,0:T(8,128)(2,1)S(1)}, u32[]{:S(2)}, u32[]{:S(2)}) %collective-permute-start.17) | collective-permute-done | bytes 270368 | tf_op jit(solution)/shard_map/ppermute | solution.py:20
  91.5 2.1 %collective-permute-done.18.refs_2_ = bf16[32,4224]{1,0:T(8,128)(2,1)S(1)} collective-permute-done((bf16[32,4224]{1,0:T(8,128)(2,1)S(1)}, bf16[32,4224]{1,0:T(8,128)(2,1)S(1)}, u32[]{:S(2)}, u32[]{:S(2)}) %collective-permute-start.18) | collective-permute-done | bytes 270368 | tf_op jit(solution)/shard_map/ppermute | solution.py:20
  93.6 3.8 %collective-permute-done.19.refs_3_ = bf16[32,4224]{1,0:T(8,128)(2,1)S(1)} collective-permute-done((bf16[32,4224]{1,0:T(8,128)(2,1)S(1)}, bf16[32,4224]{1,0:T(8,128)(2,1)S(1)}, u32[]{:S(2)}, u32[]{:S(2)}) %collective-permute-start.19) | collective-permute-done | bytes 270368 | tf_op jit(solution)/shard_map/ppermute | solution.py:341
  97.4 2.2 %collective-permute-done.20.refs_0_ = bf16[32,4224]{1,0:T(8,128)(2,1)S(1)} collective-permute-done((bf16[32,4224]{1,0:T(8,128)(2,1)S(1)}, bf16[32,4224]{1,0:T(8,128)(2,1)S(1)}, u32[]{:S(2)}, u32[]{:S(2)}) %collective-permute-start.20) | collective-permute-done | bytes 270368 | tf_op jit(solution)/shard_map/ppermute | solution.py:20
  100.3 1.5 collective-permute-start.23
  101.8 1.6 collective-permute-start.24
  103.4 1.9 collective-permute-start.25
  105.4 10.2 %shard_map.165 = (bf16[128,4096]{1,0:T(8,128)(2,1)S(1)}, bf16[128,4096]{1,0:T(8,128)(2,1)S(1)}) custom-call(bf16[128,4224]{1,0:T(8,128)(2,1)S(1)} %shard_map.164.own, bf16[128,4224]{1,0:T(8,128)(2,1)S(1)} %collective-permute-done.21.mate, bf16[4096,896]{1,0:T(8,128)(2,1)} %bitcast.85, bf16[4096,896]{1,0:T(8,128)(2,1)} %bitcast.89, ...), custom_call_target="tpu_custom_call" | custom-call | flops 5637144576 | bytes 30408704 | tf_op jit(solution)/shard_map/pallas_call | solution.py:313
  116.4 1.5 collective-permute-start.29
  118.2 1.6 collective-permute-start.31
  119.9 1.5 collective-permute-start.35
  121.4 10.2 %shard_map.167 = (bf16[128,4096]{1,0:T(8,128)(2,1)S(1)}, bf16[128,4096]{1,0:T(8,128)(2,1)S(1)}) custom-call(bf16[128,4224]{1,0:T(8,128)(2,1)S(1)} %shard_map.166.own, bf16[128,4224]{1,0:T(8,128)(2,1)S(1)} %collective-permute-done.27.mate, bf16[4096,896]{1,0:T(8,128)(2,1)} %bitcast.86, bf16[4096,896]{1,0:T(8,128)(2,1)} %bitcast.90, ...), custom_call_target="tpu_custom_call" | custom-call | flops 5637144576 | bytes 30408704 | tf_op jit(solution)/shard_map/pallas_call | solution.py:313
  132.5 4.0 %collective-permute-done.35.refs_1_ = bf16[32,4224]{1,0:T(8,128)(2,1)S(1)} collective-permute-done((bf16[32,4224]{1,0:T(8,128)(2,1)S(1)}, bf16[32,4224]{1,0:T(8,128)(2,1)S(1)}, u32[]{:S(2)}, u32[]{:S(2)}) %collective-permute-start.35) | collective-permute-done | bytes 270368 | tf_op jit(solution)/shard_map/ppermute | solution.py:20
  137.1 1.6 collective-permute-start.34
  138.6 10.2 %shard_map.169 = (bf16[128,4096]{1,0:T(8,128)(2,1)S(1)}, bf16[128,4096]{1,0:T(8,128)(2,1)S(1)}) custom-call(bf16[128,4224]{1,0:T(8,128)(2,1)S(1)} %shard_map.168.own, bf16[128,4224]{1,0:T(8,128)(2,1)S(1)} %collective-permute-done.32.mate, bf16[4096,896]{1,0:T(8,128)(2,1)} %bitcast.87, bf16[4096,896]{1,0:T(8,128)(2,1)} %bitcast.91, ...), custom_call_target="tpu_custom_call" | custom-call | flops 5637144576 | bytes 30408704 | tf_op jit(solution)/shard_map/pallas_call | solution.py:313
  150.8 1.7 collective-permute-start.39
  152.5 1.5 collective-permute-start.40
  154.5 1.7 collective-permute-start.43
  156.1 10.2 %shard_map.172 = (bf16[128,4096]{1,0:T(8,128)(2,1)S(1)}, bf16[128,4096]{1,0:T(8,128)(2,1)S(1)}) custom-call(bf16[128,4224]{1,0:T(8,128)(2,1)S(1)} %shard_map.171.own, bf16[128,4224]{1,0:T(8,128)(2,1)S(1)} %collective-permute-done.37.mate, bf16[4096,896]{1,0:T(8,128)(2,1)} %bitcast.88, bf16[4096,896]{1,0:T(8,128)(2,1)} %bitcast.92, ...), custom_call_target="tpu_custom_call" | custom-call | flops 5637144576 | bytes 30408704 | tf_op jit(solution)/shard_map/pallas_call | solution.py:313
  167.1 3.8 %collective-permute-done.43 = bf16[64,4096]{1,0:T(8,128)(2,1)S(1)} collective-permute-done((bf16[64,4096]{1,0:T(8,128)(2,1)S(1)}, bf16[64,4096]{1,0:T(8,128)(2,1)S(1)}, u32[]{:S(2)}, u32[]{:S(2)}) %collective-permute-start.43) | collective-permute-done | bytes 524320 | tf_op jit(solution)/shard_map/ppermute | solution.py:20
  171.0 1.5 collective-permute-start.44
  172.7 2.0 collective-permute-start.49
  174.8 2.0 collective-permute-done.42
  176.8 3.5 %collective-permute-done.44 = bf16[32,4096]{1,0:T(8,128)(2,1)S(1)} collective-permute-done((bf16[32,4096]{1,0:T(8,128)(2,1)S(1)}, bf16[32,4096]{1,0:T(8,128)(2,1)S(1)}, u32[]{:S(2)}, u32[]{:S(2)}) %collective-permute-start.44) | collective-permute-done | bytes 262176 | tf_op jit(solution)/shard_map/ppermute | solution.py:20
  181.9 2.9 %collective-permute-start.46 = (bf16[32,4096]{1,0:T(8,128)(2,1)S(1)}, bf16[32,4096]{1,0:T(8,128)(2,1)S(1)}, u32[]{:S(2)}, u32[]{:S(2)}) collective-permute-start(bf16[32,4096]{1,0:T(8,128)(2,1)S(1)} %add_convert_fusion.8), channel_id=1, source_target_pairs={{0,24},{4,28},{8,16},{12,20},{16,8},{20,12},{24,0},{28,4},{1,25},{... | collective-permute-start | bytes 786440 | tf_op jit(solution)/shard_map/ppermute | solution.py:20
  185.3 2.0 collective-permute-done.49
  187.3 1.9 collective-permute-done.47
  189.4 1.7 collective-permute-start.50
  191.1 12.2 %collective-permute-done.45 = bf16[32,4096]{1,0:T(8,128)(2,1)S(1)} collective-permute-done((bf16[32,4096]{1,0:T(8,128)(2,1)S(1)}, bf16[32,4096]{1,0:T(8,128)(2,1)S(1)}, u32[]{:S(2)}, u32[]{:S(2)}) %collective-permute-start.45) | collective-permute-done | bytes 262176 | tf_op jit(solution)/shard_map/ppermute | solution.py:20
  (176 shorter events, 35.2 us)
Async XLA Ops:
  3.9 6.6 %collective-permute-start = (bf16[528,128]{1,0:T(8,128)(2,1)S(1)}, bf16[528,128]{1,0:T(8,128)(2,1)S(1)}, u32[]{:S(2)}, u32[]{:S(2)}) collective-permute-start(bf16[528,128]{1,0:T(8,128)(2,1)S(1)} %pad_maximum_fusion.1), channel_id=1, source_target_pairs={{0,4},{4,0},{8,12},{12,8},{16,20},{20,16},{24,28},{28,24},{1,5},{5... | collective-permute-start | bytes 405512 | tf_op jit(solution)/shard_map/ppermute | solution.py:20
  7.0 10.9 %collective-permute-start.4 = (bf16[256,512]{1,0:T(8,128)(2,1)S(1)}, bf16[256,512]{1,0:T(8,128)(2,1)}, u32[]{:S(2)}, u32[]{:S(2)}) collective-permute-start(bf16[256,512]{1,0:T(8,128)(2,1)S(1)} %slice.200), channel_id=1, source_target_pairs={{0,8},{4,12},{8,0},{12,4},{16,24},{20,28},{24,16},{28,20},{1,9},{5... | collective-permute-start | bytes 786440 | tf_op jit(solution)/shard_map/ppermute | solution.py:20
  11.3 8.8 %collective-permute-start.1 = (bf16[528,128]{1,0:T(8,128)(2,1)S(1)}, bf16[528,128]{1,0:T(8,128)(2,1)S(1)}, u32[]{:S(2)}, u32[]{:S(2)}) collective-permute-start(bf16[528,128]{1,0:T(8,128)(2,1)S(1)} %pad_maximum_fusion.2), channel_id=1, source_target_pairs={{0,8},{4,12},{8,0},{12,4},{16,24},{20,28},{24,16},{28,20},{1,9},{5... | collective-permute-start | bytes 405512 | tf_op jit(solution)/shard_map/ppermute | solution.py:20
  13.2 8.1 %collective-permute-start.2 = (bf16[528,128]{1,0:T(8,128)(2,1)S(1)}, bf16[528,128]{1,0:T(8,128)(2,1)S(1)}, u32[]{:S(2)}, u32[]{:S(2)}) collective-permute-start(bf16[528,128]{1,0:T(8,128)(2,1)S(1)} %pad_maximum_fusion.2), channel_id=1, source_target_pairs={{0,16},{4,20},{8,24},{12,28},{16,0},{20,4},{24,8},{28,12},{1,17},{... | collective-permute-start | bytes 405512 | tf_op jit(solution)/shard_map/ppermute | solution.py:20
  15.8 9.9 %collective-permute-start.3 = (bf16[528,128]{1,0:T(8,128)(2,1)S(1)}, bf16[528,128]{1,0:T(8,128)(2,1)S(1)}, u32[]{:S(2)}, u32[]{:S(2)}) collective-permute-start(bf16[528,128]{1,0:T(8,128)(2,1)S(1)} %pad_maximum_fusion.2), channel_id=1, source_target_pairs={{0,24},{4,28},{8,16},{12,20},{16,8},{20,12},{24,0},{28,4},{1,25},{... | collective-permute-start | bytes 405512 | tf_op jit(solution)/shard_map/ppermute | solution.py:20
  26.5 5.0 %collective-permute-start.5 = (bf16[512,128]{1,0:T(8,128)(2,1)S(1)}, bf16[512,128]{1,0:T(8,128)(2,1)S(1)}, u32[]{:S(2)}, u32[]{:S(2)}) collective-permute-start(bf16[512,128]{1,0:T(8,128)(2,1)S(1)} %get-tuple-element.62), channel_id=1, source_target_pairs={{0,4},{4,0},{8,12},{12,8},{16,20},{20,16},{24,28},{28,24},{1,5},{5... | collective-permute-start | bytes 393224 | tf_op jit(solution)/shard_map/ppermute | solution.py:20
  29.3 28.7 %collective-permute-start.9 = (bf16[768,512]{1,0:T(8,128)(2,1)}, bf16[768,512]{1,0:T(8,128)(2,1)}, u32[]{:S(2)}, u32[]{:S(2)}) collective-permute-start(bf16[768,512]{1,0:T(8,128)(2,1)} %slice.201), channel_id=1, source_target_pairs={{0,8},{4,12},{8,0},{12,4},{16,24},{20,28},{24,16},{28,20},{1,9},{5... | collective-permute-start | bytes 2359304 | tf_op jit(solution)/shard_map/ppermute | solution.py:20
  33.1 9.5 %collective-permute-start.6 = (bf16[128,1024]{0,1:T(8,128)(2,1)S(1)}, bf16[128,1024]{0,1:T(8,128)(2,1)S(1)}, u32[]{:S(2)}, u32[]{:S(2)}) collective-permute-start(bf16[128,1024]{0,1:T(8,128)(2,1)S(1)} %pad_maximum_fusion), channel_id=1, source_target_pairs={{0,4},{4,0},{8,12},{12,8},{16,20},{20,16},{24,28},{28,24},{1,5},{5... | collective-permute-start | bytes 786440 | tf_op jit(solution)/shard_map/ppermute | solution.py:20
  34.6 19.8 %collective-permute-start.8 = (bf16[128,1024]{0,1:T(8,128)(2,1)S(1)}, bf16[128,1024]{0,1:T(8,128)(2,1)S(1)}, u32[]{:S(2)}, u32[]{:S(2)}) collective-permute-start(bf16[128,1024]{0,1:T(8,128)(2,1)S(1)} %pad_maximum_fusion), channel_id=1, source_target_pairs={{0,20},{4,16},{8,28},{12,24},{16,4},{20,0},{24,12},{28,8},{1,21},{... | collective-permute-start | bytes 786440 | tf_op jit(solution)/shard_map/ppermute | solution.py:20
  37.6 19.6 %collective-permute-start.7 = (bf16[128,1024]{0,1:T(8,128)(2,1)S(1)}, bf16[128,1024]{0,1:T(8,128)(2,1)S(1)}, u32[]{:S(2)}, u32[]{:S(2)}) collective-permute-start(bf16[128,1024]{0,1:T(8,128)(2,1)S(1)} %pad_maximum_fusion), channel_id=1, source_target_pairs={{0,16},{4,20},{8,24},{12,28},{16,0},{20,4},{24,8},{28,12},{1,17},{... | collective-permute-start | bytes 786440 | tf_op jit(solution)/shard_map/ppermute | solution.py:20
  62.7 8.6 %collective-permute-start.11 = (bf16[128,1024]{1,0:T(8,128)(2,1)S(1)}, bf16[128,1024]{1,0:T(8,128)(2,1)S(1)}, u32[]{:S(2)}, u32[]{:S(2)}) collective-permute-start(bf16[128,1024]{1,0:T(8,128)(2,1)S(1)} %slice.261), channel_id=1, source_target_pairs={{0,2},{1,3},{2,0},{3,1},{4,6},{5,7},{6,4},{7,5},{8,10},{9,11},{10,... | collective-permute-start | bytes 786440 | tf_op jit(solution)/shard_map/ppermute | solution.py:20
  65.4 5.8 %collective-permute-start.13 = (f32[128]{0:T(128)S(1)}, f32[128]{0:T(128)S(1)}, u32[]{:S(2)}, u32[]{:S(2)}) collective-permute-start(f32[128]{0:T(128)S(1)} %add.209), channel_id=1, source_target_pairs={{0,2},{1,3},{2,0},{3,1},{4,6},{5,7},{6,4},{7,5},{8,10},{9,11},{10,... | collective-permute-start | bytes 1544 | tf_op jit(solution)/shard_map/ppermute | solution.py:20
  71.4 4.5 %collective-permute-start.14 = (bf16[32,1024]{1,0:T(8,128)(2,1)S(1)}, bf16[32,1024]{1,0:T(8,128)(2,1)S(1)}, u32[]{:S(2)}, u32[]{:S(2)}) collective-permute-start(bf16[32,1024]{1,0:T(8,128)(2,1)S(1)} %get-tuple-element.126), channel_id=1, source_target_pairs={{0,4},{4,0},{8,12},{12,8},{16,20},{20,16},{24,28},{28,24},{1,5},{5... | collective-permute-start | bytes 196616 | tf_op jit(solution)/shard_map/ppermute | solution.py:20
  72.5 7.6 %collective-permute-start.15 = (bf16[32,1024]{1,0:T(8,128)(2,1)S(1)}, bf16[32,1024]{1,0:T(8,128)(2,1)S(1)}, u32[]{:S(2)}, u32[]{:S(2)}) collective-permute-start(bf16[32,1024]{1,0:T(8,128)(2,1)S(1)} %get-tuple-element.125), channel_id=1, source_target_pairs={{0,16},{4,20},{8,24},{12,28},{16,0},{20,4},{24,8},{28,12},{1,17},{... | collective-permute-start | bytes 196616 | tf_op jit(solution)/shard_map/ppermute | solution.py:20
  74.7 7.6 %collective-permute-start.16 = (bf16[32,1024]{1,0:T(8,128)(2,1)S(1)}, bf16[32,1024]{1,0:T(8,128)(2,1)S(1)}, u32[]{:S(2)}, u32[]{:S(2)}) collective-permute-start(bf16[32,1024]{1,0:T(8,128)(2,1)S(1)} %get-tuple-element.124), channel_id=1, source_target_pairs={{0,20},{4,16},{8,28},{12,24},{16,4},{20,0},{24,12},{28,8},{1,21},{... | collective-permute-start | bytes 196616 | tf_op jit(solution)/shard_map/ppermute | solution.py:20
  83.1 8.4 %collective-permute-start.17 = (bf16[32,4224]{1,0:T(8,128)(2,1)S(1)}, bf16[32,4224]{1,0:T(8,128)(2,1)S(1)}, u32[]{:S(2)}, u32[]{:S(2)}) collective-permute-start(bf16[32,4224]{1,0:T(8,128)(2,1)S(1)} %concatenate.40.refs_0_), channel_id=1, source_target_pairs={{0,4},{4,0},{8,12},{12,8},{16,20},{20,16},{24,28},{28,24},{1,5},{5... | collective-permute-start | bytes 811016 | tf_op jit(solution)/shard_map/ppermute | solution.py:20
  84.2 9.4 %collective-permute-start.18 = (bf16[32,4224]{1,0:T(8,128)(2,1)S(1)}, bf16[32,4224]{1,0:T(8,128)(2,1)S(1)}, u32[]{:S(2)}, u32[]{:S(2)}) collective-permute-start(bf16[32,4224]{1,0:T(8,128)(2,1)S(1)} %concatenate.40.refs_0_), channel_id=1, source_target_pairs={{0,2},{1,3},{2,0},{3,1},{4,6},{5,7},{6,4},{7,5},{8,10},{9,11},{10,... | collective-permute-start | bytes 811016 | tf_op jit(solution)/shard_map/ppermute | solution.py:20
  85.7 11.7 %collective-permute-start.19 = (bf16[32,4224]{1,0:T(8,128)(2,1)S(1)}, bf16[32,4224]{1,0:T(8,128)(2,1)S(1)}, u32[]{:S(2)}, u32[]{:S(2)}) collective-permute-start(bf16[32,4224]{1,0:T(8,128)(2,1)S(1)} %concatenate.40.refs_0_), channel_id=1, source_target_pairs={{0,6},{1,7},{2,4},{3,5},{4,2},{5,3},{6,0},{7,1},{8,14},{9,15},{10,... | collective-permute-start | bytes 811016 | tf_op jit(solution)/shard_map/ppermute | solution.py:341
  86.6 13.0 %collective-permute-start.20 = (bf16[32,4224]{1,0:T(8,128)(2,1)S(1)}, bf16[32,4224]{1,0:T(8,128)(2,1)S(1)}, u32[]{:S(2)}, u32[]{:S(2)}) collective-permute-start(bf16[32,4224]{1,0:T(8,128)(2,1)S(1)} %concatenate.40.refs_0_), channel_id=1, source_target_pairs={{0,16},{4,20},{8,24},{12,28},{16,0},{20,4},{24,8},{28,12},{1,17},{... | collective-permute-start | bytes 811016 | tf_op jit(solution)/shard_map/ppermute | solution.py:20
  99.8 15.8 %collective-permute-start.26 = (bf16[32,4224]{1,0:T(8,128)(2,1)S(1)}, bf16[32,4224]{1,0:T(8,128)(2,1)S(1)}, u32[]{:S(2)}, u32[]{:S(2)}) collective-permute-start(bf16[32,4224]{1,0:T(8,128)(2,1)S(1)} %concatenate.40.refs_0_), channel_id=1, source_target_pairs={{0,8},{4,12},{8,0},{12,4},{16,24},{20,28},{24,16},{28,20},{1,9},{5... | collective-permute-start | bytes 811016 | tf_op jit(solution)/shard_map/ppermute | solution.py:20
  99.9 15.8 %collective-permute-start.22 = (bf16[32,4224]{1,0:T(8,128)(2,1)S(1)}, bf16[32,4224]{1,0:T(8,128)(2,1)S(1)}, u32[]{:S(2)}, u32[]{:S(2)}) collective-permute-start(bf16[32,4224]{1,0:T(8,128)(2,1)S(1)} %collective-permute-done.20.refs_0_), channel_id=1, source_target_pairs={{0,4},{4,0},{8,12},{12,8},{16,20},{20,16},{24,28},{28,24},{1,5},{5... | collective-permute-start | bytes 811016 | tf_op jit(solution)/shard_map/ppermute | solution.py:20
  100.3 15.3 %collective-permute-start.23 = (bf16[32,4224]{1,0:T(8,128)(2,1)S(1)}, bf16[32,4224]{1,0:T(8,128)(2,1)S(1)}, u32[]{:S(2)}, u32[]{:S(2)}) collective-permute-start(bf16[32,4224]{1,0:T(8,128)(2,1)S(1)} %collective-permute-done.20.refs_0_), channel_id=1, source_target_pairs={{0,2},{1,3},{2,0},{3,1},{4,6},{5,7},{6,4},{7,5},{8,10},{9,11},{10,... | collective-permute-start | bytes 811016 | tf_op jit(solution)/shard_map/ppermute | solution.py:20
  101.8 13.9 %collective-permute-start.24 = (bf16[32,4224]{1,0:T(8,128)(2,1)S(1)}, bf16[32,4224]{1,0:T(8,128)(2,1)S(1)}, u32[]{:S(2)}, u32[]{:S(2)}) collective-permute-start(bf16[32,4224]{1,0:T(8,128)(2,1)S(1)} %collective-permute-done.20.refs_0_), channel_id=1, source_target_pairs={{0,6},{1,7},{2,4},{3,5},{4,2},{5,3},{6,0},{7,1},{8,14},{9,15},{10,... | collective-permute-start | bytes 811016 | tf_op jit(solution)/shard_map/ppermute | solution.py:341
  103.4 12.3 %collective-permute-start.25 = (bf16[32,4224]{1,0:T(8,128)(2,1)S(1)}, bf16[32,4224]{1,0:T(8,128)(2,1)S(1)}, u32[]{:S(2)}, u32[]{:S(2)}) collective-permute-start(bf16[32,4224]{1,0:T(8,128)(2,1)S(1)} %collective-permute-done.20.refs_0_), channel_id=1, source_target_pairs={{0,8},{4,12},{8,0},{12,4},{16,24},{20,28},{24,16},{28,20},{1,9},{5... | collective-permute-start | bytes 811016 | tf_op jit(solution)/shard_map/ppermute | solution.py:20
  115.8 4.1 %collective-permute-start.27 = (bf16[128,4224]{1,0:T(8,128)(2,1)S(1)}, bf16[128,4224]{1,0:T(8,128)(2,1)S(1)}, u32[]{:S(2)}, u32[]{:S(2)}) collective-permute-start(bf16[128,4224]{1,0:T(8,128)(2,1)S(1)} %shard_map.166.own), channel_id=1, source_target_pairs={{0,1},{1,0},{2,3},{3,2},{4,5},{5,4},{6,7},{7,6},{8,9},{9,8},{10,11... | collective-permute-start | bytes 3244040 | tf_op jit(solution)/shard_map/ppermute | solution.py:20
  115.9 16.0 %collective-permute-start.28 = (bf16[128,4096]{1,0:T(8,128)(2,1)S(1)}, bf16[128,4096]{1,0:T(8,128)(2,1)S(1)}, u32[]{:S(2)}, u32[]{:S(2)}) collective-permute-start(bf16[128,4096]{1,0:T(8,128)(2,1)S(1)} %get-tuple-element.82), channel_id=1, source_target_pairs={{0,1},{1,0},{2,3},{3,2},{4,5},{5,4},{6,7},{7,6},{8,9},{9,8},{10,11... | collective-permute-start | bytes 3145736 | tf_op jit(solution)/shard_map/ppermute | solution.py:20
  116.4 15.2 %collective-permute-start.29 = (bf16[32,4224]{1,0:T(8,128)(2,1)S(1)}, bf16[32,4224]{1,0:T(8,128)(2,1)S(1)}, u32[]{:S(2)}, u32[]{:S(2)}) collective-permute-start(bf16[32,4224]{1,0:T(8,128)(2,1)S(1)} %collective-permute-done.25.refs_0_), channel_id=1, source_target_pairs={{0,2},{1,3},{2,0},{3,1},{4,6},{5,7},{6,4},{7,5},{8,10},{9,11},{10,... | collective-permute-start | bytes 811016 | tf_op jit(solution)/shard_map/ppermute | solution.py:20
  117.9 14.0 %collective-permute-start.30 = (bf16[32,4224]{1,0:T(8,128)(2,1)S(1)}, bf16[32,4224]{1,0:T(8,128)(2,1)S(1)}, u32[]{:S(2)}, u32[]{:S(2)}) collective-permute-start(bf16[32,4224]{1,0:T(8,128)(2,1)S(1)} %collective-permute-done.25.refs_0_), channel_id=1, source_target_pairs={{0,4},{4,0},{8,12},{12,8},{16,20},{20,16},{24,28},{28,24},{1,5},{5... | collective-permute-start | bytes 811016 | tf_op jit(solution)/shard_map/ppermute | solution.py:20
  118.2 13.6 %collective-permute-start.31 = (bf16[32,4224]{1,0:T(8,128)(2,1)S(1)}, bf16[32,4224]{1,0:T(8,128)(2,1)S(1)}, u32[]{:S(2)}, u32[]{:S(2)}) collective-permute-start(bf16[32,4224]{1,0:T(8,128)(2,1)S(1)} %collective-permute-done.25.refs_0_), channel_id=1, source_target_pairs={{0,6},{1,7},{2,4},{3,5},{4,2},{5,3},{6,0},{7,1},{8,14},{9,15},{10,... | collective-permute-start | bytes 811016 | tf_op jit(solution)/shard_map/ppermute | solution.py:341
  119.9 16.6 %collective-permute-start.35 = (bf16[32,4224]{1,0:T(8,128)(2,1)S(1)}, bf16[32,4224]{1,0:T(8,128)(2,1)S(1)}, u32[]{:S(2)}, u32[]{:S(2)}) collective-permute-start(bf16[32,4224]{1,0:T(8,128)(2,1)S(1)} %collective-permute-done.26.refs_0_), channel_id=1, source_target_pairs={{0,2},{1,3},{2,0},{3,1},{4,6},{5,7},{6,4},{7,5},{8,10},{9,11},{10,... | collective-permute-start | bytes 811016 | tf_op jit(solution)/shard_map/ppermute | solution.py:20
  131.9 6.7 %collective-permute-start.32 = (bf16[128,4224]{1,0:T(8,128)(2,1)S(1)}, bf16[128,4224]{1,0:T(8,128)(2,1)S(1)}, u32[]{:S(2)}, u32[]{:S(2)}) collective-permute-start(bf16[128,4224]{1,0:T(8,128)(2,1)S(1)} %shard_map.168.own), channel_id=1, source_target_pairs={{0,1},{1,0},{2,3},{3,2},{4,5},{5,4},{6,7},{7,6},{8,9},{9,8},{10,11... | collective-permute-start | bytes 3244040 | tf_op jit(solution)/shard_map/ppermute | solution.py:20
  132.0 18.0 %collective-permute-start.33 = (bf16[128,4096]{1,0:T(8,128)(2,1)S(1)}, bf16[128,4096]{1,0:T(8,128)(2,1)S(1)}, u32[]{:S(2)}, u32[]{:S(2)}) collective-permute-start(bf16[128,4096]{1,0:T(8,128)(2,1)S(1)} %get-tuple-element.92), channel_id=1, source_target_pairs={{0,1},{1,0},{2,3},{3,2},{4,5},{5,4},{6,7},{7,6},{8,9},{9,8},{10,11... | collective-permute-start | bytes 3145736 | tf_op jit(solution)/shard_map/ppermute | solution.py:20
  136.5 13.5 %collective-permute-start.36 = (bf16[64,4224]{1,0:T(8,128)(2,1)S(1)}, bf16[64,4224]{1,0:T(8,128)(2,1)S(1)}, u32[]{:S(2)}, u32[]{:S(2)}) collective-permute-start(bf16[64,4224]{1,0:T(8,128)(2,1)S(1)} %shard_map.170), channel_id=1, source_target_pairs={{0,4},{4,0},{8,12},{12,8},{16,20},{20,16},{24,28},{28,24},{1,5},{5... | collective-permute-start | bytes 1622024 | tf_op jit(solution)/shard_map/ppermute | solution.py:20
  137.1 12.9 %collective-permute-start.34 = (bf16[64,4096]{1,0:T(8,128)(2,1)S(1)}, bf16[64,4096]{1,0:T(8,128)(2,1)S(1)}, u32[]{:S(2)}, u32[]{:S(2)}) collective-permute-start(bf16[64,4096]{1,0:T(8,128)(2,1)S(1)} %add_convert_fusion.2), channel_id=1, source_target_pairs={{0,2},{1,3},{2,0},{3,1},{4,6},{5,7},{6,4},{7,5},{8,10},{9,11},{10,... | collective-permute-start | bytes 1572872 | tf_op jit(solution)/shard_map/ppermute | solution.py:20
  150.1 6.1 %collective-permute-start.37 = (bf16[128,4224]{1,0:T(8,128)(2,1)S(1)}, bf16[128,4224]{1,0:T(8,128)(2,1)S(1)}, u32[]{:S(2)}, u32[]{:S(2)}) collective-permute-start(bf16[128,4224]{1,0:T(8,128)(2,1)S(1)} %shard_map.171.own), channel_id=1, source_target_pairs={{0,1},{1,0},{2,3},{3,2},{4,5},{5,4},{6,7},{7,6},{8,9},{9,8},{10,11... | collective-permute-start | bytes 3244040 | tf_op jit(solution)/shard_map/ppermute | solution.py:20
  150.2 4.2 %collective-permute-start.38 = (bf16[128,4096]{1,0:T(8,128)(2,1)S(1)}, bf16[128,4096]{1,0:T(8,128)(2,1)S(1)}, u32[]{:S(2)}, u32[]{:S(2)}) collective-permute-start(bf16[128,4096]{1,0:T(8,128)(2,1)S(1)} %get-tuple-element.97), channel_id=1, source_target_pairs={{0,1},{1,0},{2,3},{3,2},{4,5},{5,4},{6,7},{7,6},{8,9},{9,8},{10,11... | collective-permute-start | bytes 3145736 | tf_op jit(solution)/shard_map/ppermute | solution.py:20
  150.8 15.6 %collective-permute-start.39 = (bf16[32,4096]{1,0:T(8,128)(2,1)S(1)}, bf16[32,4096]{1,0:T(8,128)(2,1)S(1)}, u32[]{:S(2)}, u32[]{:S(2)}) collective-permute-start(bf16[32,4096]{1,0:T(8,128)(2,1)S(1)} %add_convert_fusion.13), channel_id=1, source_target_pairs={{0,4},{4,0},{8,12},{12,8},{16,20},{20,16},{24,28},{28,24},{1,5},{5... | collective-permute-start | bytes 786440 | tf_op jit(solution)/shard_map/ppermute | solution.py:20
  152.5 13.8 %collective-permute-start.40 = (bf16[64,4096]{1,0:T(8,128)(2,1)S(1)}, bf16[64,4096]{1,0:T(8,128)(2,1)S(1)}, u32[]{:S(2)}, u32[]{:S(2)}) collective-permute-start(bf16[64,4096]{1,0:T(8,128)(2,1)S(1)} %add_convert_fusion.1), channel_id=1, source_target_pairs={{0,2},{1,3},{2,0},{3,1},{4,6},{5,7},{6,4},{7,5},{8,10},{9,11},{10,... | collective-permute-start | bytes 1572872 | tf_op jit(solution)/shard_map/ppermute | solution.py:20
  154.5 16.4 %collective-permute-start.43 = (bf16[64,4096]{1,0:T(8,128)(2,1)S(1)}, bf16[64,4096]{1,0:T(8,128)(2,1)S(1)}, u32[]{:S(2)}, u32[]{:S(2)}) collective-permute-start(bf16[64,4096]{1,0:T(8,128)(2,1)S(1)} %add_convert_fusion), channel_id=1, source_target_pairs={{0,4},{4,0},{8,12},{12,8},{16,20},{20,16},{24,28},{28,24},{1,5},{5... | collective-permute-start | bytes 1572872 | tf_op jit(solution)/shard_map/ppermute | solution.py:20
  166.4 6.1 %collective-permute-start.41 = (bf16[128,4096]{1,0:T(8,128)(2,1)S(1)}, bf16[128,4096]{1,0:T(8,128)(2,1)S(1)}, u32[]{:S(2)}, u32[]{:S(2)}) collective-permute-start(bf16[128,4096]{1,0:T(8,128)(2,1)S(1)} %get-tuple-element.104), channel_id=1, source_target_pairs={{0,1},{1,0},{2,3},{3,2},{4,5},{5,4},{6,7},{7,6},{8,9},{9,8},{10,11... | collective-permute-start | bytes 3145736 | tf_op jit(solution)/shard_map/ppermute | solution.py:20
  166.6 10.2 %collective-permute-start.42 = (bf16[32,4096]{1,0:T(8,128)(2,1)S(1)}, bf16[32,4096]{1,0:T(8,128)(2,1)S(1)}, u32[]{:S(2)}, u32[]{:S(2)}) collective-permute-start(bf16[32,4096]{1,0:T(8,128)(2,1)S(1)} %add_convert_fusion.11), channel_id=1, source_target_pairs={{0,4},{4,0},{8,12},{12,8},{16,20},{20,16},{24,28},{28,24},{1,5},{5... | collective-permute-start | bytes 786440 | tf_op jit(solution)/shard_map/ppermute | solution.py:20
  171.0 9.3 %collective-permute-start.44 = (bf16[32,4096]{1,0:T(8,128)(2,1)S(1)}, bf16[32,4096]{1,0:T(8,128)(2,1)S(1)}, u32[]{:S(2)}, u32[]{:S(2)}) collective-permute-start(bf16[32,4096]{1,0:T(8,128)(2,1)S(1)} %add_convert_fusion.10), channel_id=1, source_target_pairs={{0,2},{1,3},{2,0},{3,1},{4,6},{5,7},{6,4},{7,5},{8,10},{9,11},{10,... | collective-permute-start | bytes 786440 | tf_op jit(solution)/shard_map/ppermute | solution.py:20
  172.7 14.6 %collective-permute-start.49 = (bf16[32,4096]{1,0:T(8,128)(2,1)S(1)}, bf16[32,4096]{1,0:T(8,128)(2,1)S(1)}, u32[]{:S(2)}, u32[]{:S(2)}) collective-permute-start(bf16[32,4096]{1,0:T(8,128)(2,1)S(1)} %get-tuple-element.120), channel_id=1, source_target_pairs={{0,6},{1,7},{2,4},{3,5},{4,2},{5,3},{6,0},{7,1},{8,14},{9,15},{10,... | collective-permute-start | bytes 786440 | tf_op jit(solution)/shard_map/ppermute | solution.py:341
  174.7 12.6 %collective-permute-start.48 = (bf16[32,4096]{1,0:T(8,128)(2,1)S(1)}, bf16[32,4096]{1,0:T(8,128)(2,1)S(1)}, u32[]{:S(2)}, u32[]{:S(2)}) collective-permute-start(bf16[32,4096]{1,0:T(8,128)(2,1)S(1)} %get-tuple-element.121), channel_id=1, source_target_pairs={{0,4},{4,0},{8,12},{12,8},{16,20},{20,16},{24,28},{28,24},{1,5},{5... | collective-permute-start | bytes 786440 | tf_op jit(solution)/shard_map/ppermute | solution.py:20
  180.3 8.9 %collective-permute-start.47 = (bf16[32,4096]{1,0:T(8,128)(2,1)S(1)}, bf16[32,4096]{1,0:T(8,128)(2,1)S(1)}, u32[]{:S(2)}, u32[]{:S(2)}) collective-permute-start(bf16[32,4096]{1,0:T(8,128)(2,1)S(1)} %get-tuple-element.112), channel_id=1, source_target_pairs={{0,2},{1,3},{2,0},{3,1},{4,6},{5,7},{6,4},{7,5},{8,10},{9,11},{10,... | collective-permute-start | bytes 786440 | tf_op jit(solution)/shard_map/ppermute | solution.py:20
  181.9 9.2 %collective-permute-start.46 = (bf16[32,4096]{1,0:T(8,128)(2,1)S(1)}, bf16[32,4096]{1,0:T(8,128)(2,1)S(1)}, u32[]{:S(2)}, u32[]{:S(2)}) collective-permute-start(bf16[32,4096]{1,0:T(8,128)(2,1)S(1)} %add_convert_fusion.8), channel_id=1, source_target_pairs={{0,24},{4,28},{8,16},{12,20},{16,8},{20,12},{24,0},{28,4},{1,25},{... | collective-permute-start | bytes 786440 | tf_op jit(solution)/shard_map/ppermute | solution.py:20
  184.9 18.3 %collective-permute-start.45 = (bf16[32,4096]{1,0:T(8,128)(2,1)S(1)}, bf16[32,4096]{1,0:T(8,128)(2,1)S(1)}, u32[]{:S(2)}, u32[]{:S(2)}) collective-permute-start(bf16[32,4096]{1,0:T(8,128)(2,1)S(1)} %add_convert_fusion.9), channel_id=1, source_target_pairs={{0,16},{4,20},{8,24},{12,28},{16,0},{20,4},{24,8},{28,12},{1,17},{... | collective-permute-start | bytes 786440 | tf_op jit(solution)/shard_map/ppermute | solution.py:20
  189.4 13.9 %collective-permute-start.50 = (bf16[32,4096]{1,0:T(8,128)(2,1)S(1)}, bf16[32,4096]{1,0:T(8,128)(2,1)S(1)}, u32[]{:S(2)}, u32[]{:S(2)}) collective-permute-start(bf16[32,4096]{1,0:T(8,128)(2,1)S(1)} %add_convert_fusion.5), channel_id=1, source_target_pairs={{0,8},{4,12},{8,0},{12,4},{16,24},{20,28},{24,16},{28,20},{1,9},{5... | collective-permute-start | bytes 786440 | tf_op jit(solution)/shard_map/ppermute | solution.py:20
  (16 other events, 162.1 us)

commit v9 on v8

--- a/solution.py
+++ b/solution.py
@@ -178,7 +178,10 @@
     pieces = [lax.dynamic_slice_in_dim(rows, (me_exp ^ q) * quarter, quarter, 0) for q in rel]
     own_rows = jnp.concatenate(pieces)
     group = [h + y for h in range(0, n_ctx, 4) for y in (0, 1)]
-    arrived = [own_rows] + [swap(own_rows, "ctx", r) for r in group[1:]]
+    arrived = []
+    for h in range(0, n_ctx, 4):
+        along_z = own_rows if h == 0 else swap(own_rows, "ctx", h)
+        arrived += [along_z, swap(along_z, "ctx", 1)]
     squares, arrived[1] = lax.optimization_barrier((squares, arrived[1]))
     for flip in (1, 2):
         squares = squares + swap(squares, "exp", flip)
@@ -387,7 +390,7 @@
     lane = jnp.arange(LANES, dtype=jnp.int32)
     pick = (lane % (LANES // 2) == me_ctx // PAIR).astype(F32)[None, :]
 
-    cut = out_proj.shape[0] // 4
+    cut = out_proj.shape[0] // 8 * 3
     two_parts = (swap(out_proj[:cut], "ctx", 2), out_proj[cut:])
     gated, (first_part, second_part) = mixer_rows(
         inputs, gate_input, b_proj, c_proj, step_size, decay_rate, skip_gain, start_state, two_parts

time: 205 us -> 200 us (0.976)
  starting transfers between devices: 57.2 us -> 53.2 us
  waiting for transfers between devices: 87.9 us -> 85.3 us
    ppermute x47, starting transfers between devices: 50.9 us -> 48 us  [swap(): return lax.ppermute(x, axis, [(i, i ^ flip) for i in range(size)])]
  transfers between devices with their start and end apart: 51 -> 51, of which waited for: 31 -> 28; matrix products, arithmetic and copies ran while one was open for 4% -> 4% of each run, Pallas kernels for 20% -> 21%
where the time goes in v9:
time: 200 us; the launch traced here: 199 us
  waiting for transfers between devices  85.3 us (43%)
  starting transfers between devices  53.2 us (27%)
  Pallas kernels  42 us (21%)
  other arithmetic  7.86 us (4%)
  matrix products  5.17 us (3%)
  local copies, waits for them, and re-layouts  5.13 us (3%)
    ppermute x47, waiting for transfers between devices, swap(): return lax.ppermute(x, axis, [(i, i ^ flip) for i in range(size)])  81.4 us
    ppermute x47, starting transfers between devices, swap(): return lax.ppermute(x, axis, [(i, i ^ flip) for i in range(size)])  48 us
    pallas_call x4, Pallas kernels, experts(): pl.pallas_call(expert_kernel, out_shape=(out, out), in_specs=[anywhere] *...  40.9 us
    ppermute x4, starting transfers between devices, across(): return lax.ppermute(x, ('ctx', 'exp'), pairs)  5.19 us
  transfers between devices with their start and end apart: 51, of which 28 were waited for; matrix products, arithmetic and copies ran while one was open for 4% of the time, Pallas kernels for 21%

profile of v9, /device:TPU:0, one launch (start us, length us, event | category | flops | bytes accessed | tf_op | source)
XLA Modules:
  0.0 199.3 jit_solution(12917876893589030033)
XLA Ops:
  3.9 3.1 %collective-permute-start = (bf16[528,128]{1,0:T(8,128)(2,1)S(1)}, bf16[528,128]{1,0:T(8,128)(2,1)S(1)}, u32[]{:S(2)}, u32[]{:S(2)}) collective-permute-start(bf16[528,128]{1,0:T(8,128)(2,1)S(1)} %pad_maximum_fusion.1), channel_id=1, source_target_pairs={{0,4},{4,0},{8,12},{12,8},{16,20},{20,16},{24,28},{28,24},{1,5},{5... | collective-permute-start | bytes 405512 | tf_op jit(solution)/shard_map/ppermute | solution.py:20
  7.8 1.6 collective-permute-start.4
  12.0 1.8 collective-permute-start.1
  13.8 2.6 %collective-permute-start.2 = (bf16[528,128]{1,0:T(8,128)(2,1)}, bf16[528,128]{1,0:T(8,128)(2,1)S(1)}, u32[]{:S(2)}, u32[]{:S(2)}) collective-permute-start(bf16[528,128]{1,0:T(8,128)(2,1)} %pad_maximum_fusion.2), channel_id=1, source_target_pairs={{0,16},{4,20},{8,24},{12,28},{16,0},{20,4},{24,8},{28,12},{1,17},{... | collective-permute-start | bytes 405512 | tf_op jit(solution)/shard_map/ppermute | solution.py:20
  17.8 6.5 %collective-permute-done.1.refs_0_ = bf16[528,128]{1,0:T(8,128)(2,1)S(1)} collective-permute-done((bf16[528,128]{1,0:T(8,128)(2,1)}, bf16[528,128]{1,0:T(8,128)(2,1)S(1)}, u32[]{:S(2)}, u32[]{:S(2)}) %collective-permute-start.1) | collective-permute-done | bytes 135200 | tf_op jit(solution)/shard_map/ppermute | solution.py:20
  25.0 4.3 %collective-permute-done.3.refs_2_ = bf16[528,128]{1,0:T(8,128)(2,1)S(1)} collective-permute-done((bf16[528,128]{1,0:T(8,128)(2,1)}, bf16[528,128]{1,0:T(8,128)(2,1)S(1)}, u32[]{:S(2)}, u32[]{:S(2)}) %collective-permute-start.3) | collective-permute-done | bytes 135200 | tf_op jit(solution)/shard_map/ppermute | solution.py:20
  30.6 1.4 fusion.9
  32.0 3.1 %collective-permute-done.5 = bf16[512,128]{1,0:T(8,128)(2,1)S(1)} collective-permute-done((bf16[512,128]{1,0:T(8,128)(2,1)S(1)}, bf16[512,128]{1,0:T(8,128)(2,1)S(1)}, u32[]{:S(2)}, u32[]{:S(2)}) %collective-permute-start.5) | collective-permute-done | bytes 131104 | tf_op jit(solution)/shard_map/ppermute | solution.py:20
  36.8 2.1 %collective-permute-start.9 = (bf16[640,512]{1,0:T(8,128)(2,1)S(1)}, bf16[640,512]{1,0:T(8,128)(2,1)}, u32[]{:S(2)}, u32[]{:S(2)}) collective-permute-start(bf16[640,512]{1,0:T(8,128)(2,1)S(1)} %slice.201), channel_id=1, source_target_pairs={{0,8},{4,12},{8,0},{12,4},{16,24},{20,28},{24,16},{28,20},{1,9},{5... | collective-permute-start | bytes 1966088 | tf_op jit(solution)/shard_map/ppermute | solution.py:20
  39.5 8.0 %collective-permute-done.7 = bf16[128,1024]{0,1:T(8,128)(2,1)S(1)} collective-permute-done((bf16[128,1024]{0,1:T(8,128)(2,1)S(1)}, bf16[128,1024]{0,1:T(8,128)(2,1)S(1)}, u32[]{:S(2)}, u32[]{:S(2)}) %collective-permute-start.7) | collective-permute-done | bytes 262176 | tf_op jit(solution)/shard_map/ppermute | solution.py:20
  48.6 5.5 %collective-permute-done.8 = bf16[128,1024]{0,1:T(8,128)(2,1)S(1)} collective-permute-done((bf16[128,1024]{0,1:T(8,128)(2,1)S(1)}, bf16[128,1024]{0,1:T(8,128)(2,1)S(1)}, u32[]{:S(2)}, u32[]{:S(2)}) %collective-permute-start.8) | collective-permute-done | bytes 262176 | tf_op jit(solution)/shard_map/ppermute | solution.py:20
  54.5 2.0 collective-permute-done.9
  56.5 2.5 %fusion.6 = bf16[512,1024]{1,0:T(8,128)(2,1)S(1)} fusion(bf16[512,1024]{1,0:T(8,128)(2,1)S(1)} %bitcast.98, bf16[640,512]{1,0:T(8,128)(2,1)} %collective-permute-done.9, bf16[384,512]{1,0:T(8,128)(2,1)} %collective-permute-done.4, bf16[1024,512]{1,0:T(8,128)(2,1)S(1)} %copy-done.3), kind=kOutput, calls=%fused_computation.6 | convolution fusion | flops 1080557568 | bytes 4194304 | tf_op jit(solution)/shard_map/dot_general | solution.py:24
  59.3 1.7 collective-permute-done.10
  61.2 1.6 collective-permute-start.11
  64.4 5.3 %collective-permute-done.13 = f32[128]{0:T(128)S(1)} collective-permute-done((f32[128]{0:T(128)S(1)}, f32[128]{0:T(128)S(1)}, u32[]{:S(2)}, u32[]{:S(2)}) %collective-permute-start.13) | collective-permute-done | bytes 544 | tf_op jit(solution)/shard_map/ppermute | solution.py:20
  70.7 3.6 %collective-permute-start.16 = (bf16[32,1024]{1,0:T(8,128)(2,1)S(1)}, bf16[32,1024]{1,0:T(8,128)(2,1)S(1)}, u32[]{:S(2)}, u32[]{:S(2)}) collective-permute-start(bf16[32,1024]{1,0:T(8,128)(2,1)S(1)} %get-tuple-element.124), channel_id=1, source_target_pairs={{0,20},{4,16},{8,28},{12,24},{16,4},{20,0},{24,12},{28,8},{1,21},{... | collective-permute-start | bytes 196616 | tf_op jit(solution)/shard_map/ppermute | solution.py:20
  74.3 2.4 %collective-permute-done.15 = bf16[32,1024]{1,0:T(8,128)(2,1)S(1)} collective-permute-done((bf16[32,1024]{1,0:T(8,128)(2,1)S(1)}, bf16[32,1024]{1,0:T(8,128)(2,1)S(1)}, u32[]{:S(2)}, u32[]{:S(2)}) %collective-permute-start.15) | collective-permute-done | bytes 65568 | tf_op jit(solution)/shard_map/ppermute | solution.py:20
  76.8 2.4 %collective-permute-done.16 = bf16[32,1024]{1,0:T(8,128)(2,1)S(1)} collective-permute-done((bf16[32,1024]{1,0:T(8,128)(2,1)S(1)}, bf16[32,1024]{1,0:T(8,128)(2,1)S(1)}, u32[]{:S(2)}, u32[]{:S(2)}) %collective-permute-start.16) | collective-permute-done | bytes 65568 | tf_op jit(solution)/shard_map/ppermute | solution.py:20
  80.0 1.6 collective-permute-start.18
  81.6 1.9 collective-permute-start.19
  83.8 4.9 %collective-permute-done.17.refs_1_ = bf16[32,4224]{1,0:T(8,128)(2,1)S(1)} collective-permute-done((bf16[32,4224]{1,0:T(8,128)(2,1)S(1)}, bf16[32,4224]{1,0:T(8,128)(2,1)S(1)}, u32[]{:S(2)}, u32[]{:S(2)}) %collective-permute-start.17) | collective-permute-done | bytes 270368 | tf_op jit(solution)/shard_map/ppermute | solution.py:20
  88.7 2.9 %collective-permute-done.19.refs_3_ = bf16[32,4224]{1,0:T(8,128)(2,1)S(1)} collective-permute-done((bf16[32,4224]{1,0:T(8,128)(2,1)S(1)}, bf16[32,4224]{1,0:T(8,128)(2,1)S(1)}, u32[]{:S(2)}, u32[]{:S(2)}) %collective-permute-start.19) | collective-permute-done | bytes 270368 | tf_op jit(solution)/shard_map/ppermute | solution.py:344
  91.6 2.4 %collective-permute-done.20.refs_0_ = bf16[32,4224]{1,0:T(8,128)(2,1)S(1)} collective-permute-done((bf16[32,4224]{1,0:T(8,128)(2,1)S(1)}, bf16[32,4224]{1,0:T(8,128)(2,1)S(1)}, u32[]{:S(2)}, u32[]{:S(2)}) %collective-permute-start.20) | collective-permute-done | bytes 270368 | tf_op jit(solution)/shard_map/ppermute | solution.py:20
  94.3 1.2 collective-permute-start.22
  95.4 1.5 collective-permute-start.23
  97.8 1.9 collective-permute-start.25
  99.8 10.2 %shard_map.165 = (bf16[128,4096]{1,0:T(8,128)(2,1)S(1)}, bf16[128,4096]{1,0:T(8,128)(2,1)S(1)}) custom-call(bf16[128,4224]{1,0:T(8,128)(2,1)S(1)} %shard_map.164.own, bf16[128,4224]{1,0:T(8,128)(2,1)S(1)} %collective-permute-done.21.mate, bf16[4096,896]{1,0:T(8,128)(2,1)} %bitcast.85, bf16[4096,896]{1,0:T(8,128)(2,1)} %bitcast.89, ...), custom_call_target="tpu_custom_call" | custom-call | flops 5637144576 | bytes 30408704 | tf_op jit(solution)/shard_map/pallas_call | solution.py:316
  110.8 1.5 collective-permute-start.29
  114.3 1.5 collective-permute-start.35
  115.8 10.2 %shard_map.167 = (bf16[128,4096]{1,0:T(8,128)(2,1)S(1)}, bf16[128,4096]{1,0:T(8,128)(2,1)S(1)}) custom-call(bf16[128,4224]{1,0:T(8,128)(2,1)S(1)} %shard_map.166.own, bf16[128,4224]{1,0:T(8,128)(2,1)S(1)} %collective-permute-done.27.mate, bf16[4096,896]{1,0:T(8,128)(2,1)} %bitcast.86, bf16[4096,896]{1,0:T(8,128)(2,1)} %bitcast.90, ...), custom_call_target="tpu_custom_call" | custom-call | flops 5637144576 | bytes 30408704 | tf_op jit(solution)/shard_map/pallas_call | solution.py:316
  126.9 4.0 %collective-permute-done.35.refs_1_ = bf16[32,4224]{1,0:T(8,128)(2,1)S(1)} collective-permute-done((bf16[32,4224]{1,0:T(8,128)(2,1)S(1)}, bf16[32,4224]{1,0:T(8,128)(2,1)S(1)}, u32[]{:S(2)}, u32[]{:S(2)}) %collective-permute-start.35) | collective-permute-done | bytes 270368 | tf_op jit(solution)/shard_map/ppermute | solution.py:20
  131.9 1.5 collective-permute-start.34
  133.5 10.2 %shard_map.169 = (bf16[128,4096]{1,0:T(8,128)(2,1)S(1)}, bf16[128,4096]{1,0:T(8,128)(2,1)S(1)}) custom-call(bf16[128,4224]{1,0:T(8,128)(2,1)S(1)} %shard_map.168.own, bf16[128,4224]{1,0:T(8,128)(2,1)S(1)} %collective-permute-done.32.mate, bf16[4096,896]{1,0:T(8,128)(2,1)} %bitcast.87, bf16[4096,896]{1,0:T(8,128)(2,1)} %bitcast.91, ...), custom_call_target="tpu_custom_call" | custom-call | flops 5637144576 | bytes 30408704 | tf_op jit(solution)/shard_map/pallas_call | solution.py:316
  145.6 1.2 collective-permute-start.39
  146.9 1.5 collective-permute-start.40
  149.3 1.2 collective-permute-start.43
  150.5 10.2 %shard_map.172 = (bf16[128,4096]{1,0:T(8,128)(2,1)S(1)}, bf16[128,4096]{1,0:T(8,128)(2,1)S(1)}) custom-call(bf16[128,4224]{1,0:T(8,128)(2,1)S(1)} %shard_map.171.own, bf16[128,4224]{1,0:T(8,128)(2,1)S(1)} %collective-permute-done.37.mate, bf16[4096,896]{1,0:T(8,128)(2,1)} %bitcast.88, bf16[4096,896]{1,0:T(8,128)(2,1)} %bitcast.92, ...), custom_call_target="tpu_custom_call" | custom-call | flops 5637144576 | bytes 30408704 | tf_op jit(solution)/shard_map/pallas_call | solution.py:316
  161.9 4.1 %collective-permute-done.43 = bf16[64,4096]{1,0:T(8,128)(2,1)S(1)} collective-permute-done((bf16[64,4096]{1,0:T(8,128)(2,1)S(1)}, bf16[64,4096]{1,0:T(8,128)(2,1)S(1)}, u32[]{:S(2)}, u32[]{:S(2)}) %collective-permute-start.43) | collective-permute-done | bytes 524320 | tf_op jit(solution)/shard_map/ppermute | solution.py:20
  166.1 1.5 collective-permute-start.44
  167.8 1.3 collective-permute-start.49
  169.9 2.6 %collective-permute-done.42 = bf16[32,4096]{1,0:T(8,128)(2,1)S(1)} collective-permute-done((bf16[32,4096]{1,0:T(8,128)(2,1)S(1)}, bf16[32,4096]{1,0:T(8,128)(2,1)S(1)}, u32[]{:S(2)}, u32[]{:S(2)}) %collective-permute-start.42) | collective-permute-done | bytes 262176 | tf_op jit(solution)/shard_map/ppermute | solution.py:20
  172.6 2.9 %collective-permute-done.44 = bf16[32,4096]{1,0:T(8,128)(2,1)S(1)} collective-permute-done((bf16[32,4096]{1,0:T(8,128)(2,1)S(1)}, bf16[32,4096]{1,0:T(8,128)(2,1)S(1)}, u32[]{:S(2)}, u32[]{:S(2)}) %collective-permute-start.44) | collective-permute-done | bytes 262176 | tf_op jit(solution)/shard_map/ppermute | solution.py:20
  175.4 1.4 collective-permute-start.47
  177.0 3.2 %collective-permute-start.46 = (bf16[32,4096]{1,0:T(8,128)(2,1)S(1)}, bf16[32,4096]{1,0:T(8,128)(2,1)S(1)}, u32[]{:S(2)}, u32[]{:S(2)}) collective-permute-start(bf16[32,4096]{1,0:T(8,128)(2,1)S(1)} %add_convert_fusion.8), channel_id=1, source_target_pairs={{0,24},{4,28},{8,16},{12,20},{16,8},{20,12},{24,0},{28,4},{1,25},{... | collective-permute-start | bytes 786440 | tf_op jit(solution)/shard_map/ppermute | solution.py:20
  182.0 2.0 %collective-permute-done.47 = bf16[32,4096]{1,0:T(8,128)(2,1)S(1)} collective-permute-done((bf16[32,4096]{1,0:T(8,128)(2,1)S(1)}, bf16[32,4096]{1,0:T(8,128)(2,1)S(1)}, u32[]{:S(2)}, u32[]{:S(2)}) %collective-permute-start.47) | collective-permute-done | bytes 262176 | tf_op jit(solution)/shard_map/ppermute | solution.py:20
  184.2 1.4 collective-permute-start.50
  185.6 12.7 %collective-permute-done.45 = bf16[32,4096]{1,0:T(8,128)(2,1)S(1)} collective-permute-done((bf16[32,4096]{1,0:T(8,128)(2,1)S(1)}, bf16[32,4096]{1,0:T(8,128)(2,1)S(1)}, u32[]{:S(2)}, u32[]{:S(2)}) %collective-permute-start.45) | collective-permute-done | bytes 262176 | tf_op jit(solution)/shard_map/ppermute | solution.py:20
  (176 shorter events, 32.5 us)
Async XLA Ops:
  3.9 6.6 %collective-permute-start = (bf16[528,128]{1,0:T(8,128)(2,1)S(1)}, bf16[528,128]{1,0:T(8,128)(2,1)S(1)}, u32[]{:S(2)}, u32[]{:S(2)}) collective-permute-start(bf16[528,128]{1,0:T(8,128)(2,1)S(1)} %pad_maximum_fusion.1), channel_id=1, source_target_pairs={{0,4},{4,0},{8,12},{12,8},{16,20},{20,16},{24,28},{28,24},{1,5},{5... | collective-permute-start | bytes 405512 | tf_op jit(solution)/shard_map/ppermute | solution.py:20
  7.8 21.5 %collective-permute-start.4 = (bf16[384,512]{1,0:T(8,128)(2,1)}, bf16[384,512]{1,0:T(8,128)(2,1)}, u32[]{:S(2)}, u32[]{:S(2)}) collective-permute-start(bf16[384,512]{1,0:T(8,128)(2,1)} %slice.200), channel_id=1, source_target_pairs={{0,8},{4,12},{8,0},{12,4},{16,24},{20,28},{24,16},{28,20},{1,9},{5... | collective-permute-start | bytes 1179656 | tf_op jit(solution)/shard_map/ppermute | solution.py:20
  12.0 12.4 %collective-permute-start.1 = (bf16[528,128]{1,0:T(8,128)(2,1)}, bf16[528,128]{1,0:T(8,128)(2,1)S(1)}, u32[]{:S(2)}, u32[]{:S(2)}) collective-permute-start(bf16[528,128]{1,0:T(8,128)(2,1)} %pad_maximum_fusion.2), channel_id=1, source_target_pairs={{0,8},{4,12},{8,0},{12,4},{16,24},{20,28},{24,16},{28,20},{1,9},{5... | collective-permute-start | bytes 405512 | tf_op jit(solution)/shard_map/ppermute | solution.py:20
  13.8 11.2 %collective-permute-start.2 = (bf16[528,128]{1,0:T(8,128)(2,1)}, bf16[528,128]{1,0:T(8,128)(2,1)S(1)}, u32[]{:S(2)}, u32[]{:S(2)}) collective-permute-start(bf16[528,128]{1,0:T(8,128)(2,1)} %pad_maximum_fusion.2), channel_id=1, source_target_pairs={{0,16},{4,20},{8,24},{12,28},{16,0},{20,4},{24,8},{28,12},{1,17},{... | collective-permute-start | bytes 405512 | tf_op jit(solution)/shard_map/ppermute | solution.py:20
  16.4 12.9 %collective-permute-start.3 = (bf16[528,128]{1,0:T(8,128)(2,1)}, bf16[528,128]{1,0:T(8,128)(2,1)S(1)}, u32[]{:S(2)}, u32[]{:S(2)}) collective-permute-start(bf16[528,128]{1,0:T(8,128)(2,1)} %pad_maximum_fusion.2), channel_id=1, source_target_pairs={{0,24},{4,28},{8,16},{12,20},{16,8},{20,12},{24,0},{28,4},{1,25},{... | collective-permute-start | bytes 405512 | tf_op jit(solution)/shard_map/ppermute | solution.py:20
  30.1 5.0 %collective-permute-start.5 = (bf16[512,128]{1,0:T(8,128)(2,1)S(1)}, bf16[512,128]{1,0:T(8,128)(2,1)S(1)}, u32[]{:S(2)}, u32[]{:S(2)}) collective-permute-start(bf16[512,128]{1,0:T(8,128)(2,1)S(1)} %get-tuple-element.62), channel_id=1, source_target_pairs={{0,4},{4,0},{8,12},{12,8},{16,20},{20,16},{24,28},{28,24},{1,5},{5... | collective-permute-start | bytes 393224 | tf_op jit(solution)/shard_map/ppermute | solution.py:20
  36.7 10.8 %collective-permute-start.7 = (bf16[128,1024]{0,1:T(8,128)(2,1)S(1)}, bf16[128,1024]{0,1:T(8,128)(2,1)S(1)}, u32[]{:S(2)}, u32[]{:S(2)}) collective-permute-start(bf16[128,1024]{0,1:T(8,128)(2,1)S(1)} %pad_maximum_fusion), channel_id=1, source_target_pairs={{0,16},{4,20},{8,24},{12,28},{16,0},{20,4},{24,8},{28,12},{1,17},{... | collective-permute-start | bytes 786440 | tf_op jit(solution)/shard_map/ppermute | solution.py:20
  36.8 19.6 %collective-permute-start.9 = (bf16[640,512]{1,0:T(8,128)(2,1)S(1)}, bf16[640,512]{1,0:T(8,128)(2,1)}, u32[]{:S(2)}, u32[]{:S(2)}) collective-permute-start(bf16[640,512]{1,0:T(8,128)(2,1)S(1)} %slice.201), channel_id=1, source_target_pairs={{0,8},{4,12},{8,0},{12,4},{16,24},{20,28},{24,16},{28,20},{1,9},{5... | collective-permute-start | bytes 1966088 | tf_op jit(solution)/shard_map/ppermute | solution.py:20
  39.0 9.3 %collective-permute-start.6 = (bf16[128,1024]{0,1:T(8,128)(2,1)S(1)}, bf16[128,1024]{0,1:T(8,128)(2,1)S(1)}, u32[]{:S(2)}, u32[]{:S(2)}) collective-permute-start(bf16[128,1024]{0,1:T(8,128)(2,1)S(1)} %pad_maximum_fusion), channel_id=1, source_target_pairs={{0,4},{4,0},{8,12},{12,8},{16,20},{20,16},{24,28},{28,24},{1,5},{5... | collective-permute-start | bytes 786440 | tf_op jit(solution)/shard_map/ppermute | solution.py:20
  47.5 6.6 %collective-permute-start.8 = (bf16[128,1024]{0,1:T(8,128)(2,1)S(1)}, bf16[128,1024]{0,1:T(8,128)(2,1)S(1)}, u32[]{:S(2)}, u32[]{:S(2)}) collective-permute-start(bf16[128,1024]{0,1:T(8,128)(2,1)S(1)} %collective-permute-done.7), channel_id=1, source_target_pairs={{0,4},{4,0},{8,12},{12,8},{16,20},{20,16},{24,28},{28,24},{1,5},{5... | collective-permute-start | bytes 786440 | tf_op jit(solution)/shard_map/ppermute | solution.py:20
  61.2 8.6 %collective-permute-start.11 = (bf16[128,1024]{1,0:T(8,128)(2,1)S(1)}, bf16[128,1024]{1,0:T(8,128)(2,1)S(1)}, u32[]{:S(2)}, u32[]{:S(2)}) collective-permute-start(bf16[128,1024]{1,0:T(8,128)(2,1)S(1)} %slice.261), channel_id=1, source_target_pairs={{0,2},{1,3},{2,0},{3,1},{4,6},{5,7},{6,4},{7,5},{8,10},{9,11},{10,... | collective-permute-start | bytes 786440 | tf_op jit(solution)/shard_map/ppermute | solution.py:20
  63.9 5.8 %collective-permute-start.13 = (f32[128]{0:T(128)S(1)}, f32[128]{0:T(128)S(1)}, u32[]{:S(2)}, u32[]{:S(2)}) collective-permute-start(f32[128]{0:T(128)S(1)} %add.209), channel_id=1, source_target_pairs={{0,2},{1,3},{2,0},{3,1},{4,6},{5,7},{6,4},{7,5},{8,10},{9,11},{10,... | collective-permute-start | bytes 1544 | tf_op jit(solution)/shard_map/ppermute | solution.py:20
  69.8 4.5 %collective-permute-start.14 = (bf16[32,1024]{1,0:T(8,128)(2,1)S(1)}, bf16[32,1024]{1,0:T(8,128)(2,1)S(1)}, u32[]{:S(2)}, u32[]{:S(2)}) collective-permute-start(bf16[32,1024]{1,0:T(8,128)(2,1)S(1)} %get-tuple-element.126), channel_id=1, source_target_pairs={{0,4},{4,0},{8,12},{12,8},{16,20},{20,16},{24,28},{28,24},{1,5},{5... | collective-permute-start | bytes 196616 | tf_op jit(solution)/shard_map/ppermute | solution.py:20
  70.4 6.4 %collective-permute-start.15 = (bf16[32,1024]{1,0:T(8,128)(2,1)S(1)}, bf16[32,1024]{1,0:T(8,128)(2,1)S(1)}, u32[]{:S(2)}, u32[]{:S(2)}) collective-permute-start(bf16[32,1024]{1,0:T(8,128)(2,1)S(1)} %get-tuple-element.125), channel_id=1, source_target_pairs={{0,16},{4,20},{8,24},{12,28},{16,0},{20,4},{24,8},{28,12},{1,17},{... | collective-permute-start | bytes 196616 | tf_op jit(solution)/shard_map/ppermute | solution.py:20
  70.7 8.5 %collective-permute-start.16 = (bf16[32,1024]{1,0:T(8,128)(2,1)S(1)}, bf16[32,1024]{1,0:T(8,128)(2,1)S(1)}, u32[]{:S(2)}, u32[]{:S(2)}) collective-permute-start(bf16[32,1024]{1,0:T(8,128)(2,1)S(1)} %get-tuple-element.124), channel_id=1, source_target_pairs={{0,20},{4,16},{8,28},{12,24},{16,4},{20,0},{24,12},{28,8},{1,21},{... | collective-permute-start | bytes 196616 | tf_op jit(solution)/shard_map/ppermute | solution.py:20
  79.9 8.8 %collective-permute-start.17 = (bf16[32,4224]{1,0:T(8,128)(2,1)S(1)}, bf16[32,4224]{1,0:T(8,128)(2,1)S(1)}, u32[]{:S(2)}, u32[]{:S(2)}) collective-permute-start(bf16[32,4224]{1,0:T(8,128)(2,1)S(1)} %concatenate.40.refs_0_), channel_id=1, source_target_pairs={{0,4},{4,0},{8,12},{12,8},{16,20},{20,16},{24,28},{28,24},{1,5},{5... | collective-permute-start | bytes 811016 | tf_op jit(solution)/shard_map/ppermute | solution.py:20
  80.0 8.7 %collective-permute-start.18 = (bf16[32,4224]{1,0:T(8,128)(2,1)S(1)}, bf16[32,4224]{1,0:T(8,128)(2,1)S(1)}, u32[]{:S(2)}, u32[]{:S(2)}) collective-permute-start(bf16[32,4224]{1,0:T(8,128)(2,1)S(1)} %concatenate.40.refs_0_), channel_id=1, source_target_pairs={{0,2},{1,3},{2,0},{3,1},{4,6},{5,7},{6,4},{7,5},{8,10},{9,11},{10,... | collective-permute-start | bytes 811016 | tf_op jit(solution)/shard_map/ppermute | solution.py:20
  81.6 10.1 %collective-permute-start.19 = (bf16[32,4224]{1,0:T(8,128)(2,1)S(1)}, bf16[32,4224]{1,0:T(8,128)(2,1)S(1)}, u32[]{:S(2)}, u32[]{:S(2)}) collective-permute-start(bf16[32,4224]{1,0:T(8,128)(2,1)S(1)} %concatenate.40.refs_0_), channel_id=1, source_target_pairs={{0,6},{1,7},{2,4},{3,5},{4,2},{5,3},{6,0},{7,1},{8,14},{9,15},{10,... | collective-permute-start | bytes 811016 | tf_op jit(solution)/shard_map/ppermute | solution.py:344
  83.5 10.5 %collective-permute-start.20 = (bf16[32,4224]{1,0:T(8,128)(2,1)S(1)}, bf16[32,4224]{1,0:T(8,128)(2,1)S(1)}, u32[]{:S(2)}, u32[]{:S(2)}) collective-permute-start(bf16[32,4224]{1,0:T(8,128)(2,1)S(1)} %concatenate.40.refs_0_), channel_id=1, source_target_pairs={{0,16},{4,20},{8,24},{12,28},{16,0},{20,4},{24,8},{28,12},{1,17},{... | collective-permute-start | bytes 811016 | tf_op jit(solution)/shard_map/ppermute | solution.py:20
  94.2 15.8 %collective-permute-start.26 = (bf16[32,4224]{1,0:T(8,128)(2,1)S(1)}, bf16[32,4224]{1,0:T(8,128)(2,1)S(1)}, u32[]{:S(2)}, u32[]{:S(2)}) collective-permute-start(bf16[32,4224]{1,0:T(8,128)(2,1)S(1)} %concatenate.40.refs_0_), channel_id=1, source_target_pairs={{0,8},{4,12},{8,0},{12,4},{16,24},{20,28},{24,16},{28,20},{1,9},{5... | collective-permute-start | bytes 811016 | tf_op jit(solution)/shard_map/ppermute | solution.py:20
  94.3 15.7 %collective-permute-start.22 = (bf16[32,4224]{1,0:T(8,128)(2,1)S(1)}, bf16[32,4224]{1,0:T(8,128)(2,1)S(1)}, u32[]{:S(2)}, u32[]{:S(2)}) collective-permute-start(bf16[32,4224]{1,0:T(8,128)(2,1)S(1)} %collective-permute-done.20.refs_0_), channel_id=1, source_target_pairs={{0,4},{4,0},{8,12},{12,8},{16,20},{20,16},{24,28},{28,24},{1,5},{5... | collective-permute-start | bytes 811016 | tf_op jit(solution)/shard_map/ppermute | solution.py:20
  95.4 14.6 %collective-permute-start.23 = (bf16[32,4224]{1,0:T(8,128)(2,1)S(1)}, bf16[32,4224]{1,0:T(8,128)(2,1)S(1)}, u32[]{:S(2)}, u32[]{:S(2)}) collective-permute-start(bf16[32,4224]{1,0:T(8,128)(2,1)S(1)} %collective-permute-done.20.refs_0_), channel_id=1, source_target_pairs={{0,2},{1,3},{2,0},{3,1},{4,6},{5,7},{6,4},{7,5},{8,10},{9,11},{10,... | collective-permute-start | bytes 811016 | tf_op jit(solution)/shard_map/ppermute | solution.py:20
  96.9 13.2 %collective-permute-start.24 = (bf16[32,4224]{1,0:T(8,128)(2,1)S(1)}, bf16[32,4224]{1,0:T(8,128)(2,1)S(1)}, u32[]{:S(2)}, u32[]{:S(2)}) collective-permute-start(bf16[32,4224]{1,0:T(8,128)(2,1)S(1)} %collective-permute-done.20.refs_0_), channel_id=1, source_target_pairs={{0,6},{1,7},{2,4},{3,5},{4,2},{5,3},{6,0},{7,1},{8,14},{9,15},{10,... | collective-permute-start | bytes 811016 | tf_op jit(solution)/shard_map/ppermute | solution.py:344
  97.8 12.3 %collective-permute-start.25 = (bf16[32,4224]{1,0:T(8,128)(2,1)S(1)}, bf16[32,4224]{1,0:T(8,128)(2,1)S(1)}, u32[]{:S(2)}, u32[]{:S(2)}) collective-permute-start(bf16[32,4224]{1,0:T(8,128)(2,1)S(1)} %collective-permute-done.20.refs_0_), channel_id=1, source_target_pairs={{0,8},{4,12},{8,0},{12,4},{16,24},{20,28},{24,16},{28,20},{1,9},{5... | collective-permute-start | bytes 811016 | tf_op jit(solution)/shard_map/ppermute | solution.py:20
  110.2 4.1 %collective-permute-start.27 = (bf16[128,4224]{1,0:T(8,128)(2,1)S(1)}, bf16[128,4224]{1,0:T(8,128)(2,1)S(1)}, u32[]{:S(2)}, u32[]{:S(2)}) collective-permute-start(bf16[128,4224]{1,0:T(8,128)(2,1)S(1)} %shard_map.166.own), channel_id=1, source_target_pairs={{0,1},{1,0},{2,3},{3,2},{4,5},{5,4},{6,7},{7,6},{8,9},{9,8},{10,11... | collective-permute-start | bytes 3244040 | tf_op jit(solution)/shard_map/ppermute | solution.py:20
  110.3 16.0 %collective-permute-start.28 = (bf16[128,4096]{1,0:T(8,128)(2,1)S(1)}, bf16[128,4096]{1,0:T(8,128)(2,1)S(1)}, u32[]{:S(2)}, u32[]{:S(2)}) collective-permute-start(bf16[128,4096]{1,0:T(8,128)(2,1)S(1)} %get-tuple-element.82), channel_id=1, source_target_pairs={{0,1},{1,0},{2,3},{3,2},{4,5},{5,4},{6,7},{7,6},{8,9},{9,8},{10,11... | collective-permute-start | bytes 3145736 | tf_op jit(solution)/shard_map/ppermute | solution.py:20
  110.8 15.2 %collective-permute-start.29 = (bf16[32,4224]{1,0:T(8,128)(2,1)S(1)}, bf16[32,4224]{1,0:T(8,128)(2,1)S(1)}, u32[]{:S(2)}, u32[]{:S(2)}) collective-permute-start(bf16[32,4224]{1,0:T(8,128)(2,1)S(1)} %collective-permute-done.25.refs_0_), channel_id=1, source_target_pairs={{0,2},{1,3},{2,0},{3,1},{4,6},{5,7},{6,4},{7,5},{8,10},{9,11},{10,... | collective-permute-start | bytes 811016 | tf_op jit(solution)/shard_map/ppermute | solution.py:20
  112.3 14.0 %collective-permute-start.30 = (bf16[32,4224]{1,0:T(8,128)(2,1)S(1)}, bf16[32,4224]{1,0:T(8,128)(2,1)S(1)}, u32[]{:S(2)}, u32[]{:S(2)}) collective-permute-start(bf16[32,4224]{1,0:T(8,128)(2,1)S(1)} %collective-permute-done.25.refs_0_), channel_id=1, source_target_pairs={{0,4},{4,0},{8,12},{12,8},{16,20},{20,16},{24,28},{28,24},{1,5},{5... | collective-permute-start | bytes 811016 | tf_op jit(solution)/shard_map/ppermute | solution.py:20
  113.1 13.1 %collective-permute-start.31 = (bf16[32,4224]{1,0:T(8,128)(2,1)S(1)}, bf16[32,4224]{1,0:T(8,128)(2,1)S(1)}, u32[]{:S(2)}, u32[]{:S(2)}) collective-permute-start(bf16[32,4224]{1,0:T(8,128)(2,1)S(1)} %collective-permute-done.25.refs_0_), channel_id=1, source_target_pairs={{0,6},{1,7},{2,4},{3,5},{4,2},{5,3},{6,0},{7,1},{8,14},{9,15},{10,... | collective-permute-start | bytes 811016 | tf_op jit(solution)/shard_map/ppermute | solution.py:344
  114.3 16.6 %collective-permute-start.35 = (bf16[32,4224]{1,0:T(8,128)(2,1)S(1)}, bf16[32,4224]{1,0:T(8,128)(2,1)S(1)}, u32[]{:S(2)}, u32[]{:S(2)}) collective-permute-start(bf16[32,4224]{1,0:T(8,128)(2,1)S(1)} %collective-permute-done.26.refs_0_), channel_id=1, source_target_pairs={{0,2},{1,3},{2,0},{3,1},{4,6},{5,7},{6,4},{7,5},{8,10},{9,11},{10,... | collective-permute-start | bytes 811016 | tf_op jit(solution)/shard_map/ppermute | solution.py:20
  126.3 7.1 %collective-permute-start.32 = (bf16[128,4224]{1,0:T(8,128)(2,1)S(1)}, bf16[128,4224]{1,0:T(8,128)(2,1)S(1)}, u32[]{:S(2)}, u32[]{:S(2)}) collective-permute-start(bf16[128,4224]{1,0:T(8,128)(2,1)S(1)} %shard_map.168.own), channel_id=1, source_target_pairs={{0,1},{1,0},{2,3},{3,2},{4,5},{5,4},{6,7},{7,6},{8,9},{9,8},{10,11... | collective-permute-start | bytes 3244040 | tf_op jit(solution)/shard_map/ppermute | solution.py:20
  126.4 18.4 %collective-permute-start.33 = (bf16[128,4096]{1,0:T(8,128)(2,1)S(1)}, bf16[128,4096]{1,0:T(8,128)(2,1)S(1)}, u32[]{:S(2)}, u32[]{:S(2)}) collective-permute-start(bf16[128,4096]{1,0:T(8,128)(2,1)S(1)} %get-tuple-element.92), channel_id=1, source_target_pairs={{0,1},{1,0},{2,3},{3,2},{4,5},{5,4},{6,7},{7,6},{8,9},{9,8},{10,11... | collective-permute-start | bytes 3145736 | tf_op jit(solution)/shard_map/ppermute | solution.py:20
  130.9 13.9 %collective-permute-start.36 = (bf16[64,4224]{1,0:T(8,128)(2,1)S(1)}, bf16[64,4224]{1,0:T(8,128)(2,1)S(1)}, u32[]{:S(2)}, u32[]{:S(2)}) collective-permute-start(bf16[64,4224]{1,0:T(8,128)(2,1)S(1)} %shard_map.170), channel_id=1, source_target_pairs={{0,4},{4,0},{8,12},{12,8},{16,20},{20,16},{24,28},{28,24},{1,5},{5... | collective-permute-start | bytes 1622024 | tf_op jit(solution)/shard_map/ppermute | solution.py:20
  131.9 12.9 %collective-permute-start.34 = (bf16[64,4096]{1,0:T(8,128)(2,1)S(1)}, bf16[64,4096]{1,0:T(8,128)(2,1)S(1)}, u32[]{:S(2)}, u32[]{:S(2)}) collective-permute-start(bf16[64,4096]{1,0:T(8,128)(2,1)S(1)} %add_convert_fusion.2), channel_id=1, source_target_pairs={{0,2},{1,3},{2,0},{3,1},{4,6},{5,7},{6,4},{7,5},{8,10},{9,11},{10,... | collective-permute-start | bytes 1572872 | tf_op jit(solution)/shard_map/ppermute | solution.py:20
  144.9 5.6 %collective-permute-start.37 = (bf16[128,4224]{1,0:T(8,128)(2,1)S(1)}, bf16[128,4224]{1,0:T(8,128)(2,1)S(1)}, u32[]{:S(2)}, u32[]{:S(2)}) collective-permute-start(bf16[128,4224]{1,0:T(8,128)(2,1)S(1)} %shard_map.171.own), channel_id=1, source_target_pairs={{0,1},{1,0},{2,3},{3,2},{4,5},{5,4},{6,7},{7,6},{8,9},{9,8},{10,11... | collective-permute-start | bytes 3244040 | tf_op jit(solution)/shard_map/ppermute | solution.py:20
  145.0 4.2 %collective-permute-start.38 = (bf16[128,4096]{1,0:T(8,128)(2,1)S(1)}, bf16[128,4096]{1,0:T(8,128)(2,1)S(1)}, u32[]{:S(2)}, u32[]{:S(2)}) collective-permute-start(bf16[128,4096]{1,0:T(8,128)(2,1)S(1)} %get-tuple-element.97), channel_id=1, source_target_pairs={{0,1},{1,0},{2,3},{3,2},{4,5},{5,4},{6,7},{7,6},{8,9},{9,8},{10,11... | collective-permute-start | bytes 3145736 | tf_op jit(solution)/shard_map/ppermute | solution.py:20
  145.6 15.2 %collective-permute-start.39 = (bf16[32,4096]{1,0:T(8,128)(2,1)S(1)}, bf16[32,4096]{1,0:T(8,128)(2,1)S(1)}, u32[]{:S(2)}, u32[]{:S(2)}) collective-permute-start(bf16[32,4096]{1,0:T(8,128)(2,1)S(1)} %add_convert_fusion.13), channel_id=1, source_target_pairs={{0,4},{4,0},{8,12},{12,8},{16,20},{20,16},{24,28},{28,24},{1,5},{5... | collective-permute-start | bytes 786440 | tf_op jit(solution)/shard_map/ppermute | solution.py:20
  146.9 13.8 %collective-permute-start.40 = (bf16[64,4096]{1,0:T(8,128)(2,1)S(1)}, bf16[64,4096]{1,0:T(8,128)(2,1)S(1)}, u32[]{:S(2)}, u32[]{:S(2)}) collective-permute-start(bf16[64,4096]{1,0:T(8,128)(2,1)S(1)} %add_convert_fusion.1), channel_id=1, source_target_pairs={{0,2},{1,3},{2,0},{3,1},{4,6},{5,7},{6,4},{7,5},{8,10},{9,11},{10,... | collective-permute-start | bytes 1572872 | tf_op jit(solution)/shard_map/ppermute | solution.py:20
  149.3 16.7 %collective-permute-start.43 = (bf16[64,4096]{1,0:T(8,128)(2,1)S(1)}, bf16[64,4096]{1,0:T(8,128)(2,1)S(1)}, u32[]{:S(2)}, u32[]{:S(2)}) collective-permute-start(bf16[64,4096]{1,0:T(8,128)(2,1)S(1)} %add_convert_fusion), channel_id=1, source_target_pairs={{0,4},{4,0},{8,12},{12,8},{16,20},{20,16},{24,28},{28,24},{1,5},{5... | collective-permute-start | bytes 1572872 | tf_op jit(solution)/shard_map/ppermute | solution.py:20
  160.8 6.9 %collective-permute-start.41 = (bf16[128,4096]{1,0:T(8,128)(2,1)S(1)}, bf16[128,4096]{1,0:T(8,128)(2,1)S(1)}, u32[]{:S(2)}, u32[]{:S(2)}) collective-permute-start(bf16[128,4096]{1,0:T(8,128)(2,1)S(1)} %get-tuple-element.104), channel_id=1, source_target_pairs={{0,1},{1,0},{2,3},{3,2},{4,5},{5,4},{6,7},{7,6},{8,9},{9,8},{10,11... | collective-permute-start | bytes 3145736 | tf_op jit(solution)/shard_map/ppermute | solution.py:20
  161.0 11.6 %collective-permute-start.42 = (bf16[32,4096]{1,0:T(8,128)(2,1)S(1)}, bf16[32,4096]{1,0:T(8,128)(2,1)S(1)}, u32[]{:S(2)}, u32[]{:S(2)}) collective-permute-start(bf16[32,4096]{1,0:T(8,128)(2,1)S(1)} %add_convert_fusion.11), channel_id=1, source_target_pairs={{0,4},{4,0},{8,12},{12,8},{16,20},{20,16},{24,28},{28,24},{1,5},{5... | collective-permute-start | bytes 786440 | tf_op jit(solution)/shard_map/ppermute | solution.py:20
  166.1 9.3 %collective-permute-start.44 = (bf16[32,4096]{1,0:T(8,128)(2,1)S(1)}, bf16[32,4096]{1,0:T(8,128)(2,1)S(1)}, u32[]{:S(2)}, u32[]{:S(2)}) collective-permute-start(bf16[32,4096]{1,0:T(8,128)(2,1)S(1)} %add_convert_fusion.10), channel_id=1, source_target_pairs={{0,2},{1,3},{2,0},{3,1},{4,6},{5,7},{6,4},{7,5},{8,10},{9,11},{10,... | collective-permute-start | bytes 786440 | tf_op jit(solution)/shard_map/ppermute | solution.py:20
  167.8 13.8 %collective-permute-start.49 = (bf16[32,4096]{1,0:T(8,128)(2,1)S(1)}, bf16[32,4096]{1,0:T(8,128)(2,1)S(1)}, u32[]{:S(2)}, u32[]{:S(2)}) collective-permute-start(bf16[32,4096]{1,0:T(8,128)(2,1)S(1)} %get-tuple-element.120), channel_id=1, source_target_pairs={{0,6},{1,7},{2,4},{3,5},{4,2},{5,3},{6,0},{7,1},{8,14},{9,15},{10,... | collective-permute-start | bytes 786440 | tf_op jit(solution)/shard_map/ppermute | solution.py:344
  169.1 12.9 %collective-permute-start.48 = (bf16[32,4096]{1,0:T(8,128)(2,1)S(1)}, bf16[32,4096]{1,0:T(8,128)(2,1)S(1)}, u32[]{:S(2)}, u32[]{:S(2)}) collective-permute-start(bf16[32,4096]{1,0:T(8,128)(2,1)S(1)} %get-tuple-element.121), channel_id=1, source_target_pairs={{0,4},{4,0},{8,12},{12,8},{16,20},{20,16},{24,28},{28,24},{1,5},{5... | collective-permute-start | bytes 786440 | tf_op jit(solution)/shard_map/ppermute | solution.py:20
  175.4 8.6 %collective-permute-start.47 = (bf16[32,4096]{1,0:T(8,128)(2,1)S(1)}, bf16[32,4096]{1,0:T(8,128)(2,1)S(1)}, u32[]{:S(2)}, u32[]{:S(2)}) collective-permute-start(bf16[32,4096]{1,0:T(8,128)(2,1)S(1)} %get-tuple-element.112), channel_id=1, source_target_pairs={{0,2},{1,3},{2,0},{3,1},{4,6},{5,7},{6,4},{7,5},{8,10},{9,11},{10,... | collective-permute-start | bytes 786440 | tf_op jit(solution)/shard_map/ppermute | solution.py:20
  177.0 8.6 %collective-permute-start.46 = (bf16[32,4096]{1,0:T(8,128)(2,1)S(1)}, bf16[32,4096]{1,0:T(8,128)(2,1)S(1)}, u32[]{:S(2)}, u32[]{:S(2)}) collective-permute-start(bf16[32,4096]{1,0:T(8,128)(2,1)S(1)} %add_convert_fusion.8), channel_id=1, source_target_pairs={{0,24},{4,28},{8,16},{12,20},{16,8},{20,12},{24,0},{28,4},{1,25},{... | collective-permute-start | bytes 786440 | tf_op jit(solution)/shard_map/ppermute | solution.py:20
  180.4 17.9 %collective-permute-start.45 = (bf16[32,4096]{1,0:T(8,128)(2,1)S(1)}, bf16[32,4096]{1,0:T(8,128)(2,1)S(1)}, u32[]{:S(2)}, u32[]{:S(2)}) collective-permute-start(bf16[32,4096]{1,0:T(8,128)(2,1)S(1)} %add_convert_fusion.9), channel_id=1, source_target_pairs={{0,16},{4,20},{8,24},{12,28},{16,0},{20,4},{24,8},{28,12},{1,17},{... | collective-permute-start | bytes 786440 | tf_op jit(solution)/shard_map/ppermute | solution.py:20
  184.2 14.1 %collective-permute-start.50 = (bf16[32,4096]{1,0:T(8,128)(2,1)S(1)}, bf16[32,4096]{1,0:T(8,128)(2,1)S(1)}, u32[]{:S(2)}, u32[]{:S(2)}) collective-permute-start(bf16[32,4096]{1,0:T(8,128)(2,1)S(1)} %add_convert_fusion.5), channel_id=1, source_target_pairs={{0,8},{4,12},{8,0},{12,4},{16,24},{20,28},{24,16},{28,20},{1,9},{5... | collective-permute-start | bytes 786440 | tf_op jit(solution)/shard_map/ppermute | solution.py:20
  (16 other events, 171.4 us)
